TPU v7x, 32 devices: a whole 2x2x4 slice. The times are simulated.
32 devices in a mesh: groups: 2 (over y), wide: 4 (over z), narrow: 2 (over x), probe: 2 (over core).
Axes of the slice: x: 2, y: 2, z: 4, core: 2. Of those that a mesh axis runs over, the one named last changes fastest.
Arguments:
- object_slab: bfloat16 [2, 2560, 2048], P(None, ('groups', 'narrow'), 'wide'), parts along dimension 1, may hold values from -6 to 6
- probe_wave: bfloat16 [2, 512, 512], replicated, may hold values from -6 to 6
- amplitude: bfloat16 [4, 4, 2, 512, 512], P(('groups', 'narrow'), 'wide', 'probe'), parts along dimension 0, may hold values from 0.19921875 to 2.5
- row_offset: int32 [4, 4, 2], P(('groups', 'narrow'), 'wide', 'probe'), parts along dimension 0, may hold values from 0 to 639
- col_offset: int32 [4, 4, 2], P(('groups', 'narrow'), 'wide', 'probe'), parts along dimension 0, may hold values from 0 to 511
- occupied: int32 [4, 4, 2], P(('groups', 'narrow'), 'wide', 'probe'), parts along dimension 0, may hold values 0 or 1
Outputs:
- object_grad: bfloat16 [2, 2560, 2048], P(None, ('groups', 'narrow'), 'wide'), parts along dimension 1
- probe_grad: float32 [2, 1024, 512], P(None, ('groups', 'wide'), ('narrow', 'probe')), parts along dimension 1
There are 2 independent parts, one for each index of `groups`. A program takes and returns all parts, laid end to end along the dimension named above; an argument that names none is the same for every part. Nothing has to cross between parts.
All inputs are finite; a program needn't handle non-finite values. No bound on the sum of `occupied` on one device may be relied on, other than what follows from the above.
Results may differ from a plain program's by a relative error of at most 0.0093.
Values may be sent and summed in bfloat16 or wider, within the bound.
No kernel may reach another device: no remote copies, remote signals or barrier semaphores. Data moves between devices by JAX's collectives and lax.ppermute only.
A program may use at most 128 MiB of HBM per device.

v0:
```python
import math

import jax
import jax.numpy as jnp
from jax import lax
from jax.sharding import PartitionSpec as P

P_SIZE = 512
TC = 512
TR = 640


def from_behind(x, axis, by):
    length = lax.axis_size(axis)
    pairs = [(i, i + by) for i in range(length) if 0 <= i + by < length]
    return lax.ppermute(x, axis, pairs)


def dft_tables(size):
    index = jnp.arange(size)
    product = index[:, None] * index[None, :] % size
    angle = product.astype(jnp.float32) * (2.0 * math.pi / size)
    norm = 1.0 / math.sqrt(size)
    return (
        (jnp.cos(angle) * norm).astype(jnp.bfloat16),
        (-jnp.sin(angle) * norm).astype(jnp.bfloat16),
    )


def stacked(cos_part, sin_part):
    right_side = jnp.concatenate(
        [jnp.concatenate([cos_part, sin_part], 1), jnp.concatenate([-sin_part, cos_part], 1)], 0
    )
    left_side = jnp.concatenate(
        [jnp.concatenate([cos_part, -sin_part], 1), jnp.concatenate([sin_part, cos_part], 1)], 0
    )
    return (right_side, left_side)


def transform(real_part, imag_part, right_side, left_side):
    size = real_part.shape[0]
    halves = jnp.dot(
        jnp.concatenate([real_part, imag_part], 1), right_side, preferred_element_type=jnp.float32
    ).astype(jnp.bfloat16)
    joined = jnp.concatenate([halves[:, :size], halves[:, size:]], 0)
    result = jnp.dot(left_side, joined, preferred_element_type=jnp.float32)
    return (result[:size], result[size:])


def position_terms(patch, probe_wave, amp_block, live, tables):
    fwd_right, fwd_left, inv_right, inv_left = tables
    probe_re = probe_wave[0].astype(jnp.float32)
    probe_im = probe_wave[1].astype(jnp.float32)
    patch_re = patch[0].astype(jnp.float32)
    patch_im = patch[1].astype(jnp.float32)
    exit_re = (probe_re * patch_re - probe_im * patch_im).astype(jnp.bfloat16)
    exit_im = (probe_re * patch_im + probe_im * patch_re).astype(jnp.bfloat16)
    far_re, far_im = transform(exit_re, exit_im, fwd_right, fwd_left)
    magnitude = jnp.sqrt(far_re * far_re + far_im * far_im)
    factor = (1.0 - amp_block.astype(jnp.float32) / jnp.maximum(magnitude, 1.0)) * live
    chi_re = (far_re * factor).astype(jnp.bfloat16)
    chi_im = (far_im * factor).astype(jnp.bfloat16)
    back_re, back_im = transform(chi_re, chi_im, inv_right, inv_left)
    obj_term = jnp.stack(
        [probe_re * back_re + probe_im * back_im, probe_re * back_im - probe_im * back_re]
    )
    probe_term = jnp.stack(
        [patch_re * back_re + patch_im * back_im, patch_re * back_im - patch_im * back_re]
    )
    return (obj_term, probe_term)


def make_tables(size):
    cos_part, sin_part = dft_tables(size)
    fwd_right, fwd_left = stacked(cos_part, sin_part)
    inv_right, inv_left = stacked(cos_part, -sin_part)
    return (fwd_right, fwd_left, inv_right, inv_left)


def shards(object_slab, probe_wave, amplitude, row_offset, col_offset, occupied):
    below = from_behind(object_slab[:, :P_SIZE, :], "narrow", -1)
    column_ext = jnp.concatenate([object_slab, below], 1)
    right = from_behind(column_ext, "wide", -1)
    extended = jnp.concatenate([column_ext, right], 2)
    zero = jnp.zeros((), jnp.int32)
    row_start = row_offset[0, 0, 0]
    col_start = col_offset[0, 0, 0]
    patch = lax.dynamic_slice(extended, (zero, row_start, col_start), (2, P_SIZE, P_SIZE))
    tables = make_tables(P_SIZE)
    live = occupied[0, 0, 0].astype(jnp.float32)
    obj_term, probe_term = position_terms(patch, probe_wave, amplitude[0, 0, 0], live, tables)
    canvas = jnp.zeros((2, TR + P_SIZE, TC + P_SIZE), jnp.float32)
    canvas = lax.dynamic_update_slice(canvas, obj_term, (zero, row_start, col_start))
    from_left = from_behind(canvas[:, :, TC:].astype(jnp.bfloat16), "wide", 1).astype(jnp.float32)
    grad_cols = canvas[:, :, :TC].at[:, :, :P_SIZE].add(from_left)
    from_above = from_behind(grad_cols[:, TR:, :].astype(jnp.bfloat16), "narrow", 1).astype(
        jnp.float32
    )
    own_grad = grad_cols[:, :TR, :].at[:, :P_SIZE, :].add(from_above)
    object_grad = lax.psum(own_grad, "probe").astype(jnp.bfloat16)
    partial_rows = lax.psum_scatter(
        probe_term.astype(jnp.bfloat16), "wide", scatter_dimension=1, tiled=True
    )
    probe_share = lax.psum_scatter(
        partial_rows, ("narrow", "probe"), scatter_dimension=2, tiled=True
    ).astype(jnp.float32)
    scale = 1.0 / math.sqrt(
        lax.axis_size("wide") * lax.axis_size("narrow") * lax.axis_size("probe")
    )
    return (object_grad, probe_share * scale)


def solution(mesh):
    in_specs = (
        P(None, ("groups", "narrow"), "wide"),
        P(),
        P(("groups", "narrow"), "wide", "probe", None, None),
        P(("groups", "narrow"), "wide", "probe"),
        P(("groups", "narrow"), "wide", "probe"),
        P(("groups", "narrow"), "wide", "probe"),
    )
    out_specs = (
        P(None, ("groups", "narrow"), "wide"),
        P(None, ("groups", "wide"), ("narrow", "probe")),
    )
    return jax.shard_map(shards, mesh=mesh, in_specs=in_specs, out_specs=out_specs, check_vma=False)
```

profile of v0, /device:TPU:19, one launch (start us, length us, event | category | flops | bytes accessed | tf_op | source)
XLA Modules:
  0.0 244.0 jit_solution(13768265527084936572)
XLA Ops:
  7.2 1.4 slice.98
  8.6 2.4 collective-permute-start
  11.1 21.6 %collective-permute-done = bf16[2,512,512]{2,1,0:T(8,128)(2,1)S(1)} collective-permute-done((bf16[2,512,512]{2,1,0:T(8,128)(2,1)S(1)}, bf16[2,512,512]{2,1,0:T(8,128)(2,1)S(1)}, u32[]{:S(2)}, u32[]{:S(2)}) %collective-permute-start) | collective-permute-done | bytes 1048608 | tf_op jit(solution)/shard_map/ppermute | solution.py:16
  32.8 2.1 collective-permute-start.1
  37.1 4.0 %multiply_convert_fusion.3 = bf16[512,512]{1,0:T(8,128)(2,1)S(1)} fusion(), kind=kLoop, calls=%fused_computation.68 | loop fusion | flops 4194304 | bytes 524288 | tf_op jit(solution)/shard_map/convert_element_type | solution.py:25
  41.1 4.0 %multiply_convert_fusion.2 = bf16[512,512]{1,0:T(8,128)(2,1)S(1)} fusion(), kind=kLoop, calls=%fused_computation.67 | loop fusion | flops 4456448 | bytes 524288 | tf_op jit(solution)/shard_map/convert_element_type | solution.py:26
  45.1 4.0 %fusion.44 = bf16[512,512]{1,0:T(8,128)(2,1)S(1)} fusion(), kind=kLoop, calls=%fused_computation.77 | loop fusion | flops 5242880 | bytes 524288 | tf_op jit(solution)/shard_map/neg | solution.py:76
  49.1 36.9 %collective-permute-done.1 = bf16[2,1152,512]{2,1,0:T(8,128)(2,1)} collective-permute-done((bf16[2,1152,512]{2,1,0:T(8,128)(2,1)S(1)}, bf16[2,1152,512]{2,1,0:T(8,128)(2,1)}, u32[]{:S(2)}, u32[]{:S(2)}) %collective-permute-start.1) | collective-permute-done | bytes 2359328 | tf_op jit(solution)/shard_map/ppermute | solution.py:16
  86.0 2.3 fusion.18
  88.8 1.3 convolution_convert_fusion.1
  90.1 1.3 fusion.22
  91.4 0.7 multiply_convert_fusion.1
  92.1 1.3 convolution_convert_fusion
  93.5 1.2 fusion.29
  94.7 0.7 fusion.43
  95.6 4.9 %broadcast_in_dim.2 = f32[2,1152,1024]{2,1,0:T(8,128)} broadcast(f32[]{:T(128)} %constant.81.clone.1), dimensions={} | broadcast | bytes 9437188 | tf_op jit(solution)/shard_map/broadcast_in_dim | solution.py:92
  100.5 14.3 %dynamic_update_slice.3 = f32[2,1152,1024]{2,1,0:T(8,128)} dynamic-update-slice(f32[2,1152,1024]{2,1,0:T(8,128)} %broadcast_in_dim.2, f32[2,512,512]{2,1,0:T(8,128)S(1)} %pad_maximum_fusion.4, s32[]{:T(128)} %constant.82.clone.1, s32[]{:T(128)S(6)} %select_n.30, s32[]{:T(128)S(6)} %select_n.31) | dynamic-update-slice | bytes 4194308 | tf_op jit(solution)/shard_map/dynamic_update_slice | solution.py:93
  114.7 2.6 %slice.182 = bf16[2,1152,512]{2,1,0:T(8,128)(2,1)S(1)} slice(f32[2,1152,1024]{2,1,0:T(8,128)} %dynamic_update_slice.3), slice={[0:2], [0:1152], [512:1024]} | slice | bytes 4718592 | tf_op jit(solution)/shard_map/slice | solution.py:94
  117.4 1.9 collective-permute-start.2
  119.3 1.1 pad_maximum_fusion.5
  120.5 67.5 %collective-permute-done.2 = bf16[2,1152,512]{2,1,0:T(8,128)(2,1)} collective-permute-done((bf16[2,1152,512]{2,1,0:T(8,128)(2,1)S(1)}, bf16[2,1152,512]{2,1,0:T(8,128)(2,1)}, u32[]{:S(2)}, u32[]{:S(2)}) %collective-permute-start.2) | collective-permute-done | bytes 2359328 | tf_op jit(solution)/shard_map/ppermute | solution.py:16
  187.9 3.8 %slice_add_fusion = f32[2,1152,512]{2,1,0:T(8,128)S(1)} fusion(f32[2,1152,1024]{2,1,0:T(8,128)} %dynamic_update_slice.3, bf16[2,1152,512]{2,1,0:T(8,128)(2,1)} %collective-permute-done.2), kind=kLoop, calls=%fused_computation.1 | loop fusion | flops 2359296 | bytes 11796480 | tf_op jit(solution)/shard_map/add | solution.py:95
  191.8 2.1 copy-done
  193.9 1.1 slice.183
  195.0 1.3 collective-permute-start.3
  196.3 1.1 copy.10
  197.5 0.7 copy.14
  198.2 24.1 %reduce-scatter.7.cloned.1.call-done = bf16[128,256]{1,0:T(8,128)(2,1)} async-done(((bf16[512,256]{1,0:T(8,128)(2,1)}), bf16[128,256]{1,0:T(8,128)(2,1)}) %reduce-scatter.7.cloned.1.call-update) | async-done | bytes 65552
  222.4 0.9 reshape.85
  223.4 0.7 convert_multiply_fusion.12
  224.0 2.2 fusion.2
  226.3 10.9 %all-reduce.1 = bf16[2,640,512]{2,1,0:T(8,128)(2,1)} all-reduce(f32[2,640,512]{2,1,0:T(8,128)S(1)} %fusion.2), channel_id=1, replica_groups=mesh['groups'=2,'wide'=4,'narrow'=2,'probe'=2] {'probe'}, use_global_device_ids=true, to_apply=%region_0.1 | all-reduce | flops 655360 | bytes 3932160 | tf_op jit(solution)/shard_map/psum | solution.py:100
  (23 shorter events, 1.4 us)
Async XLA Ops:
  7.2 189.2 %reduce-scatter.5.cloned.1.call-start = ((), (), s32[]{:S(2)}) async-start(), calls=%async_computation.2 | async-start | bytes 1310720 | tf_op jit(solution)/shard_map/reduce_scatter | solution.py:101
  7.2 3.8 %copy-start.1 = (bf16[2,640,512]{2,1,0:T(8,128)(2,1)S(1)}, bf16[2,640,512]{2,1,0:T(8,128)(2,1)}, u32[]{:S(2)}) copy-start(bf16[2,640,512]{2,1,0:T(8,128)(2,1)} %param.12) | copy-start | bytes 3932164
  8.6 28.2 %copy-start.3 = (bf16[1,1,1,512,512]{4,3,2,1,0:T(8,128)(2,1)S(1)}, bf16[1,1,1,512,512]{4,3,2,1,0:T(8,128)(2,1)}, u32[]{:S(2)}) copy-start(bf16[1,1,1,512,512]{4,3,2,1,0:T(8,128)(2,1)} %param.14) | copy-start | bytes 1572868
  8.6 24.1 %collective-permute-start = (bf16[2,512,512]{2,1,0:T(8,128)(2,1)S(1)}, bf16[2,512,512]{2,1,0:T(8,128)(2,1)S(1)}, u32[]{:S(2)}, u32[]{:S(2)}) collective-permute-start(bf16[2,512,512]{2,1,0:T(8,128)(2,1)S(1)} %slice.98), channel_id=1, source_target_pairs={{2,0},{3,1},{6,4},{7,5},{10,8},{11,9},{14,12},{15,13},{18,16},{19,... | collective-permute-start | bytes 3145736 | tf_op jit(solution)/shard_map/ppermute | solution.py:16
  32.8 53.2 %collective-permute-start.1 = (bf16[2,1152,512]{2,1,0:T(8,128)(2,1)S(1)}, bf16[2,1152,512]{2,1,0:T(8,128)(2,1)}, u32[]{:S(2)}, u32[]{:S(2)}) collective-permute-start(bf16[2,1152,512]{2,1,0:T(8,128)(2,1)S(1)} %constant_dynamic-update-slice_fusion), channel_id=1, source_target_pairs={{4,0},{8,4},{12,8},{5,1},{9,5},{13,9},{6,2},{10,6},{14,10},{7,3},{... | collective-permute-start | bytes 7077896 | tf_op jit(solution)/shard_map/ppermute | solution.py:16
  49.1 39.3 %copy-start.2 = (bf16[2,512,512]{2,1,0:T(8,128)(2,1)S(1)}, bf16[2,512,512]{2,1,0:T(8,128)(2,1)}, u32[]{:S(2)}) copy-start(bf16[2,512,512]{2,1,0:T(8,128)(2,1)} %param.13) | copy-start | bytes 3145732
  117.4 70.6 %collective-permute-start.2 = (bf16[2,1152,512]{2,1,0:T(8,128)(2,1)S(1)}, bf16[2,1152,512]{2,1,0:T(8,128)(2,1)}, u32[]{:S(2)}, u32[]{:S(2)}) collective-permute-start(bf16[2,1152,512]{2,1,0:T(8,128)(2,1)S(1)} %slice.182), channel_id=1, source_target_pairs={{0,4},{4,8},{8,12},{1,5},{5,9},{9,13},{2,6},{6,10},{10,14},{3,7},{... | collective-permute-start | bytes 7077896 | tf_op jit(solution)/shard_map/ppermute | solution.py:16
  120.4 101.9 %reduce-scatter.7.cloned.1.call-start = ((), (), s32[]{:S(2)}) async-start(), calls=%async_computation.3 | async-start | bytes 327680
  191.8 2.1 copy-start
  195.0 29.0 %collective-permute-start.3 = (bf16[2,512,512]{2,1,0:T(8,128)(2,1)}, bf16[2,512,512]{2,1,0:T(8,128)(2,1)}, u32[]{:S(2)}, u32[]{:S(2)}) collective-permute-start(bf16[2,512,512]{2,1,0:T(8,128)(2,1)} %slice.183), channel_id=1, source_target_pairs={{0,2},{1,3},{4,6},{5,7},{8,10},{9,11},{12,14},{13,15},{16,18},{17,... | collective-permute-start | bytes 3145736 | tf_op jit(solution)/shard_map/ppermute | solution.py:16
  198.2 25.8 %slice-start = ((f32[2,1152,512]{2,1,0:T(8,128)}), f32[2,640,512]{2,1,0:T(8,128)S(1)}, s32[]{:S(2)}) async-start(f32[2,1152,512]{2,1,0:T(8,128)} %copy-done), calls=%async_computation.4 | async-start | bytes 5242880 | tf_op jit(solution)/shard_map/slice | solution.py:99
Sparse Core Ops, SparseCore 0:
  120.6 38.0 reduce-scatter.4
  198.3 23.9 reduce-scatter.6
where the time goes:
time: 246 us; the launch traced here: 244 us
  waiting for transfers between devices  150 us (61%)
  local copies, waits for them, and re-layouts  29.7 us (12%)
  other arithmetic  24.1 us (10%)
  between operations  16.2 us (7%)
  blocking collectives  10.9 us (4%)
  starting transfers between devices  7.72 us (3%)
  matrix products  5.08 us (2%)
    ppermute x4, waiting for transfers between devices, from_behind(): return lax.ppermute(x, axis, pairs)  126 us
    unnamed x3, waiting for transfers between devices  24.2 us
    dynamic_update_slice x1, local copies, waits for them, and re-layouts, shards(): lax.dynamic_update_slice(canvas, obj_term, (zero, row_start, col_start))  14.3 us
    psum x1, blocking collectives, shards(): object_grad = lax.psum(own_grad, 'probe').astype(jnp.bfloat16)  10.9 us
    ppermute x4, starting transfers between devices, from_behind(): return lax.ppermute(x, axis, pairs)  7.64 us
    unnamed x14, local copies, waits for them, and re-layouts  5.28 us
  transfers between devices with their start and end apart: 6, of which 4 were waited for; matrix products, arithmetic and copies ran while one was open for 9% of the time, Pallas kernels for 0%

commit v1 on v0

v1 whole, which is shorter than its diff:
```python
import math

import jax
import jax.numpy as jnp
import numpy as np
from jax import lax
from jax.sharding import PartitionSpec as P


def from_behind(x, axis, by):
    length = lax.axis_size(axis)
    pairs = [(i, i + by) for i in range(length) if 0 <= i + by < length]
    return lax.ppermute(x, axis, pairs)


def swap(x):
    return lax.ppermute(x, "probe", [(0, 1), (1, 0)])


def dft_tables(size, period, rows):
    index = np.arange(size)
    product = ((np.arange(rows) % period)[:, None] * index[None, :]) % size
    angle = product.astype(np.float32) * np.float32(2.0 * math.pi / size)
    norm = np.float32(1.0 / math.sqrt(size))
    return (
        jnp.asarray(np.cos(angle) * norm, jnp.bfloat16),
        jnp.asarray(-np.sin(angle) * norm, jnp.bfloat16),
    )


def cyclic_tables(size, period, shift):
    cos_part, sin_part = dft_tables(size, period, 2 * period)
    zero = jnp.zeros((), jnp.int32)
    cos_part = lax.dynamic_slice(cos_part, (period - shift, zero), (period, size))
    sin_part = lax.dynamic_slice(sin_part, (period - shift, zero), (period, size))
    return jnp.concatenate(
        [jnp.concatenate([cos_part, sin_part], 1), jnp.concatenate([-sin_part, cos_part], 1)], 0
    )


def scatter_sum(x, axis, dim):
    length = lax.axis_size(axis)
    block = x.shape[dim] // length
    me = lax.axis_index(axis)

    def part(of):
        return lax.dynamic_slice_in_dim(x, of * block, block, dim)

    if length > 8:
        return lax.psum_scatter(x, axis, scatter_dimension=dim, tiled=True).astype(jnp.float32)
    total = part(me).astype(jnp.float32)
    for step in range(1, length):
        pairs = [(i, (i + step) % length) for i in range(length)]
        got = lax.ppermute(part(lax.rem(me + step, length)), axis, pairs)
        total = total + got.astype(jnp.float32)
    return total


def shards(object_slab, probe_wave, amplitude, row_offset, col_offset, occupied):
    bf16, f32 = jnp.bfloat16, jnp.float32
    size = probe_wave.shape[1]
    tile_rows, tile_cols = object_slab.shape[1:]
    core = lax.axis_index("probe")
    zero = jnp.zeros((), jnp.int32)
    row_start = row_offset[0, 0, 0]
    col_start = col_offset[0, 0, 0]
    corner = jnp.stack([row_start, col_start])
    other_corner = swap(corner)

    def ordered(mine, other):
        return jnp.where(core == 0, jnp.stack([mine, other]), jnp.stack([other, mine]))

    cut = size // 2
    plane = lax.dynamic_index_in_dim(object_slab, core, 0, keepdims=False)
    below_b = from_behind(plane[cut:size], "narrow", -1)
    right_a = from_behind(plane[:cut], "wide", -1)
    below_a = from_behind(plane[:cut], "narrow", -1)
    right_b = from_behind(plane[cut:], "wide", -1)
    diag_b = from_behind(below_b, "wide", -1)
    diag_a = from_behind(right_a, "narrow", -1)

    def both(*parts):
        return ordered(jnp.concatenate(parts, 0), jnp.concatenate([swap(p) for p in parts], 0))

    below = both(below_a, below_b)
    right = both(right_a, right_b)
    diag = both(diag_a, diag_b)

    right_side = cyclic_tables(size, tile_cols, col_start)
    left_inv = cyclic_tables(size, tile_rows, row_start)
    inv_right = right_side.T
    left_side = left_inv.T
    padded = jnp.pad(probe_wave, ((0, 0), (0, tile_rows - size), (0, 0)))
    padded = jnp.concatenate([padded, padded], 1)
    padded = jnp.concatenate([padded, padded], 2)
    probe = lax.dynamic_slice(
        padded, (zero, tile_rows - row_start, tile_cols - col_start), (2, tile_rows, tile_cols)
    ).astype(f32)
    row_at = lax.broadcasted_iota(jnp.int32, (tile_rows, tile_cols), 0)
    col_at = lax.broadcasted_iota(jnp.int32, (tile_rows, tile_cols), 1)

    grow = ((0, 0), (0, tile_rows - size), (0, 0))
    in_rows = row_at >= row_start
    in_cols = col_at >= col_start
    patch = jnp.where(
        in_rows,
        jnp.where(in_cols, object_slab, right),
        jnp.where(in_cols, jnp.pad(below, grow), jnp.pad(diag, grow)),
    ).astype(f32)

    exit_wave = jnp.concatenate(
        [
            (probe[0] * patch[0] - probe[1] * patch[1]).astype(bf16),
            (probe[0] * patch[1] + probe[1] * patch[0]).astype(bf16),
        ],
        1,
    )
    half = jnp.dot(exit_wave, right_side, preferred_element_type=f32).astype(bf16)
    half = jnp.concatenate([half[:, :size], half[:, size:]], 0)
    far = jnp.dot(left_side, half, preferred_element_type=f32)
    far_re, far_im = far[:size], far[size:]
    magnitude = jnp.sqrt(far_re * far_re + far_im * far_im)
    live = occupied[0, 0, 0].astype(f32)
    factor = (1.0 - amplitude[0, 0, 0].astype(f32) / jnp.maximum(magnitude, 1.0)) * live
    chi = jnp.concatenate([(far_re * factor).astype(bf16), (far_im * factor).astype(bf16)], 1)
    back_half = jnp.dot(chi, inv_right, preferred_element_type=f32).astype(bf16)
    back_half = jnp.concatenate([back_half[:, :tile_cols], back_half[:, tile_cols:]], 0)
    back = jnp.dot(left_inv, back_half, preferred_element_type=f32)
    back_re, back_im = back[:tile_rows], back[tile_rows:]
    obj = jnp.stack(
        [probe[0] * back_re + probe[1] * back_im, probe[0] * back_im - probe[1] * back_re]
    ).astype(bf16)
    probe_term = jnp.stack(
        [patch[0] * back_re + patch[1] * back_im, patch[0] * back_im - patch[1] * back_re]
    ).astype(bf16)

    sent = lax.dynamic_index_in_dim(obj, 1 - core, 0, keepdims=False)
    kept = lax.dynamic_index_in_dim(obj, core, 0, keepdims=False).astype(f32)
    got = swap(sent).astype(f32)
    got_rows = row_at >= other_corner[0]
    got_cols = col_at >= other_corner[1]

    def piece(rows_in, cols_in):
        mine = (in_rows == rows_in) & (in_cols == cols_in)
        theirs = (got_rows == rows_in) & (got_cols == cols_in)
        return jnp.where(mine, kept, 0.0) + jnp.where(theirs, got, 0.0)

    own = piece(True, True)
    to_right = piece(True, False)
    to_below = piece(False, True)[:size]
    to_diag = piece(False, False)[:size]
    from_diag_a = from_behind(to_diag[:cut].astype(bf16), "narrow", 1)
    from_diag_b = from_behind(to_diag[cut:].astype(bf16), "wide", 1)
    from_above_a = from_behind(to_below[:cut].astype(bf16), "narrow", 1)
    from_left_b = from_behind(to_right[cut:].astype(bf16), "wide", 1)
    from_left_a = from_behind((to_right[:cut] + from_diag_a.astype(f32)).astype(bf16), "wide", 1)
    from_above_b = from_behind((to_below[cut:] + from_diag_b.astype(f32)).astype(bf16), "narrow", 1)
    from_left = jnp.concatenate([from_left_a, from_left_b], 0).astype(f32)
    from_above = jnp.concatenate([from_above_a, from_above_b], 0).astype(f32)
    from_above = jnp.pad(from_above, ((0, tile_rows - size), (0, 0)))
    own = (own + from_left + from_above).astype(bf16)
    object_grad = ordered(own, swap(own))

    probe_term = jnp.concatenate([probe_term, probe_term], 1)
    probe_term = lax.dynamic_slice_in_dim(probe_term, row_start, size, 1)
    probe_term = jnp.concatenate([probe_term, probe_term], 2)
    probe_term = lax.dynamic_slice_in_dim(probe_term, col_start, size, 2)
    narrow, cores = lax.axis_size("narrow"), lax.axis_size("probe")
    width = size // (narrow * cores)
    by_core = probe_term.reshape(2, size, narrow, cores, width)
    sent = lax.dynamic_index_in_dim(by_core, 1 - core, 3, keepdims=False)
    kept = lax.dynamic_index_in_dim(by_core, core, 3, keepdims=False)
    total = kept.astype(f32) + swap(sent).astype(f32)
    total = total.astype(bf16).reshape(2, size, narrow * width)
    total = scatter_sum(total, "narrow", 2).astype(bf16)
    total = scatter_sum(total, "wide", 1)
    scale = 1.0 / math.sqrt(lax.axis_size("wide") * narrow * cores)
    return (object_grad, total * scale)


def solution(mesh):
    in_specs = (
        P(None, ("groups", "narrow"), "wide"),
        P(),
        P(("groups", "narrow"), "wide", "probe", None, None),
        P(("groups", "narrow"), "wide", "probe"),
        P(("groups", "narrow"), "wide", "probe"),
        P(("groups", "narrow"), "wide", "probe"),
    )
    out_specs = (
        P(None, ("groups", "narrow"), "wide"),
        P(None, ("groups", "wide"), ("narrow", "probe")),
    )
    return jax.shard_map(shards, mesh=mesh, in_specs=in_specs, out_specs=out_specs, check_vma=False)
```

time: 246 us -> 112 us (0.46)
  the two profiles are of different devices: /device:TPU:19 before, /device:TPU:0 now
where the time goes in v1:
time: 112 us; the launch traced here: 111 us
  starting transfers between devices  36.6 us (33%)
  other arithmetic  34.1 us (30%)
  waiting for transfers between devices  17.8 us (16%)
  local copies, waits for them, and re-layouts  13.8 us (12%)
  matrix products  5.91 us (5%)
  between operations  3.13 us (3%)
    ppermute x12, starting transfers between devices, from_behind(): return lax.ppermute(x, axis, pairs)  30.2 us
    ppermute x12, waiting for transfers between devices, from_behind(): return lax.ppermute(x, axis, pairs)  12 us
    convert_element_type x1, other arithmetic, shards(): probe = lax.dynamic_slice(padded, (zero, tile_rows - row_start, tile_cols...  5.79 us
    ppermute x4, waiting for transfers between devices, scatter_sum(): got = lax.ppermute(part(lax.rem(me + step, length)), axis, pairs)  5.74 us
    unnamed x25, local copies, waits for them, and re-layouts  4.64 us
    another operation x6, other arithmetic, ordered(): jnp.stack([mine, other])  4.39 us
    ppermute x4, starting transfers between devices, scatter_sum(): got = lax.ppermute(part(lax.rem(me + step, length)), axis, pairs)  3.94 us
    dynamic_slice x2, other arithmetic, cyclic_tables(): lax.dynamic_slice(sin_part, (period - shift, zero), (period, size))  3.84 us
  transfers between devices with their start and end apart: 26, of which 6 were waited for; matrix products, arithmetic and copies ran while one was open for 40% of the time, Pallas kernels for 0%

profile of v1, /device:TPU:0, one launch (start us, length us, event | category | flops | bytes accessed | tf_op | source)
XLA Modules:
  0.0 111.3 jit_solution(7916455331450898029)
XLA Ops:
  1.7 1.3 %collective-permute-start = (bf16[256,512]{1,0:T(8,128)(2,1)S(1)}, bf16[256,512]{1,0:T(8,128)(2,1)}, u32[]{:S(2)}, u32[]{:S(2)}) collective-permute-start(bf16[256,512]{1,0:T(8,128)(2,1)S(1)} %get-tuple-element.21), channel_id=1, source_target_pairs={{4,0},{8,4},{12,8},{5,1},{9,5},{13,9},{6,2},{10,6},{14,10},{7,3},{... | collective-permute-start | bytes 786440 | tf_op jit(solution)/shard_map/ppermute | solution.py:13
  3.0 1.3 %collective-permute-start.4 = (bf16[256,512]{1,0:T(8,128)(2,1)S(1)}, bf16[256,512]{1,0:T(8,128)(2,1)}, u32[]{:S(2)}, u32[]{:S(2)}) collective-permute-start(bf16[256,512]{1,0:T(8,128)(2,1)S(1)} %get-tuple-element.21), channel_id=1, source_target_pairs={{2,0},{3,1},{6,4},{7,5},{10,8},{11,9},{14,12},{15,13},{18,16},{19,... | collective-permute-start | bytes 786440 | tf_op jit(solution)/shard_map/ppermute | solution.py:13
  4.3 1.4 %collective-permute-start.5 = (bf16[256,512]{1,0:T(8,128)(2,1)S(1)}, bf16[256,512]{1,0:T(8,128)(2,1)}, u32[]{:S(2)}, u32[]{:S(2)}) collective-permute-start(bf16[256,512]{1,0:T(8,128)(2,1)S(1)} %get-tuple-element.20), channel_id=1, source_target_pairs={{2,0},{3,1},{6,4},{7,5},{10,8},{11,9},{14,12},{15,13},{18,16},{19,... | collective-permute-start | bytes 786440 | tf_op jit(solution)/shard_map/ppermute | solution.py:13
  6.8 1.3 %collective-permute-start.1 = (bf16[384,512]{1,0:T(8,128)(2,1)S(1)}, bf16[384,512]{1,0:T(8,128)(2,1)}, u32[]{:S(2)}, u32[]{:S(2)}) collective-permute-start(bf16[384,512]{1,0:T(8,128)(2,1)S(1)} %dynamic-slice_bitcast_fusion.1), channel_id=1, source_target_pairs={{4,0},{8,4},{12,8},{5,1},{9,5},{13,9},{6,2},{10,6},{14,10},{7,3},{... | collective-permute-start | bytes 1179656 | tf_op jit(solution)/shard_map/ppermute | solution.py:13
  9.4 2.5 %constant_dynamic-slice_fusion.7 = (bf16[640,512]{1,0:T(8,128)(2,1)}, bf16[640,512]{1,0:T(8,128)(2,1)}) fusion(bf16[1280,512]{1,0:T(8,128)(2,1)} %constant.82.clone, s32[]{:T(128)S(6)} %select_n.105), kind=kLoop, calls=%fused_computation.119 | loop fusion | flops 983040 | bytes 1966084 | tf_op jit(solution)/shard_map/dynamic_slice | solution.py:35
  13.0 5.8 %fusion.10 = f32[2,640,512]{2,1,0:T(8,128)S(1)} fusion(s32[]{:T(128)S(6)} %select_n.105, s32[]{:T(128)S(6)} %select_n.106, bf16[2,640,512]{2,1,0:T(8,128)(2,1)S(1)} %pad.17), kind=kLoop, calls=%fused_computation.36 | loop fusion | flops 5242880 | bytes 3932168 | tf_op jit(solution)/shard_map/convert_element_type | solution.py:98
  18.9 1.3 %constant_dynamic-slice_fusion.5 = (bf16[512,512]{1,0:T(8,128)(2,1)}, bf16[512,512]{1,0:T(8,128)(2,1)}, bf16[512,512]{1,0:T(8,128)(2,1)}) fusion(bf16[1024,512]{1,0:T(8,128)(2,1)S(1)} %copy-done.10, s32[]{:T(128)S(6)} %select_n.106, bf16[1024,512]{1,0:T(8,128)(2,1)S(1)} %copy-done.9), kind=kLoop, calls=%fused_computation.117 | loop fusion | flops 786432 | bytes 2621444 | tf_op jit(solution)/shard_map/dynamic_slice | solution.py:35
  20.2 1.3 %collective-permute-start.9 = (bf16[256,512]{1,0:T(8,128)(2,1)}, bf16[256,512]{1,0:T(8,128)(2,1)}, u32[]{:S(2)}, u32[]{:S(2)}) collective-permute-start(bf16[256,512]{1,0:T(8,128)(2,1)} %collective-permute-done.5), channel_id=1, source_target_pairs={{4,0},{8,4},{12,8},{5,1},{9,5},{13,9},{6,2},{10,6},{14,10},{7,3},{... | collective-permute-start | bytes 786440 | tf_op jit(solution)/shard_map/ppermute | solution.py:13
  28.1 6.3 %collective-permute-done.8 = bf16[256,512]{1,0:T(8,128)(2,1)} collective-permute-done((bf16[256,512]{1,0:T(8,128)(2,1)}, bf16[256,512]{1,0:T(8,128)(2,1)}, u32[]{:S(2)}, u32[]{:S(2)}) %collective-permute-start.8) | collective-permute-done | bytes 262176 | tf_op jit(solution)/shard_map/ppermute | solution.py:13
  39.2 1.3 %fusion.16 = f32[2,640,512]{2,1,0:T(8,128)S(1)} fusion(bf16[2,640,512]{2,1,0:T(8,128)(2,1)S(1)} %copy-done, bf16[1,640,512]{2,1,0:T(8,128)(2,1)S(1)} %maximum_bitcast_fusion.1, bf16[1,640,512]{2,1,0:T(8,128)(2,1)S(1)} %maximum_bitcast_fusion, bf16[2,512,512]{2,1,0:T(8,128)(2,1)S(1)} %maximum_select_fusion.3, ...), kind=kLoop, calls=%fused_computation.48 | loop fusion | flops 8519680 | bytes 7341185 | tf_op jit(solution)/shard_map/convert_element_type | solution.py:109
  41.8 1.5 %convolution_convert_fusion = bf16[640,1024]{1,0:T(8,128)(2,1)S(1)} fusion(bf16[640,512]{1,0:T(8,128)(2,1)S(1)} %get-tuple-element.9, bf16[640,512]{1,0:T(8,128)(2,1)S(1)} %get-tuple-element.8, bf16[512,512]{1,0:T(8,128)(2,1)S(1)} %copy-done.7, bf16[512,512]{1,0:T(8,128)(2,1)S(1)} %copy-done.6, bf16[512,512]{1,0:T(8,128)(2,1)S(1)} %copy-done.5), kind=kOutput, calls=%fused_computation.20 | convolution fusion | flops 1353842688 | bytes 4194304 | tf_op jit(solution)/shard_map/dot_general | solution.py:118
  44.8 1.6 %fusion.20 = f32[1024,512]{0,1:T(8,128)S(1)} fusion(bf16[640,512]{1,0:T(8,128)(2,1)S(1)} %get-tuple-element.19, bf16[640,512]{1,0:T(8,128)(2,1)S(1)} %get-tuple-element.18, bf16[640,512]{1,0:T(8,128)(2,1)S(1)} %copy-done.4, bf16[640,512]{1,0:T(8,128)(2,1)S(1)} %copy-done.3, bf16[640,512]{1,0:T(8,128)(2,1)S(1)} %copy-done.2), kind=kOutput, calls=%fused_computation.52 | convolution fusion | flops 1355284480 | bytes 5373952 | tf_op jit(solution)/shard_map/dot_general | solution.py:120
  47.1 1.3 %convolution_convert_fusion.1 = bf16[512,1024]{1,0:T(8,128)(2,1)S(1)} fusion(bf16[512,512]{0,1:T(8,128)(2,1)S(1)} %get-tuple-element.13, bf16[512,512]{0,1:T(8,128)(2,1)S(1)} %get-tuple-element.12, bf16[512,512]{1,0:T(8,128)(2,1)S(1)} %copy-done.7, bf16[512,512]{1,0:T(8,128)(2,1)S(1)} %copy-done.6, bf16[512,512]{1,0:T(8,128)(2,1)S(1)} %copy-done.5), kind=kOutput, calls=%fused_computation.21 | convolution fusion | flops 1084751872 | bytes 3670016 | tf_op jit(solution)/shard_map/dot_general | solution.py:126
  48.5 1.5 %fusion.31 = f32[1280,512]{1,0:T(8,128)S(1)} fusion(bf16[512,512]{1,0:T(8,128)(2,1)S(1)} %get-tuple-element.23, bf16[512,512]{1,0:T(8,128)(2,1)S(1)} %get-tuple-element.22, bf16[640,512]{1,0:T(8,128)(2,1)S(1)} %copy-done.4, bf16[640,512]{1,0:T(8,128)(2,1)S(1)} %copy-done.3, bf16[640,512]{1,0:T(8,128)(2,1)S(1)} %copy-done.2), kind=kOutput, calls=%fused_computation.72 | convolution fusion | flops 1354760192 | bytes 5636096 | tf_op jit(solution)/shard_map/dot_general | solution.py:128
  55.5 1.7 %fusion.4 = (f32[640,512]{1,0:T(8,128)}, bf16[640,512]{1,0:T(8,128)(2,1)S(1)}) fusion(bf16[640,512]{1,0:T(8,128)(2,1)S(1)} %collective-permute-done.13, pred[512]{0:T(512)(128)(4,1)S(1)} %broadcast_compare_fusion.2, pred[512]{0:T(512)(128)(4,1)S(1)} %broadcast_compare_fusion.3, pred[640]{0:T(1024)(128)(4,1)S(1)} %get-tuple-element.36, ...), kind=kLoop, calls=%fused_computation.30 | loop fusion | flops 3604480 | bytes 3934468 | tf_op jit(solution)/shard_map/add | solution.py:146
  57.1 1.9 %fusion.6 = (bf16[640,512]{1,0:T(8,128)(2,1)S(1)}, f32[640,512]{1,0:T(8,128)}) fusion(bf16[640,512]{1,0:T(8,128)(2,1)S(1)} %collective-permute-done.13, bf16[640,512]{1,0:T(8,128)(2,1)S(1)} %get-tuple-element.3, pred[512]{0:T(512)(128)(4,1)S(1)} %broadcast_compare_fusion.2, pred[512]{0:T(512)(128)(4,1)S(1)} %broadcast_compare_fusion.3, ...), kind=kLoop, calls=%fused_computation.32 | loop fusion | flops 4259840 | bytes 3280128 | tf_op jit(solution)/shard_map/convert.12
  59.9 4.9 %collective-permute-start.14 = (bf16[256,512]{1,0:T(8,128)(2,1)}, bf16[256,512]{1,0:T(8,128)(2,1)}, u32[]{:S(2)}, u32[]{:S(2)}) collective-permute-start(bf16[256,512]{1,0:T(8,128)(2,1)} %get-tuple-element.26), channel_id=1, source_target_pairs={{0,2},{1,3},{4,6},{5,7},{8,10},{9,11},{12,14},{13,15},{16,18},{17,... | collective-permute-start | bytes 786440 | tf_op jit(solution)/shard_map/ppermute | solution.py:13
  66.4 4.8 %collective-permute-start.18 = (bf16[256,512]{1,0:T(8,128)(2,1)}, bf16[256,512]{1,0:T(8,128)(2,1)}, u32[]{:S(2)}, u32[]{:S(2)}) collective-permute-start(bf16[256,512]{1,0:T(8,128)(2,1)} %get-tuple-element.27), channel_id=1, source_target_pairs={{0,4},{4,8},{8,12},{1,5},{5,9},{9,13},{2,6},{6,10},{10,14},{3,7},{... | collective-permute-start | bytes 786440 | tf_op jit(solution)/shard_map/ppermute | solution.py:13
  71.2 1.8 %slice.234 = bf16[256,512]{1,0:T(8,128)(2,1)} slice(f32[640,512]{1,0:T(8,128)} %get-tuple-element.15), slice={[0:256], [0:512]} | slice | bytes 524288 | tf_op jit(solution)/shard_map/slice | solution.py:154
  73.0 2.0 %collective-permute-start.17 = (bf16[256,512]{1,0:T(8,128)(2,1)}, bf16[256,512]{1,0:T(8,128)(2,1)}, u32[]{:S(2)}, u32[]{:S(2)}) collective-permute-start(bf16[256,512]{1,0:T(8,128)(2,1)} %slice.234), channel_id=1, source_target_pairs={{0,2},{1,3},{4,6},{5,7},{8,10},{9,11},{12,14},{13,15},{16,18},{17,... | collective-permute-start | bytes 786440 | tf_op jit(solution)/shard_map/ppermute | solution.py:13
  75.0 1.9 %slice.233 = bf16[384,512]{1,0:T(8,128)(2,1)} slice(f32[640,512]{1,0:T(8,128)} %get-tuple-element.2), slice={[256:640], [0:512]} | slice | bytes 786432 | tf_op jit(solution)/shard_map/slice | solution.py:155
  76.9 4.0 %collective-permute-start.16 = (bf16[384,512]{1,0:T(8,128)(2,1)}, bf16[384,512]{1,0:T(8,128)(2,1)}, u32[]{:S(2)}, u32[]{:S(2)}) collective-permute-start(bf16[384,512]{1,0:T(8,128)(2,1)} %slice.233), channel_id=1, source_target_pairs={{0,4},{4,8},{8,12},{1,5},{5,9},{9,13},{2,6},{6,10},{10,14},{3,7},{... | collective-permute-start | bytes 1179656 | tf_op jit(solution)/shard_map/ppermute | solution.py:13
  80.9 1.9 %fusion.48 = bf16[256,512]{1,0:T(8,128)(2,1)} fusion(f32[640,512]{1,0:T(8,128)} %get-tuple-element.2, bf16[256,512]{1,0:T(8,128)(2,1)} %collective-permute-done.14), kind=kLoop, calls=%fused_computation.99 | loop fusion | flops 393216 | bytes 1048576 | tf_op jit(solution)/shard_map/convert_element_type | solution.py:156
  82.8 4.7 %collective-permute-start.15 = (bf16[256,512]{1,0:T(8,128)(2,1)}, bf16[256,512]{1,0:T(8,128)(2,1)}, u32[]{:S(2)}, u32[]{:S(2)}) collective-permute-start(bf16[256,512]{1,0:T(8,128)(2,1)} %fusion.48), channel_id=1, source_target_pairs={{0,4},{4,8},{8,12},{1,5},{5,9},{9,13},{2,6},{6,10},{10,14},{3,7},{... | collective-permute-start | bytes 786440 | tf_op jit(solution)/shard_map/ppermute | solution.py:13
  87.4 1.9 %fusion.47 = bf16[256,512]{1,0:T(8,128)(2,1)} fusion(f32[640,512]{1,0:T(8,128)} %get-tuple-element.15, bf16[256,512]{1,0:T(8,128)(2,1)} %collective-permute-done.18), kind=kLoop, calls=%fused_computation.96 | loop fusion | flops 393216 | bytes 1048576 | tf_op jit(solution)/shard_map/convert_element_type | solution.py:157
  89.3 2.0 %collective-permute-start.19 = (bf16[256,512]{1,0:T(8,128)(2,1)}, bf16[256,512]{1,0:T(8,128)(2,1)}, u32[]{:S(2)}, u32[]{:S(2)}) collective-permute-start(bf16[256,512]{1,0:T(8,128)(2,1)} %fusion.47), channel_id=1, source_target_pairs={{0,2},{1,3},{4,6},{5,7},{8,10},{9,11},{12,14},{13,15},{16,18},{17,... | collective-permute-start | bytes 786440 | tf_op jit(solution)/shard_map/ppermute | solution.py:13
  92.0 2.6 %collective-permute-done.15 = bf16[256,512]{1,0:T(8,128)(2,1)} collective-permute-done((bf16[256,512]{1,0:T(8,128)(2,1)}, bf16[256,512]{1,0:T(8,128)(2,1)}, u32[]{:S(2)}, u32[]{:S(2)}) %collective-permute-start.15) | collective-permute-done | bytes 262176 | tf_op jit(solution)/shard_map/ppermute | solution.py:13
  94.6 3.1 %collective-permute-done.19 = bf16[256,512]{1,0:T(8,128)(2,1)} collective-permute-done((bf16[256,512]{1,0:T(8,128)(2,1)}, bf16[256,512]{1,0:T(8,128)(2,1)}, u32[]{:S(2)}, u32[]{:S(2)}) %collective-permute-start.19) | collective-permute-done | bytes 262176 | tf_op jit(solution)/shard_map/ppermute | solution.py:13
  97.7 1.8 %fusion.3 = bf16[640,512]{1,0:T(8,128)(2,1)S(1)} fusion(bf16[640,512]{1,0:T(8,128)(2,1)S(1)} %collective-permute-done.13, bf16[640,512]{1,0:T(8,128)(2,1)S(1)} %get-tuple-element.3, bf16[256,512]{1,0:T(8,128)(2,1)} %collective-permute-done.19, bf16[256,512]{1,0:T(8,128)(2,1)} %collective-permute-done.17, bf16[384,512]{1,0:T(8,128)(2,1)} %collective-permute-done.16, ...), kind=kLoop, calls=%fused_computation.29 | loop fusion | flops 6881280 | bytes 3148032 | tf_op jit(solution)/shard_map/convert_element_type | solution.py:161
  99.6 2.2 %collective-permute-done.22 = bf16[2,512,128]{2,1,0:T(8,128)(2,1)S(1)} collective-permute-done((bf16[2,512,128]{2,1,0:T(8,128)(2,1)S(1)}, bf16[2,512,128]{2,1,0:T(8,128)(2,1)S(1)}, u32[]{:S(2)}, u32[]{:S(2)}) %collective-permute-start.22) | collective-permute-done | bytes 262176 | tf_op jit(solution)/shard_map/ppermute | solution.py:54
  102.1 3.7 %collective-permute-start.25 = (bf16[2,128,128]{2,1,0:T(8,128)(2,1)S(1)}, bf16[2,128,128]{2,1,0:T(8,128)(2,1)S(1)}, u32[]{:S(2)}, u32[]{:S(2)}) collective-permute-start(bf16[2,128,128]{2,1,0:T(8,128)(2,1)S(1)} %get-tuple-element.31), channel_id=1, source_target_pairs={{0,12},{4,0},{8,4},{12,8},{1,13},{5,1},{9,5},{13,9},{2,14},{6,2},{... | collective-permute-start | bytes 196616 | tf_op jit(solution)/shard_map/ppermute | solution.py:54
  105.8 2.4 %collective-permute-done.23 = bf16[2,128,128]{2,1,0:T(8,128)(2,1)S(1)} collective-permute-done((bf16[2,128,128]{2,1,0:T(8,128)(2,1)S(1)}, bf16[2,128,128]{2,1,0:T(8,128)(2,1)S(1)}, u32[]{:S(2)}, u32[]{:S(2)}) %collective-permute-start.23) | collective-permute-done | bytes 65568 | tf_op jit(solution)/shard_map/ppermute | solution.py:54
  (98 shorter events, 29.3 us)
Async XLA Ops:
  1.7 20.3 %collective-permute-start = (bf16[256,512]{1,0:T(8,128)(2,1)S(1)}, bf16[256,512]{1,0:T(8,128)(2,1)}, u32[]{:S(2)}, u32[]{:S(2)}) collective-permute-start(bf16[256,512]{1,0:T(8,128)(2,1)S(1)} %get-tuple-element.21), channel_id=1, source_target_pairs={{4,0},{8,4},{12,8},{5,1},{9,5},{13,9},{6,2},{10,6},{14,10},{7,3},{... | collective-permute-start | bytes 786440 | tf_op jit(solution)/shard_map/ppermute | solution.py:13
  3.0 20.3 %collective-permute-start.4 = (bf16[256,512]{1,0:T(8,128)(2,1)S(1)}, bf16[256,512]{1,0:T(8,128)(2,1)}, u32[]{:S(2)}, u32[]{:S(2)}) collective-permute-start(bf16[256,512]{1,0:T(8,128)(2,1)S(1)} %get-tuple-element.21), channel_id=1, source_target_pairs={{2,0},{3,1},{6,4},{7,5},{10,8},{11,9},{14,12},{15,13},{18,16},{19,... | collective-permute-start | bytes 786440 | tf_op jit(solution)/shard_map/ppermute | solution.py:13
  4.3 7.6 %copy-start.8 = (bf16[1280,512]{1,0:T(8,128)(2,1)S(1)}, bf16[1280,512]{1,0:T(8,128)(2,1)}, u32[]{:S(2)}) copy-start(bf16[1280,512]{1,0:T(8,128)(2,1)} %constant.81.clone) | copy-start | bytes 3932164
  4.3 15.9 %collective-permute-start.5 = (bf16[256,512]{1,0:T(8,128)(2,1)S(1)}, bf16[256,512]{1,0:T(8,128)(2,1)}, u32[]{:S(2)}, u32[]{:S(2)}) collective-permute-start(bf16[256,512]{1,0:T(8,128)(2,1)S(1)} %get-tuple-element.20), channel_id=1, source_target_pairs={{2,0},{3,1},{6,4},{7,5},{10,8},{11,9},{14,12},{15,13},{18,16},{19,... | collective-permute-start | bytes 786440 | tf_op jit(solution)/shard_map/ppermute | solution.py:13
  6.8 19.7 %collective-permute-start.1 = (bf16[384,512]{1,0:T(8,128)(2,1)S(1)}, bf16[384,512]{1,0:T(8,128)(2,1)}, u32[]{:S(2)}, u32[]{:S(2)}) collective-permute-start(bf16[384,512]{1,0:T(8,128)(2,1)S(1)} %dynamic-slice_bitcast_fusion.1), channel_id=1, source_target_pairs={{4,0},{8,4},{12,8},{5,1},{9,5},{13,9},{6,2},{10,6},{14,10},{7,3},{... | collective-permute-start | bytes 1179656 | tf_op jit(solution)/shard_map/ppermute | solution.py:13
  9.4 3.5 %copy-start.1 = (bf16[2,512,512]{2,1,0:T(8,128)(2,1)S(1)}, bf16[2,512,512]{2,1,0:T(8,128)(2,1)}, u32[]{:S(2)}) copy-start(bf16[2,512,512]{2,1,0:T(8,128)(2,1)} %param.11) | copy-start | bytes 3145732
  13.0 5.8 %copy-start.9 = (bf16[1024,512]{1,0:T(8,128)(2,1)S(1)}, bf16[1024,512]{1,0:T(8,128)(2,1)}, u32[]{:S(2)}) copy-start(bf16[1024,512]{1,0:T(8,128)(2,1)} %constant.79.clone) | copy-start | bytes 3145732
  13.0 5.8 %copy-start.10 = (bf16[1024,512]{1,0:T(8,128)(2,1)S(1)}, bf16[1024,512]{1,0:T(8,128)(2,1)}, u32[]{:S(2)}) copy-start(bf16[1024,512]{1,0:T(8,128)(2,1)} %constant.80.clone) | copy-start | bytes 3145732
  20.2 14.2 %collective-permute-start.9 = (bf16[256,512]{1,0:T(8,128)(2,1)}, bf16[256,512]{1,0:T(8,128)(2,1)}, u32[]{:S(2)}, u32[]{:S(2)}) collective-permute-start(bf16[256,512]{1,0:T(8,128)(2,1)} %collective-permute-done.5), channel_id=1, source_target_pairs={{4,0},{8,4},{12,8},{5,1},{9,5},{13,9},{6,2},{10,6},{14,10},{7,3},{... | collective-permute-start | bytes 786440 | tf_op jit(solution)/shard_map/ppermute | solution.py:13
  21.5 13.5 %collective-permute-start.7 = (bf16[256,512]{1,0:T(8,128)(2,1)}, bf16[256,512]{1,0:T(8,128)(2,1)}, u32[]{:S(2)}, u32[]{:S(2)}) collective-permute-start(bf16[256,512]{1,0:T(8,128)(2,1)} %collective-permute-done.5), channel_id=1, source_target_pairs={{0,1},{1,0},{2,3},{3,2},{4,5},{5,4},{6,7},{7,6},{8,9},{9,8},{10,11... | collective-permute-start | bytes 786440 | tf_op jit(solution)/shard_map/ppermute | solution.py:17
  22.0 12.4 %collective-permute-start.8 = (bf16[256,512]{1,0:T(8,128)(2,1)}, bf16[256,512]{1,0:T(8,128)(2,1)}, u32[]{:S(2)}, u32[]{:S(2)}) collective-permute-start(bf16[256,512]{1,0:T(8,128)(2,1)} %collective-permute-done), channel_id=1, source_target_pairs={{2,0},{3,1},{6,4},{7,5},{10,8},{11,9},{14,12},{15,13},{18,16},{19,... | collective-permute-start | bytes 786440 | tf_op jit(solution)/shard_map/ppermute | solution.py:13
  23.3 11.6 %collective-permute-start.6 = (bf16[256,512]{1,0:T(8,128)(2,1)}, bf16[256,512]{1,0:T(8,128)(2,1)}, u32[]{:S(2)}, u32[]{:S(2)}) collective-permute-start(bf16[256,512]{1,0:T(8,128)(2,1)} %collective-permute-done.4), channel_id=1, source_target_pairs={{0,1},{1,0},{2,3},{3,2},{4,5},{5,4},{6,7},{7,6},{8,9},{9,8},{10,11... | collective-permute-start | bytes 786440 | tf_op jit(solution)/shard_map/ppermute | solution.py:17
  26.5 25.1 %collective-permute-start.12 = (s32[2]{0:T(128)S(1)}, s32[2]{0:T(128)S(1)}, u32[]{:S(2)}, u32[]{:S(2)}) collective-permute-start(s32[2]{0:T(128)S(1)} %pad_add_fusion), channel_id=1, source_target_pairs={{0,1},{1,0},{2,3},{3,2},{4,5},{5,4},{6,7},{7,6},{8,9},{9,8},{10,11... | collective-permute-start | bytes 32 | tf_op jit(solution)/shard_map/ppermute | solution.py:17
  34.4 3.6 %collective-permute-start.2 = (bf16[256,512]{1,0:T(8,128)(2,1)}, bf16[256,512]{1,0:T(8,128)(2,1)S(1)}, u32[]{:S(2)}, u32[]{:S(2)}) collective-permute-start(bf16[256,512]{1,0:T(8,128)(2,1)} %collective-permute-done), channel_id=1, source_target_pairs={{0,1},{1,0},{2,3},{3,2},{4,5},{5,4},{6,7},{7,6},{8,9},{9,8},{10,11... | collective-permute-start | bytes 786440 | tf_op jit(solution)/shard_map/ppermute | solution.py:17
  34.4 3.6 %collective-permute-start.3 = (bf16[384,512]{1,0:T(8,128)(2,1)}, bf16[384,512]{1,0:T(8,128)(2,1)S(1)}, u32[]{:S(2)}, u32[]{:S(2)}) collective-permute-start(bf16[384,512]{1,0:T(8,128)(2,1)} %collective-permute-done.1), channel_id=1, source_target_pairs={{0,1},{1,0},{2,3},{3,2},{4,5},{5,4},{6,7},{7,6},{8,9},{9,8},{10,11... | collective-permute-start | bytes 1179656 | tf_op jit(solution)/shard_map/ppermute | solution.py:17
  34.9 2.8 %collective-permute-start.10 = (bf16[256,512]{1,0:T(8,128)(2,1)}, bf16[256,512]{1,0:T(8,128)(2,1)S(1)}, u32[]{:S(2)}, u32[]{:S(2)}) collective-permute-start(bf16[256,512]{1,0:T(8,128)(2,1)} %collective-permute-done.8), channel_id=1, source_target_pairs={{0,1},{1,0},{2,3},{3,2},{4,5},{5,4},{6,7},{7,6},{8,9},{9,8},{10,11... | collective-permute-start | bytes 786440 | tf_op jit(solution)/shard_map/ppermute | solution.py:17
  35.0 2.8 %collective-permute-start.11 = (bf16[256,512]{1,0:T(8,128)(2,1)}, bf16[256,512]{1,0:T(8,128)(2,1)S(1)}, u32[]{:S(2)}, u32[]{:S(2)}) collective-permute-start(bf16[256,512]{1,0:T(8,128)(2,1)} %collective-permute-done.9), channel_id=1, source_target_pairs={{0,1},{1,0},{2,3},{3,2},{4,5},{5,4},{6,7},{7,6},{8,9},{9,8},{10,11... | collective-permute-start | bytes 786440 | tf_op jit(solution)/shard_map/ppermute | solution.py:17
  40.5 1.3 %copy-start.7 = (bf16[512,512]{1,0:T(8,128)(2,1)S(1)}, bf16[512,512]{1,0:T(8,128)(2,1)}, u32[]{:S(2)}) copy-start(bf16[512,512]{1,0:T(8,128)(2,1)} %get-tuple-element.35) | copy-start | bytes 1572868
  43.4 1.5 %copy-start.4 = (bf16[640,512]{1,0:T(8,128)(2,1)S(1)}, bf16[640,512]{1,0:T(8,128)(2,1)}, u32[]{:S(2)}) copy-start(bf16[640,512]{1,0:T(8,128)(2,1)} %constant_dynamic-slice_fusion.8) | copy-start | bytes 1966084
  51.5 4.0 %collective-permute-start.13 = (bf16[640,512]{1,0:T(8,128)(2,1)S(1)}, bf16[640,512]{1,0:T(8,128)(2,1)S(1)}, u32[]{:S(2)}, u32[]{:S(2)}) collective-permute-start(bf16[640,512]{1,0:T(8,128)(2,1)S(1)} %fusion.44), channel_id=1, source_target_pairs={{0,1},{1,0},{2,3},{3,2},{4,5},{5,4},{6,7},{7,6},{8,9},{9,8},{10,11... | collective-permute-start | bytes 1966088 | tf_op jit(solution)/shard_map/ppermute | solution.py:17
  59.9 21.0 %collective-permute-start.14 = (bf16[256,512]{1,0:T(8,128)(2,1)}, bf16[256,512]{1,0:T(8,128)(2,1)}, u32[]{:S(2)}, u32[]{:S(2)}) collective-permute-start(bf16[256,512]{1,0:T(8,128)(2,1)} %get-tuple-element.26), channel_id=1, source_target_pairs={{0,2},{1,3},{4,6},{5,7},{8,10},{9,11},{12,14},{13,15},{16,18},{17,... | collective-permute-start | bytes 786440 | tf_op jit(solution)/shard_map/ppermute | solution.py:13
  66.4 25.0 %collective-permute-start.21 = (bf16[2,512,2,128]{1,3,2,0:T(8,128)(2,1)S(1)}, bf16[2,512,2,128]{1,3,2,0:T(8,128)(2,1)S(1)}, u32[]{:S(2)}, u32[]{:S(2)}) collective-permute-start(bf16[2,512,2,128]{1,3,2,0:T(8,128)(2,1)S(1)} %dynamic-slice_bitcast_fusion), channel_id=1, source_target_pairs={{0,1},{1,0},{2,3},{3,2},{4,5},{5,4},{6,7},{7,6},{8,9},{9,8},{10,11... | collective-permute-start | bytes 1572872 | tf_op jit(solution)/shard_map/ppermute | solution.py:17
  66.4 21.0 %collective-permute-start.18 = (bf16[256,512]{1,0:T(8,128)(2,1)}, bf16[256,512]{1,0:T(8,128)(2,1)}, u32[]{:S(2)}, u32[]{:S(2)}) collective-permute-start(bf16[256,512]{1,0:T(8,128)(2,1)} %get-tuple-element.27), channel_id=1, source_target_pairs={{0,4},{4,8},{8,12},{1,5},{5,9},{9,13},{2,6},{6,10},{10,14},{3,7},{... | collective-permute-start | bytes 786440 | tf_op jit(solution)/shard_map/ppermute | solution.py:13
  73.0 19.0 %collective-permute-start.17 = (bf16[256,512]{1,0:T(8,128)(2,1)}, bf16[256,512]{1,0:T(8,128)(2,1)}, u32[]{:S(2)}, u32[]{:S(2)}) collective-permute-start(bf16[256,512]{1,0:T(8,128)(2,1)} %slice.234), channel_id=1, source_target_pairs={{0,2},{1,3},{4,6},{5,7},{8,10},{9,11},{12,14},{13,15},{16,18},{17,... | collective-permute-start | bytes 786440 | tf_op jit(solution)/shard_map/ppermute | solution.py:13
  76.9 15.0 %collective-permute-start.16 = (bf16[384,512]{1,0:T(8,128)(2,1)}, bf16[384,512]{1,0:T(8,128)(2,1)}, u32[]{:S(2)}, u32[]{:S(2)}) collective-permute-start(bf16[384,512]{1,0:T(8,128)(2,1)} %slice.233), channel_id=1, source_target_pairs={{0,4},{4,8},{8,12},{1,5},{5,9},{9,13},{2,6},{6,10},{10,14},{3,7},{... | collective-permute-start | bytes 1179656 | tf_op jit(solution)/shard_map/ppermute | solution.py:13
  82.8 11.8 %collective-permute-start.15 = (bf16[256,512]{1,0:T(8,128)(2,1)}, bf16[256,512]{1,0:T(8,128)(2,1)}, u32[]{:S(2)}, u32[]{:S(2)}) collective-permute-start(bf16[256,512]{1,0:T(8,128)(2,1)} %fusion.48), channel_id=1, source_target_pairs={{0,4},{4,8},{8,12},{1,5},{5,9},{9,13},{2,6},{6,10},{10,14},{3,7},{... | collective-permute-start | bytes 786440 | tf_op jit(solution)/shard_map/ppermute | solution.py:13
  89.3 8.3 %collective-permute-start.19 = (bf16[256,512]{1,0:T(8,128)(2,1)}, bf16[256,512]{1,0:T(8,128)(2,1)}, u32[]{:S(2)}, u32[]{:S(2)}) collective-permute-start(bf16[256,512]{1,0:T(8,128)(2,1)} %fusion.47), channel_id=1, source_target_pairs={{0,2},{1,3},{4,6},{5,7},{8,10},{9,11},{12,14},{13,15},{16,18},{17,... | collective-permute-start | bytes 786440 | tf_op jit(solution)/shard_map/ppermute | solution.py:13
  91.7 10.1 %collective-permute-start.22 = (bf16[2,512,128]{2,1,0:T(8,128)(2,1)S(1)}, bf16[2,512,128]{2,1,0:T(8,128)(2,1)S(1)}, u32[]{:S(2)}, u32[]{:S(2)}) collective-permute-start(bf16[2,512,128]{2,1,0:T(8,128)(2,1)S(1)} %copy.18), channel_id=1, source_target_pairs={{0,2},{2,0},{1,3},{3,1},{4,6},{6,4},{5,7},{7,5},{8,10},{10,8},{9,1... | collective-permute-start | bytes 786440 | tf_op jit(solution)/shard_map/ppermute | solution.py:54
  99.5 10.5 %collective-permute-start.20 = (bf16[640,512]{1,0:T(8,128)(2,1)S(1)}, bf16[640,512]{1,0:T(8,128)(2,1)S(1)}, u32[]{:S(2)}, u32[]{:S(2)}) collective-permute-start(bf16[640,512]{1,0:T(8,128)(2,1)S(1)} %fusion.3), channel_id=1, source_target_pairs={{0,1},{1,0},{2,3},{3,2},{4,5},{5,4},{6,7},{7,6},{8,9},{9,8},{10,11... | collective-permute-start | bytes 1966088 | tf_op jit(solution)/shard_map/ppermute | solution.py:17
  101.9 6.2 %collective-permute-start.23 = (bf16[2,128,128]{2,1,0:T(8,128)(2,1)S(1)}, bf16[2,128,128]{2,1,0:T(8,128)(2,1)S(1)}, u32[]{:S(2)}, u32[]{:S(2)}) collective-permute-start(bf16[2,128,128]{2,1,0:T(8,128)(2,1)S(1)} %get-tuple-element.30), channel_id=1, source_target_pairs={{0,4},{4,8},{8,12},{12,0},{1,5},{5,9},{9,13},{13,1},{2,6},{6,10},{... | collective-permute-start | bytes 196616 | tf_op jit(solution)/shard_map/ppermute | solution.py:54
  102.0 7.3 %collective-permute-start.24 = (bf16[2,128,128]{2,1,0:T(8,128)(2,1)S(1)}, bf16[2,128,128]{2,1,0:T(8,128)(2,1)S(1)}, u32[]{:S(2)}, u32[]{:S(2)}) collective-permute-start(bf16[2,128,128]{2,1,0:T(8,128)(2,1)S(1)} %get-tuple-element.32), channel_id=1, source_target_pairs={{0,8},{4,12},{8,0},{12,4},{1,9},{5,13},{9,1},{13,5},{2,10},{6,14},... | collective-permute-start | bytes 196616 | tf_op jit(solution)/shard_map/ppermute | solution.py:54
  102.1 7.2 %collective-permute-start.25 = (bf16[2,128,128]{2,1,0:T(8,128)(2,1)S(1)}, bf16[2,128,128]{2,1,0:T(8,128)(2,1)S(1)}, u32[]{:S(2)}, u32[]{:S(2)}) collective-permute-start(bf16[2,128,128]{2,1,0:T(8,128)(2,1)S(1)} %get-tuple-element.31), channel_id=1, source_target_pairs={{0,12},{4,0},{8,4},{12,8},{1,13},{5,1},{9,5},{13,9},{2,14},{6,2},{... | collective-permute-start | bytes 196616 | tf_op jit(solution)/shard_map/ppermute | solution.py:54
  (5 other events, 5.9 us)

commit v2 on v0

v2 whole, which is shorter than its diff:
```python
import functools
import math

import jax
import jax.numpy as jnp
import numpy as np
from jax import lax
from jax.experimental import pallas as pl
from jax.experimental.pallas import tpu as pltpu
from jax.sharding import PartitionSpec as P

BF16 = jnp.bfloat16
F32 = jnp.float32
VMEM = pl.BlockSpec(memory_space=pltpu.VMEM)
SMEM = pl.BlockSpec(memory_space=pltpu.SMEM)


def to_neighbour(x, by, along_narrow):
    wide, narrow, cores = (lax.axis_size(name) for name in ("wide", "narrow", "probe"))
    pairs = []
    for w in range(wide):
        for n in range(narrow):
            for core in range(cores):
                w_to, n_to = (w, n + by) if core == along_narrow else (w + by, n)
                if 0 <= w_to < wide and 0 <= n_to < narrow:
                    source = (w * narrow + n) * cores + core
                    pairs.append((source, (w_to * narrow + n_to) * cores + core))
    return lax.ppermute(x, ("wide", "narrow", "probe"), pairs)


def swap(x):
    return lax.ppermute(x, "probe", [(0, 1), (1, 0)])


def dft_tables(size):
    index = np.arange(size)
    product = (index[:, None] * index[None, :]) % size
    angle = product.astype(np.float32) * np.float32(2.0 * math.pi / size)
    norm = np.float32(1.0 / math.sqrt(size))
    return (
        jnp.asarray(np.cos(angle) * norm, BF16),
        jnp.asarray(-np.sin(angle) * norm, BF16),
    )


def dot(a, b):
    return jnp.dot(a, b, preferred_element_type=F32)


def iota(shape, dim):
    return lax.broadcasted_iota(jnp.int32, shape, dim)


def one_hot(equal):
    return jnp.where(equal, 1.0, 0.0).astype(BF16)


def cyclic(at, shift, period):
    back = at - shift
    return jnp.where(back < 0, back + period, back)


def call(kernel, out_shape, in_specs, scratch=(), flops=0, bytes_accessed=0, name=None):
    return pl.pallas_call(
        kernel,
        out_shape=out_shape,
        in_specs=in_specs,
        out_specs=jax.tree.map(lambda _: VMEM, out_shape),
        scratch_shapes=list(scratch),
        compiler_params=pltpu.CompilerParams(vmem_limit_bytes=48 * 1024 * 1024),
        cost_estimate=pl.CostEstimate(
            flops=flops, bytes_accessed=bytes_accessed, transcendentals=0
        ),
        name=name,
    )


def shift_tables(corner, cos_in, sin_in, probe_in, right, right_t, left_t, left, probe):
    size = cos_in.shape[0]
    rows, cols = probe.shape[1:]
    row_start, col_start = corner[0], corner[1]
    row_hot = one_hot(cyclic(iota((rows, size), 0), row_start, rows) == iota((rows, size), 1))
    row_hot_t = one_hot(cyclic(iota((size, rows), 1), row_start, rows) == iota((size, rows), 0))
    col_hot = one_hot(cyclic(iota((cols, size), 0), col_start, cols) == iota((cols, size), 1))
    col_hot_t = one_hot(cyclic(iota((size, cols), 1), col_start, cols) == iota((size, cols), 0))

    cos_part = dot(col_hot, cos_in[...]).astype(BF16)
    right[:cols, :size] = cos_part
    right[cols:, size:] = cos_part
    sin_part = dot(col_hot, sin_in[...])
    right[:cols, size:] = sin_part.astype(BF16)
    right[cols:, :size] = (-sin_part).astype(BF16)

    cos_part = dot(cos_in[...], col_hot_t).astype(BF16)
    right_t[:size, :cols] = cos_part
    right_t[size:, cols:] = cos_part
    sin_part = dot(sin_in[...], col_hot_t)
    right_t[size:, :cols] = sin_part.astype(BF16)
    right_t[:size, cols:] = (-sin_part).astype(BF16)

    cos_part = dot(row_hot, cos_in[...]).astype(BF16)
    left_t[:rows, :size] = cos_part
    left_t[rows:, size:] = cos_part
    sin_part = dot(row_hot, sin_in[...])
    left_t[:rows, size:] = sin_part.astype(BF16)
    left_t[rows:, :size] = (-sin_part).astype(BF16)

    cos_part = dot(cos_in[...], row_hot_t).astype(BF16)
    left[:size, :rows] = cos_part
    left[size:, rows:] = cos_part
    sin_part = dot(sin_in[...], row_hot_t)
    left[size:, :rows] = sin_part.astype(BF16)
    left[:size, rows:] = (-sin_part).astype(BF16)

    for plane in range(2):
        moved = dot(row_hot, probe_in[plane]).astype(BF16)
        probe[plane] = dot(moved, col_hot_t).astype(BF16)


def slot_terms(
    scalars, own, first, first2, second, second2, third, third2,
    right, right_t, left_t, left, probe, amplitude,
    sent, kept, term, exit_wave, half, chi, back_half, patch, obj,
):
    rows, cols = own.shape[1:]
    size = chi.shape[0]
    cut = first.shape[1]
    row_start, col_start, core = scalars[0], scalars[1], scalars[2]
    live = scalars[3].astype(F32)
    step = 128
    in_cols = iota((step, cols), 1) >= col_start
    core_0 = iota((step, cols), 0) * 0 + core == 0
    for start in range(0, rows, step):
        at = pl.ds(start, step)
        in_rows = iota((step, cols), 0) + start >= row_start
        upper = start < cut
        sub = pl.ds(start if upper else start - cut, step)
        planes = []
        for plane in range(2):

            def load(on_core_0, on_core_1):
                a, b = on_core_0[plane, sub], on_core_1[plane, sub]
                return jnp.where(core_0, a.astype(F32), b.astype(F32))

            side = load(first2, first) if upper else load(second2, second)
            value = jnp.where(in_cols, own[plane, at].astype(F32), side)
            if start < size:
                below = load(second, second2) if upper else load(first, first2)
                diag = load(third2, third) if upper else load(third, third2)
                value = jnp.where(in_rows, value, jnp.where(in_cols, below, diag))
            patch[plane, at] = value.astype(BF16)
            planes.append(value)
        probe_re, probe_im = probe[0, at].astype(F32), probe[1, at].astype(F32)
        exit_wave[at, :cols] = (probe_re * planes[0] - probe_im * planes[1]).astype(BF16)
        exit_wave[at, cols:] = (probe_re * planes[1] + probe_im * planes[0]).astype(BF16)

    half[:rows] = dot(exit_wave[...], right[:, :size]).astype(BF16)
    half[rows:] = dot(exit_wave[...], right[:, size:]).astype(BF16)
    wide = 256
    for start in range(0, size, wide):
        far = dot(left[...], half[:, start : start + wide])
        far_re, far_im = far[:size], far[size:]
        magnitude = jnp.sqrt(far_re * far_re + far_im * far_im)
        amp = amplitude[:, start : start + wide].astype(F32)
        factor = (1.0 - amp / jnp.maximum(magnitude, 1.0)) * live
        chi[:, start : start + wide] = (far_re * factor).astype(BF16)
        chi[:, size + start : size + start + wide] = (far_im * factor).astype(BF16)
    back_half[:size] = dot(chi[...], right_t[:, :cols]).astype(BF16)
    back_half[size:] = dot(chi[...], right_t[:, cols:]).astype(BF16)
    for start in range(0, cols, wide):
        at = slice(start, start + wide)
        back = dot(left_t[...], back_half[:, at])
        back_re, back_im = back[:rows], back[rows:]
        probe_re, probe_im = probe[0, :, at].astype(F32), probe[1, :, at].astype(F32)
        obj[0, :, at] = (probe_re * back_re + probe_im * back_im).astype(BF16)
        obj[1, :, at] = (probe_re * back_im - probe_im * back_re).astype(BF16)
        patch_re, patch_im = patch[0, :, at].astype(F32), patch[1, :, at].astype(F32)
        term[0, :, at] = (patch_re * back_re + patch_im * back_im).astype(BF16)
        term[1, :, at] = (patch_re * back_im - patch_im * back_re).astype(BF16)
    count = kept.shape[1]
    for plane in range(2):
        kept[plane] = obj[plane, pl.ds(pl.multiple_of(cut * core, 128), count)]
        sent[plane] = obj[plane, pl.ds(pl.multiple_of(cut * (1 - core), 128), count)]


def part_of(scalars, kept, got, base, at, rows_in, cols_in):
    shape = (at.size, kept.shape[2])
    row_at, col_at = iota(shape, 0) + (base + at.start), iota(shape, 1)
    masks = []
    for row_start, col_start in ((scalars[0], scalars[1]), (scalars[4], scalars[5])):
        in_rows = jnp.where(row_at >= row_start, 1, 0) == rows_in
        in_cols = jnp.where(col_at >= col_start, 1, 0) == cols_in
        masks.append(in_rows & in_cols)
    return [
        jnp.where(masks[0], kept[plane, at].astype(F32), 0.0)
        + jnp.where(masks[1], got[plane, at].astype(F32), 0.0)
        for plane in range(2)
    ]


def fill(scalars, kept, got, out, cut, rows_in, cols_in):
    step = 128
    for start in range(0, out.shape[1], step):
        at = pl.ds(start, step)
        part = part_of(scalars, kept, got, scalars[2] * cut, at, rows_in, cols_in)
        for plane in range(2):
            out[plane, at] = part[plane].astype(out.dtype)


def diag_part(scalars, kept, got, diag):
    fill(scalars, kept, got, diag, diag.shape[1], 0, 0)


def side_parts(scalars, kept, got, now, later, own):
    core, cut = scalars[2], later.shape[1]
    fill(scalars, kept, got, now, cut, core, 1 - core)
    fill(scalars, kept, got, later, cut, 1 - core, core)
    fill(scalars, kept, got, own, cut, 1, 1)


def add_kernel(a, b, out):
    out[...] = (a[...].astype(F32) + b[...].astype(F32)).astype(out.dtype)


def total_kernel(own, a, b, out):
    cut = b.shape[1]
    for plane in range(2):
        total = own[plane, :cut] + a[plane, :cut].astype(F32) + b[plane].astype(F32)
        out[plane, :cut] = total.astype(BF16)
        out[plane, cut:] = (own[plane, cut:] + a[plane, cut:].astype(F32)).astype(BF16)


def probe_parts(scalars, term, sent, kept):
    rows, cols = term.shape[1:]
    narrow, wide, _, height, width = sent.shape
    size = wide * height
    row_start, col_start, core = scalars[0], scalars[1], scalars[2]
    row_hot = one_hot(cyclic(iota((size, rows), 1), row_start, rows) == iota((size, rows), 0))
    for plane in range(2):
        moved = dot(row_hot, term[plane]).astype(BF16)
        for block in range(narrow):
            for out, owner in ((kept, core), (sent, 1 - core)):
                column = iota((cols, width), 1) + (block * 2 + owner) * width
                hot = one_hot(cyclic(iota((cols, width), 0), col_start, cols) == column)
                result = dot(moved, hot).astype(BF16)
                for row in range(wide):
                    out[block, row, plane] = result[row * height : (row + 1) * height]


def scatter_sum(x, axis):
    length = lax.axis_size(axis)
    if length > 8:
        total = lax.psum_scatter(x, axis, scatter_dimension=0, tiled=True)
        return total[0].astype(F32)
    me = lax.axis_index(axis)

    def part(of):
        return lax.dynamic_index_in_dim(x, of, 0, keepdims=False)

    total = part(me).astype(F32)
    for step in range(1, length):
        pairs = [(i, (i + step) % length) for i in range(length)]
        got = lax.ppermute(part(lax.rem(me + step, length)), axis, pairs)
        total = total + got.astype(F32)
    return total


def shards(object_slab, probe_wave, amplitude, row_offset, col_offset, occupied):
    size = probe_wave.shape[1]
    rows, cols = object_slab.shape[1:]
    core = lax.axis_index("probe")
    narrow, wide, cores = (lax.axis_size(name) for name in ("narrow", "wide", "probe"))
    corner = jnp.stack([row_offset[0, 0, 0], col_offset[0, 0, 0]])
    scalars = jnp.concatenate([corner, jnp.stack([core.astype(jnp.int32), occupied[0, 0, 0]])])

    def shape(*dims, dtype=BF16):
        return jax.ShapeDtypeStruct(dims, dtype)

    cut = size // 2
    count = rows - cut
    first = to_neighbour(lax.dynamic_slice_in_dim(object_slab, cut * (1 - core), cut, 1), -1, 0)
    second = to_neighbour(lax.dynamic_slice_in_dim(object_slab, cut * core, count, 1), -1, 0)
    third = to_neighbour(first, -1, 1)
    late_corner, first_late = lax.optimization_barrier((corner, first))

    cos_part, sin_part = dft_tables(size)
    tables = call(
        shift_tables,
        (
            shape(2 * cols, 2 * size),
            shape(2 * size, 2 * cols),
            shape(2 * rows, 2 * size),
            shape(2 * size, 2 * rows),
            shape(2, rows, cols),
        ),
        [SMEM] + [VMEM] * 3,
        flops=4 * 10**9,
        bytes_accessed=2 * 10**7,
        name="shift_tables",
    )(late_corner, cos_part, sin_part, probe_wave)
    second, tables = lax.optimization_barrier((second, tables))
    pieces = (first, swap(first_late), second, swap(second), third, swap(third))
    sent, kept, term = call(
        slot_terms,
        (shape(2, count, cols), shape(2, count, cols), shape(2, rows, cols)),
        [SMEM] + [VMEM] * 13,
        scratch=[
            pltpu.VMEM((rows, 2 * cols), BF16),
            pltpu.VMEM((2 * rows, size), BF16),
            pltpu.VMEM((size, 2 * size), BF16),
            pltpu.VMEM((2 * size, cols), BF16),
            pltpu.VMEM((2, rows, cols), BF16),
            pltpu.VMEM((2, rows, cols), BF16),
        ],
        flops=5 * 10**9,
        bytes_accessed=2 * 10**7,
        name="slot_terms",
    )(scalars, object_slab, *pieces, *tables, amplitude[0, 0, 0])

    got = swap(sent)
    scalars = jnp.concatenate([scalars, swap(corner)])
    diag = call(diag_part, shape(2, cut, cols), [SMEM, VMEM, VMEM], name="diag_part")(
        scalars, kept, got
    )
    from_first = to_neighbour(diag, 1, 0)
    now, later, own = call(
        side_parts,
        (
            shape(2, count, cols),
            shape(2, cut, cols, dtype=F32),
            shape(2, count, cols, dtype=F32),
        ),
        [SMEM, VMEM, VMEM],
        name="side_parts",
    )(scalars, kept, got)
    from_second = to_neighbour(now, 1, 0)
    later = call(add_kernel, shape(2, cut, cols), [VMEM, VMEM], name="add")(later, from_first)
    from_third = to_neighbour(later, 1, 1)
    own = call(total_kernel, shape(2, count, cols), [VMEM] * 3, name="total")(
        own, from_second, from_third
    )
    other = swap(own)
    object_grad = jnp.where(
        core == 0,
        jnp.concatenate([own[:, :cut], other], 1),
        jnp.concatenate([other[:, :cut], own], 1),
    )

    blocks = shape(narrow, wide, 2, size // wide, size // (narrow * cores))
    sent, kept = call(
        probe_parts,
        (blocks, blocks),
        [SMEM, VMEM],
        flops=2 * 10**9,
        name="probe_parts",
    )(scalars, term)
    total = (kept.astype(F32) + swap(sent).astype(F32)).astype(BF16)
    total = scatter_sum(total, "narrow").astype(BF16)
    total = scatter_sum(total, "wide")
    return (object_grad, total * (1.0 / math.sqrt(wide * narrow * cores)))


def solution(mesh):
    in_specs = (
        P(None, ("groups", "narrow"), "wide"),
        P(),
        P(("groups", "narrow"), "wide", "probe", None, None),
        P(("groups", "narrow"), "wide", "probe"),
        P(("groups", "narrow"), "wide", "probe"),
        P(("groups", "narrow"), "wide", "probe"),
    )
    out_specs = (
        P(None, ("groups", "narrow"), "wide"),
        P(None, ("groups", "wide"), ("narrow", "probe")),
    )
    return jax.shard_map(shards, mesh=mesh, in_specs=in_specs, out_specs=out_specs, check_vma=False)
```

time: 246 us -> 94.9 us (0.39)
  the two profiles are of different devices: /device:TPU:19 before, /device:TPU:0 now
where the time goes in v2:
time: 94.9 us; the launch traced here: 94.5 us
  waiting for transfers between devices  30.6 us (32%)
  Pallas kernels  27.3 us (29%)
  starting transfers between devices  22.6 us (24%)
  local copies, waits for them, and re-layouts  6.71 us (7%)
  other arithmetic  4.55 us (5%)
  between operations  2.82 us (3%)
    ppermute x6, waiting for transfers between devices, to_neighbour(): return lax.ppermute(x, ('wide', 'narrow', 'probe'), pairs)  20.3 us
    ppermute x6, starting transfers between devices, to_neighbour(): return lax.ppermute(x, ('wide', 'narrow', 'probe'), pairs)  13.2 us
    pallas_call x1, Pallas kernels, shards(): call(slot_terms, (shape(2, count, cols), shape(2, count, cols), shape(2,...  12.8 us
    ppermute x4, waiting for transfers between devices, scatter_sum(): got = lax.ppermute(part(lax.rem(me + step, length)), axis, pairs)  7.06 us
    ppermute x4, starting transfers between devices, scatter_sum(): got = lax.ppermute(part(lax.rem(me + step, length)), axis, pairs)  5.94 us
    pallas_call x1, Pallas kernels, shards(): call(shift_tables, (shape(2 * cols, 2 * size), shape(2 * size, 2 * cols),...  5.59 us
    pallas_call x1, Pallas kernels, shards(): call(probe_parts, (blocks, blocks), [SMEM, VMEM], flops=2 * 10 ** 9, name...  3.43 us
    ppermute x7, starting transfers between devices, swap(): return lax.ppermute(x, 'probe', [(0, 1), (1, 0)])  3.38 us
  transfers between devices with their start and end apart: 17, of which 10 were waited for; matrix products, arithmetic and copies ran while one was open for 5% of the time, Pallas kernels for 14%

profile of v2, /device:TPU:0, one launch (start us, length us, event | category | flops | bytes accessed | tf_op | source)
XLA Modules:
  0.0 94.5 jit_solution(13461284889887484033)
XLA Ops:
  0.7 2.0 %constant_dynamic-slice_fusion.1 = bf16[2,256,512]{2,1,0:T(8,128)(2,1)} fusion(bf16[2,640,512]{2,1,0:T(8,128)(2,1)} %own.1, s32[]{:T(128)S(6)} %select_n.35), kind=kLoop, calls=%fused_computation.13 | loop fusion | bytes 1048580 | tf_op jit(solution)/shard_map/dynamic_slice | solution.py:281
  2.7 1.3 %collective-permute-start.1 = (bf16[2,256,512]{2,1,0:T(8,128)(2,1)}, bf16[2,256,512]{2,1,0:T(8,128)(2,1)S(1)}, u32[]{:S(2)}, u32[]{:S(2)}) collective-permute-start(bf16[2,256,512]{2,1,0:T(8,128)(2,1)} %constant_dynamic-slice_fusion.1), channel_id=1, source_target_pairs={{2,0},{5,1},{6,4},{7,3},{9,5},{10,8},{11,7},{13,9},{14,12},{15,11}... | collective-permute-start | bytes 1572872 | tf_op jit(solution)/shard_map/ppermute | solution.py:28
  4.0 1.2 %constant_dynamic-slice_fusion = bf16[2,384,512]{2,1,0:T(8,128)(2,1)S(1)} fusion(bf16[2,640,512]{2,1,0:T(8,128)(2,1)} %own.1, s32[]{:T(128)S(6)} %select_n.36), kind=kLoop, calls=%fused_computation.12 | loop fusion | bytes 1572868 | tf_op jit(solution)/shard_map/dynamic_slice | solution.py:282
  5.2 1.3 %collective-permute-start.3 = (bf16[2,384,512]{2,1,0:T(8,128)(2,1)S(1)}, bf16[2,384,512]{2,1,0:T(8,128)(2,1)S(1)}, u32[]{:S(2)}, u32[]{:S(2)}) collective-permute-start(bf16[2,384,512]{2,1,0:T(8,128)(2,1)S(1)} %constant_dynamic-slice_fusion), channel_id=1, source_target_pairs={{2,0},{5,1},{6,4},{7,3},{9,5},{10,8},{11,7},{13,9},{14,12},{15,11}... | collective-permute-start | bytes 2359304 | tf_op jit(solution)/shard_map/ppermute | solution.py:28
  7.9 6.4 %collective-permute-done.1.first = bf16[2,256,512]{2,1,0:T(8,128)(2,1)S(1)} collective-permute-done((bf16[2,256,512]{2,1,0:T(8,128)(2,1)}, bf16[2,256,512]{2,1,0:T(8,128)(2,1)S(1)}, u32[]{:S(2)}, u32[]{:S(2)}) %collective-permute-start.1) | collective-permute-done | bytes 524320 | tf_op jit(solution)/shard_map/ppermute | solution.py:28
  14.3 1.3 %collective-permute-start.5 = (bf16[2,256,512]{2,1,0:T(8,128)(2,1)S(1)}, bf16[2,256,512]{2,1,0:T(8,128)(2,1)S(1)}, u32[]{:S(2)}, u32[]{:S(2)}) collective-permute-start(bf16[2,256,512]{2,1,0:T(8,128)(2,1)S(1)} %collective-permute-done.1.first), channel_id=1, source_target_pairs={{3,1},{4,0},{6,2},{7,5},{8,4},{10,6},{11,9},{12,8},{14,10},{15,13}... | collective-permute-start | bytes 1572872 | tf_op jit(solution)/shard_map/ppermute | solution.py:28
  15.6 5.6 %shift_tables.1 = (bf16[1024,1024]{1,0:T(8,128)(2,1)S(1)}, bf16[1024,1024]{1,0:T(8,128)(2,1)}, bf16[1280,1024]{1,0:T(8,128)(2,1)}, bf16[1024,1280]{1,0:T(8,128)(2,1)}, bf16[2,640,512]{2,1,0:T(8,128)(2,1)S(1)}) custom-call(s32[2]{0:T(128)S(1)} %pad_add_fusion.corner, bf16[512,512]{1,0:T(8,128)(2,1)S(1)} %copy-done.4, bf16[512,512]{1,0:T(8,128)(2,1)S(1)} %copy-done.5, ...), custom_call_target="tpu_custom_call" | custom-call | flops 4000000000 | bytes 20000000 | tf_op jit(solution)/shard_map/shift_tables/pallas_call | solution.py:287
  21.2 1.4 %copy-done.6 = bf16[1024,1024]{1,0:T(8,128)(2,1)} copy-done((bf16[1024,1024]{1,0:T(8,128)(2,1)}, bf16[1024,1024]{1,0:T(8,128)(2,1)S(1)}, u32[]{:S(2)}) %copy-start.6) | copy-done | bytes 2097176
  22.6 1.1 %copy-done.7 = bf16[2,640,512]{2,1,0:T(8,128)(2,1)} copy-done((bf16[2,640,512]{2,1,0:T(8,128)(2,1)}, bf16[2,640,512]{2,1,0:T(8,128)(2,1)S(1)}, u32[]{:S(2)}) %copy-start.7) | copy-done | bytes 1310744
  23.6 3.0 %collective-permute-done.3.second = bf16[2,384,512]{2,1,0:T(8,128)(2,1)S(1)} collective-permute-done((bf16[2,384,512]{2,1,0:T(8,128)(2,1)S(1)}, bf16[2,384,512]{2,1,0:T(8,128)(2,1)S(1)}, u32[]{:S(2)}, u32[]{:S(2)}) %collective-permute-start.3) | collective-permute-done | bytes 786464 | tf_op jit(solution)/shard_map/ppermute | solution.py:28
  27.1 1.1 %collective-permute-done.5.third = bf16[2,256,512]{2,1,0:T(8,128)(2,1)S(1)} collective-permute-done((bf16[2,256,512]{2,1,0:T(8,128)(2,1)S(1)}, bf16[2,256,512]{2,1,0:T(8,128)(2,1)S(1)}, u32[]{:S(2)}, u32[]{:S(2)}) %collective-permute-start.5) | collective-permute-done | bytes 524320 | tf_op jit(solution)/shard_map/ppermute | solution.py:28
  30.4 12.8 %slot_terms.1 = (bf16[2,384,512]{2,1,0:T(8,128)(2,1)S(1)}, bf16[2,384,512]{2,1,0:T(8,128)(2,1)S(1)}, bf16[2,640,512]{2,1,0:T(8,128)(2,1)}) custom-call(s32[4]{0:T(128)S(1)} %pad_add_fusion.1.scalars, bf16[2,640,512]{2,1,0:T(8,128)(2,1)} %own.1, bf16[2,256,512]{2,1,0:T(8,128)(2,1)S(1)} %collective-permute-done.1.first, ...), custom_call_target="tpu_custom_call" | custom-call | flops 5000000000 | bytes 20000000 | tf_op jit(solution)/shard_map/slot_terms/pallas_call | solution.py:303
  43.7 1.8 %collective-permute-done = s32[2]{0:T(128)S(1)} collective-permute-done((s32[2]{0:T(128)S(1)}, s32[2]{0:T(128)S(1)}, u32[]{:S(2)}, u32[]{:S(2)}) %collective-permute-start) | collective-permute-done | bytes 40 | tf_op jit(solution)/shard_map/ppermute | solution.py:32
  45.6 0.9 diag_part.1
  46.5 3.5 %collective-permute-start.9 = (bf16[2,256,512]{2,1,0:T(8,128)(2,1)S(1)}, bf16[2,256,512]{2,1,0:T(8,128)(2,1)S(1)}, u32[]{:S(2)}, u32[]{:S(2)}) collective-permute-start(bf16[2,256,512]{2,1,0:T(8,128)(2,1)S(1)} %diag_part.1), channel_id=1, source_target_pairs={{0,2},{1,5},{3,7},{4,6},{5,9},{7,11},{8,10},{9,13},{11,15},{12,14}... | collective-permute-start | bytes 1572872 | tf_op jit(solution)/shard_map/ppermute | solution.py:28
  50.0 3.4 %probe_parts.1 = (bf16[2,4,2,128,128]{4,3,2,1,0:T(8,128)(2,1)}, bf16[2,4,2,128,128]{4,3,2,1,0:T(8,128)(2,1)S(1)}) custom-call(s32[6]{0:T(128)S(1)} %concatenate.14.scalars, bf16[2,640,512]{2,1,0:T(8,128)(2,1)S(1)} %copy-done.8), custom_call_target="tpu_custom_call" | custom-call | flops 2000000000 | tf_op jit(solution)/shard_map/probe_parts/pallas_call | solution.py:350
  54.2 2.2 %collective-permute-start.12 = (bf16[2,4,2,128,128]{4,3,2,1,0:T(8,128)(2,1)}, bf16[2,4,2,128,128]{4,3,2,1,0:T(8,128)(2,1)}, u32[]{:S(2)}, u32[]{:S(2)}) collective-permute-start(bf16[2,4,2,128,128]{4,3,2,1,0:T(8,128)(2,1)} %get-tuple-element.43), channel_id=1, source_target_pairs={{0,1},{1,0},{2,3},{3,2},{4,5},{5,4},{6,7},{7,6},{8,9},{9,8},{10,11... | collective-permute-start | bytes 1572872 | tf_op jit(solution)/shard_map/ppermute | solution.py:32
  56.4 2.4 %side_parts.1 = (bf16[2,384,512]{2,1,0:T(8,128)(2,1)}, f32[2,256,512]{2,1,0:T(8,128)S(1)}, f32[2,384,512]{2,1,0:T(8,128)S(1)}) custom-call(s32[6]{0:T(128)S(1)} %concatenate.14.scalars, bf16[2,384,512]{2,1,0:T(8,128)(2,1)S(1)} %get-tuple-element.36.kept, bf16[2,384,512]{2,1,0:T(8,128)(2,1)S(1)} %collective-permute-done.7.got), custom_call_target="tpu_custom_call" | custom-call | tf_op jit(solution)/shard_map/side_parts/pallas_call | solution.py:326
  58.8 1.6 %collective-permute-start.8 = (bf16[2,384,512]{2,1,0:T(8,128)(2,1)}, bf16[2,384,512]{2,1,0:T(8,128)(2,1)S(1)}, u32[]{:S(2)}, u32[]{:S(2)}) collective-permute-start(bf16[2,384,512]{2,1,0:T(8,128)(2,1)} %get-tuple-element.39), channel_id=1, source_target_pairs={{0,2},{1,5},{3,7},{4,6},{5,9},{7,11},{8,10},{9,13},{11,15},{12,14}... | collective-permute-start | bytes 2359304 | tf_op jit(solution)/shard_map/ppermute | solution.py:28
  60.5 0.9 add.98
  61.4 4.3 %collective-permute-start.10 = (bf16[2,256,512]{2,1,0:T(8,128)(2,1)}, bf16[2,256,512]{2,1,0:T(8,128)(2,1)}, u32[]{:S(2)}, u32[]{:S(2)}) collective-permute-start(bf16[2,256,512]{2,1,0:T(8,128)(2,1)} %add.98), channel_id=1, source_target_pairs={{0,4},{1,3},{2,6},{4,8},{5,7},{6,10},{8,12},{9,11},{10,14},{13,15}... | collective-permute-start | bytes 1572872 | tf_op jit(solution)/shard_map/ppermute | solution.py:28
  65.7 1.2 %add_convert_fusion = bf16[2,4,2,128,128]{4,3,2,1,0:T(8,128)(2,1)S(1)} fusion(bf16[2,4,2,128,128]{4,3,2,1,0:T(8,128)(2,1)} %collective-permute-done.12, bf16[2,4,2,128,128]{4,3,2,1,0:T(8,128)(2,1)S(1)} %copy-done.1), kind=kLoop, calls=%fused_computation.1 | loop fusion | flops 1048576 | bytes 1572864 | tf_op jit(solution)/shard_map/convert_element_type | solution.py:357
  67.0 8.4 %collective-permute-done.8.a = bf16[2,384,512]{2,1,0:T(8,128)(2,1)S(1)} collective-permute-done((bf16[2,384,512]{2,1,0:T(8,128)(2,1)}, bf16[2,384,512]{2,1,0:T(8,128)(2,1)S(1)}, u32[]{:S(2)}, u32[]{:S(2)}) %collective-permute-start.8) | collective-permute-done | bytes 786464 | tf_op jit(solution)/shard_map/ppermute | solution.py:28
  75.3 1.5 %collective-permute-done.10.b = bf16[2,256,512]{2,1,0:T(8,128)(2,1)} collective-permute-done((bf16[2,256,512]{2,1,0:T(8,128)(2,1)}, bf16[2,256,512]{2,1,0:T(8,128)(2,1)}, u32[]{:S(2)}, u32[]{:S(2)}) %collective-permute-start.10) | collective-permute-done | bytes 524320 | tf_op jit(solution)/shard_map/ppermute | solution.py:28
  76.9 1.2 %total.1 = bf16[2,384,512]{2,1,0:T(8,128)(2,1)S(1)} custom-call(f32[2,384,512]{2,1,0:T(8,128)S(1)} %get-tuple-element.38.own, bf16[2,384,512]{2,1,0:T(8,128)(2,1)S(1)} %collective-permute-done.8.a, bf16[2,256,512]{2,1,0:T(8,128)(2,1)} %collective-permute-done.10.b), custom_call_target="tpu_custom_call" | custom-call | tf_op jit(solution)/shard_map/total/pallas_call | solution.py:339
  78.2 2.6 %collective-permute-done.13 = bf16[4,2,128,128]{3,2,1,0:T(8,128)(2,1)} collective-permute-done((bf16[4,2,128,128]{3,2,1,0:T(8,128)(2,1)S(1)}, bf16[4,2,128,128]{3,2,1,0:T(8,128)(2,1)}, u32[]{:S(2)}, u32[]{:S(2)}) %collective-permute-start.13) | collective-permute-done | bytes 262176 | tf_op jit(solution)/shard_map/ppermute | solution.py:263
  80.8 1.1 %fusion = bf16[4,2,128,128]{3,2,1,0:T(8,128)(2,1)S(1)} fusion(bf16[4,2,128,128]{3,2,1,0:T(8,128)(2,1)} %collective-permute-done.13, bf16[2,4,2,128,128]{4,3,2,1,0:T(8,128)(2,1)} %copy-done.9, s32[]{:T(128)S(6)} %select_n.38), kind=kLoop, calls=%fused_computation.3 | loop fusion | flops 524288 | bytes 786436 | tf_op jit(solution)/shard_map/convert_element_type | solution.py:358
  82.0 2.9 %collective-permute-start.16 = (bf16[2,128,128]{2,1,0:T(8,128)(2,1)S(1)}, bf16[2,128,128]{2,1,0:T(8,128)(2,1)S(1)}, u32[]{:S(2)}, u32[]{:S(2)}) collective-permute-start(bf16[2,128,128]{2,1,0:T(8,128)(2,1)S(1)} %get-tuple-element.45), channel_id=1, source_target_pairs={{0,12},{4,0},{8,4},{12,8},{1,13},{5,1},{9,5},{13,9},{2,14},{6,2},{... | collective-permute-start | bytes 196616 | tf_op jit(solution)/shard_map/ppermute | solution.py:263
  84.9 1.0 %collective-permute-start.15 = (bf16[2,128,128]{2,1,0:T(8,128)(2,1)S(1)}, bf16[2,128,128]{2,1,0:T(8,128)(2,1)S(1)}, u32[]{:S(2)}, u32[]{:S(2)}) collective-permute-start(bf16[2,128,128]{2,1,0:T(8,128)(2,1)S(1)} %get-tuple-element.46), channel_id=1, source_target_pairs={{0,8},{4,12},{8,0},{12,4},{1,9},{5,13},{9,1},{13,5},{2,10},{6,14},... | collective-permute-start | bytes 196616 | tf_op jit(solution)/shard_map/ppermute | solution.py:263
  85.9 1.9 %collective-permute-start.14 = (bf16[2,128,128]{2,1,0:T(8,128)(2,1)S(1)}, bf16[2,128,128]{2,1,0:T(8,128)(2,1)S(1)}, u32[]{:S(2)}, u32[]{:S(2)}) collective-permute-start(bf16[2,128,128]{2,1,0:T(8,128)(2,1)S(1)} %get-tuple-element.44), channel_id=1, source_target_pairs={{0,4},{4,8},{8,12},{12,0},{1,5},{5,9},{9,13},{13,1},{2,6},{6,10},{... | collective-permute-start | bytes 196616 | tf_op jit(solution)/shard_map/ppermute | solution.py:263
  87.9 4.4 %collective-permute-done.15 = bf16[2,128,128]{2,1,0:T(8,128)(2,1)S(1)} collective-permute-done((bf16[2,128,128]{2,1,0:T(8,128)(2,1)S(1)}, bf16[2,128,128]{2,1,0:T(8,128)(2,1)S(1)}, u32[]{:S(2)}, u32[]{:S(2)}) %collective-permute-start.15) | collective-permute-done | bytes 65568 | tf_op jit(solution)/shard_map/ppermute | solution.py:263
  93.1 1.4 %maximum_select_fusion = bf16[2,640,512]{2,1,0:T(8,128)(2,1)} fusion(bf16[2,384,512]{2,1,0:T(8,128)(2,1)S(1)} %collective-permute-done.11, bf16[2,256,512]{2,1,0:T(8,128)(2,1)S(1)} %slice.8, bf16[2,384,512]{2,1,0:T(8,128)(2,1)S(1)} %total.1, bf16[2,256,512]{2,1,0:T(8,128)(2,1)S(1)} %slice.9, pred[]{:T(512)S(6)} %eq.3), kind=kLoop, calls=%fused_computation | loop fusion | flops 5898240 | bytes 3932161 | tf_op jit(solution)/shard_map/jit(_where)/select_n | solution.py:343
  (42 shorter events, 4.6 us)
Async XLA Ops:
  0.6 14.9 %copy-start.2 = (bf16[2,512,512]{2,1,0:T(8,128)(2,1)S(1)}, bf16[2,512,512]{2,1,0:T(8,128)(2,1)}, u32[]{:S(2)}) copy-start(bf16[2,512,512]{2,1,0:T(8,128)(2,1)} %probe_in.1) | copy-start | bytes 3145732
  0.6 14.9 %copy-start.4 = (bf16[512,512]{1,0:T(8,128)(2,1)S(1)}, bf16[512,512]{1,0:T(8,128)(2,1)}, u32[]{:S(2)}) copy-start(bf16[512,512]{1,0:T(8,128)(2,1)} %constant.55.clone.cos_in) | copy-start | bytes 1572868
  0.7 14.9 %copy-start.5 = (bf16[512,512]{1,0:T(8,128)(2,1)S(1)}, bf16[512,512]{1,0:T(8,128)(2,1)}, u32[]{:S(2)}) copy-start(bf16[512,512]{1,0:T(8,128)(2,1)} %constant.56.clone.sin_in) | copy-start | bytes 1572868
  2.7 11.6 %collective-permute-start.1 = (bf16[2,256,512]{2,1,0:T(8,128)(2,1)}, bf16[2,256,512]{2,1,0:T(8,128)(2,1)S(1)}, u32[]{:S(2)}, u32[]{:S(2)}) collective-permute-start(bf16[2,256,512]{2,1,0:T(8,128)(2,1)} %constant_dynamic-slice_fusion.1), channel_id=1, source_target_pairs={{2,0},{5,1},{6,4},{7,3},{9,5},{10,8},{11,7},{13,9},{14,12},{15,11}... | collective-permute-start | bytes 1572872 | tf_op jit(solution)/shard_map/ppermute | solution.py:28
  5.2 21.4 %collective-permute-start.3 = (bf16[2,384,512]{2,1,0:T(8,128)(2,1)S(1)}, bf16[2,384,512]{2,1,0:T(8,128)(2,1)S(1)}, u32[]{:S(2)}, u32[]{:S(2)}) collective-permute-start(bf16[2,384,512]{2,1,0:T(8,128)(2,1)S(1)} %constant_dynamic-slice_fusion), channel_id=1, source_target_pairs={{2,0},{5,1},{6,4},{7,3},{9,5},{10,8},{11,7},{13,9},{14,12},{15,11}... | collective-permute-start | bytes 2359304 | tf_op jit(solution)/shard_map/ppermute | solution.py:28
  7.8 22.5 %copy-start.3 = (bf16[1,1,1,512,512]{4,3,2,1,0:T(8,128)(2,1)S(1)}, bf16[1,1,1,512,512]{4,3,2,1,0:T(8,128)(2,1)}, u32[]{:S(2)}) copy-start(bf16[1,1,1,512,512]{4,3,2,1,0:T(8,128)(2,1)} %param.10) | copy-start | bytes 1572868
  14.3 13.9 %collective-permute-start.5 = (bf16[2,256,512]{2,1,0:T(8,128)(2,1)S(1)}, bf16[2,256,512]{2,1,0:T(8,128)(2,1)S(1)}, u32[]{:S(2)}, u32[]{:S(2)}) collective-permute-start(bf16[2,256,512]{2,1,0:T(8,128)(2,1)S(1)} %collective-permute-done.1.first), channel_id=1, source_target_pairs={{3,1},{4,0},{6,2},{7,5},{8,4},{10,6},{11,9},{12,8},{14,10},{15,13}... | collective-permute-start | bytes 1572872 | tf_op jit(solution)/shard_map/ppermute | solution.py:28
  21.2 1.4 %copy-start.6 = (bf16[1024,1024]{1,0:T(8,128)(2,1)}, bf16[1024,1024]{1,0:T(8,128)(2,1)S(1)}, u32[]{:S(2)}) copy-start(bf16[1024,1024]{1,0:T(8,128)(2,1)S(1)} %get-tuple-element.31.right) | copy-start | bytes 6291460
  22.6 1.1 %copy-start.7 = (bf16[2,640,512]{2,1,0:T(8,128)(2,1)}, bf16[2,640,512]{2,1,0:T(8,128)(2,1)S(1)}, u32[]{:S(2)}) copy-start(bf16[2,640,512]{2,1,0:T(8,128)(2,1)S(1)} %get-tuple-element.35.probe) | copy-start | bytes 3932164
  26.6 3.8 %collective-permute-start.4 = (bf16[2,384,512]{2,1,0:T(8,128)(2,1)S(1)}, bf16[2,384,512]{2,1,0:T(8,128)(2,1)S(1)}, u32[]{:S(2)}, u32[]{:S(2)}) collective-permute-start(bf16[2,384,512]{2,1,0:T(8,128)(2,1)S(1)} %collective-permute-done.3.second), channel_id=1, source_target_pairs={{0,1},{1,0},{2,3},{3,2},{4,5},{5,4},{6,7},{7,6},{8,9},{9,8},{10,11... | collective-permute-start | bytes 2359304 | tf_op jit(solution)/shard_map/ppermute | solution.py:32
  26.6 3.0 %collective-permute-start.2 = (bf16[2,256,512]{2,1,0:T(8,128)(2,1)S(1)}, bf16[2,256,512]{2,1,0:T(8,128)(2,1)S(1)}, u32[]{:S(2)}, u32[]{:S(2)}) collective-permute-start(bf16[2,256,512]{2,1,0:T(8,128)(2,1)S(1)} %collective-permute-done.1.first), channel_id=1, source_target_pairs={{0,1},{1,0},{2,3},{3,2},{4,5},{5,4},{6,7},{7,6},{8,9},{9,8},{10,11... | collective-permute-start | bytes 1572872 | tf_op jit(solution)/shard_map/ppermute | solution.py:32
  28.2 2.2 %collective-permute-start.6 = (bf16[2,256,512]{2,1,0:T(8,128)(2,1)S(1)}, bf16[2,256,512]{2,1,0:T(8,128)(2,1)S(1)}, u32[]{:S(2)}, u32[]{:S(2)}) collective-permute-start(bf16[2,256,512]{2,1,0:T(8,128)(2,1)S(1)} %collective-permute-done.5.third), channel_id=1, source_target_pairs={{0,1},{1,0},{2,3},{3,2},{4,5},{5,4},{6,7},{7,6},{8,9},{9,8},{10,11... | collective-permute-start | bytes 1572872 | tf_op jit(solution)/shard_map/ppermute | solution.py:32
  43.2 2.4 %collective-permute-start.7 = (bf16[2,384,512]{2,1,0:T(8,128)(2,1)S(1)}, bf16[2,384,512]{2,1,0:T(8,128)(2,1)S(1)}, u32[]{:S(2)}, u32[]{:S(2)}) collective-permute-start(bf16[2,384,512]{2,1,0:T(8,128)(2,1)S(1)} %get-tuple-element.37), channel_id=1, source_target_pairs={{0,1},{1,0},{2,3},{3,2},{4,5},{5,4},{6,7},{7,6},{8,9},{9,8},{10,11... | collective-permute-start | bytes 2359304 | tf_op jit(solution)/shard_map/ppermute | solution.py:32
  43.4 2.2 %collective-permute-start = (s32[2]{0:T(128)S(1)}, s32[2]{0:T(128)S(1)}, u32[]{:S(2)}, u32[]{:S(2)}) collective-permute-start(s32[2]{0:T(128)S(1)} %pad_add_fusion.corner), channel_id=1, source_target_pairs={{0,1},{1,0},{2,3},{3,2},{4,5},{5,4},{6,7},{7,6},{8,9},{9,8},{10,11... | collective-permute-start | bytes 32 | tf_op jit(solution)/shard_map/ppermute | solution.py:32
  45.6 4.4 %copy-start.8 = (bf16[2,640,512]{2,1,0:T(8,128)(2,1)S(1)}, bf16[2,640,512]{2,1,0:T(8,128)(2,1)}, u32[]{:S(2)}) copy-start(bf16[2,640,512]{2,1,0:T(8,128)(2,1)} %get-tuple-element.41.term) | copy-start | bytes 3932164
  46.5 14.0 %collective-permute-start.9 = (bf16[2,256,512]{2,1,0:T(8,128)(2,1)S(1)}, bf16[2,256,512]{2,1,0:T(8,128)(2,1)S(1)}, u32[]{:S(2)}, u32[]{:S(2)}) collective-permute-start(bf16[2,256,512]{2,1,0:T(8,128)(2,1)S(1)} %diag_part.1), channel_id=1, source_target_pairs={{0,2},{1,5},{3,7},{4,6},{5,9},{7,11},{8,10},{9,13},{11,15},{12,14}... | collective-permute-start | bytes 1572872 | tf_op jit(solution)/shard_map/ppermute | solution.py:28
  53.4 0.8 copy-start
  54.2 11.4 %collective-permute-start.12 = (bf16[2,4,2,128,128]{4,3,2,1,0:T(8,128)(2,1)}, bf16[2,4,2,128,128]{4,3,2,1,0:T(8,128)(2,1)}, u32[]{:S(2)}, u32[]{:S(2)}) collective-permute-start(bf16[2,4,2,128,128]{4,3,2,1,0:T(8,128)(2,1)} %get-tuple-element.43), channel_id=1, source_target_pairs={{0,1},{1,0},{2,3},{3,2},{4,5},{5,4},{6,7},{7,6},{8,9},{9,8},{10,11... | collective-permute-start | bytes 1572872 | tf_op jit(solution)/shard_map/ppermute | solution.py:32
  58.8 6.8 %copy-start.1 = (bf16[2,4,2,128,128]{4,3,2,1,0:T(8,128)(2,1)S(1)}, bf16[2,4,2,128,128]{4,3,2,1,0:T(8,128)(2,1)}, u32[]{:S(2)}) copy-start(bf16[2,4,2,128,128]{4,3,2,1,0:T(8,128)(2,1)} %copy-done) | copy-start | bytes 1572868
  58.8 16.5 %collective-permute-start.8 = (bf16[2,384,512]{2,1,0:T(8,128)(2,1)}, bf16[2,384,512]{2,1,0:T(8,128)(2,1)S(1)}, u32[]{:S(2)}, u32[]{:S(2)}) collective-permute-start(bf16[2,384,512]{2,1,0:T(8,128)(2,1)} %get-tuple-element.39), channel_id=1, source_target_pairs={{0,2},{1,5},{3,7},{4,6},{5,9},{7,11},{8,10},{9,13},{11,15},{12,14}... | collective-permute-start | bytes 2359304 | tf_op jit(solution)/shard_map/ppermute | solution.py:28
  61.4 15.5 %collective-permute-start.10 = (bf16[2,256,512]{2,1,0:T(8,128)(2,1)}, bf16[2,256,512]{2,1,0:T(8,128)(2,1)}, u32[]{:S(2)}, u32[]{:S(2)}) collective-permute-start(bf16[2,256,512]{2,1,0:T(8,128)(2,1)} %add.98), channel_id=1, source_target_pairs={{0,4},{1,3},{2,6},{4,8},{5,7},{6,10},{8,12},{9,11},{10,14},{13,15}... | collective-permute-start | bytes 1572872 | tf_op jit(solution)/shard_map/ppermute | solution.py:28
  66.8 10.0 %copy-start.9 = (bf16[2,4,2,128,128]{4,3,2,1,0:T(8,128)(2,1)}, bf16[2,4,2,128,128]{4,3,2,1,0:T(8,128)(2,1)S(1)}, u32[]{:S(2)}) copy-start(bf16[2,4,2,128,128]{4,3,2,1,0:T(8,128)(2,1)S(1)} %add_convert_fusion) | copy-start | bytes 1572868
  66.9 14.0 %collective-permute-start.13 = (bf16[4,2,128,128]{3,2,1,0:T(8,128)(2,1)S(1)}, bf16[4,2,128,128]{3,2,1,0:T(8,128)(2,1)}, u32[]{:S(2)}, u32[]{:S(2)}) collective-permute-start(bf16[4,2,128,128]{3,2,1,0:T(8,128)(2,1)S(1)} %dynamic-slice_bitcast_fusion), channel_id=1, source_target_pairs={{0,2},{2,0},{1,3},{3,1},{4,6},{6,4},{5,7},{7,5},{8,10},{10,8},{9,1... | collective-permute-start | bytes 786440 | tf_op jit(solution)/shard_map/ppermute | solution.py:263
  78.1 14.9 %collective-permute-start.11 = (bf16[2,384,512]{2,1,0:T(8,128)(2,1)S(1)}, bf16[2,384,512]{2,1,0:T(8,128)(2,1)S(1)}, u32[]{:S(2)}, u32[]{:S(2)}) collective-permute-start(bf16[2,384,512]{2,1,0:T(8,128)(2,1)S(1)} %total.1), channel_id=1, source_target_pairs={{0,1},{1,0},{2,3},{3,2},{4,5},{5,4},{6,7},{7,6},{8,9},{9,8},{10,11... | collective-permute-start | bytes 2359304 | tf_op jit(solution)/shard_map/ppermute | solution.py:32
  82.0 5.9 %collective-permute-start.16 = (bf16[2,128,128]{2,1,0:T(8,128)(2,1)S(1)}, bf16[2,128,128]{2,1,0:T(8,128)(2,1)S(1)}, u32[]{:S(2)}, u32[]{:S(2)}) collective-permute-start(bf16[2,128,128]{2,1,0:T(8,128)(2,1)S(1)} %get-tuple-element.45), channel_id=1, source_target_pairs={{0,12},{4,0},{8,4},{12,8},{1,13},{5,1},{9,5},{13,9},{2,14},{6,2},{... | collective-permute-start | bytes 196616 | tf_op jit(solution)/shard_map/ppermute | solution.py:263
  84.9 7.4 %collective-permute-start.15 = (bf16[2,128,128]{2,1,0:T(8,128)(2,1)S(1)}, bf16[2,128,128]{2,1,0:T(8,128)(2,1)S(1)}, u32[]{:S(2)}, u32[]{:S(2)}) collective-permute-start(bf16[2,128,128]{2,1,0:T(8,128)(2,1)S(1)} %get-tuple-element.46), channel_id=1, source_target_pairs={{0,8},{4,12},{8,0},{12,4},{1,9},{5,13},{9,1},{13,5},{2,10},{6,14},... | collective-permute-start | bytes 196616 | tf_op jit(solution)/shard_map/ppermute | solution.py:263
  85.9 6.4 %collective-permute-start.14 = (bf16[2,128,128]{2,1,0:T(8,128)(2,1)S(1)}, bf16[2,128,128]{2,1,0:T(8,128)(2,1)S(1)}, u32[]{:S(2)}, u32[]{:S(2)}) collective-permute-start(bf16[2,128,128]{2,1,0:T(8,128)(2,1)S(1)} %get-tuple-element.44), channel_id=1, source_target_pairs={{0,4},{4,8},{8,12},{12,0},{1,5},{5,9},{9,13},{13,1},{2,6},{6,10},{... | collective-permute-start | bytes 196616 | tf_op jit(solution)/shard_map/ppermute | solution.py:263

commit v3 on v2

--- a/solution.py
+++ b/solution.py
@@ -13,14 +13,15 @@
 F32 = jnp.float32
 VMEM = pl.BlockSpec(memory_space=pltpu.VMEM)
 SMEM = pl.BlockSpec(memory_space=pltpu.SMEM)
-
-
-def to_neighbour(x, by, along_narrow):
+ANY = pl.BlockSpec(memory_space=pl.ANY)
+
+
+def to_neighbour(x, by, along_narrow, senders=(0, 1)):
     wide, narrow, cores = (lax.axis_size(name) for name in ("wide", "narrow", "probe"))
     pairs = []
     for w in range(wide):
         for n in range(narrow):
-            for core in range(cores):
+            for core in senders:
                 w_to, n_to = (w, n + by) if core == along_narrow else (w + by, n)
                 if 0 <= w_to < wide and 0 <= n_to < narrow:
                     source = (w * narrow + n) * cores + core
@@ -60,14 +61,14 @@
     return jnp.where(back < 0, back + period, back)
 
 
-def call(kernel, out_shape, in_specs, scratch=(), flops=0, bytes_accessed=0, name=None):
+def call(kernel, out_shape, in_specs, vmem, scratch=(), flops=0, bytes_accessed=0, name=None):
     return pl.pallas_call(
         kernel,
         out_shape=out_shape,
         in_specs=in_specs,
         out_specs=jax.tree.map(lambda _: VMEM, out_shape),
         scratch_shapes=list(scratch),
-        compiler_params=pltpu.CompilerParams(vmem_limit_bytes=48 * 1024 * 1024),
+        compiler_params=pltpu.CompilerParams(vmem_limit_bytes=vmem * 1024 * 1024),
         cost_estimate=pl.CostEstimate(
             flops=flops, bytes_accessed=bytes_accessed, transcendentals=0
         ),
@@ -75,14 +76,24 @@
     )
 
 
-def shift_tables(corner, cos_in, sin_in, probe_in, right, right_t, left_t, left, probe):
+def shift_tables(
+    width, scalars, cos_in, sin_in, probe_in,
+    right, right_t, left_t, left, probe, back_rows, back_cols, back_cols2,
+):
     size = cos_in.shape[0]
     rows, cols = probe.shape[1:]
-    row_start, col_start = corner[0], corner[1]
+    row_start, col_start, core = scalars[0], scalars[1], scalars[2]
     row_hot = one_hot(cyclic(iota((rows, size), 0), row_start, rows) == iota((rows, size), 1))
     row_hot_t = one_hot(cyclic(iota((size, rows), 1), row_start, rows) == iota((size, rows), 0))
     col_hot = one_hot(cyclic(iota((cols, size), 0), col_start, cols) == iota((cols, size), 1))
     col_hot_t = one_hot(cyclic(iota((size, cols), 1), col_start, cols) == iota((size, cols), 0))
+
+    back_rows[...] = row_hot_t
+    count = back_cols.shape[1]
+    for out, owner in ((back_cols, core), (back_cols2, 1 - core)):
+        at = iota((cols, count), 1)
+        column = at + (at // width + owner) * width
+        out[...] = one_hot(cyclic(iota((cols, count), 0), col_start, cols) == column)
 
     cos_part = dot(col_hot, cos_in[...]).astype(BF16)
     right[:cols, :size] = cos_part
@@ -119,8 +130,8 @@
 
 def slot_terms(
     scalars, own, first, first2, second, second2, third, third2,
-    right, right_t, left_t, left, probe, amplitude,
-    sent, kept, term, exit_wave, half, chi, back_half, patch, obj,
+    right, right_t, left_t, left, probe, back_rows, back_cols, back_cols2, amplitude,
+    sent, kept, probe_sent, probe_kept, exit_wave, half, chi, back_half, patch, obj, term,
 ):
     rows, cols = own.shape[1:]
     size = chi.shape[0]
@@ -182,12 +193,23 @@
         kept[plane] = obj[plane, pl.ds(pl.multiple_of(cut * core, 128), count)]
         sent[plane] = obj[plane, pl.ds(pl.multiple_of(cut * (1 - core), 128), count)]
 
-
-def part_of(scalars, kept, got, base, at, rows_in, cols_in):
+    narrow, blocks, _, height, width = probe_sent.shape
+    for plane in range(2):
+        moved = dot(back_rows[...], term[plane]).astype(BF16)
+        for out, hot in ((probe_sent, back_cols2), (probe_kept, back_cols)):
+            result = dot(moved, hot[...]).astype(BF16)
+            for column in range(narrow):
+                for row in range(blocks):
+                    out[column, row, plane] = result[
+                        row * height : (row + 1) * height, column * width : (column + 1) * width
+                    ]
+
+
+def part_of(scalars, kept, got, cut, at, rows_in, cols_in):
     shape = (at.size, kept.shape[2])
-    row_at, col_at = iota(shape, 0) + (base + at.start), iota(shape, 1)
+    row_at, col_at = iota(shape, 0) + (scalars[2] * cut + at.start), iota(shape, 1)
     masks = []
-    for row_start, col_start in ((scalars[0], scalars[1]), (scalars[4], scalars[5])):
+    for row_start, col_start in ((scalars[0], scalars[1]), (scalars[5], scalars[6])):
         in_rows = jnp.where(row_at >= row_start, 1, 0) == rows_in
         in_cols = jnp.where(col_at >= col_start, 1, 0) == cols_in
         masks.append(in_rows & in_cols)
@@ -198,71 +220,85 @@
     ]
 
 
-def fill(scalars, kept, got, out, cut, rows_in, cols_in):
+def tile_part(cut, rows_in, cols_in, scalars, kept, got, *refs):
+    *arrived, out = refs
+    fill(cut, 0, rows_in, cols_in, scalars, kept, got, arrived, out)
+
+
+def fill(cut, first, rows_in, cols_in, scalars, kept, got, arrived, out):
     step = 128
     for start in range(0, out.shape[1], step):
         at = pl.ds(start, step)
-        part = part_of(scalars, kept, got, scalars[2] * cut, at, rows_in, cols_in)
+        part = part_of(scalars, kept, got, cut, pl.ds(first + start, step), rows_in, cols_in)
         for plane in range(2):
-            out[plane, at] = part[plane].astype(out.dtype)
-
-
-def diag_part(scalars, kept, got, diag):
-    fill(scalars, kept, got, diag, diag.shape[1], 0, 0)
-
-
-def side_parts(scalars, kept, got, now, later, own):
-    core, cut = scalars[2], later.shape[1]
-    fill(scalars, kept, got, now, cut, core, 1 - core)
-    fill(scalars, kept, got, later, cut, 1 - core, core)
-    fill(scalars, kept, got, own, cut, 1, 1)
-
-
-def add_kernel(a, b, out):
-    out[...] = (a[...].astype(F32) + b[...].astype(F32)).astype(out.dtype)
-
-
-def total_kernel(own, a, b, out):
-    cut = b.shape[1]
-    for plane in range(2):
-        total = own[plane, :cut] + a[plane, :cut].astype(F32) + b[plane].astype(F32)
-        out[plane, :cut] = total.astype(BF16)
-        out[plane, cut:] = (own[plane, cut:] + a[plane, cut:].astype(F32)).astype(BF16)
-
-
-def probe_parts(scalars, term, sent, kept):
-    rows, cols = term.shape[1:]
-    narrow, wide, _, height, width = sent.shape
-    size = wide * height
-    row_start, col_start, core = scalars[0], scalars[1], scalars[2]
-    row_hot = one_hot(cyclic(iota((size, rows), 1), row_start, rows) == iota((size, rows), 0))
-    for plane in range(2):
-        moved = dot(row_hot, term[plane]).astype(BF16)
-        for block in range(narrow):
-            for out, owner in ((kept, core), (sent, 1 - core)):
-                column = iota((cols, width), 1) + (block * 2 + owner) * width
-                hot = one_hot(cyclic(iota((cols, width), 0), col_start, cols) == column)
-                result = dot(moved, hot).astype(BF16)
-                for row in range(wide):
-                    out[block, row, plane] = result[row * height : (row + 1) * height]
-
-
-def scatter_sum(x, axis):
+            for more in arrived:
+                part[plane] = part[plane] + more[plane, at].astype(F32)
+            out[plane, at] = part[plane].astype(BF16)
+
+
+def now_parts(cut, scalars, before, kept, got, upper, lower):
+    core = scalars[2]
+    fill(cut, 0, core, 1 - core, scalars, kept, got, (), upper)
+    fill(cut, upper.shape[1], core, 1 - core, scalars, kept, got, (), lower)
+
+
+def own_part(cut, scalars, before, kept, got, upper, lower, third, out):
+    fill(cut, 0, 1, 1, scalars, kept, got, (upper, third), out.at[:, :cut])
+    fill(cut, cut, 1, 1, scalars, kept, got, (lower,), out.at[:, cut:])
+
+
+def probe_sum(narrow, scalars, diag, probe_kept, probe_got, *outs):
+    me = scalars[4]
+    for step, out in enumerate(outs):
+        block = lax.rem(me + step, narrow)
+        total = probe_kept[block].astype(F32) + probe_got[block].astype(F32)
+        out[...] = total.astype(BF16)
+
+
+def sum_kernel(*refs):
+    *terms, out = refs
+    total = terms[0][...].astype(F32)
+    for term in terms[1:]:
+        total = total + term[...].astype(F32)
+    out[...] = total.astype(out.dtype)
+
+
+def scaled_sum(scale, *refs):
+    *terms, out = refs
+    sum_kernel(*terms, out)
+    out[...] = out[...] * scale
+
+
+def sum_of(*terms):
+    return call(
+        sum_kernel,
+        jax.ShapeDtypeStruct(terms[0].shape, BF16),
+        [VMEM] * len(terms),
+        8,
+        flops=8 * 10**9,
+        name="sum",
+    )(*terms)
+
+
+def scatter_parts(x, axis):
     length = lax.axis_size(axis)
     if length > 8:
-        total = lax.psum_scatter(x, axis, scatter_dimension=0, tiled=True)
-        return total[0].astype(F32)
+        return [lax.psum_scatter(x, axis, scatter_dimension=0, tiled=True)[0]]
     me = lax.axis_index(axis)
 
     def part(of):
         return lax.dynamic_index_in_dim(x, of, 0, keepdims=False)
 
-    total = part(me).astype(F32)
+    terms = [part(me)]
     for step in range(1, length):
-        pairs = [(i, (i + step) % length) for i in range(length)]
-        got = lax.ppermute(part(lax.rem(me + step, length)), axis, pairs)
-        total = total + got.astype(F32)
-    return total
+        if length & (length - 1):
+            pairs = [(i, (i + step) % length) for i in range(length)]
+            to = lax.rem(me + step, length)
+        else:
+            pairs = [(i, i ^ step) for i in range(length)]
+            to = me ^ step
+        terms.append(lax.ppermute(part(to), axis, pairs))
+    return terms
 
 
 def shards(object_slab, probe_wave, amplitude, row_offset, col_offset, occupied):
@@ -271,7 +307,8 @@
     core = lax.axis_index("probe")
     narrow, wide, cores = (lax.axis_size(name) for name in ("narrow", "wide", "probe"))
     corner = jnp.stack([row_offset[0, 0, 0], col_offset[0, 0, 0]])
-    scalars = jnp.concatenate([corner, jnp.stack([core.astype(jnp.int32), occupied[0, 0, 0]])])
+    here = [core, occupied[0, 0, 0], lax.axis_index("narrow")]
+    scalars = jnp.concatenate([corner, jnp.stack([x.astype(jnp.int32) for x in here])])
 
     def shape(*dims, dtype=BF16):
         return jax.ShapeDtypeStruct(dims, dtype)
@@ -281,29 +318,36 @@
     first = to_neighbour(lax.dynamic_slice_in_dim(object_slab, cut * (1 - core), cut, 1), -1, 0)
     second = to_neighbour(lax.dynamic_slice_in_dim(object_slab, cut * core, count, 1), -1, 0)
     third = to_neighbour(first, -1, 1)
-    late_corner, first_late = lax.optimization_barrier((corner, first))
+    late_scalars, first_late = lax.optimization_barrier((scalars, first))
 
     cos_part, sin_part = dft_tables(size)
+    width = size // (narrow * cores)
     tables = call(
-        shift_tables,
+        functools.partial(shift_tables, width),
         (
             shape(2 * cols, 2 * size),
             shape(2 * size, 2 * cols),
             shape(2 * rows, 2 * size),
             shape(2 * size, 2 * rows),
             shape(2, rows, cols),
+            shape(size, rows),
+            shape(cols, narrow * width),
+            shape(cols, narrow * width),
         ),
         [SMEM] + [VMEM] * 3,
+        20,
         flops=4 * 10**9,
         bytes_accessed=2 * 10**7,
         name="shift_tables",
-    )(late_corner, cos_part, sin_part, probe_wave)
+    )(late_scalars, cos_part, sin_part, probe_wave)
     second, tables = lax.optimization_barrier((second, tables))
     pieces = (first, swap(first_late), second, swap(second), third, swap(third))
-    sent, kept, term = call(
+    blocks = shape(narrow, wide, 2, size // wide, width)
+    sent, kept, probe_sent, probe_kept = call(
         slot_terms,
-        (shape(2, count, cols), shape(2, count, cols), shape(2, rows, cols)),
-        [SMEM] + [VMEM] * 13,
+        (shape(2, count, cols), shape(2, count, cols), blocks, blocks),
+        [SMEM] + [VMEM] * 16,
+        18,
         scratch=[
             pltpu.VMEM((rows, 2 * cols), BF16),
             pltpu.VMEM((2 * rows, size), BF16),
@@ -311,53 +355,80 @@
             pltpu.VMEM((2 * size, cols), BF16),
             pltpu.VMEM((2, rows, cols), BF16),
             pltpu.VMEM((2, rows, cols), BF16),
+            pltpu.VMEM((2, rows, cols), BF16),
         ],
-        flops=5 * 10**9,
+        flops=6 * 10**9,
         bytes_accessed=2 * 10**7,
         name="slot_terms",
     )(scalars, object_slab, *pieces, *tables, amplitude[0, 0, 0])
 
-    got = swap(sent)
+    got, probe_got = swap(sent), swap(probe_sent)
     scalars = jnp.concatenate([scalars, swap(corner)])
-    diag = call(diag_part, shape(2, cut, cols), [SMEM, VMEM, VMEM], name="diag_part")(
-        scalars, kept, got
-    )
+
+    def tile(name, kernel, height, *more, after=()):
+        return call(
+            functools.partial(kernel, cut, len(after)),
+            shape(2, height, cols),
+            [SMEM] + [ANY] * len(after) + [VMEM] * (2 + len(more)),
+            8,
+            name=name,
+        )(scalars, *after, kept, got, *more)
+
+    def diag_part(cut, skip, scalars, *refs):
+        tile_part(cut, 0, 0, scalars, *refs[skip:])
+
+    def later_part(cut, skip, scalars, *refs):
+        tile_part(cut, 1 - scalars[2], scalars[2], scalars, *refs[skip:])
+
+    diag = tile("diag_part", diag_part, cut)
     from_first = to_neighbour(diag, 1, 0)
-    now, later, own = call(
-        side_parts,
-        (
-            shape(2, count, cols),
-            shape(2, cut, cols, dtype=F32),
-            shape(2, count, cols, dtype=F32),
-        ),
-        [SMEM, VMEM, VMEM],
-        name="side_parts",
-    )(scalars, kept, got)
-    from_second = to_neighbour(now, 1, 0)
-    later = call(add_kernel, shape(2, cut, cols), [VMEM, VMEM], name="add")(later, from_first)
-    from_third = to_neighbour(later, 1, 1)
-    own = call(total_kernel, shape(2, count, cols), [VMEM] * 3, name="total")(
-        own, from_second, from_third
-    )
+    probe_blocks = call(
+        functools.partial(probe_sum, narrow),
+        (jax.ShapeDtypeStruct(blocks.shape[1:], BF16),) * narrow,
+        [SMEM, ANY, VMEM, VMEM],
+        8,
+        name="probe_sum",
+    )(scalars, diag, probe_kept, probe_got)
+    upper, lower = call(
+        functools.partial(now_parts, cut),
+        (shape(2, cut, cols), shape(2, count - cut, cols)),
+        [SMEM, ANY, VMEM, VMEM],
+        8,
+        name="now_parts",
+    )(scalars, probe_blocks[0], kept, got)
+    from_upper = to_neighbour(upper, 1, 0)
+    from_lower = to_neighbour(lower, 1, 0, senders=(1,))
+    from_third = to_neighbour(tile("later_part", later_part, cut, from_first), 1, 1)
+    received = [
+        lax.ppermute(block, "narrow", [(i, (i + step) % narrow) for i in range(narrow)])
+        for step, block in enumerate(probe_blocks)
+        if step
+    ]
+    total = sum_of(probe_blocks[0], *received)
+    terms = scatter_parts(total, "wide")
+    probe_grad = call(
+        functools.partial(scaled_sum, 1.0 / math.sqrt(wide * narrow * cores)),
+        jax.ShapeDtypeStruct(terms[0].shape, F32),
+        [VMEM] * len(terms),
+        8,
+        flops=20 * 10**9,
+        name="probe_grad",
+    )(*terms)
+    own = call(
+        functools.partial(own_part, cut),
+        shape(2, count, cols),
+        [SMEM, ANY] + [VMEM] * 5,
+        8,
+        flops=1 * 10**9,
+        name="own_part",
+    )(scalars, total, kept, got, from_upper, from_lower, from_third)
     other = swap(own)
     object_grad = jnp.where(
         core == 0,
         jnp.concatenate([own[:, :cut], other], 1),
         jnp.concatenate([other[:, :cut], own], 1),
     )
-
-    blocks = shape(narrow, wide, 2, size // wide, size // (narrow * cores))
-    sent, kept = call(
-        probe_parts,
-        (blocks, blocks),
-        [SMEM, VMEM],
-        flops=2 * 10**9,
-        name="probe_parts",
-    )(scalars, term)
-    total = (kept.astype(F32) + swap(sent).astype(F32)).astype(BF16)
-    total = scatter_sum(total, "narrow").astype(BF16)
-    total = scatter_sum(total, "wide")
-    return (object_grad, total * (1.0 / math.sqrt(wide * narrow * cores)))
+    return (object_grad, probe_grad)
 
 
 def solution(mesh):

time: 94.9 us -> 81 us (0.85)
  the two profiles are of different devices: /device:TPU:0 before, /device:TPU:19 now
where the time goes in v3:
time: 81 us; the launch traced here: 80.5 us
  starting transfers between devices  27.8 us (34%)
  Pallas kernels  21.5 us (27%)
  waiting for transfers between devices  20.5 us (25%)
  local copies, waits for them, and re-layouts  6.45 us (8%)
  between operations  2.79 us (3%)
  other arithmetic  1.49 us (2%)
    ppermute x7, waiting for transfers between devices, to_neighbour(): return lax.ppermute(x, ('wide', 'narrow', 'probe'), pairs)  15.9 us
    ppermute x7, starting transfers between devices, to_neighbour(): return lax.ppermute(x, ('wide', 'narrow', 'probe'), pairs)  15.8 us
    pallas_call x1, Pallas kernels, shards(): call(slot_terms, (shape(2, count, cols), shape(2, count, cols), blocks, b...  10.1 us
    ppermute x7, starting transfers between devices, swap(): return lax.ppermute(x, 'probe', [(0, 1), (1, 0)])  7.07 us
    pallas_call x1, Pallas kernels, shards(): call(functools.partial(shift_tables, width), (shape(2 * cols, 2 * size),...  4.78 us
    ppermute x7, waiting for transfers between devices, swap(): return lax.ppermute(x, 'probe', [(0, 1), (1, 0)])  4.6 us
    ppermute x3, starting transfers between devices, scatter_parts(): terms.append(lax.ppermute(part(to), axis, pairs))  2.77 us
    pallas_call x2, Pallas kernels, tile(): call(functools.partial(kernel, cut, len(after)), shape(2, height, cols),...  2.31 us
  transfers between devices with their start and end apart: 18, of which 10 were waited for; matrix products, arithmetic and copies ran while one was open for 3% of the time, Pallas kernels for 14%

profile of v3, /device:TPU:19, one launch (start us, length us, event | category | flops | bytes accessed | tf_op | source)
XLA Modules:
  0.0 80.5 jit_solution(8156507572666685869)
XLA Ops:
  0.7 2.0 %constant_dynamic-slice_fusion.1 = bf16[2,256,512]{2,1,0:T(8,128)(2,1)} fusion(bf16[2,640,512]{2,1,0:T(8,128)(2,1)} %own.1, s32[]{:T(128)S(6)} %select_n.28), kind=kLoop, calls=%fused_computation.6 | loop fusion | bytes 1048580 | tf_op jit(solution)/shard_map/dynamic_slice | solution.py:318
  2.7 2.1 %collective-permute-start.1 = (bf16[2,256,512]{2,1,0:T(8,128)(2,1)}, bf16[2,256,512]{2,1,0:T(8,128)(2,1)S(1)}, u32[]{:S(2)}, u32[]{:S(2)}) collective-permute-start(bf16[2,256,512]{2,1,0:T(8,128)(2,1)} %constant_dynamic-slice_fusion.1), channel_id=1, source_target_pairs={{2,0},{5,1},{6,4},{7,3},{9,5},{10,8},{11,7},{13,9},{14,12},{15,11}... | collective-permute-start | bytes 1572872 | tf_op jit(solution)/shard_map/ppermute | solution.py:29
  4.7 2.1 %constant_dynamic-slice_fusion = bf16[2,384,512]{2,1,0:T(8,128)(2,1)} fusion(bf16[2,640,512]{2,1,0:T(8,128)(2,1)} %own.1, s32[]{:T(128)S(6)} %select_n.29), kind=kLoop, calls=%fused_computation.5 | loop fusion | bytes 1572868 | tf_op jit(solution)/shard_map/dynamic_slice | solution.py:319
  6.8 2.1 %collective-permute-start.3 = (bf16[2,384,512]{2,1,0:T(8,128)(2,1)}, bf16[2,384,512]{2,1,0:T(8,128)(2,1)S(1)}, u32[]{:S(2)}, u32[]{:S(2)}) collective-permute-start(bf16[2,384,512]{2,1,0:T(8,128)(2,1)} %constant_dynamic-slice_fusion), channel_id=1, source_target_pairs={{2,0},{5,1},{6,4},{7,3},{9,5},{10,8},{11,7},{13,9},{14,12},{15,11}... | collective-permute-start | bytes 2359304 | tf_op jit(solution)/shard_map/ppermute | solution.py:29
  10.9 1.9 %collective-permute-done.1.first = bf16[2,256,512]{2,1,0:T(8,128)(2,1)S(1)} collective-permute-done((bf16[2,256,512]{2,1,0:T(8,128)(2,1)}, bf16[2,256,512]{2,1,0:T(8,128)(2,1)S(1)}, u32[]{:S(2)}, u32[]{:S(2)}) %collective-permute-start.1) | collective-permute-done | bytes 524320 | tf_op jit(solution)/shard_map/ppermute | solution.py:29
  12.8 2.5 %collective-permute-start.5 = (bf16[2,256,512]{2,1,0:T(8,128)(2,1)S(1)}, bf16[2,256,512]{2,1,0:T(8,128)(2,1)S(1)}, u32[]{:S(2)}, u32[]{:S(2)}) collective-permute-start(bf16[2,256,512]{2,1,0:T(8,128)(2,1)S(1)} %collective-permute-done.1.first), channel_id=1, source_target_pairs={{3,1},{4,0},{6,2},{7,5},{8,4},{10,6},{11,9},{12,8},{14,10},{15,13}... | collective-permute-start | bytes 1572872 | tf_op jit(solution)/shard_map/ppermute | solution.py:29
  15.3 1.0 %copy-done.6 = bf16[512,512]{1,0:T(8,128)(2,1)S(1)} copy-done((bf16[512,512]{1,0:T(8,128)(2,1)S(1)}, bf16[512,512]{1,0:T(8,128)(2,1)}, u32[]{:S(2)}) %copy-start.6) | copy-done | bytes 524312
  16.3 4.8 %shift_tables.1 = (bf16[1024,1024]{1,0:T(8,128)(2,1)S(1)}, bf16[1024,1024]{1,0:T(8,128)(2,1)S(1)}, bf16[1280,1024]{1,0:T(8,128)(2,1)S(1)}, bf16[1024,1280]{1,0:T...) custom-call(s32[5]{0:T(128)S(1)} %concatenate.15.scalars, ...), custom_call_target="tpu_custom_call" | custom-call | flops 4000000000 | bytes 20000000 | tf_op jit(solution)/shard_map/shift_tables/pallas_call | solution.py:325
  21.1 4.0 %collective-permute-done.3.second = bf16[2,384,512]{2,1,0:T(8,128)(2,1)S(1)} collective-permute-done((bf16[2,384,512]{2,1,0:T(8,128)(2,1)}, bf16[2,384,512]{2,1,0:T(8,128)(2,1)S(1)}, u32[]{:S(2)}, u32[]{:S(2)}) %collective-permute-start.3) | collective-permute-done | bytes 786464 | tf_op jit(solution)/shard_map/ppermute | solution.py:29
  25.1 1.0 %collective-permute-start.4 = (bf16[2,384,512]{2,1,0:T(8,128)(2,1)S(1)}, bf16[2,384,512]{2,1,0:T(8,128)(2,1)S(1)}, u32[]{:S(2)}, u32[]{:S(2)}) collective-permute-start(bf16[2,384,512]{2,1,0:T(8,128)(2,1)S(1)} %collective-permute-done.3.second), channel_id=1, source_target_pairs={{0,1},{1,0},{2,3},{3,2},{4,5},{5,4},{6,7},{7,6},{8,9},{9,8},{10,11... | collective-permute-start | bytes 2359304 | tf_op jit(solution)/shard_map/ppermute | solution.py:33
  26.3 1.2 %collective-permute-start.6 = (bf16[2,256,512]{2,1,0:T(8,128)(2,1)S(1)}, bf16[2,256,512]{2,1,0:T(8,128)(2,1)S(1)}, u32[]{:S(2)}, u32[]{:S(2)}) collective-permute-start(bf16[2,256,512]{2,1,0:T(8,128)(2,1)S(1)} %collective-permute-done.5.third), channel_id=1, source_target_pairs={{0,1},{1,0},{2,3},{3,2},{4,5},{5,4},{6,7},{7,6},{8,9},{9,8},{10,11... | collective-permute-start | bytes 1572872 | tf_op jit(solution)/shard_map/ppermute | solution.py:33
  27.5 1.2 %collective-permute-done.2.first2 = bf16[2,256,512]{2,1,0:T(8,128)(2,1)S(1)} collective-permute-done((bf16[2,256,512]{2,1,0:T(8,128)(2,1)S(1)}, bf16[2,256,512]{2,1,0:T(8,128)(2,1)S(1)}, u32[]{:S(2)}, u32[]{:S(2)}) %collective-permute-start.2) | collective-permute-done | bytes 524320 | tf_op jit(solution)/shard_map/ppermute | solution.py:33
  28.8 0.7 collective-permute-done.6.third2
  29.5 1.0 %copy-done.4 = bf16[2,256,512]{2,1,0:T(8,128)(2,1)S(1)} copy-done((bf16[2,256,512]{2,1,0:T(8,128)(2,1)S(1)}, bf16[2,256,512]{2,1,0:T(8,128)(2,1)}, u32[]{:S(2)}) %copy-start.4) | copy-done | bytes 524312
  30.6 10.1 %slot_terms.1 = (bf16[2,384,512]{2,1,0:T(8,128)(2,1)}, bf16[2,384,512]{2,1,0:T(8,128)(2,1)S(1)}, bf16[2,4,2,128,128]{4,3,2,1,0:T(8,128)(2,1)}, bf16[2,4,2,128,128]{4,3,2,1,0:T(8,128)(2,1)S(1)}) custom-call(s32[5]{0:T(128)S(1)} %concatenate.15.scalars, bf16[2,640,512]{2,1,0:T(8,128)(2,1)S(1)} %copy-done, bf16[2,256,512]{2,1,0:T(8,128)(2,1)S(1)} %copy-done.4, ...), custom_call_target="tpu_custom_call" | custom-call | flops 6000000000 | bytes 20000000 | tf_op jit(solution)/shard_map/slot_terms/pallas_call | solution.py:346
  41.7 1.3 %collective-permute-done = s32[2]{0:T(128)S(1)} collective-permute-done((s32[2]{0:T(128)S(1)}, s32[2]{0:T(128)S(1)}, u32[]{:S(2)}, u32[]{:S(2)}) %collective-permute-start) | collective-permute-done | bytes 40 | tf_op jit(solution)/shard_map/ppermute | solution.py:33
  43.2 0.9 %diag_part.1.diag = bf16[2,256,512]{2,1,0:T(8,128)(2,1)S(1)} custom-call(s32[7]{0:T(128)S(1)} %concatenate.14.scalars, bf16[2,384,512]{2,1,0:T(8,128)(2,1)S(1)} %get-tuple-element.48.refs_0_.kept, bf16[2,384,512]{2,1,0:T(8,128)(2,1)S(1)} %collective-permute-done.7.refs_1_.got), custom_call_target="tpu_custom_call" | custom-call | tf_op jit(solution)/shard_map/diag_part/pallas_call | solution.py:369
  44.1 4.1 %collective-permute-start.12 = (bf16[2,256,512]{2,1,0:T(8,128)(2,1)S(1)}, bf16[2,256,512]{2,1,0:T(8,128)(2,1)}, u32[]{:S(2)}, u32[]{:S(2)}) collective-permute-start(bf16[2,256,512]{2,1,0:T(8,128)(2,1)S(1)} %diag_part.1.diag), channel_id=1, source_target_pairs={{0,2},{1,5},{3,7},{4,6},{5,9},{7,11},{8,10},{9,13},{11,15},{12,14}... | collective-permute-start | bytes 1572872 | tf_op jit(solution)/shard_map/ppermute | solution.py:29
  48.2 1.3 %probe_sum.1 = (bf16[4,2,128,128]{3,2,1,0:T(8,128)(2,1)S(1)}, bf16[4,2,128,128]{3,2,1,0:T(8,128)(2,1)}) custom-call(s32[7]{0:T(128)S(1)} %concatenate.14.scalars, bf16[2,256,512]{2,1,0:T(8,128)(2,1)S(1)} %diag_part.1.diag, bf16[2,4,2,128,128]{4,3,2,1,0:T(8,128)(2,1)S(1)} %get-tuple-element.50.probe_kept, ...), custom_call_target="tpu_custom_call" | custom-call | tf_op jit(solution)/shard_map/probe_sum/pallas_call | solution.py:385
  49.5 2.1 %collective-permute-start.9 = (bf16[4,2,128,128]{3,2,1,0:T(8,128)(2,1)}, bf16[4,2,128,128]{3,2,1,0:T(8,128)(2,1)S(1)}, u32[]{:S(2)}, u32[]{:S(2)}) collective-permute-start(bf16[4,2,128,128]{3,2,1,0:T(8,128)(2,1)} %get-tuple-element.53), channel_id=1, source_target_pairs={{0,2},{2,0},{1,3},{3,1},{4,6},{6,4},{5,7},{7,5},{8,10},{10,8},{9,1... | collective-permute-start | bytes 786440 | tf_op jit(solution)/shard_map/ppermute | solution.py:403
  51.6 1.0 %now_parts.1 = (bf16[2,256,512]{2,1,0:T(8,128)(2,1)S(1)}, bf16[2,128,512]{2,1,0:T(8,128)(2,1)S(1)}) custom-call(s32[7]{0:T(128)S(1)} %concatenate.14.scalars, bf16[4,2,128,128]{3,2,1,0:T(8,128)(2,1)S(1)} %get-tuple-element.52.refs_0_.before, bf16[2,384,512]{2,1,0:T(8,128)(2,1)S(1)} %get-tuple-element.48.refs_0_.kept, ...), custom_call_target="tpu_custom_call" | custom-call | tf_op jit(solution)/shard_map/now_parts/pallas_call | solution.py:392
  52.6 1.9 %collective-permute-start.10 = (bf16[2,256,512]{2,1,0:T(8,128)(2,1)S(1)}, bf16[2,256,512]{2,1,0:T(8,128)(2,1)S(1)}, u32[]{:S(2)}, u32[]{:S(2)}) collective-permute-start(bf16[2,256,512]{2,1,0:T(8,128)(2,1)S(1)} %get-tuple-element.54), channel_id=1, source_target_pairs={{0,2},{1,5},{3,7},{4,6},{5,9},{7,11},{8,10},{9,13},{11,15},{12,14}... | collective-permute-start | bytes 1572872 | tf_op jit(solution)/shard_map/ppermute | solution.py:29
  54.6 1.9 %collective-permute-start.11 = (bf16[2,128,512]{2,1,0:T(8,128)(2,1)S(1)}, bf16[2,128,512]{2,1,0:T(8,128)(2,1)S(1)}, u32[]{:S(2)}, u32[]{:S(2)}) collective-permute-start(bf16[2,128,512]{2,1,0:T(8,128)(2,1)S(1)} %get-tuple-element.55), channel_id=1, source_target_pairs={{1,5},{3,7},{5,9},{7,11},{9,13},{11,15},{17,21},{19,23},{21,25},{2... | collective-permute-start | bytes 786440 | tf_op jit(solution)/shard_map/ppermute | solution.py:29
  56.5 1.5 %later_part.1 = bf16[2,256,512]{2,1,0:T(8,128)(2,1)S(1)} custom-call(s32[7]{0:T(128)S(1)} %concatenate.14.scalars, bf16[2,384,512]{2,1,0:T(8,128)(2,1)S(1)} %get-tuple-element.48.refs_0_.kept, bf16[2,384,512]{2,1,0:T(8,128)(2,1)S(1)} %collective-permute-done.7.refs_1_.got, bf16[2,256,512]{2,1,0:T(8,128)(2,1)} %collective-permute-done.12.refs_2_), custom_call_target="tpu_custom_call" | custom-call | tf_op jit(solution)/shard_map/later_part/pallas_call | solution.py:369
  58.0 1.3 %collective-permute-start.13 = (bf16[2,256,512]{2,1,0:T(8,128)(2,1)S(1)}, bf16[2,256,512]{2,1,0:T(8,128)(2,1)S(1)}, u32[]{:S(2)}, u32[]{:S(2)}) collective-permute-start(bf16[2,256,512]{2,1,0:T(8,128)(2,1)S(1)} %later_part.1), channel_id=1, source_target_pairs={{0,4},{1,3},{2,6},{4,8},{5,7},{6,10},{8,12},{9,11},{10,14},{13,15}... | collective-permute-start | bytes 1572872 | tf_op jit(solution)/shard_map/ppermute | solution.py:29
  59.5 2.7 %collective-permute-start.16 = (bf16[2,128,128]{2,1,0:T(8,128)(2,1)S(1)}, bf16[2,128,128]{2,1,0:T(8,128)(2,1)S(1)}, u32[]{:S(2)}, u32[]{:S(2)}) collective-permute-start(bf16[2,128,128]{2,1,0:T(8,128)(2,1)S(1)} %get-tuple-element.57), channel_id=1, source_target_pairs={{0,8},{4,12},{8,0},{12,4},{1,9},{5,13},{9,1},{13,5},{2,10},{6,14},... | collective-permute-start | bytes 196616 | tf_op jit(solution)/shard_map/ppermute | solution.py:300
  62.2 5.7 %collective-permute-done.11.lower = bf16[2,128,512]{2,1,0:T(8,128)(2,1)S(1)} collective-permute-done((bf16[2,128,512]{2,1,0:T(8,128)(2,1)S(1)}, bf16[2,128,512]{2,1,0:T(8,128)(2,1)S(1)}, u32[]{:S(2)}, u32[]{:S(2)}) %collective-permute-start.11) | collective-permute-done | bytes 262176 | tf_op jit(solution)/shard_map/ppermute | solution.py:29
  67.9 4.1 %collective-permute-done.13.third = bf16[2,256,512]{2,1,0:T(8,128)(2,1)S(1)} collective-permute-done((bf16[2,256,512]{2,1,0:T(8,128)(2,1)S(1)}, bf16[2,256,512]{2,1,0:T(8,128)(2,1)S(1)}, u32[]{:S(2)}, u32[]{:S(2)}) %collective-permute-start.13) | collective-permute-done | bytes 524320 | tf_op jit(solution)/shard_map/ppermute | solution.py:29
  72.0 1.2 %own_part.1 = bf16[2,384,512]{2,1,0:T(8,128)(2,1)S(1)} custom-call(s32[7]{0:T(128)S(1)} %concatenate.14.scalars, bf16[4,2,128,128]{3,2,1,0:T(8,128)(2,1)S(1)} %sum.1.before, bf16[2,384,512]{2,1,0:T(8,128)(2,1)S(1)} %get-tuple-element.48.refs_0_.kept, bf16[2,384,512]{2,1,0:T(8,128)(2,1)S(1)} %collective-permute-done.7.refs_1_.got, ...), custom_call_target="tpu_custom_call" | custom-call | flops 1000000000 | tf_op jit(solution)/shard_map/own_part/pallas_call | solution.py:417
  73.2 4.0 %collective-permute-start.14 = (bf16[2,384,512]{2,1,0:T(8,128)(2,1)S(1)}, bf16[2,384,512]{2,1,0:T(8,128)(2,1)S(1)}, u32[]{:S(2)}, u32[]{:S(2)}) collective-permute-start(bf16[2,384,512]{2,1,0:T(8,128)(2,1)S(1)} %own_part.1), channel_id=1, source_target_pairs={{0,1},{1,0},{2,3},{3,2},{4,5},{5,4},{6,7},{7,6},{8,9},{9,8},{10,11... | collective-permute-start | bytes 2359304 | tf_op jit(solution)/shard_map/ppermute | solution.py:33
  77.9 1.2 %collective-permute-done.14 = bf16[2,384,512]{2,1,0:T(8,128)(2,1)S(1)} collective-permute-done((bf16[2,384,512]{2,1,0:T(8,128)(2,1)S(1)}, bf16[2,384,512]{2,1,0:T(8,128)(2,1)S(1)}, u32[]{:S(2)}, u32[]{:S(2)}) %collective-permute-start.14) | collective-permute-done | bytes 786464 | tf_op jit(solution)/shard_map/ppermute | solution.py:33
  79.1 1.4 %maximum_select_fusion = bf16[2,640,512]{2,1,0:T(8,128)(2,1)} fusion(bf16[2,384,512]{2,1,0:T(8,128)(2,1)S(1)} %collective-permute-done.14, bf16[2,256,512]{2,1,0:T(8,128)(2,1)S(1)} %slice.8, bf16[2,384,512]{2,1,0:T(8,128)(2,1)S(1)} %own_part.1, bf16[2,256,512]{2,1,0:T(8,128)(2,1)S(1)} %slice.9, pred[]{:T(512)S(6)} %eq.3), kind=kLoop, calls=%fused_computation | loop fusion | flops 5898240 | bytes 3932161 | tf_op jit(solution)/shard_map/jit(_where)/select_n | solution.py:426
  (36 shorter events, 2.5 us)
Async XLA Ops:
  0.6 14.6 %copy-start.1 = (bf16[2,512,512]{2,1,0:T(8,128)(2,1)S(1)}, bf16[2,512,512]{2,1,0:T(8,128)(2,1)}, u32[]{:S(2)}) copy-start(bf16[2,512,512]{2,1,0:T(8,128)(2,1)} %probe_in.1) | copy-start | bytes 3145732
  0.6 14.6 %copy-start.5 = (bf16[512,512]{1,0:T(8,128)(2,1)S(1)}, bf16[512,512]{1,0:T(8,128)(2,1)}, u32[]{:S(2)}) copy-start(bf16[512,512]{1,0:T(8,128)(2,1)} %constant.38.clone.cos_in) | copy-start | bytes 1572868
  2.7 10.1 %collective-permute-start.1 = (bf16[2,256,512]{2,1,0:T(8,128)(2,1)}, bf16[2,256,512]{2,1,0:T(8,128)(2,1)S(1)}, u32[]{:S(2)}, u32[]{:S(2)}) collective-permute-start(bf16[2,256,512]{2,1,0:T(8,128)(2,1)} %constant_dynamic-slice_fusion.1), channel_id=1, source_target_pairs={{2,0},{5,1},{6,4},{7,3},{9,5},{10,8},{11,7},{13,9},{14,12},{15,11}... | collective-permute-start | bytes 1572872 | tf_op jit(solution)/shard_map/ppermute | solution.py:29
  6.8 18.3 %collective-permute-start.3 = (bf16[2,384,512]{2,1,0:T(8,128)(2,1)}, bf16[2,384,512]{2,1,0:T(8,128)(2,1)S(1)}, u32[]{:S(2)}, u32[]{:S(2)}) collective-permute-start(bf16[2,384,512]{2,1,0:T(8,128)(2,1)} %constant_dynamic-slice_fusion), channel_id=1, source_target_pairs={{2,0},{5,1},{6,4},{7,3},{9,5},{10,8},{11,7},{13,9},{14,12},{15,11}... | collective-permute-start | bytes 2359304 | tf_op jit(solution)/shard_map/ppermute | solution.py:29
  10.9 18.6 %copy-start = (bf16[2,640,512]{2,1,0:T(8,128)(2,1)S(1)}, bf16[2,640,512]{2,1,0:T(8,128)(2,1)}, u32[]{:S(2)}) copy-start(bf16[2,640,512]{2,1,0:T(8,128)(2,1)} %own.1) | copy-start | bytes 3932164
  10.9 18.6 %copy-start.2 = (bf16[1,1,1,512,512]{4,3,2,1,0:T(8,128)(2,1)S(1)}, bf16[1,1,1,512,512]{4,3,2,1,0:T(8,128)(2,1)}, u32[]{:S(2)}) copy-start(bf16[1,1,1,512,512]{4,3,2,1,0:T(8,128)(2,1)} %param.10) | copy-start | bytes 1572868
  12.8 13.3 %copy-start.3 = (bf16[2,256,512]{2,1,0:T(8,128)(2,1)}, bf16[2,256,512]{2,1,0:T(8,128)(2,1)S(1)}, u32[]{:S(2)}) copy-start(bf16[2,256,512]{2,1,0:T(8,128)(2,1)S(1)} %collective-permute-done.1.first) | copy-start | bytes 1572868
  12.8 13.5 %collective-permute-start.5 = (bf16[2,256,512]{2,1,0:T(8,128)(2,1)S(1)}, bf16[2,256,512]{2,1,0:T(8,128)(2,1)S(1)}, u32[]{:S(2)}, u32[]{:S(2)}) collective-permute-start(bf16[2,256,512]{2,1,0:T(8,128)(2,1)S(1)} %collective-permute-done.1.first), channel_id=1, source_target_pairs={{3,1},{4,0},{6,2},{7,5},{8,4},{10,6},{11,9},{12,8},{14,10},{15,13}... | collective-permute-start | bytes 1572872 | tf_op jit(solution)/shard_map/ppermute | solution.py:29
  15.3 1.0 %copy-start.6 = (bf16[512,512]{1,0:T(8,128)(2,1)S(1)}, bf16[512,512]{1,0:T(8,128)(2,1)}, u32[]{:S(2)}) copy-start(bf16[512,512]{1,0:T(8,128)(2,1)} %constant.39.clone.sin_in) | copy-start | bytes 1572868
  25.1 4.4 %collective-permute-start.4 = (bf16[2,384,512]{2,1,0:T(8,128)(2,1)S(1)}, bf16[2,384,512]{2,1,0:T(8,128)(2,1)S(1)}, u32[]{:S(2)}, u32[]{:S(2)}) collective-permute-start(bf16[2,384,512]{2,1,0:T(8,128)(2,1)S(1)} %collective-permute-done.3.second), channel_id=1, source_target_pairs={{0,1},{1,0},{2,3},{3,2},{4,5},{5,4},{6,7},{7,6},{8,9},{9,8},{10,11... | collective-permute-start | bytes 2359304 | tf_op jit(solution)/shard_map/ppermute | solution.py:33
  26.1 2.7 %collective-permute-start.2 = (bf16[2,256,512]{2,1,0:T(8,128)(2,1)S(1)}, bf16[2,256,512]{2,1,0:T(8,128)(2,1)S(1)}, u32[]{:S(2)}, u32[]{:S(2)}) collective-permute-start(bf16[2,256,512]{2,1,0:T(8,128)(2,1)S(1)} %collective-permute-done.1.first), channel_id=1, source_target_pairs={{0,1},{1,0},{2,3},{3,2},{4,5},{5,4},{6,7},{7,6},{8,9},{9,8},{10,11... | collective-permute-start | bytes 1572872 | tf_op jit(solution)/shard_map/ppermute | solution.py:33
  26.3 3.2 %collective-permute-start.6 = (bf16[2,256,512]{2,1,0:T(8,128)(2,1)S(1)}, bf16[2,256,512]{2,1,0:T(8,128)(2,1)S(1)}, u32[]{:S(2)}, u32[]{:S(2)}) collective-permute-start(bf16[2,256,512]{2,1,0:T(8,128)(2,1)S(1)} %collective-permute-done.5.third), channel_id=1, source_target_pairs={{0,1},{1,0},{2,3},{3,2},{4,5},{5,4},{6,7},{7,6},{8,9},{9,8},{10,11... | collective-permute-start | bytes 1572872 | tf_op jit(solution)/shard_map/ppermute | solution.py:33
  29.5 1.0 %copy-start.4 = (bf16[2,256,512]{2,1,0:T(8,128)(2,1)S(1)}, bf16[2,256,512]{2,1,0:T(8,128)(2,1)}, u32[]{:S(2)}) copy-start(bf16[2,256,512]{2,1,0:T(8,128)(2,1)} %copy-done.3) | copy-start | bytes 1572868
  40.7 2.5 %collective-permute-start.7 = (bf16[2,384,512]{2,1,0:T(8,128)(2,1)}, bf16[2,384,512]{2,1,0:T(8,128)(2,1)S(1)}, u32[]{:S(2)}, u32[]{:S(2)}) collective-permute-start(bf16[2,384,512]{2,1,0:T(8,128)(2,1)} %get-tuple-element.49), channel_id=1, source_target_pairs={{0,1},{1,0},{2,3},{3,2},{4,5},{5,4},{6,7},{7,6},{8,9},{9,8},{10,11... | collective-permute-start | bytes 2359304 | tf_op jit(solution)/shard_map/ppermute | solution.py:33
  41.1 7.1 %collective-permute-start.8 = (bf16[2,4,2,128,128]{4,3,2,1,0:T(8,128)(2,1)}, bf16[2,4,2,128,128]{4,3,2,1,0:T(8,128)(2,1)S(1)}, u32[]{:S(2)}, u32[]{:S(2)}) collective-permute-start(bf16[2,4,2,128,128]{4,3,2,1,0:T(8,128)(2,1)} %get-tuple-element.51), channel_id=1, source_target_pairs={{0,1},{1,0},{2,3},{3,2},{4,5},{5,4},{6,7},{7,6},{8,9},{9,8},{10,11... | collective-permute-start | bytes 1572872 | tf_op jit(solution)/shard_map/ppermute | solution.py:33
  41.3 1.7 %collective-permute-start = (s32[2]{0:T(128)S(1)}, s32[2]{0:T(128)S(1)}, u32[]{:S(2)}, u32[]{:S(2)}) collective-permute-start(s32[2]{0:T(128)S(1)} %pad_add_fusion), channel_id=1, source_target_pairs={{0,1},{1,0},{2,3},{3,2},{4,5},{5,4},{6,7},{7,6},{8,9},{9,8},{10,11... | collective-permute-start | bytes 32 | tf_op jit(solution)/shard_map/ppermute | solution.py:33
  44.1 12.4 %collective-permute-start.12 = (bf16[2,256,512]{2,1,0:T(8,128)(2,1)S(1)}, bf16[2,256,512]{2,1,0:T(8,128)(2,1)}, u32[]{:S(2)}, u32[]{:S(2)}) collective-permute-start(bf16[2,256,512]{2,1,0:T(8,128)(2,1)S(1)} %diag_part.1.diag), channel_id=1, source_target_pairs={{0,2},{1,5},{3,7},{4,6},{5,9},{7,11},{8,10},{9,13},{11,15},{12,14}... | collective-permute-start | bytes 1572872 | tf_op jit(solution)/shard_map/ppermute | solution.py:29
  49.5 9.8 %collective-permute-start.9 = (bf16[4,2,128,128]{3,2,1,0:T(8,128)(2,1)}, bf16[4,2,128,128]{3,2,1,0:T(8,128)(2,1)S(1)}, u32[]{:S(2)}, u32[]{:S(2)}) collective-permute-start(bf16[4,2,128,128]{3,2,1,0:T(8,128)(2,1)} %get-tuple-element.53), channel_id=1, source_target_pairs={{0,2},{2,0},{1,3},{3,1},{4,6},{6,4},{5,7},{7,5},{8,10},{10,8},{9,1... | collective-permute-start | bytes 786440 | tf_op jit(solution)/shard_map/ppermute | solution.py:403
  52.6 15.2 %collective-permute-start.10 = (bf16[2,256,512]{2,1,0:T(8,128)(2,1)S(1)}, bf16[2,256,512]{2,1,0:T(8,128)(2,1)S(1)}, u32[]{:S(2)}, u32[]{:S(2)}) collective-permute-start(bf16[2,256,512]{2,1,0:T(8,128)(2,1)S(1)} %get-tuple-element.54), channel_id=1, source_target_pairs={{0,2},{1,5},{3,7},{4,6},{5,9},{7,11},{8,10},{9,13},{11,15},{12,14}... | collective-permute-start | bytes 1572872 | tf_op jit(solution)/shard_map/ppermute | solution.py:29
  54.6 13.3 %collective-permute-start.11 = (bf16[2,128,512]{2,1,0:T(8,128)(2,1)S(1)}, bf16[2,128,512]{2,1,0:T(8,128)(2,1)S(1)}, u32[]{:S(2)}, u32[]{:S(2)}) collective-permute-start(bf16[2,128,512]{2,1,0:T(8,128)(2,1)S(1)} %get-tuple-element.55), channel_id=1, source_target_pairs={{1,5},{3,7},{5,9},{7,11},{9,13},{11,15},{17,21},{19,23},{21,25},{2... | collective-permute-start | bytes 786440 | tf_op jit(solution)/shard_map/ppermute | solution.py:29
  58.0 14.0 %collective-permute-start.13 = (bf16[2,256,512]{2,1,0:T(8,128)(2,1)S(1)}, bf16[2,256,512]{2,1,0:T(8,128)(2,1)S(1)}, u32[]{:S(2)}, u32[]{:S(2)}) collective-permute-start(bf16[2,256,512]{2,1,0:T(8,128)(2,1)S(1)} %later_part.1), channel_id=1, source_target_pairs={{0,4},{1,3},{2,6},{4,8},{5,7},{6,10},{8,12},{9,11},{10,14},{13,15}... | collective-permute-start | bytes 1572872 | tf_op jit(solution)/shard_map/ppermute | solution.py:29
  59.4 17.8 %collective-permute-start.15 = (bf16[2,128,128]{2,1,0:T(8,128)(2,1)S(1)}, bf16[2,128,128]{2,1,0:T(8,128)(2,1)S(1)}, u32[]{:S(2)}, u32[]{:S(2)}) collective-permute-start(bf16[2,128,128]{2,1,0:T(8,128)(2,1)S(1)} %get-tuple-element.58), channel_id=1, source_target_pairs={{0,4},{4,0},{8,12},{12,8},{1,5},{5,1},{9,13},{13,9},{2,6},{6,2},{1... | collective-permute-start | bytes 196616 | tf_op jit(solution)/shard_map/ppermute | solution.py:300
  59.5 17.7 %collective-permute-start.16 = (bf16[2,128,128]{2,1,0:T(8,128)(2,1)S(1)}, bf16[2,128,128]{2,1,0:T(8,128)(2,1)S(1)}, u32[]{:S(2)}, u32[]{:S(2)}) collective-permute-start(bf16[2,128,128]{2,1,0:T(8,128)(2,1)S(1)} %get-tuple-element.57), channel_id=1, source_target_pairs={{0,8},{4,12},{8,0},{12,4},{1,9},{5,13},{9,1},{13,5},{2,10},{6,14},... | collective-permute-start | bytes 196616 | tf_op jit(solution)/shard_map/ppermute | solution.py:300
  67.8 9.3 %collective-permute-start.17 = (bf16[2,128,128]{2,1,0:T(8,128)(2,1)S(1)}, bf16[2,128,128]{2,1,0:T(8,128)(2,1)S(1)}, u32[]{:S(2)}, u32[]{:S(2)}) collective-permute-start(bf16[2,128,128]{2,1,0:T(8,128)(2,1)S(1)} %get-tuple-element.56), channel_id=1, source_target_pairs={{0,12},{4,8},{8,4},{12,0},{1,13},{5,9},{9,5},{13,1},{2,14},{6,10},... | collective-permute-start | bytes 196616 | tf_op jit(solution)/shard_map/ppermute | solution.py:300
  73.2 5.9 %collective-permute-start.14 = (bf16[2,384,512]{2,1,0:T(8,128)(2,1)S(1)}, bf16[2,384,512]{2,1,0:T(8,128)(2,1)S(1)}, u32[]{:S(2)}, u32[]{:S(2)}) collective-permute-start(bf16[2,384,512]{2,1,0:T(8,128)(2,1)S(1)} %own_part.1), channel_id=1, source_target_pairs={{0,1},{1,0},{2,3},{3,2},{4,5},{5,4},{6,7},{7,6},{8,9},{9,8},{10,11... | collective-permute-start | bytes 2359304 | tf_op jit(solution)/shard_map/ppermute | solution.py:33

commit v4 on v3

v4 whole, which is shorter than its diff:
```python
import functools
import math

import jax
import jax.numpy as jnp
import numpy as np
from jax import lax
from jax.experimental import pallas as pl
from jax.experimental.pallas import tpu as pltpu
from jax.sharding import PartitionSpec as P

BF16 = jnp.bfloat16
F32 = jnp.float32
VMEM = pl.BlockSpec(memory_space=pltpu.VMEM)
SMEM = pl.BlockSpec(memory_space=pltpu.SMEM)
ANY = pl.BlockSpec(memory_space=pl.ANY)


def to_neighbour(x, by, along_narrow, senders=(0, 1)):
    wide, narrow, cores = (lax.axis_size(name) for name in ("wide", "narrow", "probe"))
    pairs = []
    for w in range(wide):
        for n in range(narrow):
            for core in senders:
                w_to, n_to = (w, n + by) if core == along_narrow else (w + by, n)
                if 0 <= w_to < wide and 0 <= n_to < narrow:
                    source = (w * narrow + n) * cores + core
                    pairs.append((source, (w_to * narrow + n_to) * cores + core))
    return lax.ppermute(x, ("wide", "narrow", "probe"), pairs)


def swap(x):
    return lax.ppermute(x, "probe", [(0, 1), (1, 0)])


def halves_first(size):
    return np.concatenate([np.arange(0, size, 2), np.arange(1, size, 2)])


def dft_tables(size):
    product = (np.arange(size)[:, None] * halves_first(size)[None, :]) % size
    angle = product.astype(np.float32) * np.float32(2.0 * math.pi / size)
    norm = np.float32(1.0 / math.sqrt(size))
    pair = (np.cos(angle) * norm, -np.sin(angle) * norm)
    return [jnp.asarray(x, BF16) for x in pair + tuple(x.T for x in pair)]


def dot(a, b):
    return jnp.dot(a, b, preferred_element_type=F32)


def iota(shape, dim):
    return lax.broadcasted_iota(jnp.int32, shape, dim)


def one_hot(equal):
    return jnp.where(equal, 1.0, 0.0).astype(BF16)


def cyclic(at, shift, period):
    back = at - shift
    return jnp.where(back < 0, back + period, back)


def call(kernel, out_shape, in_specs, vmem, scratch=(), flops=0, bytes_accessed=0, name=None):
    return pl.pallas_call(
        kernel,
        out_shape=out_shape,
        in_specs=in_specs,
        out_specs=jax.tree.map(lambda _: VMEM, out_shape),
        scratch_shapes=list(scratch),
        compiler_params=pltpu.CompilerParams(vmem_limit_bytes=vmem * 1024 * 1024),
        cost_estimate=pl.CostEstimate(
            flops=flops, bytes_accessed=bytes_accessed, transcendentals=0
        ),
        name=name,
    )


def shift_tables(
    width, scalars, cos_in, sin_in, cos_t, sin_t, probe_in, amp_in,
    right, right_t, left_t, left, probe, amplitude, back_rows, back_cols, back_cols2,
):
    size = cos_in.shape[0]
    part = size // 2
    row_start, col_start, core = scalars[0], scalars[1], scalars[2]
    row_start = jnp.where(row_start >= size, row_start - size, row_start)
    full = (size, size)

    back_rows[...] = one_hot(cyclic(iota(full, 1), row_start, size) == iota(full, 0))
    count = back_cols.shape[1]
    for out, owner in ((back_cols, core), (back_cols2, 1 - core)):
        at = iota((size, count), 1)
        column = at + (at // width + owner) * width
        out[...] = one_hot(cyclic(iota((size, count), 0), col_start, size) == column)

    for start, table, table_t in ((col_start, right, right_t), (row_start, left_t, left)):
        hot = one_hot(cyclic(iota((part, size), 0), start, size) == iota((part, size), 1))
        hot_t = one_hot(cyclic(iota((size, part), 1), start, size) == iota((size, part), 0))
        cos_part, sin_part = dot(hot, cos_in[...]), dot(hot, sin_in[...])
        cos_turn, sin_turn = dot(cos_t[...], hot_t), dot(sin_t[...], hot_t)
        for odd in range(2):
            at = slice(odd * part, (odd + 1) * part)
            table[odd, :part, :part] = cos_part[:, at].astype(BF16)
            table[odd, part:, part:] = cos_part[:, at].astype(BF16)
            table[odd, :part, part:] = sin_part[:, at].astype(BF16)
            table[odd, part:, :part] = (-sin_part[:, at]).astype(BF16)
            table_t[odd, :part, :part] = cos_turn[at].astype(BF16)
            table_t[odd, part:, part:] = cos_turn[at].astype(BF16)
            table_t[odd, part:, :part] = sin_turn[at].astype(BF16)
            table_t[odd, :part, part:] = (-sin_turn[at]).astype(BF16)

    row_hot = one_hot(cyclic(iota(full, 0), row_start, size) == iota(full, 1))
    col_hot_t = one_hot(cyclic(iota(full, 1), col_start, size) == iota(full, 0))
    for plane in range(2):
        moved = dot(row_hot, probe_in[plane]).astype(BF16)
        probe[plane] = dot(moved, col_hot_t).astype(BF16)

    def frequency(at):
        return jnp.where(at < part, 2 * at, 2 * at - (size - 1))

    moved = dot(one_hot(frequency(iota(full, 0)) == iota(full, 1)), amp_in[...]).astype(BF16)
    amplitude[...] = dot(moved, one_hot(frequency(iota(full, 1)) == iota(full, 0))).astype(BF16)


def slot_terms(
    scalars, own, first, first2, second, second2, third, third2,
    right, right_t, left_t, left, probe, amplitude, back_rows, back_cols, back_cols2,
    sent, kept, probe_sent, probe_kept, exit_wave, half, chi, back_half, patch, obj, term,
):
    rows, size = own.shape[1:]
    cut = first.shape[1]
    part = size // 2
    row_start, col_start, core = scalars[0], scalars[1], scalars[2]
    live = scalars[3].astype(F32)
    step = 128
    in_cols = iota((step, size), 1) >= col_start
    core_0 = iota((step, size), 0) * 0 + core == 0

    def tile_value(plane, row):
        def load(on_core_0, on_core_1, at):
            a, b = on_core_0[plane, pl.ds(at, step)], on_core_1[plane, pl.ds(at, step)]
            return jnp.where(core_0, a.astype(F32), b.astype(F32))

        if row < rows:
            here = own[plane, pl.ds(row, step)].astype(F32)
            side = load(first2, first, row) if row < cut else load(second2, second, row - cut)
        elif row - rows < cut:
            here = load(second, second2, row - rows)
            side = load(third2, third, row - rows)
        else:
            here = load(first, first2, row - rows - cut)
            side = load(third, third2, row - rows - cut)
        return jnp.where(in_cols, here, side)

    for start in range(0, size, step):
        at = pl.ds(start, step)
        planes = []
        for plane in range(2):
            row = start
            while row < rows:
                row += size
            value = tile_value(plane, row)
            while row > start:
                row -= size
                in_rows = iota((step, size), 0) + row >= row_start
                value = jnp.where(in_rows, tile_value(plane, row), value)
            patch[plane, at] = value.astype(BF16)
            planes.append(value)
        probe_re, probe_im = probe[0, at].astype(F32), probe[1, at].astype(F32)
        exit_re = probe_re * planes[0] - probe_im * planes[1]
        exit_im = probe_re * planes[1] + probe_im * planes[0]
        for plane, value in ((0, exit_re), (1, exit_im)):
            where = slice(plane * part, (plane + 1) * part)
            exit_wave[0, at, where] = (value[:, :part] + value[:, part:]).astype(BF16)
            exit_wave[1, at, where] = (value[:, :part] - value[:, part:]).astype(BF16)

    for odd in range(2):
        result = dot(exit_wave[odd], right[odd])
        cols = slice(odd * part, (odd + 1) * part)
        for plane in range(2):
            where = slice(plane * part, (plane + 1) * part)
            low, high = result[:part, where], result[part:, where]
            half[0, where, cols] = (low + high).astype(BF16)
            half[1, where, cols] = (low - high).astype(BF16)
    for odd in range(2):
        far = dot(left[odd], half[odd])
        far_re, far_im = far[:part], far[part:]
        magnitude = jnp.sqrt(far_re * far_re + far_im * far_im)
        at = slice(odd * part, (odd + 1) * part)
        factor = (1.0 - amplitude[at].astype(F32) / jnp.maximum(magnitude, 1.0)) * live
        for plane, value in ((0, far_re * factor), (1, far_im * factor)):
            where = slice(plane * part, (plane + 1) * part)
            chi[0, at, where] = value[:, :part].astype(BF16)
            chi[1, at, where] = value[:, part:].astype(BF16)
    for plane in range(2):
        where = slice(plane * part, (plane + 1) * part)
        even, odd = dot(chi[0], right_t[0, :, where]), dot(chi[1], right_t[1, :, where])
        for parity in range(2):
            at = slice(parity * part, (parity + 1) * part)
            back_half[parity, where, :part] = (even[at] + odd[at]).astype(BF16)
            back_half[parity, where, part:] = (even[at] - odd[at]).astype(BF16)
    for start in range(0, size, part):
        at = slice(start, start + part)
        even, odd = dot(left_t[0], back_half[0, :, at]), dot(left_t[1], back_half[1, :, at])
        for lines, back in ((slice(0, part), even + odd), (slice(part, size), even - odd)):
            back_re, back_im = back[:part], back[part:]
            probe_re, probe_im = probe[0, lines, at].astype(F32), probe[1, lines, at].astype(F32)
            obj[0, lines, at] = (probe_re * back_re + probe_im * back_im).astype(BF16)
            obj[1, lines, at] = (probe_re * back_im - probe_im * back_re).astype(BF16)
            patch_re, patch_im = patch[0, lines, at].astype(F32), patch[1, lines, at].astype(F32)
            term[0, lines, at] = (patch_re * back_re + patch_im * back_im).astype(BF16)
            term[1, lines, at] = (patch_re * back_im - patch_im * back_re).astype(BF16)
    count = kept.shape[1]
    for plane in range(2):
        obj[plane, size:] = obj[plane, : obj.shape[1] - size]
        kept[plane] = obj[plane, pl.ds(pl.multiple_of(cut * core, 128), count)]
        sent[plane] = obj[plane, pl.ds(pl.multiple_of(cut * (1 - core), 128), count)]

    narrow, blocks, _, height, width = probe_sent.shape
    for plane in range(2):
        moved = dot(back_rows[...], term[plane]).astype(BF16)
        for out, hot in ((probe_sent, back_cols2), (probe_kept, back_cols)):
            result = dot(moved, hot[...]).astype(BF16)
            for column in range(narrow):
                for row in range(blocks):
                    out[column, row, plane] = result[
                        row * height : (row + 1) * height, column * width : (column + 1) * width
                    ]


def part_of(scalars, kept, got, shape, cut, start, rows_in, cols_in):
    rows, size = shape
    step, cols = 128, kept.shape[2]
    below = (1 - rows_in) * (rows - size)
    at = pl.ds(start + below if isinstance(below, int) else pl.multiple_of(start + below, 128), step)
    row_at = iota((step, cols), 0) + (scalars[2] * cut + start + (1 - rows_in) * rows)
    col_at = iota((step, cols), 1)
    masks = []
    for row_start, col_start in ((scalars[0], scalars[1]), (scalars[5], scalars[6])):
        in_cols = jnp.where(col_at >= col_start, 1, 0) == cols_in
        masks.append((row_at >= row_start) & (row_at < row_start + size) & in_cols)
    return [
        jnp.where(masks[0], kept[plane, at].astype(F32), 0.0)
        + jnp.where(masks[1], got[plane, at].astype(F32), 0.0)
        for plane in range(2)
    ]


def tile_part(shape, cut, rows_in, cols_in, scalars, kept, got, *refs):
    *arrived, out = refs
    fill(shape, cut, 0, rows_in, cols_in, scalars, kept, got, arrived, out)


def fill(shape, cut, first, rows_in, cols_in, scalars, kept, got, arrived, out):
    step = 128
    for start in range(0, out.shape[1], step):
        at = pl.ds(start, step)
        part = part_of(scalars, kept, got, shape, cut, first + start, rows_in, cols_in)
        for plane in range(2):
            for more in arrived:
                part[plane] = part[plane] + more[plane, at].astype(F32)
            out[plane, at] = part[plane].astype(BF16)


def now_parts(shape, cut, scalars, before, kept, got, upper, lower):
    core = scalars[2]
    fill(shape, cut, 0, core, 1 - core, scalars, kept, got, (), upper)
    fill(shape, cut, cut, 1, 0, scalars, kept, got, (), lower)


def own_part(shape, cut, scalars, before, kept, got, upper, lower, third, out):
    fill(shape, cut, 0, 1, 1, scalars, kept, got, (upper, third), out.at[:, :cut])
    fill(shape, cut, cut, 1, 1, scalars, kept, got, (lower,), out.at[:, cut:])


def probe_sum(narrow, scalars, diag, probe_kept, probe_got, *outs):
    me = scalars[4]
    for step, out in enumerate(outs):
        block = lax.rem(me + step, narrow)
        total = probe_kept[block].astype(F32) + probe_got[block].astype(F32)
        out[...] = total.astype(BF16)


def sum_kernel(*refs):
    *terms, out = refs
    total = terms[0][...].astype(F32)
    for term in terms[1:]:
        total = total + term[...].astype(F32)
    out[...] = total.astype(out.dtype)


def scaled_sum(scale, *refs):
    *terms, out = refs
    sum_kernel(*terms, out)
    out[...] = out[...] * scale


def sum_of(*terms):
    return call(
        sum_kernel,
        jax.ShapeDtypeStruct(terms[0].shape, BF16),
        [VMEM] * len(terms),
        8,
        flops=8 * 10**9,
        name="sum",
    )(*terms)


def scatter_parts(x, axis):
    length = lax.axis_size(axis)
    if length > 8:
        return [lax.psum_scatter(x, axis, scatter_dimension=0, tiled=True)[0]]
    me = lax.axis_index(axis)

    def part(of):
        return lax.dynamic_index_in_dim(x, of, 0, keepdims=False)

    terms = [part(me)]
    for step in range(1, length):
        if length & (length - 1):
            pairs = [(i, (i + step) % length) for i in range(length)]
            to = lax.rem(me + step, length)
        else:
            pairs = [(i, i ^ step) for i in range(length)]
            to = me ^ step
        terms.append(lax.ppermute(part(to), axis, pairs))
    return terms


def shards(object_slab, probe_wave, amplitude, row_offset, col_offset, occupied):
    size = probe_wave.shape[1]
    rows, cols = object_slab.shape[1:]
    core = lax.axis_index("probe")
    narrow, wide, cores = (lax.axis_size(name) for name in ("narrow", "wide", "probe"))
    corner = jnp.stack([row_offset[0, 0, 0], col_offset[0, 0, 0]])
    here = [core, occupied[0, 0, 0], lax.axis_index("narrow")]
    scalars = jnp.concatenate([corner, jnp.stack([x.astype(jnp.int32) for x in here])])

    def shape(*dims, dtype=BF16):
        return jax.ShapeDtypeStruct(dims, dtype)

    cut = size // 2
    count = rows - cut
    first = to_neighbour(lax.dynamic_slice_in_dim(object_slab, cut * (1 - core), cut, 1), -1, 0)
    second = to_neighbour(lax.dynamic_slice_in_dim(object_slab, cut * core, count, 1), -1, 0)
    third = to_neighbour(first, -1, 1)
    late_scalars, first_late = lax.optimization_barrier((scalars, first))

    width = size // (narrow * cores)
    table = shape(2, size, size)
    tables = call(
        functools.partial(shift_tables, width),
        (
            (table,) * 5
            + (shape(size, size), shape(size, size))
            + (shape(cols, narrow * width),) * 2
        ),
        [SMEM] + [VMEM] * 6,
        8,
        flops=4 * 10**9,
        bytes_accessed=2 * 10**7,
        name="shift_tables",
    )(late_scalars, *dft_tables(size), probe_wave, amplitude[0, 0, 0])
    second, tables = lax.optimization_barrier((second, tables))
    pieces = (first, swap(first_late), second, swap(second), third, swap(third))
    blocks = shape(narrow, wide, 2, size // wide, width)
    sent, kept, probe_sent, probe_kept = call(
        slot_terms,
        (shape(2, count, cols), shape(2, count, cols), blocks, blocks),
        [SMEM] + [VMEM] * 16,
        18,
        scratch=[pltpu.VMEM((2, size, size), BF16)] * 5
        + [pltpu.VMEM((2, rows, size), BF16), pltpu.VMEM((2, size, size), BF16)],
        flops=6 * 10**9,
        bytes_accessed=2 * 10**7,
        name="slot_terms",
    )(scalars, object_slab, *pieces, *tables)

    got, probe_got = swap(sent), swap(probe_sent)
    scalars = jnp.concatenate([scalars, swap(corner)])

    def tile(name, kernel, height, *more, after=()):
        return call(
            functools.partial(kernel, (rows, size), cut, len(after)),
            shape(2, height, cols),
            [SMEM] + [ANY] * len(after) + [VMEM] * (2 + len(more)),
            8,
            name=name,
        )(scalars, *after, kept, got, *more)

    def diag_part(dims, cut, skip, scalars, *refs):
        tile_part(dims, cut, 0, 0, scalars, *refs[skip:])

    def later_part(dims, cut, skip, scalars, *refs):
        tile_part(dims, cut, 1 - scalars[2], scalars[2], scalars, *refs[skip:])

    diag = tile("diag_part", diag_part, cut)
    from_first = to_neighbour(diag, 1, 0)
    probe_blocks = call(
        functools.partial(probe_sum, narrow),
        (jax.ShapeDtypeStruct(blocks.shape[1:], BF16),) * narrow,
        [SMEM, ANY, VMEM, VMEM],
        8,
        name="probe_sum",
    )(scalars, diag, probe_kept, probe_got)
    upper, lower = call(
        functools.partial(now_parts, (rows, size), cut),
        (shape(2, cut, cols), shape(2, count - cut, cols)),
        [SMEM, ANY, VMEM, VMEM],
        8,
        name="now_parts",
    )(scalars, probe_blocks[0], kept, got)
    from_upper = to_neighbour(upper, 1, 0)
    from_lower = to_neighbour(lower, 1, 0, senders=(1,))
    from_third = to_neighbour(tile("later_part", later_part, cut, from_first), 1, 1)
    received = [
        lax.ppermute(block, "narrow", [(i, (i + step) % narrow) for i in range(narrow)])
        for step, block in enumerate(probe_blocks)
        if step
    ]
    total = sum_of(probe_blocks[0], *received)
    terms = scatter_parts(total, "wide")
    probe_grad = call(
        functools.partial(scaled_sum, 1.0 / math.sqrt(wide * narrow * cores)),
        jax.ShapeDtypeStruct(terms[0].shape, F32),
        [VMEM] * len(terms),
        8,
        flops=20 * 10**9,
        name="probe_grad",
    )(*terms)
    own = call(
        functools.partial(own_part, (rows, size), cut),
        shape(2, count, cols),
        [SMEM, ANY] + [VMEM] * 5,
        8,
        flops=1 * 10**9,
        name="own_part",
    )(scalars, total, kept, got, from_upper, from_lower, from_third)
    other = swap(own)
    object_grad = jnp.where(
        core == 0,
        jnp.concatenate([own[:, :cut], other], 1),
        jnp.concatenate([other[:, :cut], own], 1),
    )
    return (object_grad, probe_grad)


def solution(mesh):
    in_specs = (
        P(None, ("groups", "narrow"), "wide"),
        P(),
        P(("groups", "narrow"), "wide", "probe", None, None),
        P(("groups", "narrow"), "wide", "probe"),
        P(("groups", "narrow"), "wide", "probe"),
        P(("groups", "narrow"), "wide", "probe"),
    )
    out_specs = (
        P(None, ("groups", "narrow"), "wide"),
        P(None, ("groups", "wide"), ("narrow", "probe")),
    )
    return jax.shard_map(shards, mesh=mesh, in_specs=in_specs, out_specs=out_specs, check_vma=False)
```

time: 81 us -> 77.8 us (0.960)
  Pallas kernels: 21.5 us -> 17.1 us
  local copies, waits for them, and re-layouts: 6.45 us -> 9.57 us
  waiting for transfers between devices: 20.5 us -> 18.9 us
    unnamed x14 -> x18, local copies, waits for them, and re-layouts: 2.1 us -> 5.22 us
    pallas_call x1, Pallas kernels: 10.1 us -> 7.08 us  [shards(): call(slot_terms, (shape(2, count, cols), shape(2, count, cols), blocks, b...]
    ppermute x7, waiting for transfers between devices: 15.9 us -> 14.3 us  [to_neighbour(): return lax.ppermute(x, ('wide', 'narrow', 'probe'), pairs)]
    pallas_call x5, Pallas kernels: 9.32 us -> 7.9 us  [the longest x1 3.54 us: shards(): call(functools.partial(shift_tables, width), (table,) * 5 + (shape(size,...]
  transfers between devices with their start and end apart: 18 -> 18, of which waited for: 10 -> 10; matrix products, arithmetic and copies ran while one was open for 3% -> 3% of each run, Pallas kernels for 14% -> 13%
where the time goes in v4:
time: 77.8 us; the launch traced here: 77.2 us
  starting transfers between devices  27.4 us (35%)
  waiting for transfers between devices  18.9 us (24%)
  Pallas kernels  17.1 us (22%)
  local copies, waits for them, and re-layouts  9.57 us (12%)
  between operations  2.79 us (4%)
  other arithmetic  1.49 us (2%)
    ppermute x7, starting transfers between devices, to_neighbour(): return lax.ppermute(x, ('wide', 'narrow', 'probe'), pairs)  15.7 us
    ppermute x7, waiting for transfers between devices, to_neighbour(): return lax.ppermute(x, ('wide', 'narrow', 'probe'), pairs)  14.3 us
    pallas_call x1, Pallas kernels, shards(): call(slot_terms, (shape(2, count, cols), shape(2, count, cols), blocks, b...  7.08 us
    ppermute x7, starting transfers between devices, swap(): return lax.ppermute(x, 'probe', [(0, 1), (1, 0)])  6.85 us
    unnamed x18, local copies, waits for them, and re-layouts  5.22 us
    ppermute x7, waiting for transfers between devices, swap(): return lax.ppermute(x, 'probe', [(0, 1), (1, 0)])  4.6 us
    pallas_call x1, Pallas kernels, shards(): call(functools.partial(shift_tables, width), (table,) * 5 + (shape(size,...  3.54 us
    ppermute x3, starting transfers between devices, scatter_parts(): terms.append(lax.ppermute(part(to), axis, pairs))  2.78 us
  transfers between devices with their start and end apart: 18, of which 10 were waited for; matrix products, arithmetic and copies ran while one was open for 3% of the time, Pallas kernels for 13%

profile of v4, /device:TPU:19, one launch (start us, length us, event | category | flops | bytes accessed | tf_op | source)
XLA Modules:
  0.0 77.2 jit_solution(190038105033278683)
XLA Ops:
  0.7 2.0 %constant_dynamic-slice_fusion.1 = bf16[2,256,512]{2,1,0:T(8,128)(2,1)} fusion(bf16[2,640,512]{2,1,0:T(8,128)(2,1)} %own.1, s32[]{:T(128)S(6)} %select_n.28), kind=kLoop, calls=%fused_computation.6 | loop fusion | bytes 1048580 | tf_op jit(solution)/shard_map/dynamic_slice | solution.py:345
  2.7 2.1 %collective-permute-start.1 = (bf16[2,256,512]{2,1,0:T(8,128)(2,1)}, bf16[2,256,512]{2,1,0:T(8,128)(2,1)S(1)}, u32[]{:S(2)}, u32[]{:S(2)}) collective-permute-start(bf16[2,256,512]{2,1,0:T(8,128)(2,1)} %constant_dynamic-slice_fusion.1), channel_id=1, source_target_pairs={{2,0},{5,1},{6,4},{7,3},{9,5},{10,8},{11,7},{13,9},{14,12},{15,11}... | collective-permute-start | bytes 1572872 | tf_op jit(solution)/shard_map/ppermute | solution.py:29
  4.7 2.1 %constant_dynamic-slice_fusion = bf16[2,384,512]{2,1,0:T(8,128)(2,1)} fusion(bf16[2,640,512]{2,1,0:T(8,128)(2,1)} %own.1, s32[]{:T(128)S(6)} %select_n.29), kind=kLoop, calls=%fused_computation.5 | loop fusion | bytes 1572868 | tf_op jit(solution)/shard_map/dynamic_slice | solution.py:346
  6.8 2.1 %collective-permute-start.3 = (bf16[2,384,512]{2,1,0:T(8,128)(2,1)}, bf16[2,384,512]{2,1,0:T(8,128)(2,1)S(1)}, u32[]{:S(2)}, u32[]{:S(2)}) collective-permute-start(bf16[2,384,512]{2,1,0:T(8,128)(2,1)} %constant_dynamic-slice_fusion), channel_id=1, source_target_pairs={{2,0},{5,1},{6,4},{7,3},{9,5},{10,8},{11,7},{13,9},{14,12},{15,11}... | collective-permute-start | bytes 2359304 | tf_op jit(solution)/shard_map/ppermute | solution.py:29
  10.9 1.9 %collective-permute-done.1.first = bf16[2,256,512]{2,1,0:T(8,128)(2,1)S(1)} collective-permute-done((bf16[2,256,512]{2,1,0:T(8,128)(2,1)}, bf16[2,256,512]{2,1,0:T(8,128)(2,1)S(1)}, u32[]{:S(2)}, u32[]{:S(2)}) %collective-permute-start.1) | collective-permute-done | bytes 524320 | tf_op jit(solution)/shard_map/ppermute | solution.py:29
  12.8 2.5 %collective-permute-start.5 = (bf16[2,256,512]{2,1,0:T(8,128)(2,1)S(1)}, bf16[2,256,512]{2,1,0:T(8,128)(2,1)S(1)}, u32[]{:S(2)}, u32[]{:S(2)}) collective-permute-start(bf16[2,256,512]{2,1,0:T(8,128)(2,1)S(1)} %collective-permute-done.1.first), channel_id=1, source_target_pairs={{3,1},{4,0},{6,2},{7,5},{8,4},{10,6},{11,9},{12,8},{14,10},{15,13}... | collective-permute-start | bytes 1572872 | tf_op jit(solution)/shard_map/ppermute | solution.py:29
  15.3 1.0 %copy-done.5 = bf16[512,512]{1,0:T(8,128)(2,1)S(1)} copy-done((bf16[512,512]{1,0:T(8,128)(2,1)S(1)}, bf16[512,512]{1,0:T(8,128)(2,1)}, u32[]{:S(2)}) %copy-start.5) | copy-done | bytes 524312
  16.3 1.0 %copy-done.6 = bf16[512,512]{1,0:T(8,128)(2,1)S(1)} copy-done((bf16[512,512]{1,0:T(8,128)(2,1)S(1)}, bf16[512,512]{1,0:T(8,128)(2,1)}, u32[]{:S(2)}) %copy-start.6) | copy-done | bytes 524312
  17.4 1.0 %copy-done.7 = bf16[512,512]{1,0:T(8,128)(2,1)S(1)} copy-done((bf16[512,512]{1,0:T(8,128)(2,1)S(1)}, bf16[512,512]{1,0:T(8,128)(2,1)}, u32[]{:S(2)}) %copy-start.7) | copy-done | bytes 524312
  18.4 1.0 %copy-done.8 = bf16[512,512]{1,0:T(8,128)(2,1)S(1)} copy-done((bf16[512,512]{1,0:T(8,128)(2,1)S(1)}, bf16[512,512]{1,0:T(8,128)(2,1)}, u32[]{:S(2)}) %copy-start.8) | copy-done | bytes 524312
  19.5 3.5 %shift_tables.1 = (bf16[2,512,512]{2,1,0:T(8,128)(2,1)S(1)}, bf16[2,512,512]{2,1,0:T(8,128)(2,1)S(1)}, bf16[2,512,512]{2,1,0:T(8,128)(2,1)S(1)}, bf16[2,512,512]...) custom-call(s32[5]{0:T(128)S(1)} %concatenate.15.scalars, ...), custom_call_target="tpu_custom_call" | custom-call | flops 4000000000 | bytes 20000000 | tf_op jit(solution)/shard_map/shift_tables/pallas_call | solution.py:352
  23.0 2.1 %collective-permute-done.3.second = bf16[2,384,512]{2,1,0:T(8,128)(2,1)S(1)} collective-permute-done((bf16[2,384,512]{2,1,0:T(8,128)(2,1)}, bf16[2,384,512]{2,1,0:T(8,128)(2,1)S(1)}, u32[]{:S(2)}, u32[]{:S(2)}) %collective-permute-start.3) | collective-permute-done | bytes 786464 | tf_op jit(solution)/shard_map/ppermute | solution.py:29
  26.3 1.2 %collective-permute-start.6 = (bf16[2,256,512]{2,1,0:T(8,128)(2,1)S(1)}, bf16[2,256,512]{2,1,0:T(8,128)(2,1)S(1)}, u32[]{:S(2)}, u32[]{:S(2)}) collective-permute-start(bf16[2,256,512]{2,1,0:T(8,128)(2,1)S(1)} %collective-permute-done.5.third), channel_id=1, source_target_pairs={{0,1},{1,0},{2,3},{3,2},{4,5},{5,4},{6,7},{7,6},{8,9},{9,8},{10,11... | collective-permute-start | bytes 1572872 | tf_op jit(solution)/shard_map/ppermute | solution.py:33
  27.5 1.2 %collective-permute-done.2.first2 = bf16[2,256,512]{2,1,0:T(8,128)(2,1)S(1)} collective-permute-done((bf16[2,256,512]{2,1,0:T(8,128)(2,1)S(1)}, bf16[2,256,512]{2,1,0:T(8,128)(2,1)S(1)}, u32[]{:S(2)}, u32[]{:S(2)}) %collective-permute-start.2) | collective-permute-done | bytes 524320 | tf_op jit(solution)/shard_map/ppermute | solution.py:33
  29.5 1.0 %copy-done.4 = bf16[2,256,512]{2,1,0:T(8,128)(2,1)S(1)} copy-done((bf16[2,256,512]{2,1,0:T(8,128)(2,1)S(1)}, bf16[2,256,512]{2,1,0:T(8,128)(2,1)}, u32[]{:S(2)}) %copy-start.4) | copy-done | bytes 524312
  30.6 7.1 %slot_terms.1 = (bf16[2,384,512]{2,1,0:T(8,128)(2,1)}, bf16[2,384,512]{2,1,0:T(8,128)(2,1)S(1)}, bf16[2,4,2,128,128]{4,3,2,1,0:T(8,128)(2,1)}, bf16[2,4,2,128,128]{4,3,2,1,0:T(8,128)(2,1)S(1)}) custom-call(s32[5]{0:T(128)S(1)} %concatenate.15.scalars, bf16[2,640,512]{2,1,0:T(8,128)(2,1)S(1)} %copy-done, bf16[2,256,512]{2,1,0:T(8,128)(2,1)S(1)} %copy-done.4, ...), custom_call_target="tpu_custom_call" | custom-call | flops 6000000000 | bytes 20000000 | tf_op jit(solution)/shard_map/slot_terms/pallas_call | solution.py:368
  38.6 1.3 %collective-permute-done = s32[2]{0:T(128)S(1)} collective-permute-done((s32[2]{0:T(128)S(1)}, s32[2]{0:T(128)S(1)}, u32[]{:S(2)}, u32[]{:S(2)}) %collective-permute-start) | collective-permute-done | bytes 40 | tf_op jit(solution)/shard_map/ppermute | solution.py:33
  41.0 3.9 %collective-permute-start.12 = (bf16[2,256,512]{2,1,0:T(8,128)(2,1)S(1)}, bf16[2,256,512]{2,1,0:T(8,128)(2,1)}, u32[]{:S(2)}, u32[]{:S(2)}) collective-permute-start(bf16[2,256,512]{2,1,0:T(8,128)(2,1)S(1)} %diag_part.1.diag), channel_id=1, source_target_pairs={{0,2},{1,5},{3,7},{4,6},{5,9},{7,11},{8,10},{9,13},{11,15},{12,14}... | collective-permute-start | bytes 1572872 | tf_op jit(solution)/shard_map/ppermute | solution.py:29
  44.9 1.3 %probe_sum.1 = (bf16[4,2,128,128]{3,2,1,0:T(8,128)(2,1)S(1)}, bf16[4,2,128,128]{3,2,1,0:T(8,128)(2,1)}) custom-call(s32[7]{0:T(128)S(1)} %concatenate.14.scalars, bf16[2,256,512]{2,1,0:T(8,128)(2,1)S(1)} %diag_part.1.diag, bf16[2,4,2,128,128]{4,3,2,1,0:T(8,128)(2,1)S(1)} %get-tuple-element.54.probe_kept, ...), custom_call_target="tpu_custom_call" | custom-call | tf_op jit(solution)/shard_map/probe_sum/pallas_call | solution.py:400
  46.3 2.1 %collective-permute-start.9 = (bf16[4,2,128,128]{3,2,1,0:T(8,128)(2,1)}, bf16[4,2,128,128]{3,2,1,0:T(8,128)(2,1)S(1)}, u32[]{:S(2)}, u32[]{:S(2)}) collective-permute-start(bf16[4,2,128,128]{3,2,1,0:T(8,128)(2,1)} %get-tuple-element.57), channel_id=1, source_target_pairs={{0,2},{2,0},{1,3},{3,1},{4,6},{6,4},{5,7},{7,5},{8,10},{10,8},{9,1... | collective-permute-start | bytes 786440 | tf_op jit(solution)/shard_map/ppermute | solution.py:418
  48.4 1.0 %now_parts.1 = (bf16[2,256,512]{2,1,0:T(8,128)(2,1)S(1)}, bf16[2,128,512]{2,1,0:T(8,128)(2,1)S(1)}) custom-call(s32[7]{0:T(128)S(1)} %concatenate.14.scalars, bf16[4,2,128,128]{3,2,1,0:T(8,128)(2,1)S(1)} %get-tuple-element.56.refs_0_.before, bf16[2,384,512]{2,1,0:T(8,128)(2,1)S(1)} %get-tuple-element.52.refs_0_.kept, ...), custom_call_target="tpu_custom_call" | custom-call | tf_op jit(solution)/shard_map/now_parts/pallas_call | solution.py:407
  49.4 1.9 %collective-permute-start.10 = (bf16[2,256,512]{2,1,0:T(8,128)(2,1)S(1)}, bf16[2,256,512]{2,1,0:T(8,128)(2,1)S(1)}, u32[]{:S(2)}, u32[]{:S(2)}) collective-permute-start(bf16[2,256,512]{2,1,0:T(8,128)(2,1)S(1)} %get-tuple-element.58), channel_id=1, source_target_pairs={{0,2},{1,5},{3,7},{4,6},{5,9},{7,11},{8,10},{9,13},{11,15},{12,14}... | collective-permute-start | bytes 1572872 | tf_op jit(solution)/shard_map/ppermute | solution.py:29
  51.3 1.9 %collective-permute-start.11 = (bf16[2,128,512]{2,1,0:T(8,128)(2,1)S(1)}, bf16[2,128,512]{2,1,0:T(8,128)(2,1)S(1)}, u32[]{:S(2)}, u32[]{:S(2)}) collective-permute-start(bf16[2,128,512]{2,1,0:T(8,128)(2,1)S(1)} %get-tuple-element.59), channel_id=1, source_target_pairs={{1,5},{3,7},{5,9},{7,11},{9,13},{11,15},{17,21},{19,23},{21,25},{2... | collective-permute-start | bytes 786440 | tf_op jit(solution)/shard_map/ppermute | solution.py:29
  53.2 1.4 %later_part.1 = bf16[2,256,512]{2,1,0:T(8,128)(2,1)S(1)} custom-call(s32[7]{0:T(128)S(1)} %concatenate.14.scalars, bf16[2,384,512]{2,1,0:T(8,128)(2,1)S(1)} %get-tuple-element.52.refs_0_.kept, bf16[2,384,512]{2,1,0:T(8,128)(2,1)S(1)} %collective-permute-done.7.refs_1_.got, bf16[2,256,512]{2,1,0:T(8,128)(2,1)} %collective-permute-done.12.refs_2_), custom_call_target="tpu_custom_call" | custom-call | tf_op jit(solution)/shard_map/later_part/pallas_call | solution.py:384
  54.6 1.3 %collective-permute-start.13 = (bf16[2,256,512]{2,1,0:T(8,128)(2,1)S(1)}, bf16[2,256,512]{2,1,0:T(8,128)(2,1)S(1)}, u32[]{:S(2)}, u32[]{:S(2)}) collective-permute-start(bf16[2,256,512]{2,1,0:T(8,128)(2,1)S(1)} %later_part.1), channel_id=1, source_target_pairs={{0,4},{1,3},{2,6},{4,8},{5,7},{6,10},{8,12},{9,11},{10,14},{13,15}... | collective-permute-start | bytes 1572872 | tf_op jit(solution)/shard_map/ppermute | solution.py:29
  56.2 2.6 %collective-permute-start.16 = (bf16[2,128,128]{2,1,0:T(8,128)(2,1)S(1)}, bf16[2,128,128]{2,1,0:T(8,128)(2,1)S(1)}, u32[]{:S(2)}, u32[]{:S(2)}) collective-permute-start(bf16[2,128,128]{2,1,0:T(8,128)(2,1)S(1)} %get-tuple-element.61), channel_id=1, source_target_pairs={{0,8},{4,12},{8,0},{12,4},{1,9},{5,13},{9,1},{13,5},{2,10},{6,14},... | collective-permute-start | bytes 196616 | tf_op jit(solution)/shard_map/ppermute | solution.py:327
  58.8 5.4 %collective-permute-done.11.lower = bf16[2,128,512]{2,1,0:T(8,128)(2,1)S(1)} collective-permute-done((bf16[2,128,512]{2,1,0:T(8,128)(2,1)S(1)}, bf16[2,128,512]{2,1,0:T(8,128)(2,1)S(1)}, u32[]{:S(2)}, u32[]{:S(2)}) %collective-permute-start.11) | collective-permute-done | bytes 262176 | tf_op jit(solution)/shard_map/ppermute | solution.py:29
  64.2 4.7 %collective-permute-done.13.third = bf16[2,256,512]{2,1,0:T(8,128)(2,1)S(1)} collective-permute-done((bf16[2,256,512]{2,1,0:T(8,128)(2,1)S(1)}, bf16[2,256,512]{2,1,0:T(8,128)(2,1)S(1)}, u32[]{:S(2)}, u32[]{:S(2)}) %collective-permute-start.13) | collective-permute-done | bytes 524320 | tf_op jit(solution)/shard_map/ppermute | solution.py:29
  68.9 1.1 %own_part.1 = bf16[2,384,512]{2,1,0:T(8,128)(2,1)S(1)} custom-call(s32[7]{0:T(128)S(1)} %concatenate.14.scalars, bf16[4,2,128,128]{3,2,1,0:T(8,128)(2,1)S(1)} %sum.1.before, bf16[2,384,512]{2,1,0:T(8,128)(2,1)S(1)} %get-tuple-element.52.refs_0_.kept, bf16[2,384,512]{2,1,0:T(8,128)(2,1)S(1)} %collective-permute-done.7.refs_1_.got, ...), custom_call_target="tpu_custom_call" | custom-call | flops 1000000000 | tf_op jit(solution)/shard_map/own_part/pallas_call | solution.py:432
  70.0 3.8 %collective-permute-start.14 = (bf16[2,384,512]{2,1,0:T(8,128)(2,1)S(1)}, bf16[2,384,512]{2,1,0:T(8,128)(2,1)S(1)}, u32[]{:S(2)}, u32[]{:S(2)}) collective-permute-start(bf16[2,384,512]{2,1,0:T(8,128)(2,1)S(1)} %own_part.1), channel_id=1, source_target_pairs={{0,1},{1,0},{2,3},{3,2},{4,5},{5,4},{6,7},{7,6},{8,9},{9,8},{10,11... | collective-permute-start | bytes 2359304 | tf_op jit(solution)/shard_map/ppermute | solution.py:33
  74.6 1.2 %collective-permute-done.14 = bf16[2,384,512]{2,1,0:T(8,128)(2,1)S(1)} collective-permute-done((bf16[2,384,512]{2,1,0:T(8,128)(2,1)S(1)}, bf16[2,384,512]{2,1,0:T(8,128)(2,1)S(1)}, u32[]{:S(2)}, u32[]{:S(2)}) %collective-permute-start.14) | collective-permute-done | bytes 786464 | tf_op jit(solution)/shard_map/ppermute | solution.py:33
  75.8 1.4 %maximum_select_fusion = bf16[2,640,512]{2,1,0:T(8,128)(2,1)} fusion(bf16[2,384,512]{2,1,0:T(8,128)(2,1)S(1)} %collective-permute-done.14, bf16[2,256,512]{2,1,0:T(8,128)(2,1)S(1)} %slice.8, bf16[2,384,512]{2,1,0:T(8,128)(2,1)S(1)} %own_part.1, bf16[2,256,512]{2,1,0:T(8,128)(2,1)S(1)} %slice.9, pred[]{:T(512)S(6)} %eq.3), kind=kLoop, calls=%fused_computation | loop fusion | flops 5898240 | bytes 3932161 | tf_op jit(solution)/shard_map/jit(_where)/select_n | solution.py:441
  (40 shorter events, 5.1 us)
Async XLA Ops:
  0.6 14.6 %copy-start.1 = (bf16[2,512,512]{2,1,0:T(8,128)(2,1)S(1)}, bf16[2,512,512]{2,1,0:T(8,128)(2,1)}, u32[]{:S(2)}) copy-start(bf16[2,512,512]{2,1,0:T(8,128)(2,1)} %probe_in.1) | copy-start | bytes 3145732
  0.6 14.6 %copy-start.2 = (bf16[1,1,1,512,512]{4,3,2,1,0:T(8,128)(2,1)S(1)}, bf16[1,1,1,512,512]{4,3,2,1,0:T(8,128)(2,1)}, u32[]{:S(2)}) copy-start(bf16[1,1,1,512,512]{4,3,2,1,0:T(8,128)(2,1)} %param.12) | copy-start | bytes 1572868
  2.7 10.1 %collective-permute-start.1 = (bf16[2,256,512]{2,1,0:T(8,128)(2,1)}, bf16[2,256,512]{2,1,0:T(8,128)(2,1)S(1)}, u32[]{:S(2)}, u32[]{:S(2)}) collective-permute-start(bf16[2,256,512]{2,1,0:T(8,128)(2,1)} %constant_dynamic-slice_fusion.1), channel_id=1, source_target_pairs={{2,0},{5,1},{6,4},{7,3},{9,5},{10,8},{11,7},{13,9},{14,12},{15,11}... | collective-permute-start | bytes 1572872 | tf_op jit(solution)/shard_map/ppermute | solution.py:29
  6.8 18.3 %collective-permute-start.3 = (bf16[2,384,512]{2,1,0:T(8,128)(2,1)}, bf16[2,384,512]{2,1,0:T(8,128)(2,1)S(1)}, u32[]{:S(2)}, u32[]{:S(2)}) collective-permute-start(bf16[2,384,512]{2,1,0:T(8,128)(2,1)} %constant_dynamic-slice_fusion), channel_id=1, source_target_pairs={{2,0},{5,1},{6,4},{7,3},{9,5},{10,8},{11,7},{13,9},{14,12},{15,11}... | collective-permute-start | bytes 2359304 | tf_op jit(solution)/shard_map/ppermute | solution.py:29
  12.8 13.3 %copy-start.3 = (bf16[2,256,512]{2,1,0:T(8,128)(2,1)}, bf16[2,256,512]{2,1,0:T(8,128)(2,1)S(1)}, u32[]{:S(2)}) copy-start(bf16[2,256,512]{2,1,0:T(8,128)(2,1)S(1)} %collective-permute-done.1.first) | copy-start | bytes 1572868
  12.8 13.5 %collective-permute-start.5 = (bf16[2,256,512]{2,1,0:T(8,128)(2,1)S(1)}, bf16[2,256,512]{2,1,0:T(8,128)(2,1)S(1)}, u32[]{:S(2)}, u32[]{:S(2)}) collective-permute-start(bf16[2,256,512]{2,1,0:T(8,128)(2,1)S(1)} %collective-permute-done.1.first), channel_id=1, source_target_pairs={{3,1},{4,0},{6,2},{7,5},{8,4},{10,6},{11,9},{12,8},{14,10},{15,13}... | collective-permute-start | bytes 1572872 | tf_op jit(solution)/shard_map/ppermute | solution.py:29
  15.3 1.0 %copy-start.5 = (bf16[512,512]{1,0:T(8,128)(2,1)S(1)}, bf16[512,512]{1,0:T(8,128)(2,1)}, u32[]{:S(2)}) copy-start(bf16[512,512]{1,0:T(8,128)(2,1)} %constant.42.clone.cos_in) | copy-start | bytes 1572868
  16.3 1.0 %copy-start.6 = (bf16[512,512]{1,0:T(8,128)(2,1)S(1)}, bf16[512,512]{1,0:T(8,128)(2,1)}, u32[]{:S(2)}) copy-start(bf16[512,512]{1,0:T(8,128)(2,1)} %constant.43.clone.sin_in) | copy-start | bytes 1572868
  17.4 1.0 %copy-start.7 = (bf16[512,512]{1,0:T(8,128)(2,1)S(1)}, bf16[512,512]{1,0:T(8,128)(2,1)}, u32[]{:S(2)}) copy-start(bf16[512,512]{1,0:T(8,128)(2,1)} %constant.44.clone.cos_t) | copy-start | bytes 1572868
  18.4 1.0 %copy-start.8 = (bf16[512,512]{1,0:T(8,128)(2,1)S(1)}, bf16[512,512]{1,0:T(8,128)(2,1)}, u32[]{:S(2)}) copy-start(bf16[512,512]{1,0:T(8,128)(2,1)} %constant.45.clone.sin_t) | copy-start | bytes 1572868
  19.5 10.1 %copy-start = (bf16[2,640,512]{2,1,0:T(8,128)(2,1)S(1)}, bf16[2,640,512]{2,1,0:T(8,128)(2,1)}, u32[]{:S(2)}) copy-start(bf16[2,640,512]{2,1,0:T(8,128)(2,1)} %own.1) | copy-start | bytes 3932164
  25.1 4.4 %collective-permute-start.4 = (bf16[2,384,512]{2,1,0:T(8,128)(2,1)S(1)}, bf16[2,384,512]{2,1,0:T(8,128)(2,1)S(1)}, u32[]{:S(2)}, u32[]{:S(2)}) collective-permute-start(bf16[2,384,512]{2,1,0:T(8,128)(2,1)S(1)} %collective-permute-done.3.second), channel_id=1, source_target_pairs={{0,1},{1,0},{2,3},{3,2},{4,5},{5,4},{6,7},{7,6},{8,9},{9,8},{10,11... | collective-permute-start | bytes 2359304 | tf_op jit(solution)/shard_map/ppermute | solution.py:33
  26.1 2.7 %collective-permute-start.2 = (bf16[2,256,512]{2,1,0:T(8,128)(2,1)S(1)}, bf16[2,256,512]{2,1,0:T(8,128)(2,1)S(1)}, u32[]{:S(2)}, u32[]{:S(2)}) collective-permute-start(bf16[2,256,512]{2,1,0:T(8,128)(2,1)S(1)} %collective-permute-done.1.first), channel_id=1, source_target_pairs={{0,1},{1,0},{2,3},{3,2},{4,5},{5,4},{6,7},{7,6},{8,9},{9,8},{10,11... | collective-permute-start | bytes 1572872 | tf_op jit(solution)/shard_map/ppermute | solution.py:33
  26.3 3.2 %collective-permute-start.6 = (bf16[2,256,512]{2,1,0:T(8,128)(2,1)S(1)}, bf16[2,256,512]{2,1,0:T(8,128)(2,1)S(1)}, u32[]{:S(2)}, u32[]{:S(2)}) collective-permute-start(bf16[2,256,512]{2,1,0:T(8,128)(2,1)S(1)} %collective-permute-done.5.third), channel_id=1, source_target_pairs={{0,1},{1,0},{2,3},{3,2},{4,5},{5,4},{6,7},{7,6},{8,9},{9,8},{10,11... | collective-permute-start | bytes 1572872 | tf_op jit(solution)/shard_map/ppermute | solution.py:33
  29.5 1.0 %copy-start.4 = (bf16[2,256,512]{2,1,0:T(8,128)(2,1)S(1)}, bf16[2,256,512]{2,1,0:T(8,128)(2,1)}, u32[]{:S(2)}) copy-start(bf16[2,256,512]{2,1,0:T(8,128)(2,1)} %copy-done.3) | copy-start | bytes 1572868
  37.6 2.5 %collective-permute-start.7 = (bf16[2,384,512]{2,1,0:T(8,128)(2,1)}, bf16[2,384,512]{2,1,0:T(8,128)(2,1)S(1)}, u32[]{:S(2)}, u32[]{:S(2)}) collective-permute-start(bf16[2,384,512]{2,1,0:T(8,128)(2,1)} %get-tuple-element.53), channel_id=1, source_target_pairs={{0,1},{1,0},{2,3},{3,2},{4,5},{5,4},{6,7},{7,6},{8,9},{9,8},{10,11... | collective-permute-start | bytes 2359304 | tf_op jit(solution)/shard_map/ppermute | solution.py:33
  38.0 6.9 %collective-permute-start.8 = (bf16[2,4,2,128,128]{4,3,2,1,0:T(8,128)(2,1)}, bf16[2,4,2,128,128]{4,3,2,1,0:T(8,128)(2,1)S(1)}, u32[]{:S(2)}, u32[]{:S(2)}) collective-permute-start(bf16[2,4,2,128,128]{4,3,2,1,0:T(8,128)(2,1)} %get-tuple-element.55), channel_id=1, source_target_pairs={{0,1},{1,0},{2,3},{3,2},{4,5},{5,4},{6,7},{7,6},{8,9},{9,8},{10,11... | collective-permute-start | bytes 1572872 | tf_op jit(solution)/shard_map/ppermute | solution.py:33
  38.2 1.7 %collective-permute-start = (s32[2]{0:T(128)S(1)}, s32[2]{0:T(128)S(1)}, u32[]{:S(2)}, u32[]{:S(2)}) collective-permute-start(s32[2]{0:T(128)S(1)} %pad_add_fusion), channel_id=1, source_target_pairs={{0,1},{1,0},{2,3},{3,2},{4,5},{5,4},{6,7},{7,6},{8,9},{9,8},{10,11... | collective-permute-start | bytes 32 | tf_op jit(solution)/shard_map/ppermute | solution.py:33
  41.0 12.2 %collective-permute-start.12 = (bf16[2,256,512]{2,1,0:T(8,128)(2,1)S(1)}, bf16[2,256,512]{2,1,0:T(8,128)(2,1)}, u32[]{:S(2)}, u32[]{:S(2)}) collective-permute-start(bf16[2,256,512]{2,1,0:T(8,128)(2,1)S(1)} %diag_part.1.diag), channel_id=1, source_target_pairs={{0,2},{1,5},{3,7},{4,6},{5,9},{7,11},{8,10},{9,13},{11,15},{12,14}... | collective-permute-start | bytes 1572872 | tf_op jit(solution)/shard_map/ppermute | solution.py:29
  46.3 9.7 %collective-permute-start.9 = (bf16[4,2,128,128]{3,2,1,0:T(8,128)(2,1)}, bf16[4,2,128,128]{3,2,1,0:T(8,128)(2,1)S(1)}, u32[]{:S(2)}, u32[]{:S(2)}) collective-permute-start(bf16[4,2,128,128]{3,2,1,0:T(8,128)(2,1)} %get-tuple-element.57), channel_id=1, source_target_pairs={{0,2},{2,0},{1,3},{3,1},{4,6},{6,4},{5,7},{7,5},{8,10},{10,8},{9,1... | collective-permute-start | bytes 786440 | tf_op jit(solution)/shard_map/ppermute | solution.py:418
  49.4 14.9 %collective-permute-start.10 = (bf16[2,256,512]{2,1,0:T(8,128)(2,1)S(1)}, bf16[2,256,512]{2,1,0:T(8,128)(2,1)S(1)}, u32[]{:S(2)}, u32[]{:S(2)}) collective-permute-start(bf16[2,256,512]{2,1,0:T(8,128)(2,1)S(1)} %get-tuple-element.58), channel_id=1, source_target_pairs={{0,2},{1,5},{3,7},{4,6},{5,9},{7,11},{8,10},{9,13},{11,15},{12,14}... | collective-permute-start | bytes 1572872 | tf_op jit(solution)/shard_map/ppermute | solution.py:29
  51.3 12.9 %collective-permute-start.11 = (bf16[2,128,512]{2,1,0:T(8,128)(2,1)S(1)}, bf16[2,128,512]{2,1,0:T(8,128)(2,1)S(1)}, u32[]{:S(2)}, u32[]{:S(2)}) collective-permute-start(bf16[2,128,512]{2,1,0:T(8,128)(2,1)S(1)} %get-tuple-element.59), channel_id=1, source_target_pairs={{1,5},{3,7},{5,9},{7,11},{9,13},{11,15},{17,21},{19,23},{21,25},{2... | collective-permute-start | bytes 786440 | tf_op jit(solution)/shard_map/ppermute | solution.py:29
  54.6 14.3 %collective-permute-start.13 = (bf16[2,256,512]{2,1,0:T(8,128)(2,1)S(1)}, bf16[2,256,512]{2,1,0:T(8,128)(2,1)S(1)}, u32[]{:S(2)}, u32[]{:S(2)}) collective-permute-start(bf16[2,256,512]{2,1,0:T(8,128)(2,1)S(1)} %later_part.1), channel_id=1, source_target_pairs={{0,4},{1,3},{2,6},{4,8},{5,7},{6,10},{8,12},{9,11},{10,14},{13,15}... | collective-permute-start | bytes 1572872 | tf_op jit(solution)/shard_map/ppermute | solution.py:29
  56.1 17.8 %collective-permute-start.15 = (bf16[2,128,128]{2,1,0:T(8,128)(2,1)S(1)}, bf16[2,128,128]{2,1,0:T(8,128)(2,1)S(1)}, u32[]{:S(2)}, u32[]{:S(2)}) collective-permute-start(bf16[2,128,128]{2,1,0:T(8,128)(2,1)S(1)} %get-tuple-element.62), channel_id=1, source_target_pairs={{0,4},{4,0},{8,12},{12,8},{1,5},{5,1},{9,13},{13,9},{2,6},{6,2},{1... | collective-permute-start | bytes 196616 | tf_op jit(solution)/shard_map/ppermute | solution.py:327
  56.2 17.6 %collective-permute-start.16 = (bf16[2,128,128]{2,1,0:T(8,128)(2,1)S(1)}, bf16[2,128,128]{2,1,0:T(8,128)(2,1)S(1)}, u32[]{:S(2)}, u32[]{:S(2)}) collective-permute-start(bf16[2,128,128]{2,1,0:T(8,128)(2,1)S(1)} %get-tuple-element.61), channel_id=1, source_target_pairs={{0,8},{4,12},{8,0},{12,4},{1,9},{5,13},{9,1},{13,5},{2,10},{6,14},... | collective-permute-start | bytes 196616 | tf_op jit(solution)/shard_map/ppermute | solution.py:327
  64.2 9.6 %collective-permute-start.17 = (bf16[2,128,128]{2,1,0:T(8,128)(2,1)S(1)}, bf16[2,128,128]{2,1,0:T(8,128)(2,1)S(1)}, u32[]{:S(2)}, u32[]{:S(2)}) collective-permute-start(bf16[2,128,128]{2,1,0:T(8,128)(2,1)S(1)} %get-tuple-element.60), channel_id=1, source_target_pairs={{0,12},{4,8},{8,4},{12,0},{1,13},{5,9},{9,5},{13,1},{2,14},{6,10},... | collective-permute-start | bytes 196616 | tf_op jit(solution)/shard_map/ppermute | solution.py:327
  70.0 5.7 %collective-permute-start.14 = (bf16[2,384,512]{2,1,0:T(8,128)(2,1)S(1)}, bf16[2,384,512]{2,1,0:T(8,128)(2,1)S(1)}, u32[]{:S(2)}, u32[]{:S(2)}) collective-permute-start(bf16[2,384,512]{2,1,0:T(8,128)(2,1)S(1)} %own_part.1), channel_id=1, source_target_pairs={{0,1},{1,0},{2,3},{3,2},{4,5},{5,4},{6,7},{7,6},{8,9},{9,8},{10,11... | collective-permute-start | bytes 2359304 | tf_op jit(solution)/shard_map/ppermute | solution.py:33

commit v5 on v4

--- a/solution.py
+++ b/solution.py
@@ -125,8 +125,8 @@
 
 def slot_terms(
     scalars, own, first, first2, second, second2, third, third2,
-    right, right_t, left_t, left, probe, amplitude, back_rows, back_cols, back_cols2,
-    sent, kept, probe_sent, probe_kept, exit_wave, half, chi, back_half, patch, obj, term,
+    right, right_t, left_t, left, probe, amplitude,
+    sent, kept, term, exit_wave, half, chi, back_half, patch, obj,
 ):
     rows, size = own.shape[1:]
     cut = first.shape[1]
@@ -217,6 +217,8 @@
         kept[plane] = obj[plane, pl.ds(pl.multiple_of(cut * core, 128), count)]
         sent[plane] = obj[plane, pl.ds(pl.multiple_of(cut * (1 - core), 128), count)]
 
+
+def probe_parts(term, back_rows, back_cols, back_cols2, probe_sent, probe_kept):
     narrow, blocks, _, height, width = probe_sent.shape
     for plane in range(2):
         moved = dot(back_rows[...], term[plane]).astype(BF16)
@@ -269,8 +271,8 @@
     fill(shape, cut, cut, 1, 0, scalars, kept, got, (), lower)
 
 
-def own_part(shape, cut, scalars, before, kept, got, upper, lower, third, out):
-    fill(shape, cut, 0, 1, 1, scalars, kept, got, (upper, third), out.at[:, :cut])
+def own_part(shape, cut, scalars, before, kept, got, upper, lower, out):
+    fill(shape, cut, 0, 1, 1, scalars, kept, got, (upper,), out.at[:, :cut])
     fill(shape, cut, cut, 1, 1, scalars, kept, got, (lower,), out.at[:, cut:])
 
 
@@ -335,7 +337,8 @@
     narrow, wide, cores = (lax.axis_size(name) for name in ("narrow", "wide", "probe"))
     corner = jnp.stack([row_offset[0, 0, 0], col_offset[0, 0, 0]])
     here = [core, occupied[0, 0, 0], lax.axis_index("narrow")]
-    scalars = jnp.concatenate([corner, jnp.stack([x.astype(jnp.int32) for x in here])])
+    here = jnp.stack([x.astype(jnp.int32) for x in here])
+    scalars = jnp.concatenate([corner, here, swap(corner)])
 
     def shape(*dims, dtype=BF16):
         return jax.ShapeDtypeStruct(dims, dtype)
@@ -345,7 +348,9 @@
     first = to_neighbour(lax.dynamic_slice_in_dim(object_slab, cut * (1 - core), cut, 1), -1, 0)
     second = to_neighbour(lax.dynamic_slice_in_dim(object_slab, cut * core, count, 1), -1, 0)
     third = to_neighbour(first, -1, 1)
-    late_scalars, first_late = lax.optimization_barrier((scalars, first))
+    late_scalars, first_late, late_probe, late_amplitude, *late_tables = lax.optimization_barrier(
+        (scalars, first, probe_wave, amplitude[0, 0, 0], *dft_tables(size))
+    )
 
     width = size // (narrow * cores)
     table = shape(2, size, size)
@@ -361,24 +366,27 @@
         flops=4 * 10**9,
         bytes_accessed=2 * 10**7,
         name="shift_tables",
-    )(late_scalars, *dft_tables(size), probe_wave, amplitude[0, 0, 0])
+    )(late_scalars, *late_tables, late_probe, late_amplitude)
     second, tables = lax.optimization_barrier((second, tables))
     pieces = (first, swap(first_late), second, swap(second), third, swap(third))
     blocks = shape(narrow, wide, 2, size // wide, width)
-    sent, kept, probe_sent, probe_kept = call(
+    *tables, back_rows, back_cols, back_cols2 = tables
+    sent, kept, term = call(
         slot_terms,
-        (shape(2, count, cols), shape(2, count, cols), blocks, blocks),
-        [SMEM] + [VMEM] * 16,
+        (shape(2, count, cols), shape(2, count, cols), table),
+        [SMEM] + [VMEM] * 13,
         18,
         scratch=[pltpu.VMEM((2, size, size), BF16)] * 5
-        + [pltpu.VMEM((2, rows, size), BF16), pltpu.VMEM((2, size, size), BF16)],
+        + [pltpu.VMEM((2, rows, size), BF16)],
         flops=6 * 10**9,
         bytes_accessed=2 * 10**7,
         name="slot_terms",
     )(scalars, object_slab, *pieces, *tables)
 
+    probe_sent, probe_kept = call(
+        probe_parts, (blocks, blocks), [VMEM] * 4, 8, name="probe_parts"
+    )(term, back_rows, back_cols, back_cols2)
     got, probe_got = swap(sent), swap(probe_sent)
-    scalars = jnp.concatenate([scalars, swap(corner)])
 
     def tile(name, kernel, height, *more, after=()):
         return call(
@@ -395,7 +403,7 @@
     def later_part(dims, cut, skip, scalars, *refs):
         tile_part(dims, cut, 1 - scalars[2], scalars[2], scalars, *refs[skip:])
 
-    diag = tile("diag_part", diag_part, cut)
+    diag = tile("diag_part", diag_part, cut, after=(probe_sent,))
     from_first = to_neighbour(diag, 1, 0)
     probe_blocks = call(
         functools.partial(probe_sum, narrow),
@@ -432,16 +440,21 @@
     own = call(
         functools.partial(own_part, (rows, size), cut),
         shape(2, count, cols),
-        [SMEM, ANY] + [VMEM] * 5,
+        [SMEM, ANY] + [VMEM] * 4,
         8,
         flops=1 * 10**9,
         name="own_part",
-    )(scalars, total, kept, got, from_upper, from_lower, from_third)
-    other = swap(own)
-    object_grad = jnp.where(
-        core == 0,
-        jnp.concatenate([own[:, :cut], other], 1),
-        jnp.concatenate([other[:, :cut], own], 1),
+    )(scalars, total, kept, got, from_upper, from_lower)
+    other, last, other_last = swap(own), from_third, swap(from_third)
+    mine = own[:, :cut].astype(F32) + last.astype(F32)
+    theirs = other[:, :cut].astype(F32) + other_last.astype(F32)
+    object_grad = jnp.concatenate(
+        [
+            jnp.where(core == 0, mine, theirs).astype(BF16),
+            jnp.where(core == 0, theirs, mine).astype(BF16),
+            jnp.where(core == 0, other[:, cut:], own[:, cut:]),
+        ],
+        1,
     )
     return (object_grad, probe_grad)
 

time: 77.8 us -> 72.6 us (0.933)
  waiting for transfers between devices: 18.9 us -> 13 us
  starting transfers between devices: 27.4 us -> 32.1 us
  local copies, waits for them, and re-layouts: 9.57 us -> 7.36 us
  Pallas kernels: 17.1 us -> 15.1 us
    ppermute x7, waiting for transfers between devices: 14.3 us -> 9.71 us  [to_neighbour(): return lax.ppermute(x, ('wide', 'narrow', 'probe'), pairs)]
    ppermute x7 -> x8, starting transfers between devices: 6.85 us -> 11.2 us  [swap(): return lax.ppermute(x, 'probe', [(0, 1), (1, 0)])]
    unnamed x18 -> x14, local copies, waits for them, and re-layouts: 5.22 us -> 3.14 us
    select_n x1, other arithmetic: 1.42 us -> 0.03 us  [shards(): jnp.where(core == 0, other[:, cut:], own[:, cut:])]
    ppermute x7 -> x8, waiting for transfers between devices: 4.6 us -> 3.27 us  [swap(): return lax.ppermute(x, 'probe', [(0, 1), (1, 0)])]
    concatenate x0 -> x1, other arithmetic: none -> 1.14 us  [shards(): jnp.concatenate([jnp.where(core == 0, mine, theirs).astype(BF16), jnp.whe...]
    pallas_call x1 -> x2, Pallas kernels: 7.08 us -> 6.29 us  [the longest x1 5.04 us: shards(): call(slot_terms, (shape(2, count, cols), shape(2, count, cols), table), [...]
  transfers between devices with their start and end apart: 18 -> 19, of which waited for: 10 -> 9; matrix products, arithmetic and copies ran while one was open for 3% -> 3% of each run, Pallas kernels for 13% -> 14%
where the time goes in v5:
time: 72.6 us; the launch traced here: 71.9 us
  starting transfers between devices  32.1 us (44%)
  Pallas kernels  15.1 us (21%)
  waiting for transfers between devices  13 us (18%)
  local copies, waits for them, and re-layouts  7.36 us (10%)
  between operations  2.81 us (4%)
  other arithmetic  1.6 us (2%)
    ppermute x7, starting transfers between devices, to_neighbour(): return lax.ppermute(x, ('wide', 'narrow', 'probe'), pairs)  15.9 us
    ppermute x8, starting transfers between devices, swap(): return lax.ppermute(x, 'probe', [(0, 1), (1, 0)])  11.2 us
    ppermute x7, waiting for transfers between devices, to_neighbour(): return lax.ppermute(x, ('wide', 'narrow', 'probe'), pairs)  9.71 us
    pallas_call x1, Pallas kernels, shards(): call(slot_terms, (shape(2, count, cols), shape(2, count, cols), table), [...  5.04 us
    pallas_call x1, Pallas kernels, shards(): call(functools.partial(shift_tables, width), (table,) * 5 + (shape(size,...  3.54 us
    ppermute x8, waiting for transfers between devices, swap(): return lax.ppermute(x, 'probe', [(0, 1), (1, 0)])  3.27 us
    unnamed x14, local copies, waits for them, and re-layouts  3.14 us
    ppermute x3, starting transfers between devices, scatter_parts(): terms.append(lax.ppermute(part(to), axis, pairs))  2.78 us
  transfers between devices with their start and end apart: 19, of which 9 were waited for; matrix products, arithmetic and copies ran while one was open for 3% of the time, Pallas kernels for 14%

profile of v5, /device:TPU:19, one launch (start us, length us, event | category | flops | bytes accessed | tf_op | source)
XLA Modules:
  0.0 71.9 jit_solution(14989998408581458433)
XLA Ops:
  0.7 2.0 %constant_dynamic-slice_fusion.1 = bf16[2,256,512]{2,1,0:T(8,128)(2,1)} fusion(bf16[2,640,512]{2,1,0:T(8,128)(2,1)} %own.1, s32[]{:T(128)S(6)} %select_n.40), kind=kLoop, calls=%fused_computation.11 | loop fusion | bytes 1048580 | tf_op jit(solution)/shard_map/dynamic_slice | solution.py:348
  2.7 2.1 %collective-permute-start.1 = (bf16[2,256,512]{2,1,0:T(8,128)(2,1)}, bf16[2,256,512]{2,1,0:T(8,128)(2,1)S(1)}, u32[]{:S(2)}, u32[]{:S(2)}) collective-permute-start(bf16[2,256,512]{2,1,0:T(8,128)(2,1)} %constant_dynamic-slice_fusion.1), channel_id=1, source_target_pairs={{2,0},{5,1},{6,4},{7,3},{9,5},{10,8},{11,7},{13,9},{14,12},{15,11}... | collective-permute-start | bytes 1572872 | tf_op jit(solution)/shard_map/ppermute | solution.py:29
  4.8 2.1 %constant_dynamic-slice_fusion = bf16[2,384,512]{2,1,0:T(8,128)(2,1)} fusion(bf16[2,640,512]{2,1,0:T(8,128)(2,1)} %own.1, s32[]{:T(128)S(6)} %select_n.41), kind=kLoop, calls=%fused_computation.10 | loop fusion | bytes 1572868 | tf_op jit(solution)/shard_map/dynamic_slice | solution.py:349
  6.9 2.1 %collective-permute-start.3 = (bf16[2,384,512]{2,1,0:T(8,128)(2,1)}, bf16[2,384,512]{2,1,0:T(8,128)(2,1)S(1)}, u32[]{:S(2)}, u32[]{:S(2)}) collective-permute-start(bf16[2,384,512]{2,1,0:T(8,128)(2,1)} %constant_dynamic-slice_fusion), channel_id=1, source_target_pairs={{2,0},{5,1},{6,4},{7,3},{9,5},{10,8},{11,7},{13,9},{14,12},{15,11}... | collective-permute-start | bytes 2359304 | tf_op jit(solution)/shard_map/ppermute | solution.py:29
  11.5 1.3 %collective-permute-done.1.first = bf16[2,256,512]{2,1,0:T(8,128)(2,1)S(1)} collective-permute-done((bf16[2,256,512]{2,1,0:T(8,128)(2,1)}, bf16[2,256,512]{2,1,0:T(8,128)(2,1)S(1)}, u32[]{:S(2)}, u32[]{:S(2)}) %collective-permute-start.1) | collective-permute-done | bytes 524320 | tf_op jit(solution)/shard_map/ppermute | solution.py:29
  12.8 2.6 %collective-permute-start.5 = (bf16[2,256,512]{2,1,0:T(8,128)(2,1)S(1)}, bf16[2,256,512]{2,1,0:T(8,128)(2,1)S(1)}, u32[]{:S(2)}, u32[]{:S(2)}) collective-permute-start(bf16[2,256,512]{2,1,0:T(8,128)(2,1)S(1)} %collective-permute-done.1.first), channel_id=1, source_target_pairs={{3,1},{4,0},{6,2},{7,5},{8,4},{10,6},{11,9},{12,8},{14,10},{15,13}... | collective-permute-start | bytes 1572872 | tf_op jit(solution)/shard_map/ppermute | solution.py:29
  15.5 1.0 %copy-done.4 = bf16[512,512]{1,0:T(8,128)(2,1)S(1)} copy-done((bf16[512,512]{1,0:T(8,128)(2,1)S(1)}, bf16[512,512]{1,0:T(8,128)(2,1)}, u32[]{:S(2)}) %copy-start.4) | copy-done | bytes 524312
  16.5 1.0 %copy-done.5 = bf16[512,512]{1,0:T(8,128)(2,1)S(1)} copy-done((bf16[512,512]{1,0:T(8,128)(2,1)S(1)}, bf16[512,512]{1,0:T(8,128)(2,1)}, u32[]{:S(2)}) %copy-start.5) | copy-done | bytes 524312
  17.6 1.0 %copy-done.6 = bf16[512,512]{1,0:T(8,128)(2,1)S(1)} copy-done((bf16[512,512]{1,0:T(8,128)(2,1)S(1)}, bf16[512,512]{1,0:T(8,128)(2,1)}, u32[]{:S(2)}) %copy-start.6) | copy-done | bytes 524312
  18.6 3.5 %shift_tables.1 = (bf16[2,512,512]{2,1,0:T(8,128)(2,1)S(1)}, bf16[2,512,512]{2,1,0:T(8,128)(2,1)S(1)}, bf16[2,512,512]{2,1,0:T(8,128)(2,1)S(1)}, bf16[2,512,512]...) custom-call(s32[7]{0:T(128)S(1)} %concatenate.7.scalars, ...), custom_call_target="tpu_custom_call" | custom-call | flops 4000000000 | bytes 20000000 | tf_op jit(solution)/shard_map/shift_tables/pallas_call | solution.py:357
  22.1 2.9 %collective-permute-done.3.second = bf16[2,384,512]{2,1,0:T(8,128)(2,1)S(1)} collective-permute-done((bf16[2,384,512]{2,1,0:T(8,128)(2,1)}, bf16[2,384,512]{2,1,0:T(8,128)(2,1)S(1)}, u32[]{:S(2)}, u32[]{:S(2)}) %collective-permute-start.3) | collective-permute-done | bytes 786464 | tf_op jit(solution)/shard_map/ppermute | solution.py:29
  25.0 1.0 %collective-permute-start.4 = (bf16[2,384,512]{2,1,0:T(8,128)(2,1)S(1)}, bf16[2,384,512]{2,1,0:T(8,128)(2,1)S(1)}, u32[]{:S(2)}, u32[]{:S(2)}) collective-permute-start(bf16[2,384,512]{2,1,0:T(8,128)(2,1)S(1)} %collective-permute-done.3.second), channel_id=1, source_target_pairs={{0,1},{1,0},{2,3},{3,2},{4,5},{5,4},{6,7},{7,6},{8,9},{9,8},{10,11... | collective-permute-start | bytes 2359304 | tf_op jit(solution)/shard_map/ppermute | solution.py:33
  26.4 1.2 %collective-permute-start.6 = (bf16[2,256,512]{2,1,0:T(8,128)(2,1)S(1)}, bf16[2,256,512]{2,1,0:T(8,128)(2,1)S(1)}, u32[]{:S(2)}, u32[]{:S(2)}) collective-permute-start(bf16[2,256,512]{2,1,0:T(8,128)(2,1)S(1)} %collective-permute-done.5.third), channel_id=1, source_target_pairs={{0,1},{1,0},{2,3},{3,2},{4,5},{5,4},{6,7},{7,6},{8,9},{9,8},{10,11... | collective-permute-start | bytes 1572872 | tf_op jit(solution)/shard_map/ppermute | solution.py:33
  27.6 1.1 %collective-permute-done.2.first2 = bf16[2,256,512]{2,1,0:T(8,128)(2,1)S(1)} collective-permute-done((bf16[2,256,512]{2,1,0:T(8,128)(2,1)S(1)}, bf16[2,256,512]{2,1,0:T(8,128)(2,1)S(1)}, u32[]{:S(2)}, u32[]{:S(2)}) %collective-permute-start.2) | collective-permute-done | bytes 524320 | tf_op jit(solution)/shard_map/ppermute | solution.py:33
  28.7 0.7 %collective-permute-done.6.third2 = bf16[2,256,512]{2,1,0:T(8,128)(2,1)S(1)} collective-permute-done((bf16[2,256,512]{2,1,0:T(8,128)(2,1)S(1)}, bf16[2,256,512]{2,1,0:T(8,128)(2,1)S(1)}, u32[]{:S(2)}, u32[]{:S(2)}) %collective-permute-start.6) | collective-permute-done | bytes 524320 | tf_op jit(solution)/shard_map/ppermute | solution.py:33
  29.4 5.0 %slot_terms.1 = (bf16[2,384,512]{2,1,0:T(8,128)(2,1)S(1)}, bf16[2,384,512]{2,1,0:T(8,128)(2,1)S(1)}, bf16[2,512,512]{2,1,0:T(8,128)(2,1)S(1)}) custom-call(s32[7]{0:T(128)S(1)} %concatenate.7.scalars, bf16[2,640,512]{2,1,0:T(8,128)(2,1)S(1)} %copy-done, bf16[2,256,512]{2,1,0:T(8,128)(2,1)S(1)} %collective-permute-done.1.first, ...), custom_call_target="tpu_custom_call" | custom-call | flops 6000000000 | bytes 20000000 | tf_op jit(solution)/shard_map/slot_terms/pallas_call | solution.py:374
  34.9 1.3 %probe_parts.1 = (bf16[2,4,2,128,128]{4,3,2,1,0:T(8,128)(2,1)S(1)}, bf16[2,4,2,128,128]{4,3,2,1,0:T(8,128)(2,1)S(1)}) custom-call(bf16[2,512,512]{2,1,0:T(8,128)(2,1)S(1)} %get-tuple-element.62.term, bf16[512,512]{1,0:T(8,128)(2,1)S(1)} %get-tuple-element.63.back_rows, bf16[512,256]{1,0:T(8,128)(2,1)S(1)} %get-tuple-element.64.back_cols, ...), custom_call_target="tpu_custom_call" | custom-call | tf_op jit(solution)/shard_map/probe_parts/pallas_call | solution.py:386
  36.8 0.9 %diag_part.1.diag = bf16[2,256,512]{2,1,0:T(8,128)(2,1)S(1)} custom-call(s32[7]{0:T(128)S(1)} %concatenate.7.scalars, bf16[2,4,2,128,128]{4,3,2,1,0:T(8,128)(2,1)S(1)} %get-tuple-element.66.refs_0_, bf16[2,384,512]{2,1,0:T(8,128)(2,1)S(1)} %get-tuple-element.67.refs_1_.kept.refs_0_, bf16[2,384,512]{2,1,0:T(8,128)(2,1)S(1)} %collective-permute-done.7.refs_2_.got.refs_1_), custom_call_target="tpu_custom_call" | custom-call | tf_op jit(solution)/shard_map/diag_part/pallas_call | solution.py:392
  37.7 4.1 %collective-permute-start.12 = (bf16[2,256,512]{2,1,0:T(8,128)(2,1)S(1)}, bf16[2,256,512]{2,1,0:T(8,128)(2,1)S(1)}, u32[]{:S(2)}, u32[]{:S(2)}) collective-permute-start(bf16[2,256,512]{2,1,0:T(8,128)(2,1)S(1)} %diag_part.1.diag), channel_id=1, source_target_pairs={{0,2},{1,5},{3,7},{4,6},{5,9},{7,11},{8,10},{9,13},{11,15},{12,14}... | collective-permute-start | bytes 1572872 | tf_op jit(solution)/shard_map/ppermute | solution.py:29
  42.5 2.2 %collective-permute-start.9 = (bf16[4,2,128,128]{3,2,1,0:T(8,128)(2,1)S(1)}, bf16[4,2,128,128]{3,2,1,0:T(8,128)(2,1)S(1)}, u32[]{:S(2)}, u32[]{:S(2)}) collective-permute-start(bf16[4,2,128,128]{3,2,1,0:T(8,128)(2,1)S(1)} %get-tuple-element.71), channel_id=1, source_target_pairs={{0,2},{2,0},{1,3},{3,1},{4,6},{6,4},{5,7},{7,5},{8,10},{10,8},{9,1... | collective-permute-start | bytes 786440 | tf_op jit(solution)/shard_map/ppermute | solution.py:426
  44.6 1.0 %now_parts.1 = (bf16[2,256,512]{2,1,0:T(8,128)(2,1)S(1)}, bf16[2,128,512]{2,1,0:T(8,128)(2,1)S(1)}) custom-call(s32[7]{0:T(128)S(1)} %concatenate.7.scalars, bf16[4,2,128,128]{3,2,1,0:T(8,128)(2,1)S(1)} %get-tuple-element.70.refs_0_.before, bf16[2,384,512]{2,1,0:T(8,128)(2,1)S(1)} %get-tuple-element.67.refs_1_.kept.refs_0_, ...), custom_call_target="tpu_custom_call" | custom-call | tf_op jit(solution)/shard_map/now_parts/pallas_call | solution.py:415
  45.6 1.9 %collective-permute-start.10 = (bf16[2,256,512]{2,1,0:T(8,128)(2,1)S(1)}, bf16[2,256,512]{2,1,0:T(8,128)(2,1)S(1)}, u32[]{:S(2)}, u32[]{:S(2)}) collective-permute-start(bf16[2,256,512]{2,1,0:T(8,128)(2,1)S(1)} %get-tuple-element.72), channel_id=1, source_target_pairs={{0,2},{1,5},{3,7},{4,6},{5,9},{7,11},{8,10},{9,13},{11,15},{12,14}... | collective-permute-start | bytes 1572872 | tf_op jit(solution)/shard_map/ppermute | solution.py:29
  47.6 1.9 %collective-permute-start.11 = (bf16[2,128,512]{2,1,0:T(8,128)(2,1)S(1)}, bf16[2,128,512]{2,1,0:T(8,128)(2,1)S(1)}, u32[]{:S(2)}, u32[]{:S(2)}) collective-permute-start(bf16[2,128,512]{2,1,0:T(8,128)(2,1)S(1)} %get-tuple-element.73), channel_id=1, source_target_pairs={{1,5},{3,7},{5,9},{7,11},{9,13},{11,15},{17,21},{19,23},{21,25},{2... | collective-permute-start | bytes 786440 | tf_op jit(solution)/shard_map/ppermute | solution.py:29
  49.5 0.9 %later_part.1 = bf16[2,256,512]{2,1,0:T(8,128)(2,1)S(1)} custom-call(s32[7]{0:T(128)S(1)} %concatenate.7.scalars, bf16[2,384,512]{2,1,0:T(8,128)(2,1)S(1)} %get-tuple-element.67.refs_1_.kept.refs_0_, bf16[2,384,512]{2,1,0:T(8,128)(2,1)S(1)} %collective-permute-done.7.refs_2_.got.refs_1_, bf16[2,256,512]{2,1,0:T(8,128)(2,1)S(1)} %collective-permute-done.12.refs_2_), custom_call_target="tpu_custom_call" | custom-call | tf_op jit(solution)/shard_map/later_part/pallas_call | solution.py:392
  50.4 1.3 %collective-permute-start.13 = (bf16[2,256,512]{2,1,0:T(8,128)(2,1)S(1)}, bf16[2,256,512]{2,1,0:T(8,128)(2,1)S(1)}, u32[]{:S(2)}, u32[]{:S(2)}) collective-permute-start(bf16[2,256,512]{2,1,0:T(8,128)(2,1)S(1)} %later_part.1), channel_id=1, source_target_pairs={{0,4},{1,3},{2,6},{4,8},{5,7},{6,10},{8,12},{9,11},{10,14},{13,15}... | collective-permute-start | bytes 1572872 | tf_op jit(solution)/shard_map/ppermute | solution.py:29
  52.4 2.2 %collective-permute-start.17 = (bf16[2,128,128]{2,1,0:T(8,128)(2,1)S(1)}, bf16[2,128,128]{2,1,0:T(8,128)(2,1)S(1)}, u32[]{:S(2)}, u32[]{:S(2)}) collective-permute-start(bf16[2,128,128]{2,1,0:T(8,128)(2,1)S(1)} %get-tuple-element.77), channel_id=1, source_target_pairs={{0,8},{4,12},{8,0},{12,4},{1,9},{5,13},{9,1},{13,5},{2,10},{6,14},... | collective-permute-start | bytes 196616 | tf_op jit(solution)/shard_map/ppermute | solution.py:329
  54.6 5.2 %collective-permute-done.11.lower = bf16[2,128,512]{2,1,0:T(8,128)(2,1)S(1)} collective-permute-done((bf16[2,128,512]{2,1,0:T(8,128)(2,1)S(1)}, bf16[2,128,512]{2,1,0:T(8,128)(2,1)S(1)}, u32[]{:S(2)}, u32[]{:S(2)}) %collective-permute-start.11) | collective-permute-done | bytes 262176 | tf_op jit(solution)/shard_map/ppermute | solution.py:29
  59.8 1.1 %own_part.1 = bf16[2,384,512]{2,1,0:T(8,128)(2,1)S(1)} custom-call(s32[7]{0:T(128)S(1)} %concatenate.7.scalars, bf16[4,2,128,128]{3,2,1,0:T(8,128)(2,1)S(1)} %sum.1.before, bf16[2,384,512]{2,1,0:T(8,128)(2,1)S(1)} %get-tuple-element.67.refs_1_.kept.refs_0_, bf16[2,384,512]{2,1,0:T(8,128)(2,1)S(1)} %collective-permute-done.7.refs_2_.got.refs_1_, ...), custom_call_target="tpu_custom_call" | custom-call | flops 1000000000 | tf_op jit(solution)/shard_map/own_part/pallas_call | solution.py:440
  60.8 5.6 %collective-permute-start.14 = (bf16[2,384,512]{2,1,0:T(8,128)(2,1)S(1)}, bf16[2,384,512]{2,1,0:T(8,128)(2,1)S(1)}, u32[]{:S(2)}, u32[]{:S(2)}) collective-permute-start(bf16[2,384,512]{2,1,0:T(8,128)(2,1)S(1)} %own_part.1), channel_id=1, source_target_pairs={{0,1},{1,0},{2,3},{3,2},{4,5},{5,4},{6,7},{7,6},{8,9},{9,8},{10,11... | collective-permute-start | bytes 2359304 | tf_op jit(solution)/shard_map/ppermute | solution.py:33
  66.4 2.5 %collective-permute-start.15 = (bf16[2,256,512]{2,1,0:T(8,128)(2,1)S(1)}, bf16[2,256,512]{2,1,0:T(8,128)(2,1)S(1)}, u32[]{:S(2)}, u32[]{:S(2)}) collective-permute-start(bf16[2,256,512]{2,1,0:T(8,128)(2,1)S(1)} %collective-permute-done.13), channel_id=1, source_target_pairs={{0,1},{1,0},{2,3},{3,2},{4,5},{5,4},{6,7},{7,6},{8,9},{9,8},{10,11... | collective-permute-start | bytes 1572872 | tf_op jit(solution)/shard_map/ppermute | solution.py:33
  69.6 0.8 %collective-permute-done.15 = bf16[2,256,512]{2,1,0:T(8,128)(2,1)S(1)} collective-permute-done((bf16[2,256,512]{2,1,0:T(8,128)(2,1)S(1)}, bf16[2,256,512]{2,1,0:T(8,128)(2,1)S(1)}, u32[]{:S(2)}, u32[]{:S(2)}) %collective-permute-start.15) | collective-permute-done | bytes 524320 | tf_op jit(solution)/shard_map/ppermute | solution.py:33
  70.8 1.1 %pad_maximum_fusion = bf16[2,640,512]{2,1,0:T(8,128)(2,1)} fusion(bf16[2,128,512]{2,1,0:T(8,128)(2,1)S(1)} %slice_select_fusion, bf16[2,256,512]{2,1,0:T(8,128)(2,1)S(1)} %get-tuple-element.75, bf16[2,256,512]{2,1,0:T(8,128)(2,1)S(1)} %get-tuple-element.74), kind=kLoop, calls=%fused_computation | loop fusion | flops 3932160 | bytes 2621440 | tf_op jit(solution)/shard_map/concatenate | solution.py:451
  (38 shorter events, 4.7 us)
Async XLA Ops:
  0.6 14.8 %copy-start.1 = (bf16[2,512,512]{2,1,0:T(8,128)(2,1)S(1)}, bf16[2,512,512]{2,1,0:T(8,128)(2,1)}, u32[]{:S(2)}) copy-start(bf16[2,512,512]{2,1,0:T(8,128)(2,1)} %probe_in) | copy-start | bytes 3145732
  0.6 14.8 %copy-start.2 = (bf16[1,1,1,512,512]{4,3,2,1,0:T(8,128)(2,1)S(1)}, bf16[1,1,1,512,512]{4,3,2,1,0:T(8,128)(2,1)}, u32[]{:S(2)}) copy-start(bf16[1,1,1,512,512]{4,3,2,1,0:T(8,128)(2,1)} %param.12) | copy-start | bytes 1572868
  0.7 14.8 %copy-start.3 = (bf16[512,512]{1,0:T(8,128)(2,1)S(1)}, bf16[512,512]{1,0:T(8,128)(2,1)}, u32[]{:S(2)}) copy-start(bf16[512,512]{1,0:T(8,128)(2,1)} %constant.42.clone.cos_in) | copy-start | bytes 1572868
  2.7 10.1 %collective-permute-start.1 = (bf16[2,256,512]{2,1,0:T(8,128)(2,1)}, bf16[2,256,512]{2,1,0:T(8,128)(2,1)S(1)}, u32[]{:S(2)}, u32[]{:S(2)}) collective-permute-start(bf16[2,256,512]{2,1,0:T(8,128)(2,1)} %constant_dynamic-slice_fusion.1), channel_id=1, source_target_pairs={{2,0},{5,1},{6,4},{7,3},{9,5},{10,8},{11,7},{13,9},{14,12},{15,11}... | collective-permute-start | bytes 1572872 | tf_op jit(solution)/shard_map/ppermute | solution.py:29
  6.9 18.2 %collective-permute-start.3 = (bf16[2,384,512]{2,1,0:T(8,128)(2,1)}, bf16[2,384,512]{2,1,0:T(8,128)(2,1)S(1)}, u32[]{:S(2)}, u32[]{:S(2)}) collective-permute-start(bf16[2,384,512]{2,1,0:T(8,128)(2,1)} %constant_dynamic-slice_fusion), channel_id=1, source_target_pairs={{2,0},{5,1},{6,4},{7,3},{9,5},{10,8},{11,7},{13,9},{14,12},{15,11}... | collective-permute-start | bytes 2359304 | tf_op jit(solution)/shard_map/ppermute | solution.py:29
  10.3 1.2 %collective-permute-start = (s32[2]{0:T(128)S(1)}, s32[2]{0:T(128)S(1)}, u32[]{:S(2)}, u32[]{:S(2)}) collective-permute-start(s32[2]{0:T(128)S(1)} %pad_add_fusion), channel_id=1, source_target_pairs={{0,1},{1,0},{2,3},{3,2},{4,5},{5,4},{6,7},{7,6},{8,9},{9,8},{10,11... | collective-permute-start | bytes 32 | tf_op jit(solution)/shard_map/ppermute | solution.py:33
  12.8 16.6 %copy-start = (bf16[2,640,512]{2,1,0:T(8,128)(2,1)S(1)}, bf16[2,640,512]{2,1,0:T(8,128)(2,1)}, u32[]{:S(2)}) copy-start(bf16[2,640,512]{2,1,0:T(8,128)(2,1)} %own.1) | copy-start | bytes 3932164
  12.8 13.5 %collective-permute-start.5 = (bf16[2,256,512]{2,1,0:T(8,128)(2,1)S(1)}, bf16[2,256,512]{2,1,0:T(8,128)(2,1)S(1)}, u32[]{:S(2)}, u32[]{:S(2)}) collective-permute-start(bf16[2,256,512]{2,1,0:T(8,128)(2,1)S(1)} %collective-permute-done.1.first), channel_id=1, source_target_pairs={{3,1},{4,0},{6,2},{7,5},{8,4},{10,6},{11,9},{12,8},{14,10},{15,13}... | collective-permute-start | bytes 1572872 | tf_op jit(solution)/shard_map/ppermute | solution.py:29
  15.5 1.0 %copy-start.4 = (bf16[512,512]{1,0:T(8,128)(2,1)S(1)}, bf16[512,512]{1,0:T(8,128)(2,1)}, u32[]{:S(2)}) copy-start(bf16[512,512]{1,0:T(8,128)(2,1)} %constant.43.clone.sin_in) | copy-start | bytes 1572868
  16.5 1.0 %copy-start.5 = (bf16[512,512]{1,0:T(8,128)(2,1)S(1)}, bf16[512,512]{1,0:T(8,128)(2,1)}, u32[]{:S(2)}) copy-start(bf16[512,512]{1,0:T(8,128)(2,1)} %constant.44.clone.cos_t) | copy-start | bytes 1572868
  17.6 1.0 %copy-start.6 = (bf16[512,512]{1,0:T(8,128)(2,1)S(1)}, bf16[512,512]{1,0:T(8,128)(2,1)}, u32[]{:S(2)}) copy-start(bf16[512,512]{1,0:T(8,128)(2,1)} %constant.45.clone.sin_t) | copy-start | bytes 1572868
  25.0 4.4 %collective-permute-start.4 = (bf16[2,384,512]{2,1,0:T(8,128)(2,1)S(1)}, bf16[2,384,512]{2,1,0:T(8,128)(2,1)S(1)}, u32[]{:S(2)}, u32[]{:S(2)}) collective-permute-start(bf16[2,384,512]{2,1,0:T(8,128)(2,1)S(1)} %collective-permute-done.3.second), channel_id=1, source_target_pairs={{0,1},{1,0},{2,3},{3,2},{4,5},{5,4},{6,7},{7,6},{8,9},{9,8},{10,11... | collective-permute-start | bytes 2359304 | tf_op jit(solution)/shard_map/ppermute | solution.py:33
  26.0 2.7 %collective-permute-start.2 = (bf16[2,256,512]{2,1,0:T(8,128)(2,1)S(1)}, bf16[2,256,512]{2,1,0:T(8,128)(2,1)S(1)}, u32[]{:S(2)}, u32[]{:S(2)}) collective-permute-start(bf16[2,256,512]{2,1,0:T(8,128)(2,1)S(1)} %collective-permute-done.1.first), channel_id=1, source_target_pairs={{0,1},{1,0},{2,3},{3,2},{4,5},{5,4},{6,7},{7,6},{8,9},{9,8},{10,11... | collective-permute-start | bytes 1572872 | tf_op jit(solution)/shard_map/ppermute | solution.py:33
  26.4 3.1 %collective-permute-start.6 = (bf16[2,256,512]{2,1,0:T(8,128)(2,1)S(1)}, bf16[2,256,512]{2,1,0:T(8,128)(2,1)S(1)}, u32[]{:S(2)}, u32[]{:S(2)}) collective-permute-start(bf16[2,256,512]{2,1,0:T(8,128)(2,1)S(1)} %collective-permute-done.5.third), channel_id=1, source_target_pairs={{0,1},{1,0},{2,3},{3,2},{4,5},{5,4},{6,7},{7,6},{8,9},{9,8},{10,11... | collective-permute-start | bytes 1572872 | tf_op jit(solution)/shard_map/ppermute | solution.py:33
  34.5 2.4 %collective-permute-start.7 = (bf16[2,384,512]{2,1,0:T(8,128)(2,1)S(1)}, bf16[2,384,512]{2,1,0:T(8,128)(2,1)S(1)}, u32[]{:S(2)}, u32[]{:S(2)}) collective-permute-start(bf16[2,384,512]{2,1,0:T(8,128)(2,1)S(1)} %get-tuple-element.68), channel_id=1, source_target_pairs={{0,1},{1,0},{2,3},{3,2},{4,5},{5,4},{6,7},{7,6},{8,9},{9,8},{10,11... | collective-permute-start | bytes 2359304 | tf_op jit(solution)/shard_map/ppermute | solution.py:33
  36.2 5.6 %collective-permute-start.8 = (bf16[2,4,2,128,128]{4,3,2,1,0:T(8,128)(2,1)S(1)}, bf16[2,4,2,128,128]{4,3,2,1,0:T(8,128)(2,1)S(1)}, u32[]{:S(2)}, u32[]{:S(2)}) collective-permute-start(bf16[2,4,2,128,128]{4,3,2,1,0:T(8,128)(2,1)S(1)} %get-tuple-element.66.refs_0_), channel_id=1, source_target_pairs={{0,1},{1,0},{2,3},{3,2},{4,5},{5,4},{6,7},{7,6},{8,9},{9,8},{10,11... | collective-permute-start | bytes 1572872 | tf_op jit(solution)/shard_map/ppermute | solution.py:33
  37.7 11.8 %collective-permute-start.12 = (bf16[2,256,512]{2,1,0:T(8,128)(2,1)S(1)}, bf16[2,256,512]{2,1,0:T(8,128)(2,1)S(1)}, u32[]{:S(2)}, u32[]{:S(2)}) collective-permute-start(bf16[2,256,512]{2,1,0:T(8,128)(2,1)S(1)} %diag_part.1.diag), channel_id=1, source_target_pairs={{0,2},{1,5},{3,7},{4,6},{5,9},{7,11},{8,10},{9,13},{11,15},{12,14}... | collective-permute-start | bytes 1572872 | tf_op jit(solution)/shard_map/ppermute | solution.py:29
  42.5 9.2 %collective-permute-start.9 = (bf16[4,2,128,128]{3,2,1,0:T(8,128)(2,1)S(1)}, bf16[4,2,128,128]{3,2,1,0:T(8,128)(2,1)S(1)}, u32[]{:S(2)}, u32[]{:S(2)}) collective-permute-start(bf16[4,2,128,128]{3,2,1,0:T(8,128)(2,1)S(1)} %get-tuple-element.71), channel_id=1, source_target_pairs={{0,2},{2,0},{1,3},{3,1},{4,6},{6,4},{5,7},{7,5},{8,10},{10,8},{9,1... | collective-permute-start | bytes 786440 | tf_op jit(solution)/shard_map/ppermute | solution.py:426
  45.6 14.1 %collective-permute-start.10 = (bf16[2,256,512]{2,1,0:T(8,128)(2,1)S(1)}, bf16[2,256,512]{2,1,0:T(8,128)(2,1)S(1)}, u32[]{:S(2)}, u32[]{:S(2)}) collective-permute-start(bf16[2,256,512]{2,1,0:T(8,128)(2,1)S(1)} %get-tuple-element.72), channel_id=1, source_target_pairs={{0,2},{1,5},{3,7},{4,6},{5,9},{7,11},{8,10},{9,13},{11,15},{12,14}... | collective-permute-start | bytes 1572872 | tf_op jit(solution)/shard_map/ppermute | solution.py:29
  47.6 12.2 %collective-permute-start.11 = (bf16[2,128,512]{2,1,0:T(8,128)(2,1)S(1)}, bf16[2,128,512]{2,1,0:T(8,128)(2,1)S(1)}, u32[]{:S(2)}, u32[]{:S(2)}) collective-permute-start(bf16[2,128,512]{2,1,0:T(8,128)(2,1)S(1)} %get-tuple-element.73), channel_id=1, source_target_pairs={{1,5},{3,7},{5,9},{7,11},{9,13},{11,15},{17,21},{19,23},{21,25},{2... | collective-permute-start | bytes 786440 | tf_op jit(solution)/shard_map/ppermute | solution.py:29
  50.4 16.1 %collective-permute-start.13 = (bf16[2,256,512]{2,1,0:T(8,128)(2,1)S(1)}, bf16[2,256,512]{2,1,0:T(8,128)(2,1)S(1)}, u32[]{:S(2)}, u32[]{:S(2)}) collective-permute-start(bf16[2,256,512]{2,1,0:T(8,128)(2,1)S(1)} %later_part.1), channel_id=1, source_target_pairs={{0,4},{1,3},{2,6},{4,8},{5,7},{6,10},{8,12},{9,11},{10,14},{13,15}... | collective-permute-start | bytes 1572872 | tf_op jit(solution)/shard_map/ppermute | solution.py:29
  51.8 17.1 %collective-permute-start.16 = (bf16[2,128,128]{2,1,0:T(8,128)(2,1)S(1)}, bf16[2,128,128]{2,1,0:T(8,128)(2,1)S(1)}, u32[]{:S(2)}, u32[]{:S(2)}) collective-permute-start(bf16[2,128,128]{2,1,0:T(8,128)(2,1)S(1)} %get-tuple-element.78), channel_id=1, source_target_pairs={{0,4},{4,0},{8,12},{12,8},{1,5},{5,1},{9,13},{13,9},{2,6},{6,2},{1... | collective-permute-start | bytes 196616 | tf_op jit(solution)/shard_map/ppermute | solution.py:329
  52.4 16.5 %collective-permute-start.17 = (bf16[2,128,128]{2,1,0:T(8,128)(2,1)S(1)}, bf16[2,128,128]{2,1,0:T(8,128)(2,1)S(1)}, u32[]{:S(2)}, u32[]{:S(2)}) collective-permute-start(bf16[2,128,128]{2,1,0:T(8,128)(2,1)S(1)} %get-tuple-element.77), channel_id=1, source_target_pairs={{0,8},{4,12},{8,0},{12,4},{1,9},{5,13},{9,1},{13,5},{2,10},{6,14},... | collective-permute-start | bytes 196616 | tf_op jit(solution)/shard_map/ppermute | solution.py:329
  59.8 9.1 %collective-permute-start.18 = (bf16[2,128,128]{2,1,0:T(8,128)(2,1)S(1)}, bf16[2,128,128]{2,1,0:T(8,128)(2,1)S(1)}, u32[]{:S(2)}, u32[]{:S(2)}) collective-permute-start(bf16[2,128,128]{2,1,0:T(8,128)(2,1)S(1)} %get-tuple-element.76), channel_id=1, source_target_pairs={{0,12},{4,8},{8,4},{12,0},{1,13},{5,9},{9,5},{13,1},{2,14},{6,10},... | collective-permute-start | bytes 196616 | tf_op jit(solution)/shard_map/ppermute | solution.py:329
  60.8 8.8 %collective-permute-start.14 = (bf16[2,384,512]{2,1,0:T(8,128)(2,1)S(1)}, bf16[2,384,512]{2,1,0:T(8,128)(2,1)S(1)}, u32[]{:S(2)}, u32[]{:S(2)}) collective-permute-start(bf16[2,384,512]{2,1,0:T(8,128)(2,1)S(1)} %own_part.1), channel_id=1, source_target_pairs={{0,1},{1,0},{2,3},{3,2},{4,5},{5,4},{6,7},{7,6},{8,9},{9,8},{10,11... | collective-permute-start | bytes 2359304 | tf_op jit(solution)/shard_map/ppermute | solution.py:33
  66.4 4.0 %collective-permute-start.15 = (bf16[2,256,512]{2,1,0:T(8,128)(2,1)S(1)}, bf16[2,256,512]{2,1,0:T(8,128)(2,1)S(1)}, u32[]{:S(2)}, u32[]{:S(2)}) collective-permute-start(bf16[2,256,512]{2,1,0:T(8,128)(2,1)S(1)} %collective-permute-done.13), channel_id=1, source_target_pairs={{0,1},{1,0},{2,3},{3,2},{4,5},{5,4},{6,7},{7,6},{8,9},{9,8},{10,11... | collective-permute-start | bytes 1572872 | tf_op jit(solution)/shard_map/ppermute | solution.py:33

commit v6 on v5

--- a/solution.py
+++ b/solution.py
@@ -21,8 +21,9 @@
     pairs = []
     for w in range(wide):
         for n in range(narrow):
-            for core in senders:
-                w_to, n_to = (w, n + by) if core == along_narrow else (w + by, n)
+            for role in senders:
+                core = 1 - role
+                w_to, n_to = (w, n + by) if role == along_narrow else (w + by, n)
                 if 0 <= w_to < wide and 0 <= n_to < narrow:
                     source = (w * narrow + n) * cores + core
                     pairs.append((source, (w_to * narrow + n_to) * cores + core))
@@ -42,7 +43,7 @@
     angle = product.astype(np.float32) * np.float32(2.0 * math.pi / size)
     norm = np.float32(1.0 / math.sqrt(size))
     pair = (np.cos(angle) * norm, -np.sin(angle) * norm)
-    return [jnp.asarray(x, BF16) for x in pair + tuple(x.T for x in pair)]
+    return jnp.asarray(np.stack(pair + tuple(x.T for x in pair)), BF16)
 
 
 def dot(a, b):
@@ -78,18 +79,19 @@
 
 
 def shift_tables(
-    width, scalars, cos_in, sin_in, cos_t, sin_t, probe_in, amp_in,
-    right, right_t, left_t, left, probe, amplitude, back_rows, back_cols, back_cols2,
+    width, scalars, dft, probe_in, amp_in, first_in, before,
+    right, right_t, left_t, left, probe, amplitude, back_rows, back_cols, back_cols2, first,
 ):
-    size = cos_in.shape[0]
+    size = dft.shape[1]
     part = size // 2
+    first[...] = first_in[...]
     row_start, col_start, core = scalars[0], scalars[1], scalars[2]
     row_start = jnp.where(row_start >= size, row_start - size, row_start)
     full = (size, size)
 
     back_rows[...] = one_hot(cyclic(iota(full, 1), row_start, size) == iota(full, 0))
     count = back_cols.shape[1]
-    for out, owner in ((back_cols, core), (back_cols2, 1 - core)):
+    for out, owner in ((back_cols, 1 - core), (back_cols2, core)):
         at = iota((size, count), 1)
         column = at + (at // width + owner) * width
         out[...] = one_hot(cyclic(iota((size, count), 0), col_start, size) == column)
@@ -97,8 +99,8 @@
     for start, table, table_t in ((col_start, right, right_t), (row_start, left_t, left)):
         hot = one_hot(cyclic(iota((part, size), 0), start, size) == iota((part, size), 1))
         hot_t = one_hot(cyclic(iota((size, part), 1), start, size) == iota((size, part), 0))
-        cos_part, sin_part = dot(hot, cos_in[...]), dot(hot, sin_in[...])
-        cos_turn, sin_turn = dot(cos_t[...], hot_t), dot(sin_t[...], hot_t)
+        cos_part, sin_part = dot(hot, dft[0]), dot(hot, dft[1])
+        cos_turn, sin_turn = dot(dft[2], hot_t), dot(dft[3], hot_t)
         for odd in range(2):
             at = slice(odd * part, (odd + 1) * part)
             table[odd, :part, :part] = cos_part[:, at].astype(BF16)
@@ -121,6 +123,13 @@
 
     moved = dot(one_hot(frequency(iota(full, 0)) == iota(full, 1)), amp_in[...]).astype(BF16)
     amplitude[...] = dot(moved, one_hot(frequency(iota(full, 1)) == iota(full, 0))).astype(BF16)
+
+
+def first_rows(slab, out, second):
+    core = 1 - lax.axis_index("probe")
+    count = out.shape[1]
+    out[...] = slab[:, pl.ds(pl.multiple_of(count * (1 - core), 128), count)]
+    second[...] = slab[:, pl.ds(pl.multiple_of(count * core, 128), second.shape[1])]
 
 
 def slot_terms(
@@ -333,7 +342,7 @@
 def shards(object_slab, probe_wave, amplitude, row_offset, col_offset, occupied):
     size = probe_wave.shape[1]
     rows, cols = object_slab.shape[1:]
-    core = lax.axis_index("probe")
+    core = 1 - lax.axis_index("probe")
     narrow, wide, cores = (lax.axis_size(name) for name in ("narrow", "wide", "probe"))
     corner = jnp.stack([row_offset[0, 0, 0], col_offset[0, 0, 0]])
     here = [core, occupied[0, 0, 0], lax.axis_index("narrow")]
@@ -345,30 +354,34 @@
 
     cut = size // 2
     count = rows - cut
-    first = to_neighbour(lax.dynamic_slice_in_dim(object_slab, cut * (1 - core), cut, 1), -1, 0)
-    second = to_neighbour(lax.dynamic_slice_in_dim(object_slab, cut * core, count, 1), -1, 0)
+    start, more = call(
+        first_rows, (shape(2, cut, cols), shape(2, count, cols)), [VMEM], 8, name="first_rows"
+    )(object_slab)
+    first = to_neighbour(start, -1, 0)
+    second = to_neighbour(more, -1, 0)
     third = to_neighbour(first, -1, 1)
-    late_scalars, first_late, late_probe, late_amplitude, *late_tables = lax.optimization_barrier(
-        (scalars, first, probe_wave, amplitude[0, 0, 0], *dft_tables(size))
+    late_scalars, first_late, late_probe, late_amplitude, late_tables = lax.optimization_barrier(
+        (scalars, first, probe_wave, amplitude[0, 0, 0], dft_tables(size))
     )
 
+    first2 = swap(first_late)
     width = size // (narrow * cores)
     table = shape(2, size, size)
-    tables = call(
+    *tables, first_kept = call(
         functools.partial(shift_tables, width),
         (
             (table,) * 5
             + (shape(size, size), shape(size, size))
             + (shape(cols, narrow * width),) * 2
+            + (shape(2, cut, cols),)
         ),
-        [SMEM] + [VMEM] * 6,
-        8,
-        flops=4 * 10**9,
-        bytes_accessed=2 * 10**7,
+        [SMEM] + [VMEM] * 4 + [ANY],
+        8,
+        flops=0 * 10**9,
         name="shift_tables",
-    )(late_scalars, *late_tables, late_probe, late_amplitude)
+    )(late_scalars, late_tables, late_probe, late_amplitude, first_late, first2)
     second, tables = lax.optimization_barrier((second, tables))
-    pieces = (first, swap(first_late), second, swap(second), third, swap(third))
+    pieces = (first_kept, first2, second, swap(second), third, swap(third))
     blocks = shape(narrow, wide, 2, size // wide, width)
     *tables, back_rows, back_cols, back_cols2 = tables
     sent, kept, term = call(

time: 72.6 us -> 70.4 us (0.970)
  starting transfers between devices: 32.1 us -> 24.1 us
  waiting for transfers between devices: 13 us -> 20.8 us
  local copies, waits for them, and re-layouts: 7.36 us -> 5.28 us
    ppermute x7, waiting for transfers between devices: 9.71 us -> 15.6 us  [to_neighbour(): return lax.ppermute(x, ('wide', 'narrow', 'probe'), pairs)]
    ppermute x7, starting transfers between devices: 15.9 us -> 10.8 us  [to_neighbour(): return lax.ppermute(x, ('wide', 'narrow', 'probe'), pairs)]
    dynamic_slice x2 -> x0, local copies, waits for them, and re-layouts: 4.11 us -> none  [the longest x1 2.07 us: shards(): lax.dynamic_slice_in_dim(object_slab, cut * core, count, 1)]
    ppermute x8, starting transfers between devices: 11.2 us -> 8.44 us  [swap(): return lax.ppermute(x, 'probe', [(0, 1), (1, 0)])]
    ppermute x3, waiting for transfers between devices: 0.01 us -> 2.71 us  [scatter_parts(): terms.append(lax.ppermute(part(to), axis, pairs))]
    unnamed x14 -> x10, local copies, waits for them, and re-layouts: 3.14 us -> 5.17 us
    ppermute x8, waiting for transfers between devices: 3.27 us -> 2.54 us  [swap(): return lax.ppermute(x, 'probe', [(0, 1), (1, 0)])]
  transfers between devices with their start and end apart: 19 -> 19, of which waited for: 9 -> 10; matrix products, arithmetic and copies ran while one was open for 3% -> 0% of each run, Pallas kernels for 14% -> 14%
where the time goes in v6:
time: 70.4 us; the launch traced here: 70 us
  starting transfers between devices  24.1 us (34%)
  waiting for transfers between devices  20.8 us (30%)
  Pallas kernels  15.4 us (22%)
  local copies, waits for them, and re-layouts  5.28 us (7%)
  between operations  2.79 us (4%)
  other arithmetic  1.6 us (2%)
    ppermute x7, waiting for transfers between devices, to_neighbour(): return lax.ppermute(x, ('wide', 'narrow', 'probe'), pairs)  15.6 us
    ppermute x7, starting transfers between devices, to_neighbour(): return lax.ppermute(x, ('wide', 'narrow', 'probe'), pairs)  10.8 us
    ppermute x8, starting transfers between devices, swap(): return lax.ppermute(x, 'probe', [(0, 1), (1, 0)])  8.44 us
    pallas_call x1, Pallas kernels, shards(): call(slot_terms, (shape(2, count, cols), shape(2, count, cols), table), [...  5.28 us
    unnamed x10, local copies, waits for them, and re-layouts  5.17 us
    pallas_call x1, Pallas kernels, shards(): call(functools.partial(shift_tables, width), (table,) * 5 + (shape(size,...  3.55 us
    ppermute x3, waiting for transfers between devices, scatter_parts(): terms.append(lax.ppermute(part(to), axis, pairs))  2.71 us
    ppermute x3, starting transfers between devices, scatter_parts(): terms.append(lax.ppermute(part(to), axis, pairs))  2.71 us
  transfers between devices with their start and end apart: 19, of which 10 were waited for; matrix products, arithmetic and copies ran while one was open for 0% of the time, Pallas kernels for 14%

profile of v6, /device:TPU:19, one launch (start us, length us, event | category | flops | bytes accessed | tf_op | source)
XLA Modules:
  0.0 70.0 jit_solution(15603422031729086842)
XLA Ops:
  0.6 1.3 %copy-done.1 = bf16[2,640,512]{2,1,0:T(8,128)(2,1)S(1)} copy-done((bf16[2,640,512]{2,1,0:T(8,128)(2,1)S(1)}, bf16[2,640,512]{2,1,0:T(8,128)(2,1)}, u32[]{:S(2)}) %copy-start.1) | copy-done | bytes 1310744
  2.0 2.2 %collective-permute-start.1 = (bf16[2,256,512]{2,1,0:T(8,128)(2,1)S(1)}, bf16[2,256,512]{2,1,0:T(8,128)(2,1)S(1)}, u32[]{:S(2)}, u32[]{:S(2)}) collective-permute-start(bf16[2,256,512]{2,1,0:T(8,128)(2,1)S(1)} %get-tuple-element.38), channel_id=1, source_target_pairs={{3,1},{4,0},{7,5},{6,2},{8,4},{11,9},{10,6},{12,8},{15,13},{14,10}... | collective-permute-start | bytes 1572872 | tf_op jit(solution)/shard_map/ppermute | solution.py:30
  4.2 1.3 %collective-permute-start.3 = (bf16[2,384,512]{2,1,0:T(8,128)(2,1)S(1)}, bf16[2,384,512]{2,1,0:T(8,128)(2,1)S(1)}, u32[]{:S(2)}, u32[]{:S(2)}) collective-permute-start(bf16[2,384,512]{2,1,0:T(8,128)(2,1)S(1)} %get-tuple-element.45), channel_id=1, source_target_pairs={{3,1},{4,0},{7,5},{6,2},{8,4},{11,9},{10,6},{12,8},{15,13},{14,10}... | collective-permute-start | bytes 2359304 | tf_op jit(solution)/shard_map/ppermute | solution.py:30
  7.0 1.9 %collective-permute-start = (s32[2]{0:T(128)S(1)}, s32[2]{0:T(128)S(1)}, u32[]{:S(2)}, u32[]{:S(2)}) collective-permute-start(s32[2]{0:T(128)S(1)} %pad_add_fusion), channel_id=1, source_target_pairs={{0,1},{1,0},{2,3},{3,2},{4,5},{5,4},{6,7},{7,6},{8,9},{9,8},{10,11... | collective-permute-start | bytes 32 | tf_op jit(solution)/shard_map/ppermute | solution.py:34
  10.3 3.5 %collective-permute-start.2 = (bf16[2,256,512]{2,1,0:T(8,128)(2,1)S(1)}, bf16[2,256,512]{2,1,0:T(8,128)(2,1)S(1)}, u32[]{:S(2)}, u32[]{:S(2)}) collective-permute-start(bf16[2,256,512]{2,1,0:T(8,128)(2,1)S(1)} %collective-permute-done.1.first_in), channel_id=1, source_target_pairs={{0,1},{1,0},{2,3},{3,2},{4,5},{5,4},{6,7},{7,6},{8,9},{9,8},{10,11... | collective-permute-start | bytes 1572872 | tf_op jit(solution)/shard_map/ppermute | solution.py:34
  13.8 2.1 %collective-permute-start.5 = (bf16[2,256,512]{2,1,0:T(8,128)(2,1)S(1)}, bf16[2,256,512]{2,1,0:T(8,128)(2,1)S(1)}, u32[]{:S(2)}, u32[]{:S(2)}) collective-permute-start(bf16[2,256,512]{2,1,0:T(8,128)(2,1)S(1)} %collective-permute-done.1.first_in), channel_id=1, source_target_pairs={{2,0},{5,1},{7,3},{6,4},{9,5},{11,7},{10,8},{13,9},{15,11},{14,12}... | collective-permute-start | bytes 1572872 | tf_op jit(solution)/shard_map/ppermute | solution.py:30
  15.9 1.6 %copy-done = bf16[4,512,512]{2,1,0:T(8,128)(2,1)S(1)} copy-done((bf16[4,512,512]{2,1,0:T(8,128)(2,1)S(1)}, bf16[4,512,512]{2,1,0:T(8,128)(2,1)}, u32[]{:S(2)}) %copy-start) | copy-done | bytes 2097176
  17.5 1.2 %copy-done.3 = bf16[2,512,512]{2,1,0:T(8,128)(2,1)S(1)} copy-done((bf16[2,512,512]{2,1,0:T(8,128)(2,1)S(1)}, bf16[2,512,512]{2,1,0:T(8,128)(2,1)}, u32[]{:S(2)}) %copy-start.3) | copy-done | bytes 1048600
  18.7 1.0 %copy-done.4 = bf16[1,1,1,512,512]{4,3,2,1,0:T(8,128)(2,1)S(1)} copy-done((bf16[1,1,1,512,512]{4,3,2,1,0:T(8,128)(2,1)S(1)}, bf16[1,1,1,512,512]{4,3,2,1,0:T(8,128)(2,1)}, u32[]{:S(2)}) %copy-start.4) | copy-done | bytes 524312
  19.7 3.5 %shift_tables.1 = (bf16[2,512,512]{2,1,0:T(8,128)(2,1)S(1)}, bf16[2,512,512]{2,1,0:T(8,128)(2,1)S(1)}, bf16[2,512,512]{2,1,0:T(8,128)(2,1)S(1)}, bf16[2,512,512]...) custom-call(s32[7]{0:T(128)S(1)} %concatenate.7.scalars, ...), custom_call_target="tpu_custom_call" | custom-call | tf_op jit(solution)/shard_map/shift_tables/pallas_call | solution.py:370
  23.3 2.3 %collective-permute-start.4 = (bf16[2,384,512]{2,1,0:T(8,128)(2,1)S(1)}, bf16[2,384,512]{2,1,0:T(8,128)(2,1)S(1)}, u32[]{:S(2)}, u32[]{:S(2)}) collective-permute-start(bf16[2,384,512]{2,1,0:T(8,128)(2,1)S(1)} %collective-permute-done.3.second), channel_id=1, source_target_pairs={{0,1},{1,0},{2,3},{3,2},{4,5},{5,4},{6,7},{7,6},{8,9},{9,8},{10,11... | collective-permute-start | bytes 2359304 | tf_op jit(solution)/shard_map/ppermute | solution.py:34
  25.6 1.6 %collective-permute-done.5.third = bf16[2,256,512]{2,1,0:T(8,128)(2,1)S(1)} collective-permute-done((bf16[2,256,512]{2,1,0:T(8,128)(2,1)S(1)}, bf16[2,256,512]{2,1,0:T(8,128)(2,1)S(1)}, u32[]{:S(2)}, u32[]{:S(2)}) %collective-permute-start.5) | collective-permute-done | bytes 524320 | tf_op jit(solution)/shard_map/ppermute | solution.py:30
  27.1 1.9 %collective-permute-done.6.third2 = bf16[2,256,512]{2,1,0:T(8,128)(2,1)S(1)} collective-permute-done((bf16[2,256,512]{2,1,0:T(8,128)(2,1)S(1)}, bf16[2,256,512]{2,1,0:T(8,128)(2,1)S(1)}, u32[]{:S(2)}, u32[]{:S(2)}) %collective-permute-start.6) | collective-permute-done | bytes 524320 | tf_op jit(solution)/shard_map/ppermute | solution.py:34
  29.1 5.3 %slot_terms.1 = (bf16[2,384,512]{2,1,0:T(8,128)(2,1)S(1)}, bf16[2,384,512]{2,1,0:T(8,128)(2,1)S(1)}, bf16[2,512,512]{2,1,0:T(8,128)(2,1)S(1)}) custom-call(s32[7]{0:T(128)S(1)} %concatenate.7.scalars, bf16[2,640,512]{2,1,0:T(8,128)(2,1)S(1)} %copy-done.2, bf16[2,256,512]{2,1,0:T(8,128)(2,1)S(1)} %get-tuple-element.44.first, ...), custom_call_target="tpu_custom_call" | custom-call | flops 6000000000 | bytes 20000000 | tf_op jit(solution)/shard_map/slot_terms/pallas_call | solution.py:387
  34.5 1.3 %probe_parts.1 = (bf16[2,4,2,128,128]{4,3,2,1,0:T(8,128)(2,1)S(1)}, bf16[2,4,2,128,128]{4,3,2,1,0:T(8,128)(2,1)S(1)}) custom-call(bf16[2,512,512]{2,1,0:T(8,128)(2,1)S(1)} %get-tuple-element.62.term, bf16[512,512]{1,0:T(8,128)(2,1)S(1)} %get-tuple-element.63.back_rows, bf16[512,256]{1,0:T(8,128)(2,1)S(1)} %get-tuple-element.64.back_cols, ...), custom_call_target="tpu_custom_call" | custom-call | tf_op jit(solution)/shard_map/probe_parts/pallas_call | solution.py:399
  36.7 0.9 %diag_part.1.diag = bf16[2,256,512]{2,1,0:T(8,128)(2,1)S(1)} custom-call(s32[7]{0:T(128)S(1)} %concatenate.7.scalars, bf16[2,4,2,128,128]{4,3,2,1,0:T(8,128)(2,1)S(1)} %get-tuple-element.66.refs_0_, bf16[2,384,512]{2,1,0:T(8,128)(2,1)S(1)} %get-tuple-element.67.refs_1_.kept.refs_0_, bf16[2,384,512]{2,1,0:T(8,128)(2,1)S(1)} %collective-permute-done.7.refs_2_.got.refs_1_), custom_call_target="tpu_custom_call" | custom-call | tf_op jit(solution)/shard_map/diag_part/pallas_call | solution.py:405
  37.6 1.3 %collective-permute-start.12 = (bf16[2,256,512]{2,1,0:T(8,128)(2,1)S(1)}, bf16[2,256,512]{2,1,0:T(8,128)(2,1)S(1)}, u32[]{:S(2)}, u32[]{:S(2)}) collective-permute-start(bf16[2,256,512]{2,1,0:T(8,128)(2,1)S(1)} %diag_part.1.diag), channel_id=1, source_target_pairs={{1,3},{0,4},{2,6},{5,7},{4,8},{6,10},{9,11},{8,12},{10,14},{13,15}... | collective-permute-start | bytes 1572872 | tf_op jit(solution)/shard_map/ppermute | solution.py:30
  38.9 0.7 probe_sum.1
  39.6 2.2 %collective-permute-start.9 = (bf16[4,2,128,128]{3,2,1,0:T(8,128)(2,1)S(1)}, bf16[4,2,128,128]{3,2,1,0:T(8,128)(2,1)S(1)}, u32[]{:S(2)}, u32[]{:S(2)}) collective-permute-start(bf16[4,2,128,128]{3,2,1,0:T(8,128)(2,1)S(1)} %get-tuple-element.71), channel_id=1, source_target_pairs={{0,2},{2,0},{1,3},{3,1},{4,6},{6,4},{5,7},{7,5},{8,10},{10,8},{9,1... | collective-permute-start | bytes 786440 | tf_op jit(solution)/shard_map/ppermute | solution.py:439
  41.7 1.0 %now_parts.1 = (bf16[2,256,512]{2,1,0:T(8,128)(2,1)S(1)}, bf16[2,128,512]{2,1,0:T(8,128)(2,1)S(1)}) custom-call(s32[7]{0:T(128)S(1)} %concatenate.7.scalars, bf16[4,2,128,128]{3,2,1,0:T(8,128)(2,1)S(1)} %get-tuple-element.70.refs_0_.before, bf16[2,384,512]{2,1,0:T(8,128)(2,1)S(1)} %get-tuple-element.67.refs_1_.kept.refs_0_, ...), custom_call_target="tpu_custom_call" | custom-call | tf_op jit(solution)/shard_map/now_parts/pallas_call | solution.py:428
  42.8 1.3 %collective-permute-start.10 = (bf16[2,256,512]{2,1,0:T(8,128)(2,1)S(1)}, bf16[2,256,512]{2,1,0:T(8,128)(2,1)S(1)}, u32[]{:S(2)}, u32[]{:S(2)}) collective-permute-start(bf16[2,256,512]{2,1,0:T(8,128)(2,1)S(1)} %get-tuple-element.72), channel_id=1, source_target_pairs={{1,3},{0,4},{2,6},{5,7},{4,8},{6,10},{9,11},{8,12},{10,14},{13,15}... | collective-permute-start | bytes 1572872 | tf_op jit(solution)/shard_map/ppermute | solution.py:30
  44.1 0.7 collective-permute-start.11
  44.7 5.9 %collective-permute-done.12.refs_2_ = bf16[2,256,512]{2,1,0:T(8,128)(2,1)S(1)} collective-permute-done((bf16[2,256,512]{2,1,0:T(8,128)(2,1)S(1)}, bf16[2,256,512]{2,1,0:T(8,128)(2,1)S(1)}, u32[]{:S(2)}, u32[]{:S(2)}) %collective-permute-start.12) | collective-permute-done | bytes 524320 | tf_op jit(solution)/shard_map/ppermute | solution.py:30
  50.6 0.9 %later_part.1 = bf16[2,256,512]{2,1,0:T(8,128)(2,1)S(1)} custom-call(s32[7]{0:T(128)S(1)} %concatenate.7.scalars, bf16[2,384,512]{2,1,0:T(8,128)(2,1)S(1)} %get-tuple-element.67.refs_1_.kept.refs_0_, bf16[2,384,512]{2,1,0:T(8,128)(2,1)S(1)} %collective-permute-done.7.refs_2_.got.refs_1_, bf16[2,256,512]{2,1,0:T(8,128)(2,1)S(1)} %collective-permute-done.12.refs_2_), custom_call_target="tpu_custom_call" | custom-call | tf_op jit(solution)/shard_map/later_part/pallas_call | solution.py:405
  51.5 1.9 %collective-permute-start.13 = (bf16[2,256,512]{2,1,0:T(8,128)(2,1)S(1)}, bf16[2,256,512]{2,1,0:T(8,128)(2,1)S(1)}, u32[]{:S(2)}, u32[]{:S(2)}) collective-permute-start(bf16[2,256,512]{2,1,0:T(8,128)(2,1)S(1)} %later_part.1), channel_id=1, source_target_pairs={{1,5},{0,2},{3,7},{5,9},{4,6},{7,11},{9,13},{8,10},{11,15},{12,14}... | collective-permute-start | bytes 1572872 | tf_op jit(solution)/shard_map/ppermute | solution.py:30
  53.6 2.6 %collective-permute-start.17 = (bf16[2,128,128]{2,1,0:T(8,128)(2,1)S(1)}, bf16[2,128,128]{2,1,0:T(8,128)(2,1)S(1)}, u32[]{:S(2)}, u32[]{:S(2)}) collective-permute-start(bf16[2,128,128]{2,1,0:T(8,128)(2,1)S(1)} %get-tuple-element.77), channel_id=1, source_target_pairs={{0,8},{4,12},{8,0},{12,4},{1,9},{5,13},{9,1},{13,5},{2,10},{6,14},... | collective-permute-start | bytes 196616 | tf_op jit(solution)/shard_map/ppermute | solution.py:338
  56.2 7.0 %collective-permute-done.10.upper = bf16[2,256,512]{2,1,0:T(8,128)(2,1)S(1)} collective-permute-done((bf16[2,256,512]{2,1,0:T(8,128)(2,1)S(1)}, bf16[2,256,512]{2,1,0:T(8,128)(2,1)S(1)}, u32[]{:S(2)}, u32[]{:S(2)}) %collective-permute-start.10) | collective-permute-done | bytes 524320 | tf_op jit(solution)/shard_map/ppermute | solution.py:30
  63.3 1.1 %own_part.1 = bf16[2,384,512]{2,1,0:T(8,128)(2,1)S(1)} custom-call(s32[7]{0:T(128)S(1)} %concatenate.7.scalars, bf16[4,2,128,128]{3,2,1,0:T(8,128)(2,1)S(1)} %sum.1.before, bf16[2,384,512]{2,1,0:T(8,128)(2,1)S(1)} %get-tuple-element.67.refs_1_.kept.refs_0_, bf16[2,384,512]{2,1,0:T(8,128)(2,1)S(1)} %collective-permute-done.7.refs_2_.got.refs_1_, ...), custom_call_target="tpu_custom_call" | custom-call | flops 1000000000 | tf_op jit(solution)/shard_map/own_part/pallas_call | solution.py:453
  65.0 0.8 %collective-permute-done.17.refs_2_ = bf16[2,128,128]{2,1,0:T(8,128)(2,1)S(1)} collective-permute-done((bf16[2,128,128]{2,1,0:T(8,128)(2,1)S(1)}, bf16[2,128,128]{2,1,0:T(8,128)(2,1)S(1)}, u32[]{:S(2)}, u32[]{:S(2)}) %collective-permute-start.17) | collective-permute-done | bytes 65568 | tf_op jit(solution)/shard_map/ppermute | solution.py:338
  65.8 1.9 %collective-permute-done.18.refs_3_ = bf16[2,128,128]{2,1,0:T(8,128)(2,1)S(1)} collective-permute-done((bf16[2,128,128]{2,1,0:T(8,128)(2,1)S(1)}, bf16[2,128,128]{2,1,0:T(8,128)(2,1)S(1)}, u32[]{:S(2)}, u32[]{:S(2)}) %collective-permute-start.18) | collective-permute-done | bytes 65568 | tf_op jit(solution)/shard_map/ppermute | solution.py:338
  67.7 0.7 probe_grad.1
  68.9 1.1 %pad_maximum_fusion = bf16[2,640,512]{2,1,0:T(8,128)(2,1)} fusion(bf16[2,128,512]{2,1,0:T(8,128)(2,1)S(1)} %slice_select_fusion, bf16[2,256,512]{2,1,0:T(8,128)(2,1)S(1)} %get-tuple-element.75, bf16[2,256,512]{2,1,0:T(8,128)(2,1)S(1)} %get-tuple-element.74), kind=kLoop, calls=%fused_computation | loop fusion | flops 3932160 | bytes 2621440 | tf_op jit(solution)/shard_map/concatenate | solution.py:464
  (33 shorter events, 3.4 us)
Async XLA Ops:
  0.6 1.3 %copy-start.1 = (bf16[2,640,512]{2,1,0:T(8,128)(2,1)S(1)}, bf16[2,640,512]{2,1,0:T(8,128)(2,1)}, u32[]{:S(2)}) copy-start(bf16[2,640,512]{2,1,0:T(8,128)(2,1)} %own.1) | copy-start | bytes 3932164
  2.0 8.3 %collective-permute-start.1 = (bf16[2,256,512]{2,1,0:T(8,128)(2,1)S(1)}, bf16[2,256,512]{2,1,0:T(8,128)(2,1)S(1)}, u32[]{:S(2)}, u32[]{:S(2)}) collective-permute-start(bf16[2,256,512]{2,1,0:T(8,128)(2,1)S(1)} %get-tuple-element.38), channel_id=1, source_target_pairs={{3,1},{4,0},{7,5},{6,2},{8,4},{11,9},{10,6},{12,8},{15,13},{14,10}... | collective-permute-start | bytes 1572872 | tf_op jit(solution)/shard_map/ppermute | solution.py:30
  4.2 19.1 %collective-permute-start.3 = (bf16[2,384,512]{2,1,0:T(8,128)(2,1)S(1)}, bf16[2,384,512]{2,1,0:T(8,128)(2,1)S(1)}, u32[]{:S(2)}, u32[]{:S(2)}) collective-permute-start(bf16[2,384,512]{2,1,0:T(8,128)(2,1)S(1)} %get-tuple-element.45), channel_id=1, source_target_pairs={{3,1},{4,0},{7,5},{6,2},{8,4},{11,9},{10,6},{12,8},{15,13},{14,10}... | collective-permute-start | bytes 2359304 | tf_op jit(solution)/shard_map/ppermute | solution.py:30
  7.0 2.7 %collective-permute-start = (s32[2]{0:T(128)S(1)}, s32[2]{0:T(128)S(1)}, u32[]{:S(2)}, u32[]{:S(2)}) collective-permute-start(s32[2]{0:T(128)S(1)} %pad_add_fusion), channel_id=1, source_target_pairs={{0,1},{1,0},{2,3},{3,2},{4,5},{5,4},{6,7},{7,6},{8,9},{9,8},{10,11... | collective-permute-start | bytes 32 | tf_op jit(solution)/shard_map/ppermute | solution.py:34
  10.3 5.6 %collective-permute-start.2 = (bf16[2,256,512]{2,1,0:T(8,128)(2,1)S(1)}, bf16[2,256,512]{2,1,0:T(8,128)(2,1)S(1)}, u32[]{:S(2)}, u32[]{:S(2)}) collective-permute-start(bf16[2,256,512]{2,1,0:T(8,128)(2,1)S(1)} %collective-permute-done.1.first_in), channel_id=1, source_target_pairs={{0,1},{1,0},{2,3},{3,2},{4,5},{5,4},{6,7},{7,6},{8,9},{9,8},{10,11... | collective-permute-start | bytes 1572872 | tf_op jit(solution)/shard_map/ppermute | solution.py:34
  13.8 13.4 %collective-permute-start.5 = (bf16[2,256,512]{2,1,0:T(8,128)(2,1)S(1)}, bf16[2,256,512]{2,1,0:T(8,128)(2,1)S(1)}, u32[]{:S(2)}, u32[]{:S(2)}) collective-permute-start(bf16[2,256,512]{2,1,0:T(8,128)(2,1)S(1)} %collective-permute-done.1.first_in), channel_id=1, source_target_pairs={{2,0},{5,1},{7,3},{6,4},{9,5},{11,7},{10,8},{13,9},{15,11},{14,12}... | collective-permute-start | bytes 1572872 | tf_op jit(solution)/shard_map/ppermute | solution.py:30
  15.9 1.6 %copy-start = (bf16[4,512,512]{2,1,0:T(8,128)(2,1)S(1)}, bf16[4,512,512]{2,1,0:T(8,128)(2,1)}, u32[]{:S(2)}) copy-start(bf16[4,512,512]{2,1,0:T(8,128)(2,1)} %constant.32.clone.dft) | copy-start | bytes 6291460
  17.5 1.2 %copy-start.3 = (bf16[2,512,512]{2,1,0:T(8,128)(2,1)S(1)}, bf16[2,512,512]{2,1,0:T(8,128)(2,1)}, u32[]{:S(2)}) copy-start(bf16[2,512,512]{2,1,0:T(8,128)(2,1)} %probe_in) | copy-start | bytes 3145732
  18.7 1.0 %copy-start.4 = (bf16[1,1,1,512,512]{4,3,2,1,0:T(8,128)(2,1)S(1)}, bf16[1,1,1,512,512]{4,3,2,1,0:T(8,128)(2,1)}, u32[]{:S(2)}) copy-start(bf16[1,1,1,512,512]{4,3,2,1,0:T(8,128)(2,1)} %param.9) | copy-start | bytes 1572868
  19.7 9.3 %copy-start.2 = (bf16[2,640,512]{2,1,0:T(8,128)(2,1)S(1)}, bf16[2,640,512]{2,1,0:T(8,128)(2,1)}, u32[]{:S(2)}) copy-start(bf16[2,640,512]{2,1,0:T(8,128)(2,1)} %own.1) | copy-start | bytes 3932164
  23.3 5.8 %collective-permute-start.4 = (bf16[2,384,512]{2,1,0:T(8,128)(2,1)S(1)}, bf16[2,384,512]{2,1,0:T(8,128)(2,1)S(1)}, u32[]{:S(2)}, u32[]{:S(2)}) collective-permute-start(bf16[2,384,512]{2,1,0:T(8,128)(2,1)S(1)} %collective-permute-done.3.second), channel_id=1, source_target_pairs={{0,1},{1,0},{2,3},{3,2},{4,5},{5,4},{6,7},{7,6},{8,9},{9,8},{10,11... | collective-permute-start | bytes 2359304 | tf_op jit(solution)/shard_map/ppermute | solution.py:34
  27.1 1.9 %collective-permute-start.6 = (bf16[2,256,512]{2,1,0:T(8,128)(2,1)S(1)}, bf16[2,256,512]{2,1,0:T(8,128)(2,1)S(1)}, u32[]{:S(2)}, u32[]{:S(2)}) collective-permute-start(bf16[2,256,512]{2,1,0:T(8,128)(2,1)S(1)} %collective-permute-done.5.third), channel_id=1, source_target_pairs={{0,1},{1,0},{2,3},{3,2},{4,5},{5,4},{6,7},{7,6},{8,9},{9,8},{10,11... | collective-permute-start | bytes 1572872 | tf_op jit(solution)/shard_map/ppermute | solution.py:34
  34.3 2.4 %collective-permute-start.7 = (bf16[2,384,512]{2,1,0:T(8,128)(2,1)S(1)}, bf16[2,384,512]{2,1,0:T(8,128)(2,1)S(1)}, u32[]{:S(2)}, u32[]{:S(2)}) collective-permute-start(bf16[2,384,512]{2,1,0:T(8,128)(2,1)S(1)} %get-tuple-element.68), channel_id=1, source_target_pairs={{0,1},{1,0},{2,3},{3,2},{4,5},{5,4},{6,7},{7,6},{8,9},{9,8},{10,11... | collective-permute-start | bytes 2359304 | tf_op jit(solution)/shard_map/ppermute | solution.py:34
  35.8 3.1 %collective-permute-start.8 = (bf16[2,4,2,128,128]{4,3,2,1,0:T(8,128)(2,1)S(1)}, bf16[2,4,2,128,128]{4,3,2,1,0:T(8,128)(2,1)S(1)}, u32[]{:S(2)}, u32[]{:S(2)}) collective-permute-start(bf16[2,4,2,128,128]{4,3,2,1,0:T(8,128)(2,1)S(1)} %get-tuple-element.66.refs_0_), channel_id=1, source_target_pairs={{0,1},{1,0},{2,3},{3,2},{4,5},{5,4},{6,7},{7,6},{8,9},{9,8},{10,11... | collective-permute-start | bytes 1572872 | tf_op jit(solution)/shard_map/ppermute | solution.py:34
  37.6 13.0 %collective-permute-start.12 = (bf16[2,256,512]{2,1,0:T(8,128)(2,1)S(1)}, bf16[2,256,512]{2,1,0:T(8,128)(2,1)S(1)}, u32[]{:S(2)}, u32[]{:S(2)}) collective-permute-start(bf16[2,256,512]{2,1,0:T(8,128)(2,1)S(1)} %diag_part.1.diag), channel_id=1, source_target_pairs={{1,3},{0,4},{2,6},{5,7},{4,8},{6,10},{9,11},{8,12},{10,14},{13,15}... | collective-permute-start | bytes 1572872 | tf_op jit(solution)/shard_map/ppermute | solution.py:30
  39.6 13.8 %collective-permute-start.9 = (bf16[4,2,128,128]{3,2,1,0:T(8,128)(2,1)S(1)}, bf16[4,2,128,128]{3,2,1,0:T(8,128)(2,1)S(1)}, u32[]{:S(2)}, u32[]{:S(2)}) collective-permute-start(bf16[4,2,128,128]{3,2,1,0:T(8,128)(2,1)S(1)} %get-tuple-element.71), channel_id=1, source_target_pairs={{0,2},{2,0},{1,3},{3,1},{4,6},{6,4},{5,7},{7,5},{8,10},{10,8},{9,1... | collective-permute-start | bytes 786440 | tf_op jit(solution)/shard_map/ppermute | solution.py:439
  42.8 20.5 %collective-permute-start.10 = (bf16[2,256,512]{2,1,0:T(8,128)(2,1)S(1)}, bf16[2,256,512]{2,1,0:T(8,128)(2,1)S(1)}, u32[]{:S(2)}, u32[]{:S(2)}) collective-permute-start(bf16[2,256,512]{2,1,0:T(8,128)(2,1)S(1)} %get-tuple-element.72), channel_id=1, source_target_pairs={{1,3},{0,4},{2,6},{5,7},{4,8},{6,10},{9,11},{8,12},{10,14},{13,15}... | collective-permute-start | bytes 1572872 | tf_op jit(solution)/shard_map/ppermute | solution.py:30
  44.1 12.2 %collective-permute-start.11 = (bf16[2,128,512]{2,1,0:T(8,128)(2,1)S(1)}, bf16[2,128,512]{2,1,0:T(8,128)(2,1)S(1)}, u32[]{:S(2)}, u32[]{:S(2)}) collective-permute-start(bf16[2,128,512]{2,1,0:T(8,128)(2,1)S(1)} %get-tuple-element.73), channel_id=1, source_target_pairs={{0,4},{2,6},{4,8},{6,10},{8,12},{10,14},{16,20},{18,22},{20,24},{2... | collective-permute-start | bytes 786440 | tf_op jit(solution)/shard_map/ppermute | solution.py:30
  51.5 13.5 %collective-permute-start.13 = (bf16[2,256,512]{2,1,0:T(8,128)(2,1)S(1)}, bf16[2,256,512]{2,1,0:T(8,128)(2,1)S(1)}, u32[]{:S(2)}, u32[]{:S(2)}) collective-permute-start(bf16[2,256,512]{2,1,0:T(8,128)(2,1)S(1)} %later_part.1), channel_id=1, source_target_pairs={{1,5},{0,2},{3,7},{5,9},{4,6},{7,11},{9,13},{8,10},{11,15},{12,14}... | collective-permute-start | bytes 1572872 | tf_op jit(solution)/shard_map/ppermute | solution.py:30
  53.5 11.5 %collective-permute-start.16 = (bf16[2,128,128]{2,1,0:T(8,128)(2,1)S(1)}, bf16[2,128,128]{2,1,0:T(8,128)(2,1)S(1)}, u32[]{:S(2)}, u32[]{:S(2)}) collective-permute-start(bf16[2,128,128]{2,1,0:T(8,128)(2,1)S(1)} %get-tuple-element.78), channel_id=1, source_target_pairs={{0,4},{4,0},{8,12},{12,8},{1,5},{5,1},{9,13},{13,9},{2,6},{6,2},{1... | collective-permute-start | bytes 196616 | tf_op jit(solution)/shard_map/ppermute | solution.py:338
  53.6 12.2 %collective-permute-start.17 = (bf16[2,128,128]{2,1,0:T(8,128)(2,1)S(1)}, bf16[2,128,128]{2,1,0:T(8,128)(2,1)S(1)}, u32[]{:S(2)}, u32[]{:S(2)}) collective-permute-start(bf16[2,128,128]{2,1,0:T(8,128)(2,1)S(1)} %get-tuple-element.77), channel_id=1, source_target_pairs={{0,8},{4,12},{8,0},{12,4},{1,9},{5,13},{9,1},{13,5},{2,10},{6,14},... | collective-permute-start | bytes 196616 | tf_op jit(solution)/shard_map/ppermute | solution.py:338
  56.2 11.5 %collective-permute-start.18 = (bf16[2,128,128]{2,1,0:T(8,128)(2,1)S(1)}, bf16[2,128,128]{2,1,0:T(8,128)(2,1)S(1)}, u32[]{:S(2)}, u32[]{:S(2)}) collective-permute-start(bf16[2,128,128]{2,1,0:T(8,128)(2,1)S(1)} %get-tuple-element.76), channel_id=1, source_target_pairs={{0,12},{4,8},{8,4},{12,0},{1,13},{5,9},{9,5},{13,1},{2,14},{6,10},... | collective-permute-start | bytes 196616 | tf_op jit(solution)/shard_map/ppermute | solution.py:338
  64.3 4.1 %collective-permute-start.14 = (bf16[2,384,512]{2,1,0:T(8,128)(2,1)S(1)}, bf16[2,384,512]{2,1,0:T(8,128)(2,1)S(1)}, u32[]{:S(2)}, u32[]{:S(2)}) collective-permute-start(bf16[2,384,512]{2,1,0:T(8,128)(2,1)S(1)} %own_part.1), channel_id=1, source_target_pairs={{0,1},{1,0},{2,3},{3,2},{4,5},{5,4},{6,7},{7,6},{8,9},{9,8},{10,11... | collective-permute-start | bytes 2359304 | tf_op jit(solution)/shard_map/ppermute | solution.py:34
  64.9 3.5 %collective-permute-start.15 = (bf16[2,256,512]{2,1,0:T(8,128)(2,1)S(1)}, bf16[2,256,512]{2,1,0:T(8,128)(2,1)S(1)}, u32[]{:S(2)}, u32[]{:S(2)}) collective-permute-start(bf16[2,256,512]{2,1,0:T(8,128)(2,1)S(1)} %collective-permute-done.13), channel_id=1, source_target_pairs={{0,1},{1,0},{2,3},{3,2},{4,5},{5,4},{6,7},{7,6},{8,9},{9,8},{10,11... | collective-permute-start | bytes 1572872 | tf_op jit(solution)/shard_map/ppermute | solution.py:34

commit v7 on v6

--- a/solution.py
+++ b/solution.py
@@ -48,6 +48,10 @@
 
 def dot(a, b):
     return jnp.dot(a, b, preferred_element_type=F32)
+
+
+def rounded(x):
+    return x.astype(BF16).astype(F32)
 
 
 def iota(shape, dim):
@@ -179,13 +183,13 @@
         probe_re, probe_im = probe[0, at].astype(F32), probe[1, at].astype(F32)
         exit_re = probe_re * planes[0] - probe_im * planes[1]
         exit_im = probe_re * planes[1] + probe_im * planes[0]
-        for plane, value in ((0, exit_re), (1, exit_im)):
+        for plane, value in ((0, rounded(exit_re)), (1, rounded(exit_im))):
             where = slice(plane * part, (plane + 1) * part)
             exit_wave[0, at, where] = (value[:, :part] + value[:, part:]).astype(BF16)
             exit_wave[1, at, where] = (value[:, :part] - value[:, part:]).astype(BF16)
 
     for odd in range(2):
-        result = dot(exit_wave[odd], right[odd])
+        result = rounded(dot(exit_wave[odd], right[odd]))
         cols = slice(odd * part, (odd + 1) * part)
         for plane in range(2):
             where = slice(plane * part, (plane + 1) * part)

time: 70.4 us -> 70.6 us (level)
  no operation moved by 1% of the time
where the time goes in v7:
time: 70.6 us; the launch traced here: 70.2 us
  starting transfers between devices  24.1 us (34%)
  waiting for transfers between devices  20.8 us (29%)
  Pallas kernels  15.6 us (22%)
  local copies, waits for them, and re-layouts  5.28 us (7%)
  between operations  2.79 us (4%)
  other arithmetic  1.6 us (2%)
    ppermute x7, waiting for transfers between devices, to_neighbour(): return lax.ppermute(x, ('wide', 'narrow', 'probe'), pairs)  15.6 us
    ppermute x7, starting transfers between devices, to_neighbour(): return lax.ppermute(x, ('wide', 'narrow', 'probe'), pairs)  10.8 us
    ppermute x8, starting transfers between devices, swap(): return lax.ppermute(x, 'probe', [(0, 1), (1, 0)])  8.44 us
    pallas_call x1, Pallas kernels, shards(): call(slot_terms, (shape(2, count, cols), shape(2, count, cols), table), [...  5.44 us
    unnamed x10, local copies, waits for them, and re-layouts  5.17 us
    pallas_call x1, Pallas kernels, shards(): call(functools.partial(shift_tables, width), (table,) * 5 + (shape(size,...  3.55 us
    ppermute x3, waiting for transfers between devices, scatter_parts(): terms.append(lax.ppermute(part(to), axis, pairs))  2.71 us
    ppermute x3, starting transfers between devices, scatter_parts(): terms.append(lax.ppermute(part(to), axis, pairs))  2.71 us
  transfers between devices with their start and end apart: 19, of which 10 were waited for; matrix products, arithmetic and copies ran while one was open for 0% of the time, Pallas kernels for 14%

profile of v7, /device:TPU:19, one launch (start us, length us, event | category | flops | bytes accessed | tf_op | source)
XLA Modules:
  0.0 70.2 jit_solution(16928367172859368255)
XLA Ops:
  0.6 1.3 %copy-done.1 = bf16[2,640,512]{2,1,0:T(8,128)(2,1)S(1)} copy-done((bf16[2,640,512]{2,1,0:T(8,128)(2,1)S(1)}, bf16[2,640,512]{2,1,0:T(8,128)(2,1)}, u32[]{:S(2)}) %copy-start.1) | copy-done | bytes 1310744
  2.0 2.2 %collective-permute-start.1 = (bf16[2,256,512]{2,1,0:T(8,128)(2,1)S(1)}, bf16[2,256,512]{2,1,0:T(8,128)(2,1)S(1)}, u32[]{:S(2)}, u32[]{:S(2)}) collective-permute-start(bf16[2,256,512]{2,1,0:T(8,128)(2,1)S(1)} %get-tuple-element.38), channel_id=1, source_target_pairs={{3,1},{4,0},{7,5},{6,2},{8,4},{11,9},{10,6},{12,8},{15,13},{14,10}... | collective-permute-start | bytes 1572872 | tf_op jit(solution)/shard_map/ppermute | solution.py:30
  4.2 1.3 %collective-permute-start.3 = (bf16[2,384,512]{2,1,0:T(8,128)(2,1)S(1)}, bf16[2,384,512]{2,1,0:T(8,128)(2,1)S(1)}, u32[]{:S(2)}, u32[]{:S(2)}) collective-permute-start(bf16[2,384,512]{2,1,0:T(8,128)(2,1)S(1)} %get-tuple-element.45), channel_id=1, source_target_pairs={{3,1},{4,0},{7,5},{6,2},{8,4},{11,9},{10,6},{12,8},{15,13},{14,10}... | collective-permute-start | bytes 2359304 | tf_op jit(solution)/shard_map/ppermute | solution.py:30
  7.0 1.9 %collective-permute-start = (s32[2]{0:T(128)S(1)}, s32[2]{0:T(128)S(1)}, u32[]{:S(2)}, u32[]{:S(2)}) collective-permute-start(s32[2]{0:T(128)S(1)} %pad_add_fusion), channel_id=1, source_target_pairs={{0,1},{1,0},{2,3},{3,2},{4,5},{5,4},{6,7},{7,6},{8,9},{9,8},{10,11... | collective-permute-start | bytes 32 | tf_op jit(solution)/shard_map/ppermute | solution.py:34
  10.3 3.5 %collective-permute-start.2 = (bf16[2,256,512]{2,1,0:T(8,128)(2,1)S(1)}, bf16[2,256,512]{2,1,0:T(8,128)(2,1)S(1)}, u32[]{:S(2)}, u32[]{:S(2)}) collective-permute-start(bf16[2,256,512]{2,1,0:T(8,128)(2,1)S(1)} %collective-permute-done.1.first_in), channel_id=1, source_target_pairs={{0,1},{1,0},{2,3},{3,2},{4,5},{5,4},{6,7},{7,6},{8,9},{9,8},{10,11... | collective-permute-start | bytes 1572872 | tf_op jit(solution)/shard_map/ppermute | solution.py:34
  13.8 2.1 %collective-permute-start.5 = (bf16[2,256,512]{2,1,0:T(8,128)(2,1)S(1)}, bf16[2,256,512]{2,1,0:T(8,128)(2,1)S(1)}, u32[]{:S(2)}, u32[]{:S(2)}) collective-permute-start(bf16[2,256,512]{2,1,0:T(8,128)(2,1)S(1)} %collective-permute-done.1.first_in), channel_id=1, source_target_pairs={{2,0},{5,1},{7,3},{6,4},{9,5},{11,7},{10,8},{13,9},{15,11},{14,12}... | collective-permute-start | bytes 1572872 | tf_op jit(solution)/shard_map/ppermute | solution.py:30
  15.9 1.6 %copy-done = bf16[4,512,512]{2,1,0:T(8,128)(2,1)S(1)} copy-done((bf16[4,512,512]{2,1,0:T(8,128)(2,1)S(1)}, bf16[4,512,512]{2,1,0:T(8,128)(2,1)}, u32[]{:S(2)}) %copy-start) | copy-done | bytes 2097176
  17.5 1.2 %copy-done.3 = bf16[2,512,512]{2,1,0:T(8,128)(2,1)S(1)} copy-done((bf16[2,512,512]{2,1,0:T(8,128)(2,1)S(1)}, bf16[2,512,512]{2,1,0:T(8,128)(2,1)}, u32[]{:S(2)}) %copy-start.3) | copy-done | bytes 1048600
  18.7 1.0 %copy-done.4 = bf16[1,1,1,512,512]{4,3,2,1,0:T(8,128)(2,1)S(1)} copy-done((bf16[1,1,1,512,512]{4,3,2,1,0:T(8,128)(2,1)S(1)}, bf16[1,1,1,512,512]{4,3,2,1,0:T(8,128)(2,1)}, u32[]{:S(2)}) %copy-start.4) | copy-done | bytes 524312
  19.7 3.5 %shift_tables.1 = (bf16[2,512,512]{2,1,0:T(8,128)(2,1)S(1)}, bf16[2,512,512]{2,1,0:T(8,128)(2,1)S(1)}, bf16[2,512,512]{2,1,0:T(8,128)(2,1)S(1)}, bf16[2,512,512]...) custom-call(s32[7]{0:T(128)S(1)} %concatenate.7.scalars, ...), custom_call_target="tpu_custom_call" | custom-call | tf_op jit(solution)/shard_map/shift_tables/pallas_call | solution.py:374
  23.3 2.3 %collective-permute-start.4 = (bf16[2,384,512]{2,1,0:T(8,128)(2,1)S(1)}, bf16[2,384,512]{2,1,0:T(8,128)(2,1)S(1)}, u32[]{:S(2)}, u32[]{:S(2)}) collective-permute-start(bf16[2,384,512]{2,1,0:T(8,128)(2,1)S(1)} %collective-permute-done.3.second), channel_id=1, source_target_pairs={{0,1},{1,0},{2,3},{3,2},{4,5},{5,4},{6,7},{7,6},{8,9},{9,8},{10,11... | collective-permute-start | bytes 2359304 | tf_op jit(solution)/shard_map/ppermute | solution.py:34
  25.6 1.6 %collective-permute-done.5.third = bf16[2,256,512]{2,1,0:T(8,128)(2,1)S(1)} collective-permute-done((bf16[2,256,512]{2,1,0:T(8,128)(2,1)S(1)}, bf16[2,256,512]{2,1,0:T(8,128)(2,1)S(1)}, u32[]{:S(2)}, u32[]{:S(2)}) %collective-permute-start.5) | collective-permute-done | bytes 524320 | tf_op jit(solution)/shard_map/ppermute | solution.py:30
  27.1 1.9 %collective-permute-done.6.third2 = bf16[2,256,512]{2,1,0:T(8,128)(2,1)S(1)} collective-permute-done((bf16[2,256,512]{2,1,0:T(8,128)(2,1)S(1)}, bf16[2,256,512]{2,1,0:T(8,128)(2,1)S(1)}, u32[]{:S(2)}, u32[]{:S(2)}) %collective-permute-start.6) | collective-permute-done | bytes 524320 | tf_op jit(solution)/shard_map/ppermute | solution.py:34
  29.1 5.4 %slot_terms.1 = (bf16[2,384,512]{2,1,0:T(8,128)(2,1)S(1)}, bf16[2,384,512]{2,1,0:T(8,128)(2,1)S(1)}, bf16[2,512,512]{2,1,0:T(8,128)(2,1)S(1)}) custom-call(s32[7]{0:T(128)S(1)} %concatenate.7.scalars, bf16[2,640,512]{2,1,0:T(8,128)(2,1)S(1)} %copy-done.2, bf16[2,256,512]{2,1,0:T(8,128)(2,1)S(1)} %get-tuple-element.44.first, ...), custom_call_target="tpu_custom_call" | custom-call | flops 6000000000 | bytes 20000000 | tf_op jit(solution)/shard_map/slot_terms/pallas_call | solution.py:391
  34.7 1.3 %probe_parts.1 = (bf16[2,4,2,128,128]{4,3,2,1,0:T(8,128)(2,1)S(1)}, bf16[2,4,2,128,128]{4,3,2,1,0:T(8,128)(2,1)S(1)}) custom-call(bf16[2,512,512]{2,1,0:T(8,128)(2,1)S(1)} %get-tuple-element.62.term, bf16[512,512]{1,0:T(8,128)(2,1)S(1)} %get-tuple-element.63.back_rows, bf16[512,256]{1,0:T(8,128)(2,1)S(1)} %get-tuple-element.64.back_cols, ...), custom_call_target="tpu_custom_call" | custom-call | tf_op jit(solution)/shard_map/probe_parts/pallas_call | solution.py:403
  36.9 0.9 %diag_part.1.diag = bf16[2,256,512]{2,1,0:T(8,128)(2,1)S(1)} custom-call(s32[7]{0:T(128)S(1)} %concatenate.7.scalars, bf16[2,4,2,128,128]{4,3,2,1,0:T(8,128)(2,1)S(1)} %get-tuple-element.66.refs_0_, bf16[2,384,512]{2,1,0:T(8,128)(2,1)S(1)} %get-tuple-element.67.refs_1_.kept.refs_0_, bf16[2,384,512]{2,1,0:T(8,128)(2,1)S(1)} %collective-permute-done.7.refs_2_.got.refs_1_), custom_call_target="tpu_custom_call" | custom-call | tf_op jit(solution)/shard_map/diag_part/pallas_call | solution.py:409
  37.7 1.3 %collective-permute-start.12 = (bf16[2,256,512]{2,1,0:T(8,128)(2,1)S(1)}, bf16[2,256,512]{2,1,0:T(8,128)(2,1)S(1)}, u32[]{:S(2)}, u32[]{:S(2)}) collective-permute-start(bf16[2,256,512]{2,1,0:T(8,128)(2,1)S(1)} %diag_part.1.diag), channel_id=1, source_target_pairs={{1,3},{0,4},{2,6},{5,7},{4,8},{6,10},{9,11},{8,12},{10,14},{13,15}... | collective-permute-start | bytes 1572872 | tf_op jit(solution)/shard_map/ppermute | solution.py:30
  39.0 0.7 probe_sum.1
  39.7 2.2 %collective-permute-start.9 = (bf16[4,2,128,128]{3,2,1,0:T(8,128)(2,1)S(1)}, bf16[4,2,128,128]{3,2,1,0:T(8,128)(2,1)S(1)}, u32[]{:S(2)}, u32[]{:S(2)}) collective-permute-start(bf16[4,2,128,128]{3,2,1,0:T(8,128)(2,1)S(1)} %get-tuple-element.71), channel_id=1, source_target_pairs={{0,2},{2,0},{1,3},{3,1},{4,6},{6,4},{5,7},{7,5},{8,10},{10,8},{9,1... | collective-permute-start | bytes 786440 | tf_op jit(solution)/shard_map/ppermute | solution.py:443
  41.9 1.0 %now_parts.1 = (bf16[2,256,512]{2,1,0:T(8,128)(2,1)S(1)}, bf16[2,128,512]{2,1,0:T(8,128)(2,1)S(1)}) custom-call(s32[7]{0:T(128)S(1)} %concatenate.7.scalars, bf16[4,2,128,128]{3,2,1,0:T(8,128)(2,1)S(1)} %get-tuple-element.70.refs_0_.before, bf16[2,384,512]{2,1,0:T(8,128)(2,1)S(1)} %get-tuple-element.67.refs_1_.kept.refs_0_, ...), custom_call_target="tpu_custom_call" | custom-call | tf_op jit(solution)/shard_map/now_parts/pallas_call | solution.py:432
  42.9 1.3 %collective-permute-start.10 = (bf16[2,256,512]{2,1,0:T(8,128)(2,1)S(1)}, bf16[2,256,512]{2,1,0:T(8,128)(2,1)S(1)}, u32[]{:S(2)}, u32[]{:S(2)}) collective-permute-start(bf16[2,256,512]{2,1,0:T(8,128)(2,1)S(1)} %get-tuple-element.72), channel_id=1, source_target_pairs={{1,3},{0,4},{2,6},{5,7},{4,8},{6,10},{9,11},{8,12},{10,14},{13,15}... | collective-permute-start | bytes 1572872 | tf_op jit(solution)/shard_map/ppermute | solution.py:30
  44.2 0.7 collective-permute-start.11
  44.9 5.9 %collective-permute-done.12.refs_2_ = bf16[2,256,512]{2,1,0:T(8,128)(2,1)S(1)} collective-permute-done((bf16[2,256,512]{2,1,0:T(8,128)(2,1)S(1)}, bf16[2,256,512]{2,1,0:T(8,128)(2,1)S(1)}, u32[]{:S(2)}, u32[]{:S(2)}) %collective-permute-start.12) | collective-permute-done | bytes 524320 | tf_op jit(solution)/shard_map/ppermute | solution.py:30
  50.8 0.9 %later_part.1 = bf16[2,256,512]{2,1,0:T(8,128)(2,1)S(1)} custom-call(s32[7]{0:T(128)S(1)} %concatenate.7.scalars, bf16[2,384,512]{2,1,0:T(8,128)(2,1)S(1)} %get-tuple-element.67.refs_1_.kept.refs_0_, bf16[2,384,512]{2,1,0:T(8,128)(2,1)S(1)} %collective-permute-done.7.refs_2_.got.refs_1_, bf16[2,256,512]{2,1,0:T(8,128)(2,1)S(1)} %collective-permute-done.12.refs_2_), custom_call_target="tpu_custom_call" | custom-call | tf_op jit(solution)/shard_map/later_part/pallas_call | solution.py:409
  51.6 1.9 %collective-permute-start.13 = (bf16[2,256,512]{2,1,0:T(8,128)(2,1)S(1)}, bf16[2,256,512]{2,1,0:T(8,128)(2,1)S(1)}, u32[]{:S(2)}, u32[]{:S(2)}) collective-permute-start(bf16[2,256,512]{2,1,0:T(8,128)(2,1)S(1)} %later_part.1), channel_id=1, source_target_pairs={{1,5},{0,2},{3,7},{5,9},{4,6},{7,11},{9,13},{8,10},{11,15},{12,14}... | collective-permute-start | bytes 1572872 | tf_op jit(solution)/shard_map/ppermute | solution.py:30
  53.8 2.6 %collective-permute-start.17 = (bf16[2,128,128]{2,1,0:T(8,128)(2,1)S(1)}, bf16[2,128,128]{2,1,0:T(8,128)(2,1)S(1)}, u32[]{:S(2)}, u32[]{:S(2)}) collective-permute-start(bf16[2,128,128]{2,1,0:T(8,128)(2,1)S(1)} %get-tuple-element.77), channel_id=1, source_target_pairs={{0,8},{4,12},{8,0},{12,4},{1,9},{5,13},{9,1},{13,5},{2,10},{6,14},... | collective-permute-start | bytes 196616 | tf_op jit(solution)/shard_map/ppermute | solution.py:342
  56.4 7.0 %collective-permute-done.10.upper = bf16[2,256,512]{2,1,0:T(8,128)(2,1)S(1)} collective-permute-done((bf16[2,256,512]{2,1,0:T(8,128)(2,1)S(1)}, bf16[2,256,512]{2,1,0:T(8,128)(2,1)S(1)}, u32[]{:S(2)}, u32[]{:S(2)}) %collective-permute-start.10) | collective-permute-done | bytes 524320 | tf_op jit(solution)/shard_map/ppermute | solution.py:30
  63.4 1.1 %own_part.1 = bf16[2,384,512]{2,1,0:T(8,128)(2,1)S(1)} custom-call(s32[7]{0:T(128)S(1)} %concatenate.7.scalars, bf16[4,2,128,128]{3,2,1,0:T(8,128)(2,1)S(1)} %sum.1.before, bf16[2,384,512]{2,1,0:T(8,128)(2,1)S(1)} %get-tuple-element.67.refs_1_.kept.refs_0_, bf16[2,384,512]{2,1,0:T(8,128)(2,1)S(1)} %collective-permute-done.7.refs_2_.got.refs_1_, ...), custom_call_target="tpu_custom_call" | custom-call | flops 1000000000 | tf_op jit(solution)/shard_map/own_part/pallas_call | solution.py:457
  65.2 0.8 %collective-permute-done.17.refs_2_ = bf16[2,128,128]{2,1,0:T(8,128)(2,1)S(1)} collective-permute-done((bf16[2,128,128]{2,1,0:T(8,128)(2,1)S(1)}, bf16[2,128,128]{2,1,0:T(8,128)(2,1)S(1)}, u32[]{:S(2)}, u32[]{:S(2)}) %collective-permute-start.17) | collective-permute-done | bytes 65568 | tf_op jit(solution)/shard_map/ppermute | solution.py:342
  66.0 1.9 %collective-permute-done.18.refs_3_ = bf16[2,128,128]{2,1,0:T(8,128)(2,1)S(1)} collective-permute-done((bf16[2,128,128]{2,1,0:T(8,128)(2,1)S(1)}, bf16[2,128,128]{2,1,0:T(8,128)(2,1)S(1)}, u32[]{:S(2)}, u32[]{:S(2)}) %collective-permute-start.18) | collective-permute-done | bytes 65568 | tf_op jit(solution)/shard_map/ppermute | solution.py:342
  67.9 0.7 probe_grad.1
  69.0 1.1 %pad_maximum_fusion = bf16[2,640,512]{2,1,0:T(8,128)(2,1)} fusion(bf16[2,128,512]{2,1,0:T(8,128)(2,1)S(1)} %slice_select_fusion, bf16[2,256,512]{2,1,0:T(8,128)(2,1)S(1)} %get-tuple-element.75, bf16[2,256,512]{2,1,0:T(8,128)(2,1)S(1)} %get-tuple-element.74), kind=kLoop, calls=%fused_computation | loop fusion | flops 3932160 | bytes 2621440 | tf_op jit(solution)/shard_map/concatenate | solution.py:468
  (33 shorter events, 3.4 us)
Async XLA Ops:
  0.6 1.3 %copy-start.1 = (bf16[2,640,512]{2,1,0:T(8,128)(2,1)S(1)}, bf16[2,640,512]{2,1,0:T(8,128)(2,1)}, u32[]{:S(2)}) copy-start(bf16[2,640,512]{2,1,0:T(8,128)(2,1)} %own.1) | copy-start | bytes 3932164
  2.0 8.3 %collective-permute-start.1 = (bf16[2,256,512]{2,1,0:T(8,128)(2,1)S(1)}, bf16[2,256,512]{2,1,0:T(8,128)(2,1)S(1)}, u32[]{:S(2)}, u32[]{:S(2)}) collective-permute-start(bf16[2,256,512]{2,1,0:T(8,128)(2,1)S(1)} %get-tuple-element.38), channel_id=1, source_target_pairs={{3,1},{4,0},{7,5},{6,2},{8,4},{11,9},{10,6},{12,8},{15,13},{14,10}... | collective-permute-start | bytes 1572872 | tf_op jit(solution)/shard_map/ppermute | solution.py:30
  4.2 19.1 %collective-permute-start.3 = (bf16[2,384,512]{2,1,0:T(8,128)(2,1)S(1)}, bf16[2,384,512]{2,1,0:T(8,128)(2,1)S(1)}, u32[]{:S(2)}, u32[]{:S(2)}) collective-permute-start(bf16[2,384,512]{2,1,0:T(8,128)(2,1)S(1)} %get-tuple-element.45), channel_id=1, source_target_pairs={{3,1},{4,0},{7,5},{6,2},{8,4},{11,9},{10,6},{12,8},{15,13},{14,10}... | collective-permute-start | bytes 2359304 | tf_op jit(solution)/shard_map/ppermute | solution.py:30
  7.0 2.7 %collective-permute-start = (s32[2]{0:T(128)S(1)}, s32[2]{0:T(128)S(1)}, u32[]{:S(2)}, u32[]{:S(2)}) collective-permute-start(s32[2]{0:T(128)S(1)} %pad_add_fusion), channel_id=1, source_target_pairs={{0,1},{1,0},{2,3},{3,2},{4,5},{5,4},{6,7},{7,6},{8,9},{9,8},{10,11... | collective-permute-start | bytes 32 | tf_op jit(solution)/shard_map/ppermute | solution.py:34
  10.3 5.6 %collective-permute-start.2 = (bf16[2,256,512]{2,1,0:T(8,128)(2,1)S(1)}, bf16[2,256,512]{2,1,0:T(8,128)(2,1)S(1)}, u32[]{:S(2)}, u32[]{:S(2)}) collective-permute-start(bf16[2,256,512]{2,1,0:T(8,128)(2,1)S(1)} %collective-permute-done.1.first_in), channel_id=1, source_target_pairs={{0,1},{1,0},{2,3},{3,2},{4,5},{5,4},{6,7},{7,6},{8,9},{9,8},{10,11... | collective-permute-start | bytes 1572872 | tf_op jit(solution)/shard_map/ppermute | solution.py:34
  13.8 13.4 %collective-permute-start.5 = (bf16[2,256,512]{2,1,0:T(8,128)(2,1)S(1)}, bf16[2,256,512]{2,1,0:T(8,128)(2,1)S(1)}, u32[]{:S(2)}, u32[]{:S(2)}) collective-permute-start(bf16[2,256,512]{2,1,0:T(8,128)(2,1)S(1)} %collective-permute-done.1.first_in), channel_id=1, source_target_pairs={{2,0},{5,1},{7,3},{6,4},{9,5},{11,7},{10,8},{13,9},{15,11},{14,12}... | collective-permute-start | bytes 1572872 | tf_op jit(solution)/shard_map/ppermute | solution.py:30
  15.9 1.6 %copy-start = (bf16[4,512,512]{2,1,0:T(8,128)(2,1)S(1)}, bf16[4,512,512]{2,1,0:T(8,128)(2,1)}, u32[]{:S(2)}) copy-start(bf16[4,512,512]{2,1,0:T(8,128)(2,1)} %constant.32.clone.dft) | copy-start | bytes 6291460
  17.5 1.2 %copy-start.3 = (bf16[2,512,512]{2,1,0:T(8,128)(2,1)S(1)}, bf16[2,512,512]{2,1,0:T(8,128)(2,1)}, u32[]{:S(2)}) copy-start(bf16[2,512,512]{2,1,0:T(8,128)(2,1)} %probe_in) | copy-start | bytes 3145732
  18.7 1.0 %copy-start.4 = (bf16[1,1,1,512,512]{4,3,2,1,0:T(8,128)(2,1)S(1)}, bf16[1,1,1,512,512]{4,3,2,1,0:T(8,128)(2,1)}, u32[]{:S(2)}) copy-start(bf16[1,1,1,512,512]{4,3,2,1,0:T(8,128)(2,1)} %param.9) | copy-start | bytes 1572868
  19.7 9.3 %copy-start.2 = (bf16[2,640,512]{2,1,0:T(8,128)(2,1)S(1)}, bf16[2,640,512]{2,1,0:T(8,128)(2,1)}, u32[]{:S(2)}) copy-start(bf16[2,640,512]{2,1,0:T(8,128)(2,1)} %own.1) | copy-start | bytes 3932164
  23.3 5.8 %collective-permute-start.4 = (bf16[2,384,512]{2,1,0:T(8,128)(2,1)S(1)}, bf16[2,384,512]{2,1,0:T(8,128)(2,1)S(1)}, u32[]{:S(2)}, u32[]{:S(2)}) collective-permute-start(bf16[2,384,512]{2,1,0:T(8,128)(2,1)S(1)} %collective-permute-done.3.second), channel_id=1, source_target_pairs={{0,1},{1,0},{2,3},{3,2},{4,5},{5,4},{6,7},{7,6},{8,9},{9,8},{10,11... | collective-permute-start | bytes 2359304 | tf_op jit(solution)/shard_map/ppermute | solution.py:34
  27.1 1.9 %collective-permute-start.6 = (bf16[2,256,512]{2,1,0:T(8,128)(2,1)S(1)}, bf16[2,256,512]{2,1,0:T(8,128)(2,1)S(1)}, u32[]{:S(2)}, u32[]{:S(2)}) collective-permute-start(bf16[2,256,512]{2,1,0:T(8,128)(2,1)S(1)} %collective-permute-done.5.third), channel_id=1, source_target_pairs={{0,1},{1,0},{2,3},{3,2},{4,5},{5,4},{6,7},{7,6},{8,9},{9,8},{10,11... | collective-permute-start | bytes 1572872 | tf_op jit(solution)/shard_map/ppermute | solution.py:34
  34.5 2.4 %collective-permute-start.7 = (bf16[2,384,512]{2,1,0:T(8,128)(2,1)S(1)}, bf16[2,384,512]{2,1,0:T(8,128)(2,1)S(1)}, u32[]{:S(2)}, u32[]{:S(2)}) collective-permute-start(bf16[2,384,512]{2,1,0:T(8,128)(2,1)S(1)} %get-tuple-element.68), channel_id=1, source_target_pairs={{0,1},{1,0},{2,3},{3,2},{4,5},{5,4},{6,7},{7,6},{8,9},{9,8},{10,11... | collective-permute-start | bytes 2359304 | tf_op jit(solution)/shard_map/ppermute | solution.py:34
  36.0 3.1 %collective-permute-start.8 = (bf16[2,4,2,128,128]{4,3,2,1,0:T(8,128)(2,1)S(1)}, bf16[2,4,2,128,128]{4,3,2,1,0:T(8,128)(2,1)S(1)}, u32[]{:S(2)}, u32[]{:S(2)}) collective-permute-start(bf16[2,4,2,128,128]{4,3,2,1,0:T(8,128)(2,1)S(1)} %get-tuple-element.66.refs_0_), channel_id=1, source_target_pairs={{0,1},{1,0},{2,3},{3,2},{4,5},{5,4},{6,7},{7,6},{8,9},{9,8},{10,11... | collective-permute-start | bytes 1572872 | tf_op jit(solution)/shard_map/ppermute | solution.py:34
  37.7 13.0 %collective-permute-start.12 = (bf16[2,256,512]{2,1,0:T(8,128)(2,1)S(1)}, bf16[2,256,512]{2,1,0:T(8,128)(2,1)S(1)}, u32[]{:S(2)}, u32[]{:S(2)}) collective-permute-start(bf16[2,256,512]{2,1,0:T(8,128)(2,1)S(1)} %diag_part.1.diag), channel_id=1, source_target_pairs={{1,3},{0,4},{2,6},{5,7},{4,8},{6,10},{9,11},{8,12},{10,14},{13,15}... | collective-permute-start | bytes 1572872 | tf_op jit(solution)/shard_map/ppermute | solution.py:30
  39.7 13.8 %collective-permute-start.9 = (bf16[4,2,128,128]{3,2,1,0:T(8,128)(2,1)S(1)}, bf16[4,2,128,128]{3,2,1,0:T(8,128)(2,1)S(1)}, u32[]{:S(2)}, u32[]{:S(2)}) collective-permute-start(bf16[4,2,128,128]{3,2,1,0:T(8,128)(2,1)S(1)} %get-tuple-element.71), channel_id=1, source_target_pairs={{0,2},{2,0},{1,3},{3,1},{4,6},{6,4},{5,7},{7,5},{8,10},{10,8},{9,1... | collective-permute-start | bytes 786440 | tf_op jit(solution)/shard_map/ppermute | solution.py:443
  42.9 20.5 %collective-permute-start.10 = (bf16[2,256,512]{2,1,0:T(8,128)(2,1)S(1)}, bf16[2,256,512]{2,1,0:T(8,128)(2,1)S(1)}, u32[]{:S(2)}, u32[]{:S(2)}) collective-permute-start(bf16[2,256,512]{2,1,0:T(8,128)(2,1)S(1)} %get-tuple-element.72), channel_id=1, source_target_pairs={{1,3},{0,4},{2,6},{5,7},{4,8},{6,10},{9,11},{8,12},{10,14},{13,15}... | collective-permute-start | bytes 1572872 | tf_op jit(solution)/shard_map/ppermute | solution.py:30
  44.2 12.2 %collective-permute-start.11 = (bf16[2,128,512]{2,1,0:T(8,128)(2,1)S(1)}, bf16[2,128,512]{2,1,0:T(8,128)(2,1)S(1)}, u32[]{:S(2)}, u32[]{:S(2)}) collective-permute-start(bf16[2,128,512]{2,1,0:T(8,128)(2,1)S(1)} %get-tuple-element.73), channel_id=1, source_target_pairs={{0,4},{2,6},{4,8},{6,10},{8,12},{10,14},{16,20},{18,22},{20,24},{2... | collective-permute-start | bytes 786440 | tf_op jit(solution)/shard_map/ppermute | solution.py:30
  51.6 13.5 %collective-permute-start.13 = (bf16[2,256,512]{2,1,0:T(8,128)(2,1)S(1)}, bf16[2,256,512]{2,1,0:T(8,128)(2,1)S(1)}, u32[]{:S(2)}, u32[]{:S(2)}) collective-permute-start(bf16[2,256,512]{2,1,0:T(8,128)(2,1)S(1)} %later_part.1), channel_id=1, source_target_pairs={{1,5},{0,2},{3,7},{5,9},{4,6},{7,11},{9,13},{8,10},{11,15},{12,14}... | collective-permute-start | bytes 1572872 | tf_op jit(solution)/shard_map/ppermute | solution.py:30
  53.7 11.5 %collective-permute-start.16 = (bf16[2,128,128]{2,1,0:T(8,128)(2,1)S(1)}, bf16[2,128,128]{2,1,0:T(8,128)(2,1)S(1)}, u32[]{:S(2)}, u32[]{:S(2)}) collective-permute-start(bf16[2,128,128]{2,1,0:T(8,128)(2,1)S(1)} %get-tuple-element.78), channel_id=1, source_target_pairs={{0,4},{4,0},{8,12},{12,8},{1,5},{5,1},{9,13},{13,9},{2,6},{6,2},{1... | collective-permute-start | bytes 196616 | tf_op jit(solution)/shard_map/ppermute | solution.py:342
  53.8 12.2 %collective-permute-start.17 = (bf16[2,128,128]{2,1,0:T(8,128)(2,1)S(1)}, bf16[2,128,128]{2,1,0:T(8,128)(2,1)S(1)}, u32[]{:S(2)}, u32[]{:S(2)}) collective-permute-start(bf16[2,128,128]{2,1,0:T(8,128)(2,1)S(1)} %get-tuple-element.77), channel_id=1, source_target_pairs={{0,8},{4,12},{8,0},{12,4},{1,9},{5,13},{9,1},{13,5},{2,10},{6,14},... | collective-permute-start | bytes 196616 | tf_op jit(solution)/shard_map/ppermute | solution.py:342
  56.4 11.5 %collective-permute-start.18 = (bf16[2,128,128]{2,1,0:T(8,128)(2,1)S(1)}, bf16[2,128,128]{2,1,0:T(8,128)(2,1)S(1)}, u32[]{:S(2)}, u32[]{:S(2)}) collective-permute-start(bf16[2,128,128]{2,1,0:T(8,128)(2,1)S(1)} %get-tuple-element.76), channel_id=1, source_target_pairs={{0,12},{4,8},{8,4},{12,0},{1,13},{5,9},{9,5},{13,1},{2,14},{6,10},... | collective-permute-start | bytes 196616 | tf_op jit(solution)/shard_map/ppermute | solution.py:342
  64.5 4.1 %collective-permute-start.14 = (bf16[2,384,512]{2,1,0:T(8,128)(2,1)S(1)}, bf16[2,384,512]{2,1,0:T(8,128)(2,1)S(1)}, u32[]{:S(2)}, u32[]{:S(2)}) collective-permute-start(bf16[2,384,512]{2,1,0:T(8,128)(2,1)S(1)} %own_part.1), channel_id=1, source_target_pairs={{0,1},{1,0},{2,3},{3,2},{4,5},{5,4},{6,7},{7,6},{8,9},{9,8},{10,11... | collective-permute-start | bytes 2359304 | tf_op jit(solution)/shard_map/ppermute | solution.py:34
  65.1 3.5 %collective-permute-start.15 = (bf16[2,256,512]{2,1,0:T(8,128)(2,1)S(1)}, bf16[2,256,512]{2,1,0:T(8,128)(2,1)S(1)}, u32[]{:S(2)}, u32[]{:S(2)}) collective-permute-start(bf16[2,256,512]{2,1,0:T(8,128)(2,1)S(1)} %collective-permute-done.13), channel_id=1, source_target_pairs={{0,1},{1,0},{2,3},{3,2},{4,5},{5,4},{6,7},{7,6},{8,9},{9,8},{10,11... | collective-permute-start | bytes 1572872 | tf_op jit(solution)/shard_map/ppermute | solution.py:34

commit v8 on v6

--- a/solution.py
+++ b/solution.py
@@ -144,12 +144,10 @@
     live = scalars[3].astype(F32)
     step = 128
     in_cols = iota((step, size), 1) >= col_start
-    core_0 = iota((step, size), 0) * 0 + core == 0
-
-    def tile_value(plane, row):
+
+    def tile_value(on, plane, row):
         def load(on_core_0, on_core_1, at):
-            a, b = on_core_0[plane, pl.ds(at, step)], on_core_1[plane, pl.ds(at, step)]
-            return jnp.where(core_0, a.astype(F32), b.astype(F32))
+            return (on_core_1 if on else on_core_0)[plane, pl.ds(at, step)].astype(F32)
 
         if row < rows:
             here = own[plane, pl.ds(row, step)].astype(F32)
@@ -162,27 +160,31 @@
             side = load(third, third2, row - rows - cut)
         return jnp.where(in_cols, here, side)
 
-    for start in range(0, size, step):
-        at = pl.ds(start, step)
-        planes = []
-        for plane in range(2):
-            row = start
-            while row < rows:
-                row += size
-            value = tile_value(plane, row)
-            while row > start:
-                row -= size
-                in_rows = iota((step, size), 0) + row >= row_start
-                value = jnp.where(in_rows, tile_value(plane, row), value)
-            patch[plane, at] = value.astype(BF16)
-            planes.append(value)
-        probe_re, probe_im = probe[0, at].astype(F32), probe[1, at].astype(F32)
-        exit_re = probe_re * planes[0] - probe_im * planes[1]
-        exit_im = probe_re * planes[1] + probe_im * planes[0]
-        for plane, value in ((0, exit_re), (1, exit_im)):
-            where = slice(plane * part, (plane + 1) * part)
-            exit_wave[0, at, where] = (value[:, :part] + value[:, part:]).astype(BF16)
-            exit_wave[1, at, where] = (value[:, :part] - value[:, part:]).astype(BF16)
+    def assemble(on):
+        for start in range(0, size, step):
+            at = pl.ds(start, step)
+            planes = []
+            for plane in range(2):
+                row = start
+                while row < rows:
+                    row += size
+                value = tile_value(on, plane, row)
+                while row > start:
+                    row -= size
+                    in_rows = iota((step, size), 0) + row >= row_start
+                    value = jnp.where(in_rows, tile_value(on, plane, row), value)
+                patch[plane, at] = value.astype(BF16)
+                planes.append(value)
+            probe_re, probe_im = probe[0, at].astype(F32), probe[1, at].astype(F32)
+            exit_re = probe_re * planes[0] - probe_im * planes[1]
+            exit_im = probe_re * planes[1] + probe_im * planes[0]
+            for plane, value in ((0, exit_re), (1, exit_im)):
+                where = slice(plane * part, (plane + 1) * part)
+                exit_wave[0, at, where] = (value[:, :part] + value[:, part:]).astype(BF16)
+                exit_wave[1, at, where] = (value[:, :part] - value[:, part:]).astype(BF16)
+
+    for on in range(2):
+        pl.when(core == on)(functools.partial(assemble, on))
 
     for odd in range(2):
         result = dot(exit_wave[odd], right[odd])

time: 70.4 us -> 70.4 us (level)
  no operation moved by 1% of the time
where the time goes in v8:
time: 70.4 us; the launch traced here: 70 us
  starting transfers between devices  24.1 us (34%)
  waiting for transfers between devices  20.8 us (30%)
  Pallas kernels  15.4 us (22%)
  local copies, waits for them, and re-layouts  5.28 us (7%)
  between operations  2.79 us (4%)
  other arithmetic  1.6 us (2%)
    ppermute x7, waiting for transfers between devices, to_neighbour(): return lax.ppermute(x, ('wide', 'narrow', 'probe'), pairs)  15.6 us
    ppermute x7, starting transfers between devices, to_neighbour(): return lax.ppermute(x, ('wide', 'narrow', 'probe'), pairs)  10.8 us
    ppermute x8, starting transfers between devices, swap(): return lax.ppermute(x, 'probe', [(0, 1), (1, 0)])  8.44 us
    pallas_call x1, Pallas kernels, shards(): call(slot_terms, (shape(2, count, cols), shape(2, count, cols), table), [...  5.29 us
    unnamed x10, local copies, waits for them, and re-layouts  5.17 us
    pallas_call x1, Pallas kernels, shards(): call(functools.partial(shift_tables, width), (table,) * 5 + (shape(size,...  3.55 us
    ppermute x3, waiting for transfers between devices, scatter_parts(): terms.append(lax.ppermute(part(to), axis, pairs))  2.71 us
    ppermute x3, starting transfers between devices, scatter_parts(): terms.append(lax.ppermute(part(to), axis, pairs))  2.71 us
  transfers between devices with their start and end apart: 19, of which 10 were waited for; matrix products, arithmetic and copies ran while one was open for 0% of the time, Pallas kernels for 14%

profile of v8, /device:TPU:19, one launch (start us, length us, event | category | flops | bytes accessed | tf_op | source)
XLA Modules:
  0.0 70.0 jit_solution(14046453307261608551)
XLA Ops:
  0.6 1.3 %copy-done.1 = bf16[2,640,512]{2,1,0:T(8,128)(2,1)S(1)} copy-done((bf16[2,640,512]{2,1,0:T(8,128)(2,1)S(1)}, bf16[2,640,512]{2,1,0:T(8,128)(2,1)}, u32[]{:S(2)}) %copy-start.1) | copy-done | bytes 1310744
  2.0 2.2 %collective-permute-start.1 = (bf16[2,256,512]{2,1,0:T(8,128)(2,1)S(1)}, bf16[2,256,512]{2,1,0:T(8,128)(2,1)S(1)}, u32[]{:S(2)}, u32[]{:S(2)}) collective-permute-start(bf16[2,256,512]{2,1,0:T(8,128)(2,1)S(1)} %get-tuple-element.38), channel_id=1, source_target_pairs={{3,1},{4,0},{7,5},{6,2},{8,4},{11,9},{10,6},{12,8},{15,13},{14,10}... | collective-permute-start | bytes 1572872 | tf_op jit(solution)/shard_map/ppermute | solution.py:30
  4.2 1.3 %collective-permute-start.3 = (bf16[2,384,512]{2,1,0:T(8,128)(2,1)S(1)}, bf16[2,384,512]{2,1,0:T(8,128)(2,1)S(1)}, u32[]{:S(2)}, u32[]{:S(2)}) collective-permute-start(bf16[2,384,512]{2,1,0:T(8,128)(2,1)S(1)} %get-tuple-element.45), channel_id=1, source_target_pairs={{3,1},{4,0},{7,5},{6,2},{8,4},{11,9},{10,6},{12,8},{15,13},{14,10}... | collective-permute-start | bytes 2359304 | tf_op jit(solution)/shard_map/ppermute | solution.py:30
  7.0 1.9 %collective-permute-start = (s32[2]{0:T(128)S(1)}, s32[2]{0:T(128)S(1)}, u32[]{:S(2)}, u32[]{:S(2)}) collective-permute-start(s32[2]{0:T(128)S(1)} %pad_add_fusion), channel_id=1, source_target_pairs={{0,1},{1,0},{2,3},{3,2},{4,5},{5,4},{6,7},{7,6},{8,9},{9,8},{10,11... | collective-permute-start | bytes 32 | tf_op jit(solution)/shard_map/ppermute | solution.py:34
  10.3 3.5 %collective-permute-start.2 = (bf16[2,256,512]{2,1,0:T(8,128)(2,1)S(1)}, bf16[2,256,512]{2,1,0:T(8,128)(2,1)S(1)}, u32[]{:S(2)}, u32[]{:S(2)}) collective-permute-start(bf16[2,256,512]{2,1,0:T(8,128)(2,1)S(1)} %collective-permute-done.1.first_in), channel_id=1, source_target_pairs={{0,1},{1,0},{2,3},{3,2},{4,5},{5,4},{6,7},{7,6},{8,9},{9,8},{10,11... | collective-permute-start | bytes 1572872 | tf_op jit(solution)/shard_map/ppermute | solution.py:34
  13.8 2.1 %collective-permute-start.5 = (bf16[2,256,512]{2,1,0:T(8,128)(2,1)S(1)}, bf16[2,256,512]{2,1,0:T(8,128)(2,1)S(1)}, u32[]{:S(2)}, u32[]{:S(2)}) collective-permute-start(bf16[2,256,512]{2,1,0:T(8,128)(2,1)S(1)} %collective-permute-done.1.first_in), channel_id=1, source_target_pairs={{2,0},{5,1},{7,3},{6,4},{9,5},{11,7},{10,8},{13,9},{15,11},{14,12}... | collective-permute-start | bytes 1572872 | tf_op jit(solution)/shard_map/ppermute | solution.py:30
  15.9 1.6 %copy-done = bf16[4,512,512]{2,1,0:T(8,128)(2,1)S(1)} copy-done((bf16[4,512,512]{2,1,0:T(8,128)(2,1)S(1)}, bf16[4,512,512]{2,1,0:T(8,128)(2,1)}, u32[]{:S(2)}) %copy-start) | copy-done | bytes 2097176
  17.5 1.2 %copy-done.3 = bf16[2,512,512]{2,1,0:T(8,128)(2,1)S(1)} copy-done((bf16[2,512,512]{2,1,0:T(8,128)(2,1)S(1)}, bf16[2,512,512]{2,1,0:T(8,128)(2,1)}, u32[]{:S(2)}) %copy-start.3) | copy-done | bytes 1048600
  18.7 1.0 %copy-done.4 = bf16[1,1,1,512,512]{4,3,2,1,0:T(8,128)(2,1)S(1)} copy-done((bf16[1,1,1,512,512]{4,3,2,1,0:T(8,128)(2,1)S(1)}, bf16[1,1,1,512,512]{4,3,2,1,0:T(8,128)(2,1)}, u32[]{:S(2)}) %copy-start.4) | copy-done | bytes 524312
  19.7 3.5 %shift_tables.1 = (bf16[2,512,512]{2,1,0:T(8,128)(2,1)S(1)}, bf16[2,512,512]{2,1,0:T(8,128)(2,1)S(1)}, bf16[2,512,512]{2,1,0:T(8,128)(2,1)S(1)}, bf16[2,512,512]...) custom-call(s32[7]{0:T(128)S(1)} %concatenate.7.scalars, ...), custom_call_target="tpu_custom_call" | custom-call | tf_op jit(solution)/shard_map/shift_tables/pallas_call | solution.py:372
  23.3 2.3 %collective-permute-start.4 = (bf16[2,384,512]{2,1,0:T(8,128)(2,1)S(1)}, bf16[2,384,512]{2,1,0:T(8,128)(2,1)S(1)}, u32[]{:S(2)}, u32[]{:S(2)}) collective-permute-start(bf16[2,384,512]{2,1,0:T(8,128)(2,1)S(1)} %collective-permute-done.3.second), channel_id=1, source_target_pairs={{0,1},{1,0},{2,3},{3,2},{4,5},{5,4},{6,7},{7,6},{8,9},{9,8},{10,11... | collective-permute-start | bytes 2359304 | tf_op jit(solution)/shard_map/ppermute | solution.py:34
  25.6 1.6 %collective-permute-done.5.third = bf16[2,256,512]{2,1,0:T(8,128)(2,1)S(1)} collective-permute-done((bf16[2,256,512]{2,1,0:T(8,128)(2,1)S(1)}, bf16[2,256,512]{2,1,0:T(8,128)(2,1)S(1)}, u32[]{:S(2)}, u32[]{:S(2)}) %collective-permute-start.5) | collective-permute-done | bytes 524320 | tf_op jit(solution)/shard_map/ppermute | solution.py:30
  27.1 1.9 %collective-permute-done.6.third2 = bf16[2,256,512]{2,1,0:T(8,128)(2,1)S(1)} collective-permute-done((bf16[2,256,512]{2,1,0:T(8,128)(2,1)S(1)}, bf16[2,256,512]{2,1,0:T(8,128)(2,1)S(1)}, u32[]{:S(2)}, u32[]{:S(2)}) %collective-permute-start.6) | collective-permute-done | bytes 524320 | tf_op jit(solution)/shard_map/ppermute | solution.py:34
  29.1 5.3 %slot_terms.1 = (bf16[2,384,512]{2,1,0:T(8,128)(2,1)S(1)}, bf16[2,384,512]{2,1,0:T(8,128)(2,1)S(1)}, bf16[2,512,512]{2,1,0:T(8,128)(2,1)S(1)}) custom-call(s32[7]{0:T(128)S(1)} %concatenate.7.scalars, bf16[2,640,512]{2,1,0:T(8,128)(2,1)S(1)} %copy-done.2, bf16[2,256,512]{2,1,0:T(8,128)(2,1)S(1)} %get-tuple-element.44.first, ...), custom_call_target="tpu_custom_call" | custom-call | flops 6000000000 | bytes 20000000 | tf_op jit(solution)/shard_map/slot_terms/pallas_call | solution.py:389
  34.5 1.3 %probe_parts.1 = (bf16[2,4,2,128,128]{4,3,2,1,0:T(8,128)(2,1)S(1)}, bf16[2,4,2,128,128]{4,3,2,1,0:T(8,128)(2,1)S(1)}) custom-call(bf16[2,512,512]{2,1,0:T(8,128)(2,1)S(1)} %get-tuple-element.62.term, bf16[512,512]{1,0:T(8,128)(2,1)S(1)} %get-tuple-element.63.back_rows, bf16[512,256]{1,0:T(8,128)(2,1)S(1)} %get-tuple-element.64.back_cols, ...), custom_call_target="tpu_custom_call" | custom-call | tf_op jit(solution)/shard_map/probe_parts/pallas_call | solution.py:401
  36.7 0.9 %diag_part.1.diag = bf16[2,256,512]{2,1,0:T(8,128)(2,1)S(1)} custom-call(s32[7]{0:T(128)S(1)} %concatenate.7.scalars, bf16[2,4,2,128,128]{4,3,2,1,0:T(8,128)(2,1)S(1)} %get-tuple-element.66.refs_0_, bf16[2,384,512]{2,1,0:T(8,128)(2,1)S(1)} %get-tuple-element.67.refs_1_.kept.refs_0_, bf16[2,384,512]{2,1,0:T(8,128)(2,1)S(1)} %collective-permute-done.7.refs_2_.got.refs_1_), custom_call_target="tpu_custom_call" | custom-call | tf_op jit(solution)/shard_map/diag_part/pallas_call | solution.py:407
  37.6 1.3 %collective-permute-start.12 = (bf16[2,256,512]{2,1,0:T(8,128)(2,1)S(1)}, bf16[2,256,512]{2,1,0:T(8,128)(2,1)S(1)}, u32[]{:S(2)}, u32[]{:S(2)}) collective-permute-start(bf16[2,256,512]{2,1,0:T(8,128)(2,1)S(1)} %diag_part.1.diag), channel_id=1, source_target_pairs={{1,3},{0,4},{2,6},{5,7},{4,8},{6,10},{9,11},{8,12},{10,14},{13,15}... | collective-permute-start | bytes 1572872 | tf_op jit(solution)/shard_map/ppermute | solution.py:30
  38.9 0.7 probe_sum.1
  39.6 2.2 %collective-permute-start.9 = (bf16[4,2,128,128]{3,2,1,0:T(8,128)(2,1)S(1)}, bf16[4,2,128,128]{3,2,1,0:T(8,128)(2,1)S(1)}, u32[]{:S(2)}, u32[]{:S(2)}) collective-permute-start(bf16[4,2,128,128]{3,2,1,0:T(8,128)(2,1)S(1)} %get-tuple-element.71), channel_id=1, source_target_pairs={{0,2},{2,0},{1,3},{3,1},{4,6},{6,4},{5,7},{7,5},{8,10},{10,8},{9,1... | collective-permute-start | bytes 786440 | tf_op jit(solution)/shard_map/ppermute | solution.py:441
  41.7 1.0 %now_parts.1 = (bf16[2,256,512]{2,1,0:T(8,128)(2,1)S(1)}, bf16[2,128,512]{2,1,0:T(8,128)(2,1)S(1)}) custom-call(s32[7]{0:T(128)S(1)} %concatenate.7.scalars, bf16[4,2,128,128]{3,2,1,0:T(8,128)(2,1)S(1)} %get-tuple-element.70.refs_0_.before, bf16[2,384,512]{2,1,0:T(8,128)(2,1)S(1)} %get-tuple-element.67.refs_1_.kept.refs_0_, ...), custom_call_target="tpu_custom_call" | custom-call | tf_op jit(solution)/shard_map/now_parts/pallas_call | solution.py:430
  42.8 1.3 %collective-permute-start.10 = (bf16[2,256,512]{2,1,0:T(8,128)(2,1)S(1)}, bf16[2,256,512]{2,1,0:T(8,128)(2,1)S(1)}, u32[]{:S(2)}, u32[]{:S(2)}) collective-permute-start(bf16[2,256,512]{2,1,0:T(8,128)(2,1)S(1)} %get-tuple-element.72), channel_id=1, source_target_pairs={{1,3},{0,4},{2,6},{5,7},{4,8},{6,10},{9,11},{8,12},{10,14},{13,15}... | collective-permute-start | bytes 1572872 | tf_op jit(solution)/shard_map/ppermute | solution.py:30
  44.1 0.7 collective-permute-start.11
  44.8 5.9 %collective-permute-done.12.refs_2_ = bf16[2,256,512]{2,1,0:T(8,128)(2,1)S(1)} collective-permute-done((bf16[2,256,512]{2,1,0:T(8,128)(2,1)S(1)}, bf16[2,256,512]{2,1,0:T(8,128)(2,1)S(1)}, u32[]{:S(2)}, u32[]{:S(2)}) %collective-permute-start.12) | collective-permute-done | bytes 524320 | tf_op jit(solution)/shard_map/ppermute | solution.py:30
  50.6 0.9 %later_part.1 = bf16[2,256,512]{2,1,0:T(8,128)(2,1)S(1)} custom-call(s32[7]{0:T(128)S(1)} %concatenate.7.scalars, bf16[2,384,512]{2,1,0:T(8,128)(2,1)S(1)} %get-tuple-element.67.refs_1_.kept.refs_0_, bf16[2,384,512]{2,1,0:T(8,128)(2,1)S(1)} %collective-permute-done.7.refs_2_.got.refs_1_, bf16[2,256,512]{2,1,0:T(8,128)(2,1)S(1)} %collective-permute-done.12.refs_2_), custom_call_target="tpu_custom_call" | custom-call | tf_op jit(solution)/shard_map/later_part/pallas_call | solution.py:407
  51.5 1.9 %collective-permute-start.13 = (bf16[2,256,512]{2,1,0:T(8,128)(2,1)S(1)}, bf16[2,256,512]{2,1,0:T(8,128)(2,1)S(1)}, u32[]{:S(2)}, u32[]{:S(2)}) collective-permute-start(bf16[2,256,512]{2,1,0:T(8,128)(2,1)S(1)} %later_part.1), channel_id=1, source_target_pairs={{1,5},{0,2},{3,7},{5,9},{4,6},{7,11},{9,13},{8,10},{11,15},{12,14}... | collective-permute-start | bytes 1572872 | tf_op jit(solution)/shard_map/ppermute | solution.py:30
  53.6 2.6 %collective-permute-start.17 = (bf16[2,128,128]{2,1,0:T(8,128)(2,1)S(1)}, bf16[2,128,128]{2,1,0:T(8,128)(2,1)S(1)}, u32[]{:S(2)}, u32[]{:S(2)}) collective-permute-start(bf16[2,128,128]{2,1,0:T(8,128)(2,1)S(1)} %get-tuple-element.77), channel_id=1, source_target_pairs={{0,8},{4,12},{8,0},{12,4},{1,9},{5,13},{9,1},{13,5},{2,10},{6,14},... | collective-permute-start | bytes 196616 | tf_op jit(solution)/shard_map/ppermute | solution.py:340
  56.3 7.0 %collective-permute-done.10.upper = bf16[2,256,512]{2,1,0:T(8,128)(2,1)S(1)} collective-permute-done((bf16[2,256,512]{2,1,0:T(8,128)(2,1)S(1)}, bf16[2,256,512]{2,1,0:T(8,128)(2,1)S(1)}, u32[]{:S(2)}, u32[]{:S(2)}) %collective-permute-start.10) | collective-permute-done | bytes 524320 | tf_op jit(solution)/shard_map/ppermute | solution.py:30
  63.3 1.1 %own_part.1 = bf16[2,384,512]{2,1,0:T(8,128)(2,1)S(1)} custom-call(s32[7]{0:T(128)S(1)} %concatenate.7.scalars, bf16[4,2,128,128]{3,2,1,0:T(8,128)(2,1)S(1)} %sum.1.before, bf16[2,384,512]{2,1,0:T(8,128)(2,1)S(1)} %get-tuple-element.67.refs_1_.kept.refs_0_, bf16[2,384,512]{2,1,0:T(8,128)(2,1)S(1)} %collective-permute-done.7.refs_2_.got.refs_1_, ...), custom_call_target="tpu_custom_call" | custom-call | flops 1000000000 | tf_op jit(solution)/shard_map/own_part/pallas_call | solution.py:455
  65.0 0.8 %collective-permute-done.17.refs_2_ = bf16[2,128,128]{2,1,0:T(8,128)(2,1)S(1)} collective-permute-done((bf16[2,128,128]{2,1,0:T(8,128)(2,1)S(1)}, bf16[2,128,128]{2,1,0:T(8,128)(2,1)S(1)}, u32[]{:S(2)}, u32[]{:S(2)}) %collective-permute-start.17) | collective-permute-done | bytes 65568 | tf_op jit(solution)/shard_map/ppermute | solution.py:340
  65.8 1.9 %collective-permute-done.18.refs_3_ = bf16[2,128,128]{2,1,0:T(8,128)(2,1)S(1)} collective-permute-done((bf16[2,128,128]{2,1,0:T(8,128)(2,1)S(1)}, bf16[2,128,128]{2,1,0:T(8,128)(2,1)S(1)}, u32[]{:S(2)}, u32[]{:S(2)}) %collective-permute-start.18) | collective-permute-done | bytes 65568 | tf_op jit(solution)/shard_map/ppermute | solution.py:340
  67.8 0.7 probe_grad.1
  68.9 1.1 %pad_maximum_fusion = bf16[2,640,512]{2,1,0:T(8,128)(2,1)} fusion(bf16[2,128,512]{2,1,0:T(8,128)(2,1)S(1)} %slice_select_fusion, bf16[2,256,512]{2,1,0:T(8,128)(2,1)S(1)} %get-tuple-element.75, bf16[2,256,512]{2,1,0:T(8,128)(2,1)S(1)} %get-tuple-element.74), kind=kLoop, calls=%fused_computation | loop fusion | flops 3932160 | bytes 2621440 | tf_op jit(solution)/shard_map/concatenate | solution.py:466
  (33 shorter events, 3.4 us)
Async XLA Ops:
  0.6 1.3 %copy-start.1 = (bf16[2,640,512]{2,1,0:T(8,128)(2,1)S(1)}, bf16[2,640,512]{2,1,0:T(8,128)(2,1)}, u32[]{:S(2)}) copy-start(bf16[2,640,512]{2,1,0:T(8,128)(2,1)} %own.1) | copy-start | bytes 3932164
  2.0 8.3 %collective-permute-start.1 = (bf16[2,256,512]{2,1,0:T(8,128)(2,1)S(1)}, bf16[2,256,512]{2,1,0:T(8,128)(2,1)S(1)}, u32[]{:S(2)}, u32[]{:S(2)}) collective-permute-start(bf16[2,256,512]{2,1,0:T(8,128)(2,1)S(1)} %get-tuple-element.38), channel_id=1, source_target_pairs={{3,1},{4,0},{7,5},{6,2},{8,4},{11,9},{10,6},{12,8},{15,13},{14,10}... | collective-permute-start | bytes 1572872 | tf_op jit(solution)/shard_map/ppermute | solution.py:30
  4.2 19.1 %collective-permute-start.3 = (bf16[2,384,512]{2,1,0:T(8,128)(2,1)S(1)}, bf16[2,384,512]{2,1,0:T(8,128)(2,1)S(1)}, u32[]{:S(2)}, u32[]{:S(2)}) collective-permute-start(bf16[2,384,512]{2,1,0:T(8,128)(2,1)S(1)} %get-tuple-element.45), channel_id=1, source_target_pairs={{3,1},{4,0},{7,5},{6,2},{8,4},{11,9},{10,6},{12,8},{15,13},{14,10}... | collective-permute-start | bytes 2359304 | tf_op jit(solution)/shard_map/ppermute | solution.py:30
  7.0 2.7 %collective-permute-start = (s32[2]{0:T(128)S(1)}, s32[2]{0:T(128)S(1)}, u32[]{:S(2)}, u32[]{:S(2)}) collective-permute-start(s32[2]{0:T(128)S(1)} %pad_add_fusion), channel_id=1, source_target_pairs={{0,1},{1,0},{2,3},{3,2},{4,5},{5,4},{6,7},{7,6},{8,9},{9,8},{10,11... | collective-permute-start | bytes 32 | tf_op jit(solution)/shard_map/ppermute | solution.py:34
  10.3 5.6 %collective-permute-start.2 = (bf16[2,256,512]{2,1,0:T(8,128)(2,1)S(1)}, bf16[2,256,512]{2,1,0:T(8,128)(2,1)S(1)}, u32[]{:S(2)}, u32[]{:S(2)}) collective-permute-start(bf16[2,256,512]{2,1,0:T(8,128)(2,1)S(1)} %collective-permute-done.1.first_in), channel_id=1, source_target_pairs={{0,1},{1,0},{2,3},{3,2},{4,5},{5,4},{6,7},{7,6},{8,9},{9,8},{10,11... | collective-permute-start | bytes 1572872 | tf_op jit(solution)/shard_map/ppermute | solution.py:34
  13.8 13.4 %collective-permute-start.5 = (bf16[2,256,512]{2,1,0:T(8,128)(2,1)S(1)}, bf16[2,256,512]{2,1,0:T(8,128)(2,1)S(1)}, u32[]{:S(2)}, u32[]{:S(2)}) collective-permute-start(bf16[2,256,512]{2,1,0:T(8,128)(2,1)S(1)} %collective-permute-done.1.first_in), channel_id=1, source_target_pairs={{2,0},{5,1},{7,3},{6,4},{9,5},{11,7},{10,8},{13,9},{15,11},{14,12}... | collective-permute-start | bytes 1572872 | tf_op jit(solution)/shard_map/ppermute | solution.py:30
  15.9 1.6 %copy-start = (bf16[4,512,512]{2,1,0:T(8,128)(2,1)S(1)}, bf16[4,512,512]{2,1,0:T(8,128)(2,1)}, u32[]{:S(2)}) copy-start(bf16[4,512,512]{2,1,0:T(8,128)(2,1)} %constant.32.clone.dft) | copy-start | bytes 6291460
  17.5 1.2 %copy-start.3 = (bf16[2,512,512]{2,1,0:T(8,128)(2,1)S(1)}, bf16[2,512,512]{2,1,0:T(8,128)(2,1)}, u32[]{:S(2)}) copy-start(bf16[2,512,512]{2,1,0:T(8,128)(2,1)} %probe_in) | copy-start | bytes 3145732
  18.7 1.0 %copy-start.4 = (bf16[1,1,1,512,512]{4,3,2,1,0:T(8,128)(2,1)S(1)}, bf16[1,1,1,512,512]{4,3,2,1,0:T(8,128)(2,1)}, u32[]{:S(2)}) copy-start(bf16[1,1,1,512,512]{4,3,2,1,0:T(8,128)(2,1)} %param.9) | copy-start | bytes 1572868
  19.7 9.3 %copy-start.2 = (bf16[2,640,512]{2,1,0:T(8,128)(2,1)S(1)}, bf16[2,640,512]{2,1,0:T(8,128)(2,1)}, u32[]{:S(2)}) copy-start(bf16[2,640,512]{2,1,0:T(8,128)(2,1)} %own.1) | copy-start | bytes 3932164
  23.3 5.8 %collective-permute-start.4 = (bf16[2,384,512]{2,1,0:T(8,128)(2,1)S(1)}, bf16[2,384,512]{2,1,0:T(8,128)(2,1)S(1)}, u32[]{:S(2)}, u32[]{:S(2)}) collective-permute-start(bf16[2,384,512]{2,1,0:T(8,128)(2,1)S(1)} %collective-permute-done.3.second), channel_id=1, source_target_pairs={{0,1},{1,0},{2,3},{3,2},{4,5},{5,4},{6,7},{7,6},{8,9},{9,8},{10,11... | collective-permute-start | bytes 2359304 | tf_op jit(solution)/shard_map/ppermute | solution.py:34
  27.1 1.9 %collective-permute-start.6 = (bf16[2,256,512]{2,1,0:T(8,128)(2,1)S(1)}, bf16[2,256,512]{2,1,0:T(8,128)(2,1)S(1)}, u32[]{:S(2)}, u32[]{:S(2)}) collective-permute-start(bf16[2,256,512]{2,1,0:T(8,128)(2,1)S(1)} %collective-permute-done.5.third), channel_id=1, source_target_pairs={{0,1},{1,0},{2,3},{3,2},{4,5},{5,4},{6,7},{7,6},{8,9},{9,8},{10,11... | collective-permute-start | bytes 1572872 | tf_op jit(solution)/shard_map/ppermute | solution.py:34
  34.4 2.4 %collective-permute-start.7 = (bf16[2,384,512]{2,1,0:T(8,128)(2,1)S(1)}, bf16[2,384,512]{2,1,0:T(8,128)(2,1)S(1)}, u32[]{:S(2)}, u32[]{:S(2)}) collective-permute-start(bf16[2,384,512]{2,1,0:T(8,128)(2,1)S(1)} %get-tuple-element.68), channel_id=1, source_target_pairs={{0,1},{1,0},{2,3},{3,2},{4,5},{5,4},{6,7},{7,6},{8,9},{9,8},{10,11... | collective-permute-start | bytes 2359304 | tf_op jit(solution)/shard_map/ppermute | solution.py:34
  35.8 3.1 %collective-permute-start.8 = (bf16[2,4,2,128,128]{4,3,2,1,0:T(8,128)(2,1)S(1)}, bf16[2,4,2,128,128]{4,3,2,1,0:T(8,128)(2,1)S(1)}, u32[]{:S(2)}, u32[]{:S(2)}) collective-permute-start(bf16[2,4,2,128,128]{4,3,2,1,0:T(8,128)(2,1)S(1)} %get-tuple-element.66.refs_0_), channel_id=1, source_target_pairs={{0,1},{1,0},{2,3},{3,2},{4,5},{5,4},{6,7},{7,6},{8,9},{9,8},{10,11... | collective-permute-start | bytes 1572872 | tf_op jit(solution)/shard_map/ppermute | solution.py:34
  37.6 13.0 %collective-permute-start.12 = (bf16[2,256,512]{2,1,0:T(8,128)(2,1)S(1)}, bf16[2,256,512]{2,1,0:T(8,128)(2,1)S(1)}, u32[]{:S(2)}, u32[]{:S(2)}) collective-permute-start(bf16[2,256,512]{2,1,0:T(8,128)(2,1)S(1)} %diag_part.1.diag), channel_id=1, source_target_pairs={{1,3},{0,4},{2,6},{5,7},{4,8},{6,10},{9,11},{8,12},{10,14},{13,15}... | collective-permute-start | bytes 1572872 | tf_op jit(solution)/shard_map/ppermute | solution.py:30
  39.6 13.8 %collective-permute-start.9 = (bf16[4,2,128,128]{3,2,1,0:T(8,128)(2,1)S(1)}, bf16[4,2,128,128]{3,2,1,0:T(8,128)(2,1)S(1)}, u32[]{:S(2)}, u32[]{:S(2)}) collective-permute-start(bf16[4,2,128,128]{3,2,1,0:T(8,128)(2,1)S(1)} %get-tuple-element.71), channel_id=1, source_target_pairs={{0,2},{2,0},{1,3},{3,1},{4,6},{6,4},{5,7},{7,5},{8,10},{10,8},{9,1... | collective-permute-start | bytes 786440 | tf_op jit(solution)/shard_map/ppermute | solution.py:441
  42.8 20.5 %collective-permute-start.10 = (bf16[2,256,512]{2,1,0:T(8,128)(2,1)S(1)}, bf16[2,256,512]{2,1,0:T(8,128)(2,1)S(1)}, u32[]{:S(2)}, u32[]{:S(2)}) collective-permute-start(bf16[2,256,512]{2,1,0:T(8,128)(2,1)S(1)} %get-tuple-element.72), channel_id=1, source_target_pairs={{1,3},{0,4},{2,6},{5,7},{4,8},{6,10},{9,11},{8,12},{10,14},{13,15}... | collective-permute-start | bytes 1572872 | tf_op jit(solution)/shard_map/ppermute | solution.py:30
  44.1 12.2 %collective-permute-start.11 = (bf16[2,128,512]{2,1,0:T(8,128)(2,1)S(1)}, bf16[2,128,512]{2,1,0:T(8,128)(2,1)S(1)}, u32[]{:S(2)}, u32[]{:S(2)}) collective-permute-start(bf16[2,128,512]{2,1,0:T(8,128)(2,1)S(1)} %get-tuple-element.73), channel_id=1, source_target_pairs={{0,4},{2,6},{4,8},{6,10},{8,12},{10,14},{16,20},{18,22},{20,24},{2... | collective-permute-start | bytes 786440 | tf_op jit(solution)/shard_map/ppermute | solution.py:30
  51.5 13.5 %collective-permute-start.13 = (bf16[2,256,512]{2,1,0:T(8,128)(2,1)S(1)}, bf16[2,256,512]{2,1,0:T(8,128)(2,1)S(1)}, u32[]{:S(2)}, u32[]{:S(2)}) collective-permute-start(bf16[2,256,512]{2,1,0:T(8,128)(2,1)S(1)} %later_part.1), channel_id=1, source_target_pairs={{1,5},{0,2},{3,7},{5,9},{4,6},{7,11},{9,13},{8,10},{11,15},{12,14}... | collective-permute-start | bytes 1572872 | tf_op jit(solution)/shard_map/ppermute | solution.py:30
  53.5 11.5 %collective-permute-start.16 = (bf16[2,128,128]{2,1,0:T(8,128)(2,1)S(1)}, bf16[2,128,128]{2,1,0:T(8,128)(2,1)S(1)}, u32[]{:S(2)}, u32[]{:S(2)}) collective-permute-start(bf16[2,128,128]{2,1,0:T(8,128)(2,1)S(1)} %get-tuple-element.78), channel_id=1, source_target_pairs={{0,4},{4,0},{8,12},{12,8},{1,5},{5,1},{9,13},{13,9},{2,6},{6,2},{1... | collective-permute-start | bytes 196616 | tf_op jit(solution)/shard_map/ppermute | solution.py:340
  53.6 12.2 %collective-permute-start.17 = (bf16[2,128,128]{2,1,0:T(8,128)(2,1)S(1)}, bf16[2,128,128]{2,1,0:T(8,128)(2,1)S(1)}, u32[]{:S(2)}, u32[]{:S(2)}) collective-permute-start(bf16[2,128,128]{2,1,0:T(8,128)(2,1)S(1)} %get-tuple-element.77), channel_id=1, source_target_pairs={{0,8},{4,12},{8,0},{12,4},{1,9},{5,13},{9,1},{13,5},{2,10},{6,14},... | collective-permute-start | bytes 196616 | tf_op jit(solution)/shard_map/ppermute | solution.py:340
  56.2 11.5 %collective-permute-start.18 = (bf16[2,128,128]{2,1,0:T(8,128)(2,1)S(1)}, bf16[2,128,128]{2,1,0:T(8,128)(2,1)S(1)}, u32[]{:S(2)}, u32[]{:S(2)}) collective-permute-start(bf16[2,128,128]{2,1,0:T(8,128)(2,1)S(1)} %get-tuple-element.76), channel_id=1, source_target_pairs={{0,12},{4,8},{8,4},{12,0},{1,13},{5,9},{9,5},{13,1},{2,14},{6,10},... | collective-permute-start | bytes 196616 | tf_op jit(solution)/shard_map/ppermute | solution.py:340
  64.3 4.1 %collective-permute-start.14 = (bf16[2,384,512]{2,1,0:T(8,128)(2,1)S(1)}, bf16[2,384,512]{2,1,0:T(8,128)(2,1)S(1)}, u32[]{:S(2)}, u32[]{:S(2)}) collective-permute-start(bf16[2,384,512]{2,1,0:T(8,128)(2,1)S(1)} %own_part.1), channel_id=1, source_target_pairs={{0,1},{1,0},{2,3},{3,2},{4,5},{5,4},{6,7},{7,6},{8,9},{9,8},{10,11... | collective-permute-start | bytes 2359304 | tf_op jit(solution)/shard_map/ppermute | solution.py:34
  65.0 3.5 %collective-permute-start.15 = (bf16[2,256,512]{2,1,0:T(8,128)(2,1)S(1)}, bf16[2,256,512]{2,1,0:T(8,128)(2,1)S(1)}, u32[]{:S(2)}, u32[]{:S(2)}) collective-permute-start(bf16[2,256,512]{2,1,0:T(8,128)(2,1)S(1)} %collective-permute-done.13), channel_id=1, source_target_pairs={{0,1},{1,0},{2,3},{3,2},{4,5},{5,4},{6,7},{7,6},{8,9},{9,8},{10,11... | collective-permute-start | bytes 1572872 | tf_op jit(solution)/shard_map/ppermute | solution.py:34

commit v9 on v6

--- a/solution.py
+++ b/solution.py
@@ -388,7 +388,7 @@
         slot_terms,
         (shape(2, count, cols), shape(2, count, cols), table),
         [SMEM] + [VMEM] * 13,
-        18,
+        24,
         scratch=[pltpu.VMEM((2, size, size), BF16)] * 5
         + [pltpu.VMEM((2, rows, size), BF16)],
         flops=6 * 10**9,

time: 70.4 us -> 70.4 us (level)
  no operation moved by 1% of the time
where the time goes in v9:
time: 70.4 us; the launch traced here: 70 us
  starting transfers between devices  24.1 us (34%)
  waiting for transfers between devices  20.8 us (30%)
  Pallas kernels  15.4 us (22%)
  local copies, waits for them, and re-layouts  5.28 us (7%)
  between operations  2.79 us (4%)
  other arithmetic  1.6 us (2%)
    ppermute x7, waiting for transfers between devices, to_neighbour(): return lax.ppermute(x, ('wide', 'narrow', 'probe'), pairs)  15.6 us
    ppermute x7, starting transfers between devices, to_neighbour(): return lax.ppermute(x, ('wide', 'narrow', 'probe'), pairs)  10.8 us
    ppermute x8, starting transfers between devices, swap(): return lax.ppermute(x, 'probe', [(0, 1), (1, 0)])  8.44 us
    pallas_call x1, Pallas kernels, shards(): call(slot_terms, (shape(2, count, cols), shape(2, count, cols), table), [...  5.28 us
    unnamed x10, local copies, waits for them, and re-layouts  5.17 us
    pallas_call x1, Pallas kernels, shards(): call(functools.partial(shift_tables, width), (table,) * 5 + (shape(size,...  3.55 us
    ppermute x3, waiting for transfers between devices, scatter_parts(): terms.append(lax.ppermute(part(to), axis, pairs))  2.71 us
    ppermute x3, starting transfers between devices, scatter_parts(): terms.append(lax.ppermute(part(to), axis, pairs))  2.71 us
  transfers between devices with their start and end apart: 19, of which 10 were waited for; matrix products, arithmetic and copies ran while one was open for 0% of the time, Pallas kernels for 14%

profile of v9, /device:TPU:19, one launch (start us, length us, event | category | flops | bytes accessed | tf_op | source)
XLA Modules:
  0.0 70.0 jit_solution(14444419983163980842)
XLA Ops:
  0.6 1.3 %copy-done.1 = bf16[2,640,512]{2,1,0:T(8,128)(2,1)S(1)} copy-done((bf16[2,640,512]{2,1,0:T(8,128)(2,1)S(1)}, bf16[2,640,512]{2,1,0:T(8,128)(2,1)}, u32[]{:S(2)}) %copy-start.1) | copy-done | bytes 1310744
  2.0 2.2 %collective-permute-start.1 = (bf16[2,256,512]{2,1,0:T(8,128)(2,1)S(1)}, bf16[2,256,512]{2,1,0:T(8,128)(2,1)S(1)}, u32[]{:S(2)}, u32[]{:S(2)}) collective-permute-start(bf16[2,256,512]{2,1,0:T(8,128)(2,1)S(1)} %get-tuple-element.38), channel_id=1, source_target_pairs={{3,1},{4,0},{7,5},{6,2},{8,4},{11,9},{10,6},{12,8},{15,13},{14,10}... | collective-permute-start | bytes 1572872 | tf_op jit(solution)/shard_map/ppermute | solution.py:30
  4.2 1.3 %collective-permute-start.3 = (bf16[2,384,512]{2,1,0:T(8,128)(2,1)S(1)}, bf16[2,384,512]{2,1,0:T(8,128)(2,1)S(1)}, u32[]{:S(2)}, u32[]{:S(2)}) collective-permute-start(bf16[2,384,512]{2,1,0:T(8,128)(2,1)S(1)} %get-tuple-element.45), channel_id=1, source_target_pairs={{3,1},{4,0},{7,5},{6,2},{8,4},{11,9},{10,6},{12,8},{15,13},{14,10}... | collective-permute-start | bytes 2359304 | tf_op jit(solution)/shard_map/ppermute | solution.py:30
  7.0 1.9 %collective-permute-start = (s32[2]{0:T(128)S(1)}, s32[2]{0:T(128)S(1)}, u32[]{:S(2)}, u32[]{:S(2)}) collective-permute-start(s32[2]{0:T(128)S(1)} %pad_add_fusion), channel_id=1, source_target_pairs={{0,1},{1,0},{2,3},{3,2},{4,5},{5,4},{6,7},{7,6},{8,9},{9,8},{10,11... | collective-permute-start | bytes 32 | tf_op jit(solution)/shard_map/ppermute | solution.py:34
  10.3 3.5 %collective-permute-start.2 = (bf16[2,256,512]{2,1,0:T(8,128)(2,1)S(1)}, bf16[2,256,512]{2,1,0:T(8,128)(2,1)S(1)}, u32[]{:S(2)}, u32[]{:S(2)}) collective-permute-start(bf16[2,256,512]{2,1,0:T(8,128)(2,1)S(1)} %collective-permute-done.1.first_in), channel_id=1, source_target_pairs={{0,1},{1,0},{2,3},{3,2},{4,5},{5,4},{6,7},{7,6},{8,9},{9,8},{10,11... | collective-permute-start | bytes 1572872 | tf_op jit(solution)/shard_map/ppermute | solution.py:34
  13.8 2.1 %collective-permute-start.5 = (bf16[2,256,512]{2,1,0:T(8,128)(2,1)S(1)}, bf16[2,256,512]{2,1,0:T(8,128)(2,1)S(1)}, u32[]{:S(2)}, u32[]{:S(2)}) collective-permute-start(bf16[2,256,512]{2,1,0:T(8,128)(2,1)S(1)} %collective-permute-done.1.first_in), channel_id=1, source_target_pairs={{2,0},{5,1},{7,3},{6,4},{9,5},{11,7},{10,8},{13,9},{15,11},{14,12}... | collective-permute-start | bytes 1572872 | tf_op jit(solution)/shard_map/ppermute | solution.py:30
  15.9 1.6 %copy-done = bf16[4,512,512]{2,1,0:T(8,128)(2,1)S(1)} copy-done((bf16[4,512,512]{2,1,0:T(8,128)(2,1)S(1)}, bf16[4,512,512]{2,1,0:T(8,128)(2,1)}, u32[]{:S(2)}) %copy-start) | copy-done | bytes 2097176
  17.5 1.2 %copy-done.3 = bf16[2,512,512]{2,1,0:T(8,128)(2,1)S(1)} copy-done((bf16[2,512,512]{2,1,0:T(8,128)(2,1)S(1)}, bf16[2,512,512]{2,1,0:T(8,128)(2,1)}, u32[]{:S(2)}) %copy-start.3) | copy-done | bytes 1048600
  18.7 1.0 %copy-done.4 = bf16[1,1,1,512,512]{4,3,2,1,0:T(8,128)(2,1)S(1)} copy-done((bf16[1,1,1,512,512]{4,3,2,1,0:T(8,128)(2,1)S(1)}, bf16[1,1,1,512,512]{4,3,2,1,0:T(8,128)(2,1)}, u32[]{:S(2)}) %copy-start.4) | copy-done | bytes 524312
  19.7 3.5 %shift_tables.1 = (bf16[2,512,512]{2,1,0:T(8,128)(2,1)S(1)}, bf16[2,512,512]{2,1,0:T(8,128)(2,1)S(1)}, bf16[2,512,512]{2,1,0:T(8,128)(2,1)S(1)}, bf16[2,512,512]...) custom-call(s32[7]{0:T(128)S(1)} %concatenate.7.scalars, ...), custom_call_target="tpu_custom_call" | custom-call | tf_op jit(solution)/shard_map/shift_tables/pallas_call | solution.py:370
  23.3 2.3 %collective-permute-start.4 = (bf16[2,384,512]{2,1,0:T(8,128)(2,1)S(1)}, bf16[2,384,512]{2,1,0:T(8,128)(2,1)S(1)}, u32[]{:S(2)}, u32[]{:S(2)}) collective-permute-start(bf16[2,384,512]{2,1,0:T(8,128)(2,1)S(1)} %collective-permute-done.3.second), channel_id=1, source_target_pairs={{0,1},{1,0},{2,3},{3,2},{4,5},{5,4},{6,7},{7,6},{8,9},{9,8},{10,11... | collective-permute-start | bytes 2359304 | tf_op jit(solution)/shard_map/ppermute | solution.py:34
  25.6 1.6 %collective-permute-done.5.third = bf16[2,256,512]{2,1,0:T(8,128)(2,1)S(1)} collective-permute-done((bf16[2,256,512]{2,1,0:T(8,128)(2,1)S(1)}, bf16[2,256,512]{2,1,0:T(8,128)(2,1)S(1)}, u32[]{:S(2)}, u32[]{:S(2)}) %collective-permute-start.5) | collective-permute-done | bytes 524320 | tf_op jit(solution)/shard_map/ppermute | solution.py:30
  27.1 1.9 %collective-permute-done.6.third2 = bf16[2,256,512]{2,1,0:T(8,128)(2,1)S(1)} collective-permute-done((bf16[2,256,512]{2,1,0:T(8,128)(2,1)S(1)}, bf16[2,256,512]{2,1,0:T(8,128)(2,1)S(1)}, u32[]{:S(2)}, u32[]{:S(2)}) %collective-permute-start.6) | collective-permute-done | bytes 524320 | tf_op jit(solution)/shard_map/ppermute | solution.py:34
  29.1 5.3 %slot_terms.1 = (bf16[2,384,512]{2,1,0:T(8,128)(2,1)S(1)}, bf16[2,384,512]{2,1,0:T(8,128)(2,1)S(1)}, bf16[2,512,512]{2,1,0:T(8,128)(2,1)S(1)}) custom-call(s32[7]{0:T(128)S(1)} %concatenate.7.scalars, bf16[2,640,512]{2,1,0:T(8,128)(2,1)S(1)} %copy-done.2, bf16[2,256,512]{2,1,0:T(8,128)(2,1)S(1)} %get-tuple-element.44.first, ...), custom_call_target="tpu_custom_call" | custom-call | flops 6000000000 | bytes 20000000 | tf_op jit(solution)/shard_map/slot_terms/pallas_call | solution.py:387
  34.5 1.3 %probe_parts.1 = (bf16[2,4,2,128,128]{4,3,2,1,0:T(8,128)(2,1)S(1)}, bf16[2,4,2,128,128]{4,3,2,1,0:T(8,128)(2,1)S(1)}) custom-call(bf16[2,512,512]{2,1,0:T(8,128)(2,1)S(1)} %get-tuple-element.62.term, bf16[512,512]{1,0:T(8,128)(2,1)S(1)} %get-tuple-element.63.back_rows, bf16[512,256]{1,0:T(8,128)(2,1)S(1)} %get-tuple-element.64.back_cols, ...), custom_call_target="tpu_custom_call" | custom-call | tf_op jit(solution)/shard_map/probe_parts/pallas_call | solution.py:399
  36.7 0.9 %diag_part.1.diag = bf16[2,256,512]{2,1,0:T(8,128)(2,1)S(1)} custom-call(s32[7]{0:T(128)S(1)} %concatenate.7.scalars, bf16[2,4,2,128,128]{4,3,2,1,0:T(8,128)(2,1)S(1)} %get-tuple-element.66.refs_0_, bf16[2,384,512]{2,1,0:T(8,128)(2,1)S(1)} %get-tuple-element.67.refs_1_.kept.refs_0_, bf16[2,384,512]{2,1,0:T(8,128)(2,1)S(1)} %collective-permute-done.7.refs_2_.got.refs_1_), custom_call_target="tpu_custom_call" | custom-call | tf_op jit(solution)/shard_map/diag_part/pallas_call | solution.py:405
  37.6 1.3 %collective-permute-start.12 = (bf16[2,256,512]{2,1,0:T(8,128)(2,1)S(1)}, bf16[2,256,512]{2,1,0:T(8,128)(2,1)S(1)}, u32[]{:S(2)}, u32[]{:S(2)}) collective-permute-start(bf16[2,256,512]{2,1,0:T(8,128)(2,1)S(1)} %diag_part.1.diag), channel_id=1, source_target_pairs={{1,3},{0,4},{2,6},{5,7},{4,8},{6,10},{9,11},{8,12},{10,14},{13,15}... | collective-permute-start | bytes 1572872 | tf_op jit(solution)/shard_map/ppermute | solution.py:30
  38.9 0.7 probe_sum.1
  39.6 2.2 %collective-permute-start.9 = (bf16[4,2,128,128]{3,2,1,0:T(8,128)(2,1)S(1)}, bf16[4,2,128,128]{3,2,1,0:T(8,128)(2,1)S(1)}, u32[]{:S(2)}, u32[]{:S(2)}) collective-permute-start(bf16[4,2,128,128]{3,2,1,0:T(8,128)(2,1)S(1)} %get-tuple-element.71), channel_id=1, source_target_pairs={{0,2},{2,0},{1,3},{3,1},{4,6},{6,4},{5,7},{7,5},{8,10},{10,8},{9,1... | collective-permute-start | bytes 786440 | tf_op jit(solution)/shard_map/ppermute | solution.py:439
  41.7 1.0 %now_parts.1 = (bf16[2,256,512]{2,1,0:T(8,128)(2,1)S(1)}, bf16[2,128,512]{2,1,0:T(8,128)(2,1)S(1)}) custom-call(s32[7]{0:T(128)S(1)} %concatenate.7.scalars, bf16[4,2,128,128]{3,2,1,0:T(8,128)(2,1)S(1)} %get-tuple-element.70.refs_0_.before, bf16[2,384,512]{2,1,0:T(8,128)(2,1)S(1)} %get-tuple-element.67.refs_1_.kept.refs_0_, ...), custom_call_target="tpu_custom_call" | custom-call | tf_op jit(solution)/shard_map/now_parts/pallas_call | solution.py:428
  42.8 1.3 %collective-permute-start.10 = (bf16[2,256,512]{2,1,0:T(8,128)(2,1)S(1)}, bf16[2,256,512]{2,1,0:T(8,128)(2,1)S(1)}, u32[]{:S(2)}, u32[]{:S(2)}) collective-permute-start(bf16[2,256,512]{2,1,0:T(8,128)(2,1)S(1)} %get-tuple-element.72), channel_id=1, source_target_pairs={{1,3},{0,4},{2,6},{5,7},{4,8},{6,10},{9,11},{8,12},{10,14},{13,15}... | collective-permute-start | bytes 1572872 | tf_op jit(solution)/shard_map/ppermute | solution.py:30
  44.1 0.7 collective-permute-start.11
  44.7 5.9 %collective-permute-done.12.refs_2_ = bf16[2,256,512]{2,1,0:T(8,128)(2,1)S(1)} collective-permute-done((bf16[2,256,512]{2,1,0:T(8,128)(2,1)S(1)}, bf16[2,256,512]{2,1,0:T(8,128)(2,1)S(1)}, u32[]{:S(2)}, u32[]{:S(2)}) %collective-permute-start.12) | collective-permute-done | bytes 524320 | tf_op jit(solution)/shard_map/ppermute | solution.py:30
  50.6 0.9 %later_part.1 = bf16[2,256,512]{2,1,0:T(8,128)(2,1)S(1)} custom-call(s32[7]{0:T(128)S(1)} %concatenate.7.scalars, bf16[2,384,512]{2,1,0:T(8,128)(2,1)S(1)} %get-tuple-element.67.refs_1_.kept.refs_0_, bf16[2,384,512]{2,1,0:T(8,128)(2,1)S(1)} %collective-permute-done.7.refs_2_.got.refs_1_, bf16[2,256,512]{2,1,0:T(8,128)(2,1)S(1)} %collective-permute-done.12.refs_2_), custom_call_target="tpu_custom_call" | custom-call | tf_op jit(solution)/shard_map/later_part/pallas_call | solution.py:405
  51.5 1.9 %collective-permute-start.13 = (bf16[2,256,512]{2,1,0:T(8,128)(2,1)S(1)}, bf16[2,256,512]{2,1,0:T(8,128)(2,1)S(1)}, u32[]{:S(2)}, u32[]{:S(2)}) collective-permute-start(bf16[2,256,512]{2,1,0:T(8,128)(2,1)S(1)} %later_part.1), channel_id=1, source_target_pairs={{1,5},{0,2},{3,7},{5,9},{4,6},{7,11},{9,13},{8,10},{11,15},{12,14}... | collective-permute-start | bytes 1572872 | tf_op jit(solution)/shard_map/ppermute | solution.py:30
  53.6 2.6 %collective-permute-start.17 = (bf16[2,128,128]{2,1,0:T(8,128)(2,1)S(1)}, bf16[2,128,128]{2,1,0:T(8,128)(2,1)S(1)}, u32[]{:S(2)}, u32[]{:S(2)}) collective-permute-start(bf16[2,128,128]{2,1,0:T(8,128)(2,1)S(1)} %get-tuple-element.77), channel_id=1, source_target_pairs={{0,8},{4,12},{8,0},{12,4},{1,9},{5,13},{9,1},{13,5},{2,10},{6,14},... | collective-permute-start | bytes 196616 | tf_op jit(solution)/shard_map/ppermute | solution.py:338
  56.2 7.0 %collective-permute-done.10.upper = bf16[2,256,512]{2,1,0:T(8,128)(2,1)S(1)} collective-permute-done((bf16[2,256,512]{2,1,0:T(8,128)(2,1)S(1)}, bf16[2,256,512]{2,1,0:T(8,128)(2,1)S(1)}, u32[]{:S(2)}, u32[]{:S(2)}) %collective-permute-start.10) | collective-permute-done | bytes 524320 | tf_op jit(solution)/shard_map/ppermute | solution.py:30
  63.3 1.1 %own_part.1 = bf16[2,384,512]{2,1,0:T(8,128)(2,1)S(1)} custom-call(s32[7]{0:T(128)S(1)} %concatenate.7.scalars, bf16[4,2,128,128]{3,2,1,0:T(8,128)(2,1)S(1)} %sum.1.before, bf16[2,384,512]{2,1,0:T(8,128)(2,1)S(1)} %get-tuple-element.67.refs_1_.kept.refs_0_, bf16[2,384,512]{2,1,0:T(8,128)(2,1)S(1)} %collective-permute-done.7.refs_2_.got.refs_1_, ...), custom_call_target="tpu_custom_call" | custom-call | flops 1000000000 | tf_op jit(solution)/shard_map/own_part/pallas_call | solution.py:453
  65.0 0.8 %collective-permute-done.17.refs_2_ = bf16[2,128,128]{2,1,0:T(8,128)(2,1)S(1)} collective-permute-done((bf16[2,128,128]{2,1,0:T(8,128)(2,1)S(1)}, bf16[2,128,128]{2,1,0:T(8,128)(2,1)S(1)}, u32[]{:S(2)}, u32[]{:S(2)}) %collective-permute-start.17) | collective-permute-done | bytes 65568 | tf_op jit(solution)/shard_map/ppermute | solution.py:338
  65.8 1.9 %collective-permute-done.18.refs_3_ = bf16[2,128,128]{2,1,0:T(8,128)(2,1)S(1)} collective-permute-done((bf16[2,128,128]{2,1,0:T(8,128)(2,1)S(1)}, bf16[2,128,128]{2,1,0:T(8,128)(2,1)S(1)}, u32[]{:S(2)}, u32[]{:S(2)}) %collective-permute-start.18) | collective-permute-done | bytes 65568 | tf_op jit(solution)/shard_map/ppermute | solution.py:338
  67.7 0.7 probe_grad.1
  68.8 1.1 %pad_maximum_fusion = bf16[2,640,512]{2,1,0:T(8,128)(2,1)} fusion(bf16[2,128,512]{2,1,0:T(8,128)(2,1)S(1)} %slice_select_fusion, bf16[2,256,512]{2,1,0:T(8,128)(2,1)S(1)} %get-tuple-element.75, bf16[2,256,512]{2,1,0:T(8,128)(2,1)S(1)} %get-tuple-element.74), kind=kLoop, calls=%fused_computation | loop fusion | flops 3932160 | bytes 2621440 | tf_op jit(solution)/shard_map/concatenate | solution.py:464
  (33 shorter events, 3.4 us)
Async XLA Ops:
  0.6 1.3 %copy-start.1 = (bf16[2,640,512]{2,1,0:T(8,128)(2,1)S(1)}, bf16[2,640,512]{2,1,0:T(8,128)(2,1)}, u32[]{:S(2)}) copy-start(bf16[2,640,512]{2,1,0:T(8,128)(2,1)} %own.1) | copy-start | bytes 3932164
  2.0 8.3 %collective-permute-start.1 = (bf16[2,256,512]{2,1,0:T(8,128)(2,1)S(1)}, bf16[2,256,512]{2,1,0:T(8,128)(2,1)S(1)}, u32[]{:S(2)}, u32[]{:S(2)}) collective-permute-start(bf16[2,256,512]{2,1,0:T(8,128)(2,1)S(1)} %get-tuple-element.38), channel_id=1, source_target_pairs={{3,1},{4,0},{7,5},{6,2},{8,4},{11,9},{10,6},{12,8},{15,13},{14,10}... | collective-permute-start | bytes 1572872 | tf_op jit(solution)/shard_map/ppermute | solution.py:30
  4.2 19.1 %collective-permute-start.3 = (bf16[2,384,512]{2,1,0:T(8,128)(2,1)S(1)}, bf16[2,384,512]{2,1,0:T(8,128)(2,1)S(1)}, u32[]{:S(2)}, u32[]{:S(2)}) collective-permute-start(bf16[2,384,512]{2,1,0:T(8,128)(2,1)S(1)} %get-tuple-element.45), channel_id=1, source_target_pairs={{3,1},{4,0},{7,5},{6,2},{8,4},{11,9},{10,6},{12,8},{15,13},{14,10}... | collective-permute-start | bytes 2359304 | tf_op jit(solution)/shard_map/ppermute | solution.py:30
  7.0 2.7 %collective-permute-start = (s32[2]{0:T(128)S(1)}, s32[2]{0:T(128)S(1)}, u32[]{:S(2)}, u32[]{:S(2)}) collective-permute-start(s32[2]{0:T(128)S(1)} %pad_add_fusion), channel_id=1, source_target_pairs={{0,1},{1,0},{2,3},{3,2},{4,5},{5,4},{6,7},{7,6},{8,9},{9,8},{10,11... | collective-permute-start | bytes 32 | tf_op jit(solution)/shard_map/ppermute | solution.py:34
  10.3 5.6 %collective-permute-start.2 = (bf16[2,256,512]{2,1,0:T(8,128)(2,1)S(1)}, bf16[2,256,512]{2,1,0:T(8,128)(2,1)S(1)}, u32[]{:S(2)}, u32[]{:S(2)}) collective-permute-start(bf16[2,256,512]{2,1,0:T(8,128)(2,1)S(1)} %collective-permute-done.1.first_in), channel_id=1, source_target_pairs={{0,1},{1,0},{2,3},{3,2},{4,5},{5,4},{6,7},{7,6},{8,9},{9,8},{10,11... | collective-permute-start | bytes 1572872 | tf_op jit(solution)/shard_map/ppermute | solution.py:34
  13.8 13.4 %collective-permute-start.5 = (bf16[2,256,512]{2,1,0:T(8,128)(2,1)S(1)}, bf16[2,256,512]{2,1,0:T(8,128)(2,1)S(1)}, u32[]{:S(2)}, u32[]{:S(2)}) collective-permute-start(bf16[2,256,512]{2,1,0:T(8,128)(2,1)S(1)} %collective-permute-done.1.first_in), channel_id=1, source_target_pairs={{2,0},{5,1},{7,3},{6,4},{9,5},{11,7},{10,8},{13,9},{15,11},{14,12}... | collective-permute-start | bytes 1572872 | tf_op jit(solution)/shard_map/ppermute | solution.py:30
  15.9 1.6 %copy-start = (bf16[4,512,512]{2,1,0:T(8,128)(2,1)S(1)}, bf16[4,512,512]{2,1,0:T(8,128)(2,1)}, u32[]{:S(2)}) copy-start(bf16[4,512,512]{2,1,0:T(8,128)(2,1)} %constant.32.clone.dft) | copy-start | bytes 6291460
  17.5 1.2 %copy-start.3 = (bf16[2,512,512]{2,1,0:T(8,128)(2,1)S(1)}, bf16[2,512,512]{2,1,0:T(8,128)(2,1)}, u32[]{:S(2)}) copy-start(bf16[2,512,512]{2,1,0:T(8,128)(2,1)} %probe_in) | copy-start | bytes 3145732
  18.7 1.0 %copy-start.4 = (bf16[1,1,1,512,512]{4,3,2,1,0:T(8,128)(2,1)S(1)}, bf16[1,1,1,512,512]{4,3,2,1,0:T(8,128)(2,1)}, u32[]{:S(2)}) copy-start(bf16[1,1,1,512,512]{4,3,2,1,0:T(8,128)(2,1)} %param.9) | copy-start | bytes 1572868
  19.7 9.3 %copy-start.2 = (bf16[2,640,512]{2,1,0:T(8,128)(2,1)S(1)}, bf16[2,640,512]{2,1,0:T(8,128)(2,1)}, u32[]{:S(2)}) copy-start(bf16[2,640,512]{2,1,0:T(8,128)(2,1)} %own.1) | copy-start | bytes 3932164
  23.3 5.8 %collective-permute-start.4 = (bf16[2,384,512]{2,1,0:T(8,128)(2,1)S(1)}, bf16[2,384,512]{2,1,0:T(8,128)(2,1)S(1)}, u32[]{:S(2)}, u32[]{:S(2)}) collective-permute-start(bf16[2,384,512]{2,1,0:T(8,128)(2,1)S(1)} %collective-permute-done.3.second), channel_id=1, source_target_pairs={{0,1},{1,0},{2,3},{3,2},{4,5},{5,4},{6,7},{7,6},{8,9},{9,8},{10,11... | collective-permute-start | bytes 2359304 | tf_op jit(solution)/shard_map/ppermute | solution.py:34
  27.1 1.9 %collective-permute-start.6 = (bf16[2,256,512]{2,1,0:T(8,128)(2,1)S(1)}, bf16[2,256,512]{2,1,0:T(8,128)(2,1)S(1)}, u32[]{:S(2)}, u32[]{:S(2)}) collective-permute-start(bf16[2,256,512]{2,1,0:T(8,128)(2,1)S(1)} %collective-permute-done.5.third), channel_id=1, source_target_pairs={{0,1},{1,0},{2,3},{3,2},{4,5},{5,4},{6,7},{7,6},{8,9},{9,8},{10,11... | collective-permute-start | bytes 1572872 | tf_op jit(solution)/shard_map/ppermute | solution.py:34
  34.3 2.4 %collective-permute-start.7 = (bf16[2,384,512]{2,1,0:T(8,128)(2,1)S(1)}, bf16[2,384,512]{2,1,0:T(8,128)(2,1)S(1)}, u32[]{:S(2)}, u32[]{:S(2)}) collective-permute-start(bf16[2,384,512]{2,1,0:T(8,128)(2,1)S(1)} %get-tuple-element.68), channel_id=1, source_target_pairs={{0,1},{1,0},{2,3},{3,2},{4,5},{5,4},{6,7},{7,6},{8,9},{9,8},{10,11... | collective-permute-start | bytes 2359304 | tf_op jit(solution)/shard_map/ppermute | solution.py:34
  35.8 3.1 %collective-permute-start.8 = (bf16[2,4,2,128,128]{4,3,2,1,0:T(8,128)(2,1)S(1)}, bf16[2,4,2,128,128]{4,3,2,1,0:T(8,128)(2,1)S(1)}, u32[]{:S(2)}, u32[]{:S(2)}) collective-permute-start(bf16[2,4,2,128,128]{4,3,2,1,0:T(8,128)(2,1)S(1)} %get-tuple-element.66.refs_0_), channel_id=1, source_target_pairs={{0,1},{1,0},{2,3},{3,2},{4,5},{5,4},{6,7},{7,6},{8,9},{9,8},{10,11... | collective-permute-start | bytes 1572872 | tf_op jit(solution)/shard_map/ppermute | solution.py:34
  37.6 13.0 %collective-permute-start.12 = (bf16[2,256,512]{2,1,0:T(8,128)(2,1)S(1)}, bf16[2,256,512]{2,1,0:T(8,128)(2,1)S(1)}, u32[]{:S(2)}, u32[]{:S(2)}) collective-permute-start(bf16[2,256,512]{2,1,0:T(8,128)(2,1)S(1)} %diag_part.1.diag), channel_id=1, source_target_pairs={{1,3},{0,4},{2,6},{5,7},{4,8},{6,10},{9,11},{8,12},{10,14},{13,15}... | collective-permute-start | bytes 1572872 | tf_op jit(solution)/shard_map/ppermute | solution.py:30
  39.6 13.8 %collective-permute-start.9 = (bf16[4,2,128,128]{3,2,1,0:T(8,128)(2,1)S(1)}, bf16[4,2,128,128]{3,2,1,0:T(8,128)(2,1)S(1)}, u32[]{:S(2)}, u32[]{:S(2)}) collective-permute-start(bf16[4,2,128,128]{3,2,1,0:T(8,128)(2,1)S(1)} %get-tuple-element.71), channel_id=1, source_target_pairs={{0,2},{2,0},{1,3},{3,1},{4,6},{6,4},{5,7},{7,5},{8,10},{10,8},{9,1... | collective-permute-start | bytes 786440 | tf_op jit(solution)/shard_map/ppermute | solution.py:439
  42.8 20.5 %collective-permute-start.10 = (bf16[2,256,512]{2,1,0:T(8,128)(2,1)S(1)}, bf16[2,256,512]{2,1,0:T(8,128)(2,1)S(1)}, u32[]{:S(2)}, u32[]{:S(2)}) collective-permute-start(bf16[2,256,512]{2,1,0:T(8,128)(2,1)S(1)} %get-tuple-element.72), channel_id=1, source_target_pairs={{1,3},{0,4},{2,6},{5,7},{4,8},{6,10},{9,11},{8,12},{10,14},{13,15}... | collective-permute-start | bytes 1572872 | tf_op jit(solution)/shard_map/ppermute | solution.py:30
  44.1 12.2 %collective-permute-start.11 = (bf16[2,128,512]{2,1,0:T(8,128)(2,1)S(1)}, bf16[2,128,512]{2,1,0:T(8,128)(2,1)S(1)}, u32[]{:S(2)}, u32[]{:S(2)}) collective-permute-start(bf16[2,128,512]{2,1,0:T(8,128)(2,1)S(1)} %get-tuple-element.73), channel_id=1, source_target_pairs={{0,4},{2,6},{4,8},{6,10},{8,12},{10,14},{16,20},{18,22},{20,24},{2... | collective-permute-start | bytes 786440 | tf_op jit(solution)/shard_map/ppermute | solution.py:30
  51.5 13.5 %collective-permute-start.13 = (bf16[2,256,512]{2,1,0:T(8,128)(2,1)S(1)}, bf16[2,256,512]{2,1,0:T(8,128)(2,1)S(1)}, u32[]{:S(2)}, u32[]{:S(2)}) collective-permute-start(bf16[2,256,512]{2,1,0:T(8,128)(2,1)S(1)} %later_part.1), channel_id=1, source_target_pairs={{1,5},{0,2},{3,7},{5,9},{4,6},{7,11},{9,13},{8,10},{11,15},{12,14}... | collective-permute-start | bytes 1572872 | tf_op jit(solution)/shard_map/ppermute | solution.py:30
  53.5 11.5 %collective-permute-start.16 = (bf16[2,128,128]{2,1,0:T(8,128)(2,1)S(1)}, bf16[2,128,128]{2,1,0:T(8,128)(2,1)S(1)}, u32[]{:S(2)}, u32[]{:S(2)}) collective-permute-start(bf16[2,128,128]{2,1,0:T(8,128)(2,1)S(1)} %get-tuple-element.78), channel_id=1, source_target_pairs={{0,4},{4,0},{8,12},{12,8},{1,5},{5,1},{9,13},{13,9},{2,6},{6,2},{1... | collective-permute-start | bytes 196616 | tf_op jit(solution)/shard_map/ppermute | solution.py:338
  53.6 12.2 %collective-permute-start.17 = (bf16[2,128,128]{2,1,0:T(8,128)(2,1)S(1)}, bf16[2,128,128]{2,1,0:T(8,128)(2,1)S(1)}, u32[]{:S(2)}, u32[]{:S(2)}) collective-permute-start(bf16[2,128,128]{2,1,0:T(8,128)(2,1)S(1)} %get-tuple-element.77), channel_id=1, source_target_pairs={{0,8},{4,12},{8,0},{12,4},{1,9},{5,13},{9,1},{13,5},{2,10},{6,14},... | collective-permute-start | bytes 196616 | tf_op jit(solution)/shard_map/ppermute | solution.py:338
  56.2 11.5 %collective-permute-start.18 = (bf16[2,128,128]{2,1,0:T(8,128)(2,1)S(1)}, bf16[2,128,128]{2,1,0:T(8,128)(2,1)S(1)}, u32[]{:S(2)}, u32[]{:S(2)}) collective-permute-start(bf16[2,128,128]{2,1,0:T(8,128)(2,1)S(1)} %get-tuple-element.76), channel_id=1, source_target_pairs={{0,12},{4,8},{8,4},{12,0},{1,13},{5,9},{9,5},{13,1},{2,14},{6,10},... | collective-permute-start | bytes 196616 | tf_op jit(solution)/shard_map/ppermute | solution.py:338
  64.3 4.1 %collective-permute-start.14 = (bf16[2,384,512]{2,1,0:T(8,128)(2,1)S(1)}, bf16[2,384,512]{2,1,0:T(8,128)(2,1)S(1)}, u32[]{:S(2)}, u32[]{:S(2)}) collective-permute-start(bf16[2,384,512]{2,1,0:T(8,128)(2,1)S(1)} %own_part.1), channel_id=1, source_target_pairs={{0,1},{1,0},{2,3},{3,2},{4,5},{5,4},{6,7},{7,6},{8,9},{9,8},{10,11... | collective-permute-start | bytes 2359304 | tf_op jit(solution)/shard_map/ppermute | solution.py:34
  64.9 3.5 %collective-permute-start.15 = (bf16[2,256,512]{2,1,0:T(8,128)(2,1)S(1)}, bf16[2,256,512]{2,1,0:T(8,128)(2,1)S(1)}, u32[]{:S(2)}, u32[]{:S(2)}) collective-permute-start(bf16[2,256,512]{2,1,0:T(8,128)(2,1)S(1)} %collective-permute-done.13), channel_id=1, source_target_pairs={{0,1},{1,0},{2,3},{3,2},{4,5},{5,4},{6,7},{7,6},{8,9},{9,8},{10,11... | collective-permute-start | bytes 1572872 | tf_op jit(solution)/shard_map/ppermute | solution.py:34
